TPU v7x, 128 devices: a whole 4x4x4 slice. The times are simulated.
128 devices in a mesh: sect: 2 (over x_lo), rr: 8 (over x_hi, y), row: 8 (over z, core).
Axes of the slice: x: 4 (x_hi: 2, x_lo: 2; x = x_hi * 2 + x_lo), y: 4, z: 4, core: 2. Of those that a mesh axis runs over, the one named last changes fastest.
Arguments:
- packet: float32 [2, 512, 256, 512], P('sect', 'rr', 'row'), may hold values from -6 to 6
- previous: float32 [2, 512, 256, 512], P('sect', 'rr', 'row'), may hold values from -6 to 6
- potential: float32 [2, 512, 256, 512], P('sect', 'rr', 'row'), may hold values from 0 to 4
- rotation: float32 [2, 512, 256], P('sect', 'rr', 'row'), may hold values from 0.1 to 1
- angular: float32 [2, 512, 512], P('sect'), as said below
- damping: float32 [2, 512, 256], P('sect', 'rr', 'row'), may hold values from 0.3 to 0.9
- absorber: int32 [2, 512, 256], P('sect', 'rr', 'row'), may hold values from 0 to 1, as said below
- stencil_index: int32 [4, 512, 256], P(None, 'rr', 'row'), may hold values from 0 to 511
- stencil_weight: float32 [4, 512, 256], P(None, 'rr', 'row'), may hold values from -3 to 3
Outputs:
- latest: float32 [2, 512, 256, 512], P('sect', 'rr', 'row')
- earlier: float32 [2, 512, 256, 512], P('sect', 'rr', 'row')
Inputs may be any that keep to these rules, and one draw needn't show every extreme that they name: `absorber`: zero at every point whose R index is below 510. `angular`: symmetric.
All inputs are finite; a program needn't handle non-finite values.
Results may differ from a plain program's by a relative error of at most 0.0001.
Values sent between devices are 32-bit elements; how exact they have to be, the bound alone decides.
No kernel may reach another device: no remote copies, remote signals or barrier semaphores. Data moves between devices by JAX's collectives and lax.ppermute only.
A program may use at most 128 MiB of HBM per device.

v0:
```python
import jax
import jax.numpy as jnp
from jax import lax
from jax.sharding import PartitionSpec as P

BAND = 2
ITERS = 2


kinetic_radial = 0.5
kinetic_vibration = 0.5
energy_middle = 7.5
energy_half = 8.0


def extended(cells, sides, width):
    for axis, dim in sides:
        count = lax.axis_size(axis)
        ends = count - 1
        head = lax.slice_in_dim(cells, 0, width, axis=dim)
        tail = lax.slice_in_dim(cells, cells.shape[dim] - width, cells.shape[dim], axis=dim)
        cells = jnp.concatenate(
            [
                lax.ppermute(tail, axis, [(i, (i + 1) % count) for i in range(ends)]),
                cells,
                lax.ppermute(head, axis, [((i + 1) % count, i) for i in range(ends)]),
            ],
            axis=dim,
        )
    return cells


def from_behind(value, axis, steps):
    count = lax.axis_size(axis)
    initial, last = (max(0, -steps), min(count, count - steps))
    return lax.ppermute(value, axis, [(source, source + steps) for source in range(initial, last)])


def curvature(padded, count, axis):
    parts = [lax.slice_in_dim(padded, k, k + count, axis=axis) for k in range(5)]
    return (-parts[0] + 16.0 * parts[1] - 30.0 * parts[2] + 16.0 * parts[3] - parts[4]) / 12.0


def scaled_hamilton(field, rotation, angular, potential):
    count_r = field.shape[0]
    count_v = field.shape[1]
    width = field.shape[2]
    padded = extended(field, (("rr", 0), ("row", 1)), 2)
    radial = curvature(padded[:, 2:-2], count_r, 0)
    vibration = curvature(padded[2:-2], count_v, 1)
    turned = jnp.dot(field.reshape(-1, width), angular, precision=lax.Precision.HIGHEST).reshape(
        field.shape
    )
    energy = (
        -kinetic_radial * radial
        - kinetic_vibration * vibration
        + rotation[:, :, None] * turned
        + potential * field
    )
    return (energy - energy_middle * field) / energy_half


def interpolate(band_table, stencil_index, stencil_weight, width):
    count_r = stencil_index.shape[1]
    count_v = stencil_index.shape[2]
    source = jnp.zeros((count_r, count_v, width), jnp.float32)
    for stencil in range(4):
        picked = jnp.take(band_table, stencil_index[stencil].reshape(-1), axis=0).reshape(
            count_r, count_v, width
        )
        source = source + stencil_weight[stencil][:, :, None] * picked
    return source


def local(
    packet, previous, potential, rotation, angular, damping, absorber, stencil_index, stencil_weight
):
    count_r = packet.shape[1]
    count_v = packet.shape[2]
    width = packet.shape[3]
    retained = (1.0 - absorber[0].astype(jnp.float32) * (1.0 - damping[0]))[:, :, None]
    is_product = (lax.axis_index("sect") == 1).astype(jnp.float32)
    current = packet[0]
    earlier = previous[0]
    for iteration in range(ITERS):
        scaled = scaled_hamilton(current, rotation[0], angular[0], potential[0])
        update = 2.0 * scaled - retained * earlier
        leaving = (1.0 - retained) * update
        band_piece = jnp.transpose(leaving[count_r - BAND :], (1, 0, 2)).reshape(
            count_v * BAND, width
        )
        crossed = from_behind(band_piece, "sect", 1)
        gathered = lax.all_gather(crossed, ("rr", "row"), axis=0, tiled=True)
        offset = (lax.axis_size("rr") - 1) * lax.axis_size("row") * count_v * BAND
        band_table = gathered[offset:]
        source = interpolate(band_table, stencil_index, stencil_weight, width)
        advanced = retained * update + is_product * source
        earlier = current
        current = advanced
    return (current[None], earlier[None])


def solution(mesh):
    in_specs = (
        P("sect", "rr", "row", None),
        P("sect", "rr", "row", None),
        P("sect", "rr", "row", None),
        P("sect", "rr", "row"),
        P("sect", None, None),
        P("sect", "rr", "row"),
        P("sect", "rr", "row"),
        P(None, "rr", "row"),
        P(None, "rr", "row"),
    )
    out_specs = (P("sect", "rr", "row", None), P("sect", "rr", "row", None))
    return jax.shard_map(local, mesh=mesh, in_specs=in_specs, out_specs=out_specs, check_vma=False)
```

profile of v0, /device:TPU:7, one launch (start us, length us, event | category | flops | bytes accessed | tf_op | source)
XLA Modules:
  0.0 391.1 jit_solution(8478856652263088424)
XLA Ops:
  7.3 1.1 slice_bitcast_fusion.1
  8.3 3.2 collective-permute-start
  11.5 5.7 %collective-permute-start.1 = (f32[2,32,512]{2,1,0:T(8,128)S(1)}, f32[2,32,512]{2,1,0:T(8,128)S(1)}, u32[]{:S(2)}, u32[]{:S(2)}) collective-permute-start(f32[2,32,512]{2,1,0:T(8,128)S(1)} %get-tuple-element.16), channel_id=1, source_target_pairs={{8,0},{16,8},{24,16},{32,24},{40,32},{48,40},{56,48},{9,1},{17,9},... | collective-permute-start | bytes 393224 | tf_op jit(solution)/shard_map/ppermute | solution.py:26
  17.2 1.0 collective-permute-done
  18.2 1.0 collective-permute-done.1
  19.2 1.8 pad_maximum_fusion.11
  21.0 5.2 %collective-permute-start.2 = (f32[68,2,512]{2,1,0:T(2,128)S(1)}, f32[68,2,512]{2,1,0:T(2,128)S(1)}, u32[]{:S(2)}, u32[]{:S(2)}) collective-permute-start(f32[68,2,512]{2,1,0:T(2,128)S(1)} %get-tuple-element.11), channel_id=1, source_target_pairs={{0,1},{1,2},{2,3},{3,4},{4,5},{5,6},{6,7},{8,9},{9,10},{10,11},{11... | collective-permute-start | bytes 835592 | tf_op jit(solution)/shard_map/ppermute | solution.py:24
  26.2 1.9 collective-permute-start.3
  28.5 1.2 collective-permute-done.2
  29.7 4.4 %collective-permute-done.3 = f32[68,2,512]{2,1,0:T(2,128)S(1)} collective-permute-done((f32[68,2,512]{2,1,0:T(2,128)S(1)}, f32[68,2,512]{2,1,0:T(2,128)S(1)}, u32[]{:S(2)}, u32[]{:S(2)}) %collective-permute-start.3) | collective-permute-done | bytes 278560 | tf_op jit(solution)/shard_map/ppermute | solution.py:26
  34.1 7.3 %maximum_maximum_fusion = (f32[68,34,512]{2,1,0:T(8,128)}, f32[68,34,512]{2,1,0:T(8,128)}) fusion(f32[2,32,512]{2,1,0:T(8,128)S(1)} %collective-permute-done.1, f32[64,32,512]{2,1,0:T(8,128)} %bitcast.54, f32[2,32,512]{2,1,0:T(8,128)S(1)} %collective-permute-done, f32[68,2,512]{2,1,0:T(2,128)S(1)} %collective-permute-done.2, ...), kind=kLoop, calls=%fused_computation.8 | loop fusion | flops 7102464 | bytes 14483456 | tf_op jit(solution)/shard_map/concatenate | solution.py:22
  41.5 17.0 %fusion.25 = f32[64,32,512]{2,1,0:T(8,128)} fusion(f32[64,32,512]{2,1,0:T(8,128)S(1)} %bitcast.55, f32[2,32,512]{2,1,0:T(8,128)S(1)} %collective-permute-done.1, f32[2,32,512]{2,1,0:T(8,128)S(1)} %collective-permute-done, f32[68,34,512]{2,1,0:T(8,128)} %get-tuple-element.10, f32[68,34,512]{2,1,0:T(8,128)} %get-tuple-element.9, ...), kind=kOutput, calls=%fused_computation.45 | convolution fusion | flops 6474956800 | bytes 39124992 | tf_op jit(solution)/shard_map/dot_general | solution.py:51
  58.4 1.0 fusion.43
  59.4 0.1 copy.23
  59.5 0.1 reshape.79
  59.6 1.3 collective-permute-start.4
  60.9 4.4 %collective-permute-done.4 = f32[64,512]{1,0:T(8,128)S(1)} collective-permute-done((f32[64,512]{1,0:T(8,128)S(1)}, f32[64,512]{1,0:T(8,128)S(1)}, u32[]{:S(2)}, u32[]{:S(2)}) %collective-permute-start.4) | collective-permute-done | bytes 131104 | tf_op jit(solution)/shard_map/ppermute | solution.py:36
  65.3 0.7 copy-done.12
  67.2 81.8 %all-gather.3.cloned.1.call-done = f32[4096,512]{1,0:T(8,128)} async-done(((f32[64,512]{1,0:T(8,128)}), f32[4096,512]{1,0:T(8,128)}) %all-gather.3.cloned.1.call-update) | async-done | bytes 8388624 | tf_op jit(solution)/shard_map/all_gather | solution.py:93
  149.0 1.3 slice.218
  150.3 8.9 %gather_fusion.3 = f32[2048,512]{1,0:T(8,128)} fusion(f32[512,512]{1,0:T(8,128)S(1)} %slice.218, s32[2048]{0:T(1024)S(1)} %fusion.47), kind=kCustom, calls=%fused_computation.3.clone | custom fusion | bytes 8396800 | tf_op jit(solution)/shard_map/jit(_take)/gather | solution.py:68
  159.2 8.9 %gather_fusion.2 = f32[2048,512]{1,0:T(8,128)} fusion(f32[512,512]{1,0:T(8,128)S(1)} %slice.218, s32[2048]{0:T(1024)S(1)} %fusion.46), kind=kCustom, calls=%fused_computation.2.clone | custom fusion | bytes 8396800 | tf_op jit(solution)/shard_map/jit(_take)/gather | solution.py:68
  168.1 8.9 %gather_fusion.1 = f32[2048,512]{1,0:T(8,128)} fusion(f32[512,512]{1,0:T(8,128)S(1)} %slice.218, s32[2048]{0:T(1024)S(1)} %fusion.45), kind=kCustom, calls=%fused_computation.1.clone | custom fusion | bytes 8396800 | tf_op jit(solution)/shard_map/jit(_take)/gather | solution.py:68
  177.0 8.9 %gather_fusion = f32[2048,512]{1,0:T(8,128)} fusion(f32[512,512]{1,0:T(8,128)S(1)} %slice.218, s32[2048]{0:T(1024)S(1)} %fusion.44), kind=kCustom, calls=%fused_computation.clone | custom fusion | bytes 8396800 | tf_op jit(solution)/shard_map/jit(_take)/gather | solution.py:68
  185.9 2.6 broadcast_select_fusion.4
  188.5 0.8 copy-done.9
  189.4 0.5 broadcast_select_fusion.5
  189.8 1.7 copy-done.8
  191.5 0.5 broadcast_select_fusion.6
  192.0 1.7 copy-done.7
  193.7 0.5 broadcast_select_fusion.7
  194.2 1.7 copy-done.10
  195.9 1.9 multiply_add_fusion
  197.9 2.9 collective-permute-start.5
  200.8 6.0 %collective-permute-start.6 = (f32[2,32,512]{2,1,0:T(8,128)S(1)}, f32[2,32,512]{2,1,0:T(8,128)S(1)}, u32[]{:S(2)}, u32[]{:S(2)}) collective-permute-start(f32[2,32,512]{2,1,0:T(8,128)S(1)} %get-tuple-element.14), channel_id=1, source_target_pairs={{8,0},{16,8},{24,16},{32,24},{40,32},{48,40},{56,48},{9,1},{17,9},... | collective-permute-start | bytes 393224 | tf_op jit(solution)/shard_map/ppermute | solution.py:26
  206.8 1.4 collective-permute-done.5
  208.2 0.9 collective-permute-done.6
  209.1 0.3 pad_maximum_fusion.8
  209.4 4.4 %collective-permute-start.7 = (f32[68,2,512]{2,1,0:T(2,128)S(1)}, f32[68,2,512]{2,1,0:T(2,128)S(1)}, u32[]{:S(2)}, u32[]{:S(2)}) collective-permute-start(f32[68,2,512]{2,1,0:T(2,128)S(1)} %get-tuple-element.7), channel_id=1, source_target_pairs={{0,1},{1,2},{2,3},{3,4},{4,5},{5,6},{6,7},{8,9},{9,10},{10,11},{11... | collective-permute-start | bytes 835592 | tf_op jit(solution)/shard_map/ppermute | solution.py:24
  213.8 2.1 collective-permute-start.8
  215.9 1.4 collective-permute-done.7
  217.3 4.4 %collective-permute-done.8 = f32[68,2,512]{2,1,0:T(2,128)S(1)} collective-permute-done((f32[68,2,512]{2,1,0:T(2,128)S(1)}, f32[68,2,512]{2,1,0:T(2,128)S(1)}, u32[]{:S(2)}, u32[]{:S(2)}) %collective-permute-start.8) | collective-permute-done | bytes 278560 | tf_op jit(solution)/shard_map/ppermute | solution.py:26
  221.7 5.1 %maximum_maximum_fusion.1 = (f32[68,34,512]{2,1,0:T(8,128)}, f32[68,34,512]{2,1,0:T(8,128)}) fusion(f32[2,32,512]{2,1,0:T(8,128)S(1)} %collective-permute-done.6, f32[64,32,512]{2,1,0:T(8,128)S(1)} %multiply_add_fusion, f32[2,32,512]{2,1,0:T(8,128)S(1)} %collective-permute-done.5, f32[68,2,512]{2,1,0:T(2,128)S(1)} %collective-permute-done.7, ...), kind=kLoop, calls=%fused_computation.10 | loop fusion | flops 7102464 | bytes 14483456 | tf_op jit(solution)/shard_map/concatenate | solution.py:22
  226.8 17.0 %fusion.10 = f32[64,32,512]{2,1,0:T(8,128)} fusion(f32[64,32,512]{2,1,0:T(8,128)S(1)} %multiply_add_fusion, f32[2,32,512]{2,1,0:T(8,128)S(1)} %collective-permute-done.6, f32[2,32,512]{2,1,0:T(8,128)S(1)} %collective-permute-done.5, f32[68,34,512]{2,1,0:T(8,128)} %get-tuple-element.6, f32[68,34,512]{2,1,0:T(8,128)} %get-tuple-element.5, ...), kind=kOutput, calls=%fused_computation.30 | convolution fusion | flops 6474956800 | bytes 39124992 | tf_op jit(solution)/shard_map/dot_general | solution.py:51
  243.7 1.0 fusion.42
  244.7 0.1 copy.30
  244.9 1.3 collective-permute-start.9
  246.2 4.4 %collective-permute-done.9 = f32[64,512]{1,0:T(8,128)S(1)} collective-permute-done((f32[64,512]{1,0:T(8,128)S(1)}, f32[64,512]{1,0:T(8,128)S(1)}, u32[]{:S(2)}, u32[]{:S(2)}) %collective-permute-start.9) | collective-permute-done | bytes 131104 | tf_op jit(solution)/shard_map/ppermute | solution.py:36
  250.6 0.6 copy-done.13
  251.3 82.7 %all-gather.5.cloned.1.call-done = f32[4096,512]{1,0:T(8,128)} async-done(((f32[64,512]{1,0:T(8,128)}), f32[4096,512]{1,0:T(8,128)}) %all-gather.5.cloned.1.call-update) | async-done | bytes 8388624 | tf_op jit(solution)/shard_map/all_gather | solution.py:93
  334.0 1.3 slice.231
  335.3 8.9 %gather_fusion.7 = f32[2048,512]{1,0:T(8,128)} fusion(f32[512,512]{1,0:T(8,128)S(1)} %slice.231, s32[2048]{0:T(1024)S(1)} %fusion.47), kind=kCustom, calls=%fused_computation.7.clone | custom fusion | bytes 8396800 | tf_op jit(solution)/shard_map/jit(_take)/gather | solution.py:68
  344.2 8.9 %gather_fusion.6 = f32[2048,512]{1,0:T(8,128)} fusion(f32[512,512]{1,0:T(8,128)S(1)} %slice.231, s32[2048]{0:T(1024)S(1)} %fusion.46), kind=kCustom, calls=%fused_computation.6.clone | custom fusion | bytes 8396800 | tf_op jit(solution)/shard_map/jit(_take)/gather | solution.py:68
  353.1 8.9 %gather_fusion.5 = f32[2048,512]{1,0:T(8,128)} fusion(f32[512,512]{1,0:T(8,128)S(1)} %slice.231, s32[2048]{0:T(1024)S(1)} %fusion.45), kind=kCustom, calls=%fused_computation.5.clone | custom fusion | bytes 8396800 | tf_op jit(solution)/shard_map/jit(_take)/gather | solution.py:68
  362.0 8.9 %gather_fusion.4 = f32[2048,512]{1,0:T(8,128)} fusion(f32[512,512]{1,0:T(8,128)S(1)} %slice.231, s32[2048]{0:T(1024)S(1)} %fusion.44), kind=kCustom, calls=%fused_computation.4.clone | custom fusion | bytes 8396800 | tf_op jit(solution)/shard_map/jit(_take)/gather | solution.py:68
  370.9 2.6 broadcast_select_fusion
  373.5 0.8 copy-done.6
  374.3 0.5 broadcast_select_fusion.1
  374.8 1.7 copy-done.5
  376.5 0.5 broadcast_select_fusion.2
  377.0 1.7 copy-done.4
  378.7 0.5 broadcast_select_fusion.3
  379.2 1.7 copy-done.11
  380.9 3.4 add_bitcast_fusion
  (61 shorter events, 1.6 us)
Async XLA Ops:
  7.2 34.3 %copy-start = (f32[1,512,512]{2,1,0:T(8,128)S(1)}, f32[1,512,512]{2,1,0:T(8,128)}, u32[]{:S(2)}) copy-start(f32[1,512,512]{2,1,0:T(8,128)} %param.15) | copy-start | bytes 3145732
  7.2 21.0 %copy-start.16 = (f32[1,64,32]{1,2,0:T(8,128)S(1)}, f32[1,64,32]{1,2,0:T(8,128)}, u32[]{:S(2)}) copy-start(f32[1,64,32]{1,2,0:T(8,128)} %param.14) | copy-start | bytes 24580
  7.2 21.0 %copy-start.18 = (s32[1,64,32]{1,2,0:T(8,128)S(1)}, s32[1,64,32]{1,2,0:T(8,128)}, u32[]{:S(2)}) copy-start(s32[1,64,32]{1,2,0:T(8,128)} %param.17) | copy-start | bytes 24580
  7.2 21.0 %copy-start.17 = (f32[1,64,32]{1,2,0:T(8,128)S(1)}, f32[1,64,32]{1,2,0:T(8,128)}, u32[]{:S(2)}) copy-start(f32[1,64,32]{1,2,0:T(8,128)} %param.16) | copy-start | bytes 24580
  7.2 141.8 %all-gather.3.cloned.1.call-start = ((), (), s32[]{:S(2)}) async-start(), calls=%async_computation | async-start | bytes 8519680 | tf_op jit(solution)/shard_map/all_gather | solution.py:93
  8.3 9.9 %collective-permute-start = (f32[2,32,512]{2,1,0:T(8,128)S(1)}, f32[2,32,512]{2,1,0:T(8,128)S(1)}, u32[]{:S(2)}, u32[]{:S(2)}) collective-permute-start(f32[2,32,512]{2,1,0:T(8,128)S(1)} %get-tuple-element.15), channel_id=1, source_target_pairs={{0,8},{8,16},{16,24},{24,32},{32,40},{40,48},{48,56},{1,9},{9,17},... | collective-permute-start | bytes 393224 | tf_op jit(solution)/shard_map/ppermute | solution.py:24
  11.5 7.6 %collective-permute-start.1 = (f32[2,32,512]{2,1,0:T(8,128)S(1)}, f32[2,32,512]{2,1,0:T(8,128)S(1)}, u32[]{:S(2)}, u32[]{:S(2)}) collective-permute-start(f32[2,32,512]{2,1,0:T(8,128)S(1)} %get-tuple-element.16), channel_id=1, source_target_pairs={{8,0},{16,8},{24,16},{32,24},{40,32},{48,40},{56,48},{9,1},{17,9},... | collective-permute-start | bytes 393224 | tf_op jit(solution)/shard_map/ppermute | solution.py:26
  21.0 8.7 %collective-permute-start.2 = (f32[68,2,512]{2,1,0:T(2,128)S(1)}, f32[68,2,512]{2,1,0:T(2,128)S(1)}, u32[]{:S(2)}, u32[]{:S(2)}) collective-permute-start(f32[68,2,512]{2,1,0:T(2,128)S(1)} %get-tuple-element.11), channel_id=1, source_target_pairs={{0,1},{1,2},{2,3},{3,4},{4,5},{5,6},{6,7},{8,9},{9,10},{10,11},{11... | collective-permute-start | bytes 835592 | tf_op jit(solution)/shard_map/ppermute | solution.py:24
  26.2 7.9 %collective-permute-start.3 = (f32[68,2,512]{2,1,0:T(2,128)S(1)}, f32[68,2,512]{2,1,0:T(2,128)S(1)}, u32[]{:S(2)}, u32[]{:S(2)}) collective-permute-start(f32[68,2,512]{2,1,0:T(2,128)S(1)} %get-tuple-element.12), channel_id=1, source_target_pairs={{1,0},{2,1},{3,2},{4,3},{5,4},{6,5},{7,6},{9,8},{10,9},{11,10},{12... | collective-permute-start | bytes 835592 | tf_op jit(solution)/shard_map/ppermute | solution.py:26
  28.5 12.9 %copy-start.3 = (f32[1,64,32,512]{3,2,1,0:T(8,128)S(1)}, f32[1,64,32,512]{3,2,1,0:T(8,128)}, u32[]{:S(2)}) copy-start(f32[1,64,32,512]{3,2,1,0:T(8,128)} %param.11) | copy-start | bytes 12582916
  41.4 24.6 %copy-start.14 = (s32[4,64,32]{1,2,0:T(8,128)S(1)}, s32[4,64,32]{1,2,0:T(8,128)}, u32[]{:S(2)}) copy-start(s32[4,64,32]{1,2,0:T(8,128)} %param.18) | copy-start | bytes 98308
  41.5 25.3 %copy-start.15 = (f32[4,64,32]{1,2,0:T(8,128)S(1)}, f32[4,64,32]{1,2,0:T(8,128)}, u32[]{:S(2)}) copy-start(f32[4,64,32]{1,2,0:T(8,128)} %param.19) | copy-start | bytes 98308
  59.6 5.7 %collective-permute-start.4 = (f32[64,512]{1,0:T(8,128)S(1)}, f32[64,512]{1,0:T(8,128)S(1)}, u32[]{:S(2)}, u32[]{:S(2)}) collective-permute-start(f32[64,512]{1,0:T(8,128)S(1)} %reshape.79), channel_id=1, source_target_pairs={{0,64},{1,65},{2,66},{3,67},{4,68},{5,69},{6,70},{7,71},{8,72},{9,... | collective-permute-start | bytes 393224 | tf_op jit(solution)/shard_map/ppermute | solution.py:36
  65.3 0.7 copy-start.12
  66.0 267.9 %all-gather.5.cloned.1.call-start = ((), (), s32[]{:S(2)}) async-start(), calls=%async_computation.1 | async-start | bytes 8519680 | tf_op jit(solution)/shard_map/all_gather | solution.py:93
  185.9 3.4 copy-start.9
  189.3 2.2 copy-start.8
  191.5 2.2 copy-start.7
  193.7 2.2 copy-start.10
  197.9 28.9 %copy-start.2 = (f32[64,32,512]{2,1,0:T(8,128)}, f32[64,32,512]{2,1,0:T(8,128)S(1)}, u32[]{:S(2)}) copy-start(f32[64,32,512]{2,1,0:T(8,128)S(1)} %multiply_add_fusion) | copy-start | bytes 12582916
  197.9 10.3 %collective-permute-start.5 = (f32[2,32,512]{2,1,0:T(8,128)S(1)}, f32[2,32,512]{2,1,0:T(8,128)S(1)}, u32[]{:S(2)}, u32[]{:S(2)}) collective-permute-start(f32[2,32,512]{2,1,0:T(8,128)S(1)} %get-tuple-element.13), channel_id=1, source_target_pairs={{0,8},{8,16},{16,24},{24,32},{32,40},{40,48},{48,56},{1,9},{9,17},... | collective-permute-start | bytes 393224 | tf_op jit(solution)/shard_map/ppermute | solution.py:24
  200.8 8.3 %collective-permute-start.6 = (f32[2,32,512]{2,1,0:T(8,128)S(1)}, f32[2,32,512]{2,1,0:T(8,128)S(1)}, u32[]{:S(2)}, u32[]{:S(2)}) collective-permute-start(f32[2,32,512]{2,1,0:T(8,128)S(1)} %get-tuple-element.14), channel_id=1, source_target_pairs={{8,0},{16,8},{24,16},{32,24},{40,32},{48,40},{56,48},{9,1},{17,9},... | collective-permute-start | bytes 393224 | tf_op jit(solution)/shard_map/ppermute | solution.py:26
  209.4 7.9 %collective-permute-start.7 = (f32[68,2,512]{2,1,0:T(2,128)S(1)}, f32[68,2,512]{2,1,0:T(2,128)S(1)}, u32[]{:S(2)}, u32[]{:S(2)}) collective-permute-start(f32[68,2,512]{2,1,0:T(2,128)S(1)} %get-tuple-element.7), channel_id=1, source_target_pairs={{0,1},{1,2},{2,3},{3,4},{4,5},{5,6},{6,7},{8,9},{9,10},{10,11},{11... | collective-permute-start | bytes 835592 | tf_op jit(solution)/shard_map/ppermute | solution.py:24
  213.8 7.9 %collective-permute-start.8 = (f32[68,2,512]{2,1,0:T(2,128)S(1)}, f32[68,2,512]{2,1,0:T(2,128)S(1)}, u32[]{:S(2)}, u32[]{:S(2)}) collective-permute-start(f32[68,2,512]{2,1,0:T(2,128)S(1)} %get-tuple-element.8), channel_id=1, source_target_pairs={{1,0},{2,1},{3,2},{4,3},{5,4},{6,5},{7,6},{9,8},{10,9},{11,10},{12... | collective-permute-start | bytes 835592 | tf_op jit(solution)/shard_map/ppermute | solution.py:26
  244.9 5.7 %collective-permute-start.9 = (f32[64,512]{1,0:T(8,128)S(1)}, f32[64,512]{1,0:T(8,128)S(1)}, u32[]{:S(2)}, u32[]{:S(2)}) collective-permute-start(f32[64,512]{1,0:T(8,128)S(1)} %reshape.84), channel_id=1, source_target_pairs={{0,64},{1,65},{2,66},{3,67},{4,68},{5,69},{6,70},{7,71},{8,72},{9,... | collective-permute-start | bytes 393224 | tf_op jit(solution)/shard_map/ppermute | solution.py:36
  250.6 0.7 copy-start.13
  370.9 3.4 copy-start.6
  374.3 2.2 copy-start.5
  376.5 2.2 copy-start.4
  378.7 2.2 copy-start.11
  380.9 3.4 copy-start.1
Sparse Core Ops, SparseCore 0:
  66.1 82.8 all-gather.2
  251.4 82.4 all-gather.4
where the time goes:
time: 394 us; the launch traced here: 391 us
  waiting for transfers between devices  189 us (48%)
  local copies, waits for them, and re-layouts  89.9 us (23%)
  starting transfers between devices  34.1 us (9%)
  matrix products  33.9 us (9%)
  other arithmetic  29.9 us (8%)
  between operations  14.5 us (4%)
    all_gather x2, waiting for transfers between devices, local(): gathered = lax.all_gather(crossed, ('rr', 'row'), axis=0, tiled=True)  164 us
    gather x8, local copies, waits for them, and re-layouts, interpolate(): jnp.take(band_table, stencil_index[stencil].reshape(-1), axis=0)  71.2 us
    dot_general x2, matrix products, scaled_hamilton(): jnp.dot(field.reshape(-1, width), angular, precision=lax.Precision.HIGHEST)  33.9 us
    ppermute x4, starting transfers between devices, extended(): lax.ppermute(tail, axis, [(i, (i + 1) % count) for i in range(ends)])  15.8 us
    ppermute x4, starting transfers between devices, extended(): lax.ppermute(head, axis, [((i + 1) % count, i) for i in range(ends)])  15.7 us
    unnamed x39, local copies, waits for them, and re-layouts  13.4 us
    concatenate x2, other arithmetic, extended(): jnp.concatenate([lax.ppermute(tail, axis, [(i, (i + 1) % count) for i in...  12.5 us
    ppermute x4, waiting for transfers between devices, extended(): lax.ppermute(head, axis, [((i + 1) % count, i) for i in range(ends)])  10.6 us
  transfers between devices with their start and end apart: 12, of which 12 were waited for; matrix products, arithmetic and copies ran while one was open for 0% of the time, Pallas kernels for 0%

commit v1 on v0

v1 whole, which is shorter than its diff:
```python
import functools

import jax
import jax.numpy as jnp
from jax import lax
from jax.experimental import pallas as pl
from jax.experimental.pallas import tpu as pltpu
from jax.sharding import PartitionSpec as P

BAND = 2
STENCILS = 4
HALO = 2
LANES = 128
CHUNK = 8
FAR = 2
POINT = 16
ROT, RET, POS, WEIGHT = 0, 1, 2, 6
MIB = 1 << 20
F32 = jnp.float32
BF16 = jnp.bfloat16

SIDE1 = -16.0 / 96.0
SIDE2 = 1.0 / 96.0
MIDDLE = 2.0 * 30.0 / 96.0 - 7.5 / 4.0


def halves(value):
    high = value.astype(BF16)
    low = (value - high.astype(F32)).astype(BF16)
    return high, low


def product(left, right_high, right_low):
    high, low = left
    total = jnp.dot(high, right_high, preferred_element_type=F32)
    total += jnp.dot(low, right_high, preferred_element_type=F32)
    return total + jnp.dot(high, right_low, preferred_element_type=F32)


def doubled_hamilton(field, index, start, count, lanes, turned, potential, rotation):
    def at(shift_r, shift_v):
        return field[index + shift_r, pl.ds(start + shift_v, count), lanes]

    middle = at(0, 0)
    near = at(-1, 0) + at(1, 0) + (at(0, -1) + at(0, 1))
    far = at(-2, 0) + at(2, 0) + (at(0, -2) + at(0, 2))
    return (
        SIDE1 * near
        + SIDE2 * far
        + (0.25 * potential + MIDDLE) * middle
        + (0.25 * rotation) * turned
    )


def split_kernel(matrix, high, low):
    high[...], low[...] = halves(matrix[...])


def split(matrix):
    return pl.pallas_call(
        split_kernel,
        out_shape=[jax.ShapeDtypeStruct(matrix.shape, BF16)] * 2,
        name="split_angular",
    )(matrix)


def band_kernel(
    flag, packet, previous, potential, points, left, right, high, low, out, field, later, turned
):
    width = packet.shape[2]
    rows = packet.shape[1]
    base = 16
    wide = rows + 16

    @pl.when(flag[0] == 1)
    def _():
        field[...] = jnp.zeros_like(field)
        later[...] = jnp.zeros_like(later)
        for k in range(2, 8):
            field[k, base : base + rows] = packet[k]
        for k in range(4):
            field[4 + k, base - 4 : base] = left[4 * k : 4 * k + 4]
            field[4 + k, base + rows : base + rows + 4] = right[4 * k : 4 * k + 4]
        window = field[4:8, base - 8 : base + rows + 8].reshape(4 * wide, width)
        turned[...] = product(halves(window), high[...], low[...])
        for k in range(4):
            own = points[(4 + k) * rows : (5 + k) * rows]
            rotation = own[:, ROT : ROT + 1]
            retained = own[:, RET : RET + 1]
            for at in range(0, width, LANES):
                lanes = slice(at, at + LANES)
                update = doubled_hamilton(
                    field, 4 + k, base, rows, lanes,
                    turned[k * wide + 8 : k * wide + 8 + rows, lanes], potential[4 + k, :, lanes], rotation,
                ) - retained * previous[4 + k, :, lanes]
                later[k, base : base + rows, lanes] = retained * update
                if k >= 2:
                    out[(k - 2) * rows : (k - 1) * rows, lanes] = (1.0 - retained) * update
        for k in range(2, 4):
            for slab, place, inside in ((left, base - 8, 6), (right, base + rows, 0)):
                at = 16 + 2 * (k - 2)
                prev, pot, rot, ret = (slab[at + 4 * n : at + 4 * n + 2] for n in range(4))
                update = doubled_hamilton(
                    field, 4 + k, place + inside, 2, slice(None),
                    turned[k * wide + place - base + 8 + inside : k * wide + place - base + 10 + inside], pot, rot,
                ) - ret * prev
                later[k, place + inside : place + inside + 2] = ret * update
        window = later[2:4, base : base + rows].reshape(2 * rows, width)
        turned[0 : 2 * rows] = product(halves(window), high[...], low[...])
        for k in range(2, 4):
            own = points[(4 + k) * rows : (5 + k) * rows]
            rotation = own[:, ROT : ROT + 1]
            retained = own[:, RET : RET + 1]
            for at in range(0, width, LANES):
                lanes = slice(at, at + LANES)
                update = doubled_hamilton(
                    later, k, base, rows, lanes,
                    turned[(k - 2) * rows : (k - 1) * rows, lanes], potential[4 + k, :, lanes], rotation,
                ) - retained * field[4 + k, base : base + rows, lanes]
                out[k * rows : (k + 1) * rows, lanes] = (1.0 - retained) * update

    @pl.when(flag[0] == 0)
    def _():
        out[...] = jnp.zeros_like(out)


def bands(flag, packet, previous, potential, points, left, right, high, low):
    count_r, count_v, width = packet.shape
    last = count_r // CHUNK - 1
    block = pl.BlockSpec((CHUNK, count_v, width), lambda i: (last, 0, 0))

    def whole(shape):
        return pl.BlockSpec(shape, lambda i: (0,) * len(shape))

    rows = 2 * BAND * count_v
    return pl.pallas_call(
        band_kernel,
        grid=(1,),
        in_specs=[
            pl.BlockSpec(memory_space=pltpu.SMEM),
            block, block, block,
            pl.BlockSpec((CHUNK * count_v, POINT), lambda i: (last, 0)),
            whole(left.shape), whole(right.shape), whole(high.shape), whole(low.shape),
        ],
        out_specs=whole((rows, width)),
        out_shape=jax.ShapeDtypeStruct((rows, width), F32),
        scratch_shapes=[
            pltpu.VMEM((CHUNK + 2, count_v + 32, width), F32),
            pltpu.VMEM((6, count_v + 32, width), F32),
            pltpu.VMEM((4 * (count_v + 16), width), F32),
        ],
        compiler_params=pltpu.CompilerParams(vmem_limit_bytes=48 * MIB),
        cost_estimate=pl.CostEstimate(flops=400_000_000, bytes_accessed=6 * MIB, transcendentals=0),
        name="both_bands",
    )(flag, packet, previous, potential, points, left, right, high, low)


def first_kernel(
    packet, before, after, previous, potential, points, up, down, left, right, high, low, out, field, turned
):
    step = pl.program_id(0)
    steps = pl.num_programs(0)
    count, rows, width = packet.shape
    base = 8
    field[HALO : HALO + count, base : base + rows] = packet[...]
    field[0:HALO, base : base + rows] = jnp.where(step == 0, up[...].reshape(before.shape), before[...])
    field[HALO + count :, base : base + rows] = jnp.where(step == steps - 1, down[...].reshape(after.shape), after[...])
    start = pl.multiple_of(step * (HALO * count), HALO * count)
    sides = (left[pl.ds(start, HALO * count)], right[pl.ds(start, HALO * count)])
    for k in range(count):
        field[HALO + k, base - HALO : base] = sides[0][HALO * k : HALO * (k + 1)]
        field[HALO + k, base + rows : base + rows + HALO] = sides[1][HALO * k : HALO * (k + 1)]
    turned[...] = product(halves(packet[...].reshape(count * rows, width)), high[...], low[...])
    for k in range(count):
        own = points[k * rows : (k + 1) * rows]
        rotation = own[:, ROT : ROT + 1]
        retained = own[:, RET : RET + 1]
        for at in range(0, width, LANES):
            lanes = slice(at, at + LANES)
            update = doubled_hamilton(
                field, HALO + k, base, rows, lanes,
                turned[k * rows : (k + 1) * rows, lanes], potential[k, :, lanes], rotation,
            ) - retained * previous[k, :, lanes]
            out[k, :, lanes] = retained * update


def first(packet, previous, potential, points, halos, high, low):
    count_r, count_v, width = packet.shape
    per = CHUNK // HALO
    steps = count_r // CHUNK
    block = pl.BlockSpec((CHUNK, count_v, width), lambda i: (i, 0, 0))
    edge = (HALO, count_v, width)

    def whole(shape):
        return pl.BlockSpec(shape, lambda i: (0,) * len(shape))

    up, down, left, right = halos
    return pl.pallas_call(
        first_kernel,
        grid=(steps,),
        in_specs=[
            block,
            pl.BlockSpec(edge, lambda i: (jnp.maximum(i * per - 1, 0), 0, 0)),
            pl.BlockSpec(edge, lambda i: (jnp.minimum((i + 1) * per, steps * per - 1), 0, 0)),
            block, block,
            pl.BlockSpec((CHUNK * count_v, POINT), lambda i: (i, 0)),
            whole(up.shape), whole(down.shape), whole(left.shape), whole(right.shape),
            whole(high.shape), whole(low.shape),
        ],
        out_specs=block,
        out_shape=jax.ShapeDtypeStruct(packet.shape, F32),
        scratch_shapes=[
            pltpu.VMEM((CHUNK + 2 * HALO, count_v + 16, width), F32),
            pltpu.VMEM((CHUNK * count_v, width), F32),
        ],
        compiler_params=pltpu.CompilerParams(vmem_limit_bytes=48 * MIB),
        cost_estimate=pl.CostEstimate(flops=7_000_000_000, bytes_accessed=20 * MIB, transcendentals=0),
        name="first_iteration",
    )(packet, packet, packet, previous, potential, points, up, down, left, right, high, low)


def stencil_kernel(points, high, low):
    rows = points.shape[0]
    width = high.shape[1]
    columns = lax.broadcasted_iota(jnp.int32, (rows, width), 1).astype(F32)
    total = jnp.zeros((rows, width), F32)
    for n in range(STENCILS):
        place = points[:, POS + n : POS + n + 1]
        weight = points[:, WEIGHT + n : WEIGHT + n + 1]
        total += jnp.where(columns == place, weight, 0.0)
    high[...], low[...] = halves(total)


def stencil_matrix(points, width):
    rows = points.shape[0]
    tile = 128
    out = pl.BlockSpec((tile, width), lambda i: (i, 0))
    return pl.pallas_call(
        stencil_kernel,
        grid=(rows // tile,),
        in_specs=[pl.BlockSpec((tile, POINT), lambda i: (i, 0))],
        out_specs=[out, out],
        out_shape=[jax.ShapeDtypeStruct((rows, width), BF16)] * 2,
        cost_estimate=pl.CostEstimate(flops=12_000_000, bytes_accessed=6 * MIB, transcendentals=0),
        name="stencil_matrix",
    )(points)


def last_kernel(
    flag, first_packet, packet, potential, points, up, down, left, right,
    high, low, stencil_high, stencil_low, edge_high, edge_low, own_table, other_table,
    earlier, latest, field, turned, table,
):
    step = pl.program_id(0)
    steps = pl.num_programs(0) // 2
    count, rows, width = packet.shape
    base = 8
    count_r = steps * count
    is_product = flag[0] == 1
    quarter = own_table.shape[1]
    half = quarter // 2
    pieces = own_table.shape[0]

    @pl.when((step == 0) & is_product)
    def _():
        for side, ref in enumerate((own_table, other_table)):
            for k in range(pieces):
                at = (side * pieces + k) * half
                for band in range(2):
                    upper, lower = halves(ref[k, band * half : (band + 1) * half])
                    table[2 * band, at : at + half] = upper
                    table[2 * band + 1, at : at + half] = lower

    @pl.when(step < steps)
    def _():
        here = pl.multiple_of(step * count, count)

        @pl.when(is_product)
        def _():
            turned[...] = product((stencil_high[...], stencil_low[...]), table[0], table[1])
            for k in range(count):
                value = first_packet[k] + turned[k * rows : (k + 1) * rows]
                field[HALO + here + k, base : base + rows] = value
                earlier[k] = value

        @pl.when(jnp.logical_not(is_product))
        def _():
            field[pl.ds(HALO + here, count), base : base + rows] = first_packet[...]
            earlier[...] = first_packet[...]

    @pl.when(step == 0)
    def _():
        edges = HALO * rows
        sides = HALO * count_r

        def put(up_value, down_value, left_value, right_value):
            for k in range(HALO):
                field[k, base : base + rows] = up_value[k * rows : (k + 1) * rows]
                field[HALO + count_r + k, base : base + rows] = down_value[k * rows : (k + 1) * rows]
            for k in range(count_r):
                field[HALO + k, base - HALO : base] = left_value[HALO * k : HALO * (k + 1)]
                field[HALO + k, base + rows : base + rows + HALO] = right_value[HALO * k : HALO * (k + 1)]

        @pl.when(is_product)
        def _():
            source = product((edge_high[...], edge_low[...]), table[0], table[1])
            put(
                up[...] + source[:edges],
                down[...] + source[edges : 2 * edges],
                left[...] + source[2 * edges : 2 * edges + sides],
                right[...] + source[2 * edges + sides :],
            )

        @pl.when(jnp.logical_not(is_product))
        def _():
            put(up[...], down[...], left[...], right[...])

    @pl.when(step >= steps)
    def _():
        here = pl.multiple_of((step - steps) * count, count)
        window = field[pl.ds(HALO + here, count), base : base + rows].reshape(count * rows, width)
        turned[...] = product(halves(window), high[...], low[...])

        for k in range(count):
            own = points[k * rows : (k + 1) * rows]
            rotation = own[:, ROT : ROT + 1]
            retained = own[:, RET : RET + 1]
            for at in range(0, width, LANES):
                lanes = slice(at, at + LANES)
                update = doubled_hamilton(
                    field, HALO + here + k, base, rows, lanes,
                    turned[k * rows : (k + 1) * rows, lanes], potential[k, :, lanes], rotation,
                ) - retained * packet[k, :, lanes]
                latest[k, :, lanes] = retained * update

        @pl.when(is_product)
        def _():
            turned[...] = product((stencil_high[...], stencil_low[...]), table[2], table[3])
            for k in range(count):
                latest[k] += turned[k * rows : (k + 1) * rows]


def last(flag, first_packet, packet, potential, points, halos, high, low, matrix, edges, tables):
    count_r, count_v, width = packet.shape
    steps = count_r // CHUNK

    def early(i):
        return jnp.minimum(i, steps - 1)

    def late(i):
        return jnp.maximum(i - steps, 0)

    def block(where):
        return pl.BlockSpec((CHUNK, count_v, width), lambda i: (where(i), 0, 0))

    def whole(shape):
        return pl.BlockSpec(shape, lambda i: (0,) * len(shape))

    rows = CHUNK * count_v
    stencil = pl.BlockSpec((rows, matrix[0].shape[1]), lambda i: (i % steps, 0))
    return pl.pallas_call(
        last_kernel,
        grid=(2 * steps,),
        in_specs=[
            pl.BlockSpec(memory_space=pltpu.SMEM),
            block(early), block(late), block(late),
            pl.BlockSpec((rows, POINT), lambda i: (late(i), 0)),
            *[whole(halo.shape) for halo in halos],
            whole(high.shape), whole(low.shape), stencil, stencil,
            *[whole(edge.shape) for edge in edges],
            *[whole(table.shape) for table in tables],
        ],
        out_specs=[block(early), block(late)],
        out_shape=[jax.ShapeDtypeStruct(packet.shape, F32)] * 2,
        scratch_shapes=[
            pltpu.VMEM((count_r + 2 * HALO, count_v + 16, width), F32),
            pltpu.VMEM((rows, width), F32),
            pltpu.VMEM((4, matrix[0].shape[1], width), BF16),
        ],
        compiler_params=pltpu.CompilerParams(vmem_limit_bytes=56 * MIB),
        cost_estimate=pl.CostEstimate(flops=20_000_000_000, bytes_accessed=36 * MIB, transcendentals=0),
        name="last_iteration",
    )(flag, first_packet, packet, potential, points, *halos, high, low, *matrix, *edges, *tables)


def neighbours(axis, upward, downward):
    count = lax.axis_size(axis)
    return (
        lax.ppermute(upward, axis, [(i, i + 1) for i in range(count - 1)]),
        lax.ppermute(downward, axis, [(i + 1, i) for i in range(count - 1)]),
    )


def exchange(edges):
    top, bottom, first_columns, last_columns = edges
    left, right = neighbours("row", last_columns, first_columns)
    up, down = neighbours("rr", bottom, top)
    return up, down, left, right


def edges_of(field):
    width = field.shape[-1]
    return (
        field[:HALO].reshape(-1, width),
        field[-HALO:].reshape(-1, width),
        field[:, :HALO].reshape(-1, width),
        field[:, -HALO:].reshape(-1, width),
    )


def with_points(slab, values):
    width = slab.shape[-1]
    rows = values.reshape(-1, width)
    return jnp.concatenate([slab, jnp.pad(rows, ((0, -rows.shape[0] % 8), (0, 0)))], axis=0)


def local(packet, previous, potential, rotation, angular, damping, absorber, stencil_index, stencil_weight):
    packet, previous, potential = packet[0], previous[0], potential[0]
    rotation, angular = rotation[0], angular[0]
    count_r, count_v, width = packet.shape
    retained = 1.0 - absorber[0].astype(F32) * (1.0 - damping[0])
    sect = lax.axis_index("sect")
    rr = lax.axis_index("rr")
    row = lax.axis_index("row")
    sections, count_rr, count_row = (lax.axis_size(name) for name in ("sect", "rr", "row"))
    cores = 2
    chips = count_row // cores
    is_source = ((sect == 0) & (rr == count_rr - 1)).astype(jnp.int32)[None]
    is_product = (sect == 1).astype(jnp.int32)[None]

    def band_slab(far, near):
        spread = jnp.concatenate(
            [value[-BAND:, near].reshape(-1, 1) for value in (rotation, retained)], axis=0
        )
        return jnp.concatenate(
            [
                packet[-2 * BAND :, far].reshape(-1, width),
                previous[-BAND:, near].reshape(-1, width),
                potential[-BAND:, near].reshape(-1, width),
                jnp.broadcast_to(spread, (spread.shape[0], width)),
            ],
            axis=0,
        )

    firsts = band_slab(slice(0, 4), slice(0, 2))
    lasts = band_slab(slice(-4, None), slice(-2, None))
    sources = (count_rr - 1) * count_row
    axes = ("sect", "rr", "row")
    band_left = lax.ppermute(lasts, axes, [(sources + i, sources + i + 1) for i in range(count_row - 1)])
    band_right = lax.ppermute(firsts, axes, [(sources + i + 1, sources + i) for i in range(count_row - 1)])

    high, low = split(angular)
    index = stencil_index
    per = count_v * BAND
    owner = index // per
    inside = index % per
    slot = (
        ((owner + row) % cores) * chips + (row // cores - owner // cores) % chips
    ) * per + (inside % BAND) * count_v + inside // BAND
    table_points = jnp.concatenate([slot.astype(F32), stencil_weight], axis=0)
    canonical = jnp.concatenate([index.astype(F32), stencil_weight], axis=0)
    points = jnp.concatenate([rotation[None], retained[None], table_points], axis=0)
    points = jnp.pad(points, ((0, POINT - points.shape[0]), (0, 0), (0, 0)))
    points = jnp.transpose(points, (1, 2, 0)).reshape(count_r * count_v, POINT)

    table = bands(is_source, packet, previous, potential, points, band_left, band_right, high, low)

    plane = ("sect", "rr")
    half = count_rr // FAR
    start = count_rr - 1
    entries = [count_rr + (k + 1) * half - 1 for k in range(FAR)]
    piece = sum(lax.ppermute(table, plane, [(start, entry)]) for entry in entries)
    spread = piece
    for shift in (1, half - 1, 2):
        spread = spread + lax.ppermute(
            piece, plane, [(entry, entry - (half - 1) + (half - 1 + shift) % half) for entry in entries]
        )
    line = ("sect", "row")

    def around(shift):
        pairs = []
        for chip in range(chips):
            for core in range(cores):
                pairs.append(
                    (count_row + chip * cores + core, count_row + ((chip + shift) % chips) * cores + core)
                )
        return lax.ppermute(spread, line, pairs)

    own = jnp.stack([spread, around(1), around(2), around(3)], axis=0)
    other = lax.ppermute(
        own, line, [(count_row + i, count_row + i + 1 - 2 * (i % cores)) for i in range(count_row)]
    )

    cut = edges_of(packet)
    cut_points = (canonical[:, :HALO], canonical[:, -HALO:], canonical[:, :, :HALO], canonical[:, :, -HALO:])
    cut_points = [jnp.transpose(value, (1, 2, 0)) for value in cut_points]
    halos = exchange([with_points(slab, value) for slab, value in zip(cut, cut_points)])
    lengths = [slab.shape[0] for slab in cut]
    one = first(packet, previous, potential, points, [h[:n] for h, n in zip(halos, lengths)], high, low)
    later = exchange(edges_of(one))

    edge_points = jnp.concatenate(
        [h[n : n + n * 8 // width].reshape(n, 8) for h, n in zip(halos, lengths)], axis=0
    )
    edge_index = edge_points[:, :STENCILS].astype(jnp.int32)
    edge_owner = edge_index // per
    edge_inside = edge_index % per
    edge_slot = (
        ((edge_owner + row) % cores) * chips + (row // cores - edge_owner // cores) % chips
    ) * per + (edge_inside % BAND) * count_v + edge_inside // BAND
    edge_points = jnp.concatenate([edge_slot.astype(F32), edge_points[:, STENCILS:]], axis=1)
    edge_points = jnp.pad(edge_points, ((0, 0), (POS, POINT - POS - 2 * STENCILS)))
    columns = count_row * per
    matrix = stencil_matrix(points, columns)
    edge_matrix = stencil_matrix(edge_points, columns)

    earlier, latest = last(
        is_product, one, packet, potential, points, later, high, low, matrix, edge_matrix, (own, other)
    )
    return latest[None], earlier[None]


def solution(mesh):
    in_specs = (
        P("sect", "rr", "row", None),
        P("sect", "rr", "row", None),
        P("sect", "rr", "row", None),
        P("sect", "rr", "row"),
        P("sect", None, None),
        P("sect", "rr", "row"),
        P("sect", "rr", "row"),
        P(None, "rr", "row"),
        P(None, "rr", "row"),
    )
    out_specs = (P("sect", "rr", "row", None), P("sect", "rr", "row", None))
    return jax.shard_map(local, mesh=mesh, in_specs=in_specs, out_specs=out_specs, check_vma=False)
```

time: 394 us -> 155 us (0.39)
  waiting for transfers between devices: 189 us -> 5.24 us
  local copies, waits for them, and re-layouts: 89.9 us -> 25.1 us
  Pallas kernels: 0 us -> 56.9 us
  matrix products: 33.9 us -> 0 us
  other arithmetic: 29.9 us -> 10.1 us
  starting transfers between devices: 34.1 us -> 53.3 us
  between operations: 14.5 us -> 1.26 us
    all_gather x2 -> x0, waiting for transfers between devices: 164 us -> none  [local(): gathered = lax.all_gather(crossed, ('rr', 'row'), axis=0, tiled=True)]
    gather x8 -> x0, local copies, waits for them, and re-layouts: 71.2 us -> none  [interpolate(): jnp.take(band_table, stencil_index[stencil].reshape(-1), axis=0)]
    pallas_call x0 -> x6, Pallas kernels: none -> 56.9 us  [the longest x1 26.3 us: last(): pl.pallas_call(last_kernel, grid=(2 * steps,), in_specs=[pl.BlockSpec(mem...]
    dot_general x2 -> x0, matrix products: 33.9 us -> none  [scaled_hamilton(): jnp.dot(field.reshape(-1, width), angular, precision=lax.Precision.HIGHEST)]
    ppermute x10 -> x19, starting transfers between devices: 34 us -> 53.3 us  [the longest x4 16.2 us: neighbours(): lax.ppermute(upward, axis, [(i, i + 1) for i in range(count - 1)])]
    ppermute x10 -> x19, waiting for transfers between devices: 24.4 us -> 5.24 us  [the longest x3 3.54 us: local(): lax.ppermute(piece, plane, [(entry, entry - (half - 1) + (half - 1 + shif...]
    slice x10 -> x21, local copies, waits for them, and re-layouts: 4.06 us -> 15.3 us  [the longest x4 3.78 us: local(): h[:n]]
    unnamed x39 -> x32, local copies, waits for them, and re-layouts: 13.4 us -> 3.64 us
  transfers between devices with their start and end apart: 12 -> 19, of which waited for: 12 -> 2; matrix products, arithmetic and copies ran while one was open for 0% -> 17% of each run, Pallas kernels for 0% -> 20%
where the time goes in v1:
time: 155 us; the launch traced here: 152 us
  Pallas kernels  56.9 us (37%)
  starting transfers between devices  53.3 us (34%)
  local copies, waits for them, and re-layouts  25.1 us (16%)
  other arithmetic  10.1 us (7%)
  waiting for transfers between devices  5.24 us (3%)
    pallas_call x1, Pallas kernels, last(): pl.pallas_call(last_kernel, grid=(2 * steps,), in_specs=[pl.BlockSpec(mem...  26.3 us
    ppermute x4, starting transfers between devices, neighbours(): lax.ppermute(upward, axis, [(i, i + 1) for i in range(count - 1)])  16.2 us
    ppermute x4, starting transfers between devices, neighbours(): lax.ppermute(downward, axis, [(i + 1, i) for i in range(count - 1)])  15.5 us
    pallas_call x2, Pallas kernels, stencil_matrix(): pl.pallas_call(stencil_kernel, grid=(rows // tile,), in_specs=[pl.BlockSp...  13.8 us
    pallas_call x1, Pallas kernels, first(): pl.pallas_call(first_kernel, grid=(steps,), in_specs=[block, pl.BlockSpec...  12.7 us
    ppermute x3, starting transfers between devices, around(): return lax.ppermute(spread, line, pairs)  11.2 us
    ppermute x1, starting transfers between devices, local(): lax.ppermute(own, line, [(count_row + i, count_row + i + 1 - 2 * (i % cor...  4.38 us
    slice x4, local copies, waits for them, and re-layouts, local(): h[:n]  3.78 us
  transfers between devices with their start and end apart: 19, of which 2 were waited for; matrix products, arithmetic and copies ran while one was open for 17% of the time, Pallas kernels for 20%

profile of v1, /device:TPU:7, one launch (start us, length us, event | category | flops | bytes accessed | tf_op | source)
XLA Modules:
  0.0 151.9 jit_solution(17850991543264369294)
XLA Ops:
  0.6 0.8 fusion.49
  1.6 0.7 multiply_subtract_fusion
  2.6 0.8 fusion.42
  3.4 0.8 fusion.43
  4.2 0.9 fusion.41
  5.3 0.7 collective-permute-start.8
  6.6 0.7 collective-permute-start.9
  7.3 1.0 fusion.47
  8.3 1.1 fusion.48
  9.4 1.0 fusion.4
  10.5 0.3 copy.31
  10.9 5.5 %collective-permute-start.1 = (f32[72,512]{1,0:T(8,128)S(1)}, f32[72,512]{1,0:T(8,128)}, u32[]{:S(2)}, u32[]{:S(2)}) collective-permute-start(f32[72,512]{1,0:T(8,128)S(1)} %select_maximum_fusion.5), channel_id=1, source_target_pairs={{8,0},{16,8},{24,16},{32,24},{40,32},{48,40},{56,48},{9,1},{17,9},... | collective-permute-start | bytes 442376 | tf_op jit(solution)/shard_map/ppermute | solution.py:390
  16.4 0.3 copy.30
  16.7 0.7 select_maximum_fusion.6
  17.4 1.9 %collective-permute-start = (f32[72,512]{1,0:T(8,128)}, f32[72,512]{1,0:T(8,128)}, u32[]{:S(2)}, u32[]{:S(2)}) collective-permute-start(f32[72,512]{1,0:T(8,128)} %select_maximum_fusion.6), channel_id=1, source_target_pairs={{0,8},{8,16},{16,24},{24,32},{32,40},{40,48},{48,56},{1,9},{9,17},... | collective-permute-start | bytes 442376 | tf_op jit(solution)/shard_map/ppermute | solution.py:389
  19.3 0.9 fusion
  20.2 0.9 copy.29
  21.2 2.7 %split_angular.1 = (bf16[512,512]{1,0:T(8,128)(2,1)}, bf16[512,512]{1,0:T(8,128)(2,1)}) custom-call(f32[512,512]{1,0:T(8,128)} %bitcast.51), custom_call_target="tpu_custom_call" | custom-call | tf_op jit(solution)/shard_map/split_angular/pallas_call | solution.py:60
  23.9 1.0 copy-done.2
  24.9 1.0 copy-done.4
  26.0 1.4 both_bands.1
  27.4 0.7 collective-permute-start.11
  28.1 0.7 collective-permute-start.10
  28.8 1.8 %fusion.46 = (f32[64,2,512]{2,1,0:T(2,128)S(1)}, f32[64,2,512]{2,1,0:T(2,128)S(1)}) fusion(f32[64,32,512]{2,1,0:T(8,128)} %bitcast.39), kind=kLoop, calls=%fused_computation.121 | loop fusion | bytes 1048576 | tf_op jit(solution)/shard_map/slice | solution.py:406
  30.6 0.7 collective-permute-start.14
  31.3 1.4 collective-permute-start.13
  32.7 1.3 collective-permute-start.12
  34.1 0.7 reshape.103
  35.0 0.7 reshape.101
  35.9 0.2 reshape.100
  36.1 1.4 select_maximum_fusion
  37.5 1.4 select_maximum_fusion.1
  38.9 4.4 %collective-permute-start.2 = (f32[136,512]{1,0:T(8,128)}, f32[136,512]{1,0:T(8,128)}, u32[]{:S(2)}, u32[]{:S(2)}) collective-permute-start(f32[136,512]{1,0:T(8,128)} %select_maximum_fusion.1), channel_id=1, source_target_pairs={{0,1},{1,2},{2,3},{3,4},{4,5},{5,6},{6,7},{8,9},{9,10},{10,11},{11... | collective-permute-start | bytes 835592 | tf_op jit(solution)/shard_map/ppermute | solution.py:389
  43.3 1.9 %collective-permute-start.3 = (f32[136,512]{1,0:T(8,128)}, f32[136,512]{1,0:T(8,128)}, u32[]{:S(2)}, u32[]{:S(2)}) collective-permute-start(f32[136,512]{1,0:T(8,128)} %select_maximum_fusion), channel_id=1, source_target_pairs={{1,0},{2,1},{3,2},{4,3},{5,4},{6,5},{7,6},{9,8},{10,9},{11,10},{12... | collective-permute-start | bytes 835592 | tf_op jit(solution)/shard_map/ppermute | solution.py:390
  45.3 3.5 %collective-permute-done.12 = f32[128,512]{1,0:T(8,128)} collective-permute-done((f32[128,512]{1,0:T(8,128)S(1)}, f32[128,512]{1,0:T(8,128)}, u32[]{:S(2)}, u32[]{:S(2)}) %collective-permute-start.12) | collective-permute-done | bytes 262176 | tf_op jit(solution)/shard_map/ppermute | solution.py:475
  48.8 1.2 add_add_fusion
  50.0 2.7 %collective-permute-start.17 = (f32[128,512]{1,0:T(8,128)S(1)}, f32[128,512]{1,0:T(8,128)S(1)}, u32[]{:S(2)}, u32[]{:S(2)}) collective-permute-start(f32[128,512]{1,0:T(8,128)S(1)} %add_add_fusion), channel_id=1, source_target_pairs={{64,70},{65,71},{66,64},{67,65},{68,66},{69,67},{70,68},{71,69},{7... | collective-permute-start | bytes 786440 | tf_op jit(solution)/shard_map/ppermute | solution.py:487
  52.7 6.6 %collective-permute-start.16 = (f32[128,512]{1,0:T(8,128)S(1)}, f32[128,512]{1,0:T(8,128)S(1)}, u32[]{:S(2)}, u32[]{:S(2)}) collective-permute-start(f32[128,512]{1,0:T(8,128)S(1)} %add_add_fusion), channel_id=1, source_target_pairs={{64,68},{65,69},{66,70},{67,71},{68,64},{69,65},{70,66},{71,67},{7... | collective-permute-start | bytes 786440 | tf_op jit(solution)/shard_map/ppermute | solution.py:487
  59.3 1.9 %collective-permute-start.15 = (f32[128,512]{1,0:T(8,128)S(1)}, f32[128,512]{1,0:T(8,128)S(1)}, u32[]{:S(2)}, u32[]{:S(2)}) collective-permute-start(f32[128,512]{1,0:T(8,128)S(1)} %add_add_fusion), channel_id=1, source_target_pairs={{64,66},{65,67},{66,68},{67,69},{68,70},{69,71},{70,64},{71,65},{7... | collective-permute-start | bytes 786440 | tf_op jit(solution)/shard_map/ppermute | solution.py:487
  61.2 10.9 %stencil_matrix.2 = (bf16[2048,512]{1,0:T(8,128)(2,1)}, bf16[2048,512]{1,0:T(8,128)(2,1)}) custom-call(f32[2048,16]{1,0:T(8,128)} %bitcast.34), custom_call_target="tpu_custom_call" | custom-call | flops 12000000 | bytes 6291456 | tf_op jit(solution)/shard_map/stencil_matrix/pallas_call | solution.py:238
  72.1 0.8 slice_reduce_fusion
  73.1 0.9 slice.135.down
  74.1 0.9 slice.132.up
  75.0 1.0 slice.139.left
  76.0 1.0 slice.141.right
  77.0 0.7 copy-done.9
  77.8 1.2 pad_maximum_fusion.own_table
  79.0 4.4 %collective-permute-start.18 = (f32[4,128,512]{2,1,0:T(8,128)S(1)}, f32[4,128,512]{2,1,0:T(8,128)}, u32[]{:S(2)}, u32[]{:S(2)}) collective-permute-start(f32[4,128,512]{2,1,0:T(8,128)S(1)} %pad_maximum_fusion.own_table), channel_id=1, source_target_pairs={{64,65},{65,64},{66,67},{67,66},{68,69},{69,68},{70,71},{71,70},{7... | collective-permute-start | bytes 3145736 | tf_op jit(solution)/shard_map/ppermute | solution.py:490
  83.5 12.7 %first_iteration.1.first_packet = f32[64,32,512]{2,1,0:T(8,128)} custom-call(f32[64,32,512]{2,1,0:T(8,128)} %bitcast.40, f32[64,32,512]{2,1,0:T(8,128)} %bitcast.41, f32[64,32,512]{2,1,0:T(8,128)} %bitcast.42, f32[64,32,512]{2,1,0:T(8,128)} %bitcast.46, f32[64,32,512]{2,1,0:T(8,128)} %bitcast.49, f32[2048,16]{1,0:T(8,128)S(1)} %bitcast.36, ...), custom_call_target="tpu_custom_call" | custom-call | flops 7000000000 | bytes 20971520 | tf_op jit(solution)/shard_map/first_iteration/pallas_call | solution.py:198
  96.2 0.7 slice.148
  97.1 0.7 slice.149
  97.9 1.0 fusion.45
  99.0 5.9 %collective-permute-start.4 = (f32[64,512]{1,0:T(8,128)S(1)}, f32[64,512]{1,0:T(8,128)S(1)}, u32[]{:S(2)}, u32[]{:S(2)}) collective-permute-start(f32[64,512]{1,0:T(8,128)S(1)} %bitcast.59), channel_id=1, source_target_pairs={{0,8},{8,16},{16,24},{24,32},{32,40},{40,48},{48,56},{1,9},{9,17},... | collective-permute-start | bytes 393224 | tf_op jit(solution)/shard_map/ppermute | solution.py:389
  104.9 6.2 %collective-permute-start.5 = (f32[64,512]{1,0:T(8,128)S(1)}, f32[64,512]{1,0:T(8,128)S(1)}, u32[]{:S(2)}, u32[]{:S(2)}) collective-permute-start(f32[64,512]{1,0:T(8,128)S(1)} %bitcast.58), channel_id=1, source_target_pairs={{8,0},{16,8},{24,16},{32,24},{40,32},{48,40},{56,48},{9,1},{17,9},... | collective-permute-start | bytes 393224 | tf_op jit(solution)/shard_map/ppermute | solution.py:390
  111.1 1.8 %fusion.44 = (f32[64,2,512]{2,1,0:T(2,128)S(1)}, f32[64,2,512]{2,1,0:T(2,128)S(1)}) fusion(f32[64,32,512]{2,1,0:T(8,128)} %first_iteration.1.first_packet), kind=kLoop, calls=%fused_computation.119 | loop fusion | bytes 1048576 | tf_op jit(solution)/shard_map/slice | solution.py:406
  112.9 0.2 reshape.107
  113.0 0.2 reshape.106
  113.2 4.0 %collective-permute-start.6 = (f32[128,512]{1,0:T(8,128)S(1)}, f32[128,512]{1,0:T(8,128)S(1)}, u32[]{:S(2)}, u32[]{:S(2)}) collective-permute-start(f32[128,512]{1,0:T(8,128)S(1)} %reshape.106), channel_id=1, source_target_pairs={{0,1},{1,2},{2,3},{3,4},{4,5},{5,6},{6,7},{8,9},{9,10},{10,11},{11... | collective-permute-start | bytes 786440 | tf_op jit(solution)/shard_map/ppermute | solution.py:389
  117.3 1.9 %collective-permute-start.7 = (f32[128,512]{1,0:T(8,128)S(1)}, f32[128,512]{1,0:T(8,128)S(1)}, u32[]{:S(2)}, u32[]{:S(2)}) collective-permute-start(f32[128,512]{1,0:T(8,128)S(1)} %reshape.107), channel_id=1, source_target_pairs={{1,0},{2,1},{3,2},{4,3},{5,4},{6,5},{7,6},{9,8},{10,9},{11,10},{12... | collective-permute-start | bytes 786440 | tf_op jit(solution)/shard_map/ppermute | solution.py:390
  119.5 0.8 pad.27.points
  120.3 3.0 %stencil_matrix.3 = (bf16[384,512]{1,0:T(8,128)(2,1)}, bf16[384,512]{1,0:T(8,128)(2,1)}) custom-call(f32[384,16]{1,0:T(8,128)} %pad.27.points), custom_call_target="tpu_custom_call" | custom-call | flops 12000000 | bytes 6291456 | tf_op jit(solution)/shard_map/stencil_matrix/pallas_call | solution.py:238
  123.3 1.7 %collective-permute-done.7.right = f32[128,512]{1,0:T(8,128)S(1)} collective-permute-done((f32[128,512]{1,0:T(8,128)S(1)}, f32[128,512]{1,0:T(8,128)S(1)}, u32[]{:S(2)}, u32[]{:S(2)}) %collective-permute-start.7) | collective-permute-done | bytes 262176 | tf_op jit(solution)/shard_map/ppermute | solution.py:390
  125.0 0.7 copy-done.13
  125.7 26.3 %last_iteration.1 = (f32[64,32,512]{2,1,0:T(8,128)}, f32[64,32,512]{2,1,0:T(8,128)}) custom-call(s32[1]{0:T(128)} %bitcast.flag, f32[64,32,512]{2,1,0:T(8,128)} %first_iteration.1.first_packet, f32[64,32,512]{2,1,0:T(8,128)} %bitcast.43, f32[64,32,512]{2,1,0:T(8,128)} %bitcast.50, f32[2048,16]{1,0:T(8,128)} %bitcast.35, f32[64,512]{1,0:T(8,128)} %copy-done.14, ...), custom_call_target="tpu_custom_call" | custom-call | flops 20000000000 | bytes 37748736 | tf_op jit(solution)/shard_map/last_iteration/pallas_call | solution.py:361
  (87 shorter events, 3.1 us)
Async XLA Ops:
  5.3 18.5 %collective-permute-start.8 = (f32[32,512]{1,0:T(8,128)S(1)}, f32[32,512]{1,0:T(8,128)S(1)}, u32[]{:S(2)}, u32[]{:S(2)}) collective-permute-start(f32[32,512]{1,0:T(8,128)S(1)} %maximum_maximum_fusion), channel_id=1, source_target_pairs={{56,57},{57,58},{58,59},{59,60},{60,61},{61,62},{62,63}} | collective-permute-start | bytes 196616 | tf_op jit(solution)/shard_map/ppermute | solution.py:449
  6.6 17.2 %collective-permute-start.9 = (f32[32,512]{1,0:T(8,128)S(1)}, f32[32,512]{1,0:T(8,128)S(1)}, u32[]{:S(2)}, u32[]{:S(2)}) collective-permute-start(f32[32,512]{1,0:T(8,128)S(1)} %maximum_maximum_fusion.1), channel_id=1, source_target_pairs={{57,56},{58,57},{59,58},{60,59},{61,60},{62,61},{63,62}} | collective-permute-start | bytes 196616 | tf_op jit(solution)/shard_map/ppermute | solution.py:450
  10.9 41.8 %collective-permute-start.1 = (f32[72,512]{1,0:T(8,128)S(1)}, f32[72,512]{1,0:T(8,128)}, u32[]{:S(2)}, u32[]{:S(2)}) collective-permute-start(f32[72,512]{1,0:T(8,128)S(1)} %select_maximum_fusion.5), channel_id=1, source_target_pairs={{8,0},{16,8},{24,16},{32,24},{40,32},{48,40},{56,48},{9,1},{17,9},... | collective-permute-start | bytes 442376 | tf_op jit(solution)/shard_map/ppermute | solution.py:390
  17.4 41.9 %collective-permute-start = (f32[72,512]{1,0:T(8,128)}, f32[72,512]{1,0:T(8,128)}, u32[]{:S(2)}, u32[]{:S(2)}) collective-permute-start(f32[72,512]{1,0:T(8,128)} %select_maximum_fusion.6), channel_id=1, source_target_pairs={{0,8},{8,16},{16,24},{24,32},{32,40},{40,48},{48,56},{1,9},{9,17},... | collective-permute-start | bytes 442376 | tf_op jit(solution)/shard_map/ppermute | solution.py:389
  21.2 6.2 %copy-start = (f32[64,32,16]{2,1,0:T(8,128)}, f32[64,32,16]{2,1,0:T(8,128)S(1)}, u32[]{:S(2)}) copy-start(f32[64,32,16]{2,1,0:T(8,128)S(1)} %copy.29) | copy-start | bytes 393220
  23.9 1.0 copy-start.2
  24.9 1.0 copy-start.4
  26.0 8.0 %copy-start.7 = (f32[4,64,32]{1,2,0:T(8,128)S(1)}, f32[4,64,32]{1,2,0:T(8,128)}, u32[]{:S(2)}) copy-start(f32[4,64,32]{1,2,0:T(8,128)} %param.17) | copy-start | bytes 98308
  27.4 3.2 %collective-permute-start.11 = (f32[128,512]{1,0:T(8,128)S(1)}, f32[128,512]{1,0:T(8,128)S(1)}, u32[]{:S(2)}, u32[]{:S(2)}) collective-permute-start(f32[128,512]{1,0:T(8,128)S(1)} %both_bands.1), channel_id=1, source_target_pairs={{56,120},{57,121},{58,122},{59,123},{60,124},{61,125},{62,126},{63... | collective-permute-start | bytes 786440 | tf_op jit(solution)/shard_map/ppermute | solution.py:472
  28.1 2.5 %collective-permute-start.10 = (f32[128,512]{1,0:T(8,128)S(1)}, f32[128,512]{1,0:T(8,128)S(1)}, u32[]{:S(2)}, u32[]{:S(2)}) collective-permute-start(f32[128,512]{1,0:T(8,128)S(1)} %both_bands.1), channel_id=1, source_target_pairs={{56,88},{57,89},{58,90},{59,91},{60,92},{61,93},{62,94},{63,95}} | collective-permute-start | bytes 786440 | tf_op jit(solution)/shard_map/ppermute | solution.py:472
  30.6 8.3 %collective-permute-start.14 = (f32[128,512]{1,0:T(8,128)S(1)}, f32[128,512]{1,0:T(8,128)S(1)}, u32[]{:S(2)}, u32[]{:S(2)}) collective-permute-start(f32[128,512]{1,0:T(8,128)S(1)} %add.115), channel_id=1, source_target_pairs={{88,72},{120,104},{89,73},{121,105},{90,74},{122,106},{91,75},{123... | collective-permute-start | bytes 786440 | tf_op jit(solution)/shard_map/ppermute | solution.py:475
  31.3 12.0 %collective-permute-start.13 = (f32[128,512]{1,0:T(8,128)S(1)}, f32[128,512]{1,0:T(8,128)}, u32[]{:S(2)}, u32[]{:S(2)}) collective-permute-start(f32[128,512]{1,0:T(8,128)S(1)} %add.115), channel_id=1, source_target_pairs={{88,80},{120,112},{89,81},{121,113},{90,82},{122,114},{91,83},{123... | collective-permute-start | bytes 786440 | tf_op jit(solution)/shard_map/ppermute | solution.py:475
  32.7 16.1 %collective-permute-start.12 = (f32[128,512]{1,0:T(8,128)S(1)}, f32[128,512]{1,0:T(8,128)}, u32[]{:S(2)}, u32[]{:S(2)}) collective-permute-start(f32[128,512]{1,0:T(8,128)S(1)} %add.115), channel_id=1, source_target_pairs={{88,64},{120,96},{89,65},{121,97},{90,66},{122,98},{91,67},{123,99... | collective-permute-start | bytes 786440 | tf_op jit(solution)/shard_map/ppermute | solution.py:475
  35.0 48.5 %copy-start.1 = (f32[64,32,16]{2,1,0:T(8,128)S(1)}, f32[64,32,16]{2,1,0:T(8,128)}, u32[]{:S(2)}) copy-start(f32[64,32,16]{2,1,0:T(8,128)} %copy-done) | copy-start | bytes 393220
  35.0 48.5 %copy-start.3 = (bf16[512,512]{1,0:T(8,128)(2,1)S(1)}, bf16[512,512]{1,0:T(8,128)(2,1)}, u32[]{:S(2)}) copy-start(bf16[512,512]{1,0:T(8,128)(2,1)} %get-tuple-element.10.high) | copy-start | bytes 1572868
  35.0 48.5 %copy-start.5 = (bf16[512,512]{1,0:T(8,128)(2,1)S(1)}, bf16[512,512]{1,0:T(8,128)(2,1)}, u32[]{:S(2)}) copy-start(bf16[512,512]{1,0:T(8,128)(2,1)} %get-tuple-element.11.low) | copy-start | bytes 1572868
  38.9 6.3 %copy-start.8 = (f32[128,512]{1,0:T(8,128)}, f32[128,512]{1,0:T(8,128)S(1)}, u32[]{:S(2)}) copy-start(f32[128,512]{1,0:T(8,128)S(1)} %collective-permute-done.14) | copy-start | bytes 786436
  38.9 36.1 %collective-permute-start.2 = (f32[136,512]{1,0:T(8,128)}, f32[136,512]{1,0:T(8,128)}, u32[]{:S(2)}, u32[]{:S(2)}) collective-permute-start(f32[136,512]{1,0:T(8,128)} %select_maximum_fusion.1), channel_id=1, source_target_pairs={{0,1},{1,2},{2,3},{3,4},{4,5},{5,6},{6,7},{8,9},{9,10},{10,11},{11... | collective-permute-start | bytes 835592 | tf_op jit(solution)/shard_map/ppermute | solution.py:389
  43.3 32.6 %collective-permute-start.3 = (f32[136,512]{1,0:T(8,128)}, f32[136,512]{1,0:T(8,128)}, u32[]{:S(2)}, u32[]{:S(2)}) collective-permute-start(f32[136,512]{1,0:T(8,128)} %select_maximum_fusion), channel_id=1, source_target_pairs={{1,0},{2,1},{3,2},{4,3},{5,4},{6,5},{7,6},{9,8},{10,9},{11,10},{12... | collective-permute-start | bytes 835592 | tf_op jit(solution)/shard_map/ppermute | solution.py:390
  50.0 27.0 %collective-permute-start.17 = (f32[128,512]{1,0:T(8,128)S(1)}, f32[128,512]{1,0:T(8,128)S(1)}, u32[]{:S(2)}, u32[]{:S(2)}) collective-permute-start(f32[128,512]{1,0:T(8,128)S(1)} %add_add_fusion), channel_id=1, source_target_pairs={{64,70},{65,71},{66,64},{67,65},{68,66},{69,67},{70,68},{71,69},{7... | collective-permute-start | bytes 786440 | tf_op jit(solution)/shard_map/ppermute | solution.py:487
  52.7 24.3 %collective-permute-start.16 = (f32[128,512]{1,0:T(8,128)S(1)}, f32[128,512]{1,0:T(8,128)S(1)}, u32[]{:S(2)}, u32[]{:S(2)}) collective-permute-start(f32[128,512]{1,0:T(8,128)S(1)} %add_add_fusion), channel_id=1, source_target_pairs={{64,68},{65,69},{66,70},{67,71},{68,64},{69,65},{70,66},{71,67},{7... | collective-permute-start | bytes 786440 | tf_op jit(solution)/shard_map/ppermute | solution.py:487
  59.3 17.7 %collective-permute-start.15 = (f32[128,512]{1,0:T(8,128)S(1)}, f32[128,512]{1,0:T(8,128)S(1)}, u32[]{:S(2)}, u32[]{:S(2)}) collective-permute-start(f32[128,512]{1,0:T(8,128)S(1)} %add_add_fusion), channel_id=1, source_target_pairs={{64,66},{65,67},{66,68},{67,69},{68,70},{69,71},{70,64},{71,65},{7... | collective-permute-start | bytes 786440 | tf_op jit(solution)/shard_map/ppermute | solution.py:487
  77.0 0.7 copy-start.9
  77.0 0.8 copy-start.10
  77.0 0.8 copy-start.11
  79.0 17.2 %copy-start.6 = (f32[4,128,512]{2,1,0:T(8,128)}, f32[4,128,512]{2,1,0:T(8,128)S(1)}, u32[]{:S(2)}) copy-start(f32[4,128,512]{2,1,0:T(8,128)S(1)} %pad_maximum_fusion.own_table) | copy-start | bytes 3145732
  79.0 45.9 %collective-permute-start.18 = (f32[4,128,512]{2,1,0:T(8,128)S(1)}, f32[4,128,512]{2,1,0:T(8,128)}, u32[]{:S(2)}, u32[]{:S(2)}) collective-permute-start(f32[4,128,512]{2,1,0:T(8,128)S(1)} %pad_maximum_fusion.own_table), channel_id=1, source_target_pairs={{64,65},{65,64},{66,67},{67,66},{68,69},{69,68},{70,71},{71,70},{7... | collective-permute-start | bytes 3145736 | tf_op jit(solution)/shard_map/ppermute | solution.py:490
  99.0 24.3 %collective-permute-start.4 = (f32[64,512]{1,0:T(8,128)S(1)}, f32[64,512]{1,0:T(8,128)S(1)}, u32[]{:S(2)}, u32[]{:S(2)}) collective-permute-start(f32[64,512]{1,0:T(8,128)S(1)} %bitcast.59), channel_id=1, source_target_pairs={{0,8},{8,16},{16,24},{24,32},{32,40},{40,48},{48,56},{1,9},{9,17},... | collective-permute-start | bytes 393224 | tf_op jit(solution)/shard_map/ppermute | solution.py:389
  104.9 18.4 %collective-permute-start.5 = (f32[64,512]{1,0:T(8,128)S(1)}, f32[64,512]{1,0:T(8,128)S(1)}, u32[]{:S(2)}, u32[]{:S(2)}) collective-permute-start(f32[64,512]{1,0:T(8,128)S(1)} %bitcast.58), channel_id=1, source_target_pairs={{8,0},{16,8},{24,16},{32,24},{40,32},{48,40},{56,48},{9,1},{17,9},... | collective-permute-start | bytes 393224 | tf_op jit(solution)/shard_map/ppermute | solution.py:390
  113.2 10.0 %collective-permute-start.6 = (f32[128,512]{1,0:T(8,128)S(1)}, f32[128,512]{1,0:T(8,128)S(1)}, u32[]{:S(2)}, u32[]{:S(2)}) collective-permute-start(f32[128,512]{1,0:T(8,128)S(1)} %reshape.106), channel_id=1, source_target_pairs={{0,1},{1,2},{2,3},{3,4},{4,5},{5,6},{6,7},{8,9},{9,10},{10,11},{11... | collective-permute-start | bytes 786440 | tf_op jit(solution)/shard_map/ppermute | solution.py:389
  117.3 7.7 %collective-permute-start.7 = (f32[128,512]{1,0:T(8,128)S(1)}, f32[128,512]{1,0:T(8,128)S(1)}, u32[]{:S(2)}, u32[]{:S(2)}) collective-permute-start(f32[128,512]{1,0:T(8,128)S(1)} %reshape.107), channel_id=1, source_target_pairs={{1,0},{2,1},{3,2},{4,3},{5,4},{6,5},{7,6},{9,8},{10,9},{11,10},{12... | collective-permute-start | bytes 786440 | tf_op jit(solution)/shard_map/ppermute | solution.py:390
  123.3 1.7 %copy-start.14 = (f32[64,512]{1,0:T(8,128)}, f32[64,512]{1,0:T(8,128)S(1)}, u32[]{:S(2)}) copy-start(f32[64,512]{1,0:T(8,128)S(1)} %collective-permute-done.4.up) | copy-start | bytes 393220
  123.3 1.7 %copy-start.15 = (f32[64,512]{1,0:T(8,128)}, f32[64,512]{1,0:T(8,128)S(1)}, u32[]{:S(2)}) copy-start(f32[64,512]{1,0:T(8,128)S(1)} %collective-permute-done.5.down) | copy-start | bytes 393220
  123.3 1.7 %copy-start.12 = (f32[128,512]{1,0:T(8,128)}, f32[128,512]{1,0:T(8,128)S(1)}, u32[]{:S(2)}) copy-start(f32[128,512]{1,0:T(8,128)S(1)} %collective-permute-done.6.left) | copy-start | bytes 786436
  125.0 0.7 copy-start.13

commit v2 on v0

v2 whole, which is shorter than its diff:
```python
import functools

import jax
import jax.numpy as jnp
from jax import lax
from jax.experimental import pallas as pl
from jax.experimental.pallas import tpu as pltpu
from jax.sharding import PartitionSpec as P

BAND = 2
STENCILS = 4
HALO = 2
LANES = 128
CHUNK = 16
LAST = 8
CORES = 2
FAR = 2
SOURCE, PRODUCT, CORE, CHIP = range(4)
ROT, RET, INDEX, WEIGHT, TABLES = 0, 1, 2, 6, 10
EXTRA = 2 * STENCILS * HALO
MIB = 1 << 20
F32 = jnp.float32
BF16 = jnp.bfloat16
ANY = pl.BlockSpec(memory_space=pl.ANY)
SMEM = pl.BlockSpec(memory_space=pltpu.SMEM)
VMEM = pl.BlockSpec(memory_space=pltpu.VMEM)

SIDE1 = -16.0 / 96.0
SIDE2 = 1.0 / 96.0
MIDDLE = 2.0 * 30.0 / 96.0 - 7.5 / 4.0


def halves(value):
    high = value.astype(BF16)
    low = (value - high.astype(F32)).astype(BF16)
    return high, low


def product(left, right_high, right_low):
    high, low = left
    total = jnp.dot(high, right_high, preferred_element_type=F32)
    total += jnp.dot(low, right_high, preferred_element_type=F32)
    return total + jnp.dot(high, right_low, preferred_element_type=F32)


def doubled_hamilton(field, index, start, count, lanes, turned, potential, rotation):
    def at(shift_r, shift_v):
        return field[index + shift_r, pl.ds(start + shift_v, count), lanes]

    middle = at(0, 0)
    near = at(-1, 0) + at(1, 0) + (at(0, -1) + at(0, 1))
    far = at(-2, 0) + at(2, 0) + (at(0, -2) + at(0, 2))
    return (
        SIDE1 * near
        + SIDE2 * far
        + (0.25 * potential + MIDDLE) * middle
        + (0.25 * rotation) * turned
    )


def retained_of(damping, absorber):
    return 1.0 - absorber.astype(F32) * (1.0 - damping)


def band_slab_kernel(where, rotation, damping, absorber, packet, previous, potential, firsts, lasts, held, sems):
    count_r, rows, width = packet.shape

    @pl.when(where[SOURCE] == 1)
    def _():
        copies = [
            pltpu.make_async_copy(ref.at[pl.ds(count_r - 4, 4)], held.at[n], sems.at[n])
            for n, ref in enumerate((packet, previous, potential))
        ]
        for copy in copies:
            copy.start()
        for out, near in ((firsts, 0), (lasts, rows - 2)):
            for k in range(BAND):
                for r in range(2):
                    at = (count_r - BAND + k, near + r)
                    ret = retained_of(damping[at], absorber[at])
                    out[24 + 2 * k + r : 25 + 2 * k + r] = jnp.full((1, width), rotation[at], F32)
                    out[28 + 2 * k + r : 29 + 2 * k + r] = jnp.full((1, width), ret, F32)
        for copy in copies:
            copy.wait()
        for out, far, near in ((firsts, 0, 0), (lasts, rows - 4, rows - 2)):
            for k in range(4):
                out[4 * k : 4 * k + 4] = held[0, k, far : far + 4]
            for k in range(BAND):
                out[16 + 2 * k : 18 + 2 * k] = held[1, 2 + k, near : near + 2]
                out[20 + 2 * k : 22 + 2 * k] = held[2, 2 + k, near : near + 2]


def band_slabs(where, rotation, damping, absorber, packet, previous, potential):
    _, rows, width = packet.shape
    return pl.pallas_call(
        band_slab_kernel,
        in_specs=[SMEM, SMEM, SMEM, SMEM, ANY, ANY, ANY],
        out_specs=[VMEM, VMEM],
        out_shape=[jax.ShapeDtypeStruct((32, width), F32)] * 2,
        scratch_shapes=[pltpu.VMEM((3, 4, rows, width), F32), pltpu.SemaphoreType.DMA((3,))],
        name="band_slabs",
    )(where, rotation, damping, absorber, packet, previous, potential)


def band_kernel(
    where, packet, previous, potential, tables, left, right, high, low, out, field, later, turned, held, sems
):
    count_r, rows, width = packet.shape
    base = 16
    wide = rows + 16

    @pl.when(where[SOURCE] == 1)
    def _():
        copies = [
            pltpu.make_async_copy(packet.at[pl.ds(count_r - 6, 6)], field.at[pl.ds(2, 6), pl.ds(base, rows)], sems.at[0]),
            pltpu.make_async_copy(previous.at[pl.ds(count_r - 4, 4)], held.at[0], sems.at[1]),
            pltpu.make_async_copy(potential.at[pl.ds(count_r - 4, 4)], held.at[1], sems.at[2]),
        ]
        later[...] = jnp.zeros_like(later)
        field[0:2] = jnp.zeros_like(field[0:2])
        field[8:10] = jnp.zeros_like(field[8:10])
        for k in range(2, 8):
            field[k, 0:base] = jnp.zeros((base, width), F32)
            field[k, base + rows :] = jnp.zeros((base, width), F32)
        for copy in copies:
            copy.start()
        for k in range(4):
            field[4 + k, base - 4 : base] = left[4 * k : 4 * k + 4]
            field[4 + k, base + rows : base + rows + 4] = right[4 * k : 4 * k + 4]
        columns = [
            (tables[ROT, :, count_r - 4 + k : count_r - 3 + k], tables[RET, :, count_r - 4 + k : count_r - 3 + k])
            for k in range(4)
        ]
        columns = [tuple(jnp.broadcast_to(c, (rows, LANES)) for c in pair) for pair in columns]
        for copy in copies:
            copy.wait()
        window = field[4:8, base - 8 : base + rows + 8].reshape(4 * wide, width)
        turned[...] = product(halves(window), high[...], low[...])
        for k in range(4):
            rotation, retained = columns[k]
            for at in range(0, width, LANES):
                lanes = slice(at, at + LANES)
                update = doubled_hamilton(
                    field, 4 + k, base, rows, lanes,
                    turned[k * wide + 8 : k * wide + 8 + rows, lanes], held[1, k, :, lanes], rotation,
                ) - retained * held[0, k, :, lanes]
                later[k, base : base + rows, lanes] = retained * update
                if k >= 2:
                    out[(k - 2) * rows : (k - 1) * rows, lanes] = (1.0 - retained) * update
        for k in range(2, 4):
            for slab, place, inside in ((left, base - 8, 6), (right, base + rows, 0)):
                at = 16 + 2 * (k - 2)
                prev, pot, rot, ret = (slab[at + 4 * n : at + 4 * n + 2] for n in range(4))
                update = doubled_hamilton(
                    field, 4 + k, place + inside, 2, slice(None),
                    turned[k * wide + place - base + 8 + inside : k * wide + place - base + 10 + inside], pot, rot,
                ) - ret * prev
                later[k, place + inside : place + inside + 2] = ret * update
        window = later[2:4, base : base + rows].reshape(2 * rows, width)
        turned[0 : 2 * rows] = product(halves(window), high[...], low[...])
        for k in range(2, 4):
            rotation, retained = columns[k]
            for at in range(0, width, LANES):
                lanes = slice(at, at + LANES)
                update = doubled_hamilton(
                    later, k, base, rows, lanes,
                    turned[(k - 2) * rows : (k - 1) * rows, lanes], held[1, k, :, lanes], rotation,
                ) - retained * field[4 + k, base : base + rows, lanes]
                out[k * rows : (k + 1) * rows, lanes] = (1.0 - retained) * update


def bands(where, packet, previous, potential, tables, left, right, high, low):
    _, rows, width = packet.shape
    return pl.pallas_call(
        band_kernel,
        in_specs=[SMEM, ANY, ANY, ANY, VMEM, VMEM, VMEM, VMEM, VMEM],
        out_specs=VMEM,
        out_shape=jax.ShapeDtypeStruct((2 * BAND * rows, width), F32),
        scratch_shapes=[
            pltpu.VMEM((10, rows + 32, width), F32),
            pltpu.VMEM((6, rows + 32, width), F32),
            pltpu.VMEM((4 * (rows + 16), width), F32),
            pltpu.VMEM((2, 4, rows, width), F32),
            pltpu.SemaphoreType.DMA((3,)),
        ],
        compiler_params=pltpu.CompilerParams(vmem_limit_bytes=16 * MIB),
        cost_estimate=pl.CostEstimate(flops=400_000_000, bytes_accessed=4 * MIB, transcendentals=0),
        name="both_bands",
    )(where, packet, previous, potential, tables, left, right, high, low)


def prepare_kernel(
    packet, rotation, damping, absorber, index, weight, angular, after,
    top, bottom, first, last, tables, high, low, ends, sides, square, sems,
):
    count_r, rows, width = packet.shape
    copies = [
        pltpu.make_async_copy(packet.at[pl.ds(0, HALO)], ends.at[0], sems.at[0]),
        pltpu.make_async_copy(packet.at[pl.ds(count_r - HALO, HALO)], ends.at[1], sems.at[1]),
        pltpu.make_async_copy(packet.at[:, pl.ds(0, 8)], sides.at[0], sems.at[2]),
        pltpu.make_async_copy(packet.at[:, pl.ds(rows - 8, 8)], sides.at[1], sems.at[3]),
    ]
    for copy in copies:
        copy.start()
    square[...] = jnp.zeros_like(square)
    values = [rotation[...], retained_of(damping[...], absorber[...])]
    values += [index[n].astype(F32) for n in range(STENCILS)]
    values += [weight[n] for n in range(STENCILS)]
    for n, value in enumerate(values):
        square[0:count_r, 0:rows] = value
        turned = square[...].T[0:rows]
        tables[n] = turned
        if n >= INDEX:
            at = (n - INDEX) * HALO
            edges = HALO * rows
            columns = HALO * count_r
            top[edges + at : edges + at + HALO, 0:rows] = value[0:HALO]
            bottom[edges + at : edges + at + HALO, 0:rows] = value[count_r - HALO :]
            first[columns + at : columns + at + HALO, 0:LANES] = turned[0:HALO]
            last[columns + at : columns + at + HALO, 0:LANES] = turned[rows - HALO : rows]
    high[...], low[...] = halves(angular[...])
    for copy in copies:
        copy.wait()
    for out, n in ((top, 0), (bottom, 1)):
        for k in range(HALO):
            out[k * rows : (k + 1) * rows] = ends[n, k]
    for out, n, near in ((first, 0, 0), (last, 1, 8 - HALO)):
        for k in range(count_r):
            for r in range(HALO):
                out[r * count_r + k : r * count_r + k + 1] = sides[n, k, near + r : near + r + 1]


def prepare(packet, rotation, damping, absorber, index, weight, angular, after):
    count_r, rows, width = packet.shape
    ends = jax.ShapeDtypeStruct((HALO * rows + EXTRA, width), F32)
    sides = jax.ShapeDtypeStruct((HALO * count_r + EXTRA, width), F32)
    part = jax.ShapeDtypeStruct(angular.shape, BF16)
    return pl.pallas_call(
        prepare_kernel,
        in_specs=[ANY, VMEM, VMEM, VMEM, VMEM, VMEM, VMEM, ANY],
        out_specs=[VMEM] * 7,
        out_shape=[ends, ends, sides, sides, jax.ShapeDtypeStruct((TABLES, rows, LANES), F32), part, part],
        scratch_shapes=[
            pltpu.VMEM((2, HALO, rows, width), F32),
            pltpu.VMEM((2, count_r, 8, width), F32),
            pltpu.VMEM((LANES, LANES), F32),
            pltpu.SemaphoreType.DMA((4,)),
        ],
        compiler_params=pltpu.CompilerParams(vmem_limit_bytes=16 * MIB),
        cost_estimate=pl.CostEstimate(flops=1_000_000, bytes_accessed=6 * MIB, transcendentals=0),
        name="prepare",
    )(packet, rotation, damping, absorber, index, weight, angular, after)


def put_sides(sides, left, right, count_r, left_more=None, right_more=None):
    def body(k, carry):
        for r in range(HALO):
            at = pl.ds(r * count_r + k, 1)
            before, behind = left[at], right[at]
            if left_more is not None:
                before, behind = before + left_more[at], behind + right_more[at]
            sides[k, r : r + 1] = behind
            sides[k, 8 - HALO + r : 8 - HALO + r + 1] = before
        return carry

    lax.fori_loop(0, count_r, body, 0, unroll=8)


def advance(step, chunk, field, sides, previous, potential, tables, high, low, put):
    rows = previous.shape[1]
    width = previous.shape[2]
    here = step * chunk
    shift = lax.rem(LANES - here, LANES)
    columns = [pltpu.roll(tables[n], shift, 1) for n in (ROT, RET)]
    window = field[pl.ds(HALO + here, chunk)].reshape(chunk * rows, width)
    split = halves(window)
    wide = 2 * LANES
    for tile in range(0, width, wide):
        turned = product(split, high[:, tile : tile + wide], low[:, tile : tile + wide])
        for k in range(chunk):
            rotation = jnp.broadcast_to(0.25 * columns[0][:, k : k + 1], (rows, LANES))
            retained = jnp.broadcast_to(columns[1][:, k : k + 1], (rows, LANES))
            for at in range(tile, tile + wide, LANES):
                lanes = slice(at, at + LANES)

                def row(shift):
                    return field[HALO + here + k + shift, :, lanes]

                middle = row(0)
                ring = jnp.concatenate([middle, sides[here + k, :, lanes]], axis=0)
                around = [pltpu.roll(ring, s, 0)[:rows] for s in (1, rows + 7, 2, rows + 6)]
                near = row(-1) + row(1) + (around[0] + around[1])
                far = row(-2) + row(2) + (around[2] + around[3])
                update = (
                    SIDE1 * near
                    + SIDE2 * far
                    + (0.25 * potential[here + k, :, lanes] + MIDDLE) * middle
                    + rotation * turned[k * rows : (k + 1) * rows, at - tile : at - tile + LANES]
                    - retained * previous[here + k, :, lanes]
                )
                put(here + k, lanes, retained * update)


def pieces(count, chunk):
    return [pl.ds(n * chunk, chunk) for n in range(count // chunk)]


def first_kernel(
    packet, previous, potential, tables, up, down, left, right, high, low, after,
    out, top, bottom, first, last, field, prev, pot, done, sides, sems,
):
    count_r, rows, width = packet.shape
    steps = count_r // CHUNK
    into = []
    for n, part in enumerate(pieces(count_r, CHUNK)):
        into.append(
            [
                pltpu.make_async_copy(packet.at[part], field.at[pl.ds(HALO + n * CHUNK, CHUNK)], sems.at[0, n]),
                pltpu.make_async_copy(previous.at[part], prev.at[part], sems.at[1, n]),
                pltpu.make_async_copy(potential.at[part], pot.at[part], sems.at[2, n]),
            ]
        )
    for group in into:
        for copy in group:
            copy.start()
    for k in range(HALO):
        field[k] = up[k * rows : (k + 1) * rows]
        field[HALO + count_r + k] = down[k * rows : (k + 1) * rows]
    put_sides(sides, left, right, count_r)
    into[0][0].wait()
    outs = []
    for step in range(steps):
        if step + 1 < steps:
            into[step + 1][0].wait()
        into[step][1].wait()
        into[step][2].wait()

        def put(k, lanes, value):
            done[k, :, lanes] = value

        advance(step, CHUNK, field, sides, prev, pot, tables, high, low, put)
        part = pl.ds(step * CHUNK, CHUNK)
        outs.append(pltpu.make_async_copy(done.at[part], out.at[part], sems.at[3, step]))
        outs[-1].start()
        for k in range(step * CHUNK, (step + 1) * CHUNK):
            for r in range(HALO):
                first[r * count_r + k : r * count_r + k + 1] = done[k, r : r + 1]
                last[r * count_r + k : r * count_r + k + 1] = done[k, rows - HALO + r : rows - HALO + r + 1]
    for k in range(HALO):
        top[k * rows : (k + 1) * rows] = done[k]
        bottom[k * rows : (k + 1) * rows] = done[count_r - HALO + k]
    for copy in outs:
        copy.wait()


def first_iteration(packet, previous, potential, tables, halos, high, low, after):
    count_r, rows, width = packet.shape
    ends = jax.ShapeDtypeStruct((HALO * rows, width), F32)
    sides = jax.ShapeDtypeStruct((HALO * count_r, width), F32)
    return pl.pallas_call(
        first_kernel,
        in_specs=[ANY, ANY, ANY, *[VMEM] * 7, ANY],
        out_specs=[ANY, *[VMEM] * 4],
        out_shape=[jax.ShapeDtypeStruct(packet.shape, F32), ends, ends, sides, sides],
        scratch_shapes=[
            pltpu.VMEM((count_r + 2 * HALO, rows, width), F32),
            pltpu.VMEM(packet.shape, F32),
            pltpu.VMEM(packet.shape, F32),
            pltpu.VMEM(packet.shape, F32),
            pltpu.VMEM((count_r, 8, width), F32),
            pltpu.SemaphoreType.DMA((4, count_r // CHUNK)),
        ],
        compiler_params=pltpu.CompilerParams(vmem_limit_bytes=40 * MIB),
        cost_estimate=pl.CostEstimate(flops=7_000_000_000, bytes_accessed=20 * MIB, transcendentals=0),
        name="first_iteration",
    )(packet, previous, potential, tables, *halos, high, low, after)


def stencil_kernel(where, tables, up, down, left, right, after, high, low, edge_high, edge_low, square):
    _, rows, _ = tables.shape
    count_r = left.shape[0] // HALO - EXTRA // HALO
    width = high.shape[1]
    per = rows * BAND
    shift_owner = per.bit_length() - 1
    chips = width // per // CORES

    def place(value):
        index = value.astype(jnp.int32)
        owner = index >> shift_owner
        inside = index & (per - 1)
        core = (owner & 1) ^ where[CORE]
        chip = (where[CHIP] - (owner >> 1)) & (chips - 1)
        slot = ((core * chips + chip) << shift_owner) + (inside & 1) * rows + (inside >> 1)
        return slot.astype(F32)

    column = lax.broadcasted_iota(jnp.int32, (32, LANES), 1).astype(F32)

    def fill(at, places, weights, high_out, low_out):
        places = [jnp.broadcast_to(p, (32, LANES)) for p in places]
        weights = [jnp.broadcast_to(w, (32, LANES)) for w in weights]
        for tile in range(0, width, LANES):
            here = column + float(tile)
            total = jnp.where(here == places[0], weights[0], 0.0)
            for n in range(1, STENCILS):
                total += jnp.where(here == places[n], weights[n], 0.0)
            upper, lower = halves(total)
            high_out[pl.ds(at, 32), tile : tile + LANES] = upper
            low_out[pl.ds(at, 32), tile : tile + LANES] = lower

    @pl.when(where[PRODUCT] == 1)
    def _():
        places = [place(tables[INDEX + n]) for n in range(STENCILS)]
        weights = [tables[WEIGHT + n] for n in range(STENCILS)]
        group = 8

        def body(step, carry):
            shift = lax.rem(LANES - step * group, LANES)
            moved = [pltpu.roll(value, shift, 1) for value in places + weights]
            for k in range(group):
                cut = [value[:, k : k + 1] for value in moved]
                at = pl.multiple_of((step * group + k) * rows, rows)
                fill(at, cut[:STENCILS], cut[STENCILS:], high, low)
            return carry

        lax.fori_loop(0, count_r // group, body, 0)

        square[...] = jnp.zeros_like(square)
        for n, side in enumerate((up, down, left, right)):
            begin = side.shape[0] - EXTRA
            square[n * EXTRA : n * EXTRA + EXTRA // 2] = place(side[begin : begin + EXTRA // 2, 0:LANES])
            square[n * EXTRA + EXTRA // 2 : (n + 1) * EXTRA] = side[begin + EXTRA // 2 : begin + EXTRA, 0:LANES]
        turned = square[...].T
        at = 0
        for n, length in enumerate((rows, rows, count_r, count_r)):
            for e in range(HALO):
                for begin in range(0, length, 32):
                    cut = [
                        turned[begin : begin + 32, n * EXTRA + HALO * m + e : n * EXTRA + HALO * m + e + 1]
                        for m in range(2 * STENCILS)
                    ]
                    fill(at, cut[:STENCILS], cut[STENCILS:], edge_high, edge_low)
                    at += 32


def stencil_matrix(where, tables, halos, columns, after):
    rows = tables.shape[1]
    count_r = halos[2].shape[0] // HALO - EXTRA // HALO
    points = jax.ShapeDtypeStruct((count_r * rows, columns), BF16)
    edges = jax.ShapeDtypeStruct((2 * HALO * (rows + count_r), columns), BF16)
    return pl.pallas_call(
        stencil_kernel,
        in_specs=[SMEM, *[VMEM] * 5, ANY],
        out_specs=[VMEM] * 4,
        out_shape=[points, points, edges, edges],
        scratch_shapes=[pltpu.VMEM((LANES, LANES), F32)],
        compiler_params=pltpu.CompilerParams(vmem_limit_bytes=16 * MIB),
        cost_estimate=pl.CostEstimate(flops=15_000_000, bytes_accessed=6 * MIB, transcendentals=0),
        name="stencil_matrix",
    )(where, tables, *halos, after)


def last_kernel(
    where, one, packet, potential, tables, up, down, left, right, high, low,
    stencil_high, stencil_low, edge_high, edge_low, own_table, other_table,
    earlier, latest, field, prev, pot, done, sides, split_high, split_low, table, source, sems,
):
    count_r, rows, width = packet.shape
    steps = count_r // LAST
    is_product = where[PRODUCT] == 1
    quarter = own_table.shape[1]
    half = quarter // 2
    chips = own_table.shape[0]
    size = LAST * rows
    parts = pieces(count_r, LAST)

    def field_part(n):
        return field.at[pl.ds(HALO + n * LAST, LAST)]

    ones, highs, lows, prevs, pots = [], [], [], [], []
    for n, part in enumerate(parts):
        cut = pl.ds(n * size, size)
        ones.append(pltpu.make_async_copy(one.at[part], field_part(n), sems.at[0, n]))
        highs.append(pltpu.make_async_copy(stencil_high.at[cut], split_high.at[cut], sems.at[1, n]))
        lows.append(pltpu.make_async_copy(stencil_low.at[cut], split_low.at[cut], sems.at[2, n]))
        prevs.append(pltpu.make_async_copy(packet.at[part], prev.at[part], sems.at[3, n]))
        pots.append(pltpu.make_async_copy(potential.at[part], pot.at[part], sems.at[4, n]))
    earliers = [pltpu.make_async_copy(field_part(n), earlier.at[part], sems.at[5, n]) for n, part in enumerate(parts)]
    latests = [pltpu.make_async_copy(done.at[part], latest.at[part], sems.at[6, n]) for n, part in enumerate(parts)]

    def put_ends(up_value, down_value):
        for k in range(HALO):
            field[k] = up_value[k * rows : (k + 1) * rows]
            field[HALO + count_r + k] = down_value[k * rows : (k + 1) * rows]

    @pl.when(is_product)
    def _():
        for n in range(steps):
            ones[n].start()
            highs[n].start()
            lows[n].start()
        for n in range(steps):
            prevs[n].start()
            pots[n].start()
        for side, ref in enumerate((own_table, other_table)):
            for k in range(chips):
                at = (side * chips + k) * half
                for band in range(2):
                    upper, lower = halves(ref[k, band * half : (band + 1) * half])
                    table[2 * band, at : at + half] = upper
                    table[2 * band + 1, at : at + half] = lower
        source[...] = product((edge_high[...], edge_low[...]), table[0], table[1])
        edges = HALO * rows
        columns = HALO * count_r
        put_ends(up[...] + source[:edges], down[...] + source[edges : 2 * edges])
        put_sides(
            sides, left, right, count_r,
            source.at[pl.ds(2 * edges, columns)], source.at[pl.ds(2 * edges + columns, columns)],
        )
        for n in range(steps):
            ones[n].wait()
            highs[n].wait()
            lows[n].wait()
            cut = pl.ds(n * size, size)
            weights = (split_high[cut], split_low[cut])
            here = pl.ds(HALO + n * LAST, LAST)
            field[here] = field[here] + product(weights, table[0], table[1]).reshape(LAST, rows, width)
            done[parts[n]] = product(weights, table[2], table[3]).reshape(LAST, rows, width)
            earliers[n].start()

    @pl.when(jnp.logical_not(is_product))
    def _():
        for n in range(steps):
            ones[n].start()
            prevs[n].start()
            pots[n].start()
        put_ends(up, down)
        put_sides(sides, left, right, count_r)
        done[...] = jnp.zeros_like(done)
        for n in range(steps):
            ones[n].wait()
            earliers[n].start()

    def put(k, lanes, value):
        done[k, :, lanes] += value

    for n in range(steps):
        prevs[n].wait()
        pots[n].wait()
        advance(n, LAST, field, sides, prev, pot, tables, high, low, put)
        latests[n].start()
    for copy in earliers + latests:
        copy.wait()


def last_iteration(where, one, packet, potential, tables, halos, high, low, matrices, band_tables):
    count_r, rows, width = packet.shape
    steps = count_r // LAST
    columns = matrices[0].shape[1]
    return pl.pallas_call(
        last_kernel,
        in_specs=[SMEM, ANY, ANY, ANY, *[VMEM] * 7, ANY, ANY, *[VMEM] * 4],
        out_specs=[ANY, ANY],
        out_shape=[jax.ShapeDtypeStruct(packet.shape, F32)] * 2,
        scratch_shapes=[
            pltpu.VMEM((count_r + 2 * HALO, rows, width), F32),
            pltpu.VMEM(packet.shape, F32),
            pltpu.VMEM(packet.shape, F32),
            pltpu.VMEM(packet.shape, F32),
            pltpu.VMEM((count_r, 8, width), F32),
            pltpu.VMEM((count_r * rows, columns), BF16),
            pltpu.VMEM((count_r * rows, columns), BF16),
            pltpu.VMEM((4, columns, width), BF16),
            pltpu.VMEM((2 * HALO * (rows + count_r), width), F32),
            pltpu.SemaphoreType.DMA((7, steps)),
        ],
        compiler_params=pltpu.CompilerParams(vmem_limit_bytes=56 * MIB),
        cost_estimate=pl.CostEstimate(flops=20_000_000_000, bytes_accessed=36 * MIB, transcendentals=0),
        name="last_iteration",
    )(where, one, packet, potential, tables, *halos, high, low, *matrices, *band_tables)


def neighbours(axis, upward, downward):
    count = lax.axis_size(axis)
    return (
        lax.ppermute(upward, axis, [(i, i + 1) for i in range(count - 1)]),
        lax.ppermute(downward, axis, [(i + 1, i) for i in range(count - 1)]),
    )


def exchange(top, bottom, first, last):
    left, right = neighbours("row", last, first)
    up, down = neighbours("rr", bottom, top)
    return up, down, left, right


def local(packet, previous, potential, rotation, angular, damping, absorber, stencil_index, stencil_weight):
    packet, previous, potential = packet[0], previous[0], potential[0]
    rotation, angular, damping, absorber = rotation[0], angular[0], damping[0], absorber[0]
    count_r, rows, width = packet.shape
    sect = lax.axis_index("sect")
    rr = lax.axis_index("rr")
    row = lax.axis_index("row")
    count_rr, count_row = (lax.axis_size(name) for name in ("rr", "row"))
    chips = count_row // CORES
    where = jnp.stack(
        [((sect == 0) & (rr == count_rr - 1)).astype(jnp.int32), sect, row % CORES, row // CORES]
    ).astype(jnp.int32)

    firsts, lasts = band_slabs(where, rotation, damping, absorber, packet, previous, potential)
    axes = ("sect", "rr", "row")
    sources = (count_rr - 1) * count_row
    band_left = lax.ppermute(lasts, axes, [(sources + i, sources + i + 1) for i in range(count_row - 1)])
    band_right = lax.ppermute(firsts, axes, [(sources + i + 1, sources + i) for i in range(count_row - 1)])

    top, bottom, first, last, tables, high, low = prepare(
        packet, rotation, damping, absorber, stencil_index, stencil_weight, angular, firsts
    )
    table = bands(where, packet, previous, potential, tables, band_left, band_right, high, low)
    halos = exchange(top, bottom, first, last)

    plane = ("sect", "rr")
    half = count_rr // FAR
    start = count_rr - 1
    entries = [count_rr + (k + 1) * half - 1 for k in range(FAR)]
    piece = sum(lax.ppermute(table, plane, [(start, entry)]) for entry in entries)
    spread = piece
    for shift in (1, half - 1, 2):
        spread = spread + lax.ppermute(
            piece, plane, [(entry, entry - (half - 1) + (half - 1 + shift) % half) for entry in entries]
        )
    line = ("sect", "row")

    def around(shift):
        pairs = []
        for chip in range(chips):
            for core in range(CORES):
                pairs.append(
                    (count_row + chip * CORES + core, count_row + ((chip + shift) % chips) * CORES + core)
                )
        return lax.ppermute(spread, line, pairs)

    own = jnp.stack([spread, around(1), around(2), around(3)], axis=0)
    other = lax.ppermute(
        own, line, [(count_row + i, count_row + i + 1 - 2 * (i % CORES)) for i in range(count_row)]
    )

    one, *edges = first_iteration(packet, previous, potential, tables, halos, high, low, table)
    matrices = stencil_matrix(where, tables, halos, count_row * rows * BAND, piece)
    later = exchange(*edges)
    earlier, latest = last_iteration(
        where, one, packet, potential, tables, later, high, low, matrices, (own, other)
    )
    return latest[None], earlier[None]


def solution(mesh):
    in_specs = (
        P("sect", "rr", "row", None),
        P("sect", "rr", "row", None),
        P("sect", "rr", "row", None),
        P("sect", "rr", "row"),
        P("sect", None, None),
        P("sect", "rr", "row"),
        P("sect", "rr", "row"),
        P(None, "rr", "row"),
        P(None, "rr", "row"),
    )
    out_specs = (P("sect", "rr", "row", None), P("sect", "rr", "row", None))
    return jax.shard_map(local, mesh=mesh, in_specs=in_specs, out_specs=out_specs, check_vma=False)
```

time: 394 us -> 136 us (0.35)
  waiting for transfers between devices: 189 us -> 23.1 us
  local copies, waits for them, and re-layouts: 89.9 us -> 20 us
  Pallas kernels: 0 us -> 40.3 us
  matrix products: 33.9 us -> 0 us
  other arithmetic: 29.9 us -> 0.84 us
  starting transfers between devices: 34.1 us -> 49 us
  between operations: 14.5 us -> 1.37 us
    all_gather x2 -> x0, waiting for transfers between devices: 164 us -> none  [local(): gathered = lax.all_gather(crossed, ('rr', 'row'), axis=0, tiled=True)]
    gather x8 -> x0, local copies, waits for them, and re-layouts: 71.2 us -> none  [interpolate(): jnp.take(band_table, stencil_index[stencil].reshape(-1), axis=0)]
    pallas_call x0 -> x6, Pallas kernels: none -> 40.3 us  [the longest x1 20.5 us: last_iteration(): pl.pallas_call(last_kernel, in_specs=[SMEM, ANY, ANY, ANY, *[VMEM] * 7, A...]
    dot_general x2 -> x0, matrix products: 33.9 us -> none  [scaled_hamilton(): jnp.dot(field.reshape(-1, width), angular, precision=lax.Precision.HIGHEST)]
    ppermute x10 -> x19, starting transfers between devices: 34 us -> 49 us  [the longest x4 17.4 us: neighbours(): lax.ppermute(downward, axis, [(i + 1, i) for i in range(count - 1)])]
    concatenate x2 -> x0, other arithmetic: 12.5 us -> none  [extended(): jnp.concatenate([lax.ppermute(tail, axis, [(i, (i + 1) % count) for i in...]
    select_n x8 -> x0, other arithmetic: 7.99 us -> none  [interpolate(): jnp.take(band_table, stencil_index[stencil].reshape(-1), axis=0)]
    unnamed x39 -> x57, local copies, waits for them, and re-layouts: 13.4 us -> 20 us
  transfers between devices with their start and end apart: 12 -> 19, of which waited for: 12 -> 3; matrix products, arithmetic and copies ran while one was open for 0% -> 0% of each run, Pallas kernels for 0% -> 12%
where the time goes in v2:
time: 136 us; the launch traced here: 135 us
  starting transfers between devices  49 us (36%)
  Pallas kernels  40.3 us (30%)
  waiting for transfers between devices  23.1 us (17%)
  local copies, waits for them, and re-layouts  20 us (15%)
  between operations  1.37 us (1%)
    ppermute x3, waiting for transfers between devices, local(): lax.ppermute(piece, plane, [(entry, entry - (half - 1) + (half - 1 + shif...  21.1 us
    pallas_call x1, Pallas kernels, last_iteration(): pl.pallas_call(last_kernel, in_specs=[SMEM, ANY, ANY, ANY, *[VMEM] * 7, A...  20.5 us
    unnamed x57, local copies, waits for them, and re-layouts  20 us
    ppermute x4, starting transfers between devices, neighbours(): lax.ppermute(downward, axis, [(i + 1, i) for i in range(count - 1)])  17.4 us
    ppermute x4, starting transfers between devices, neighbours(): lax.ppermute(upward, axis, [(i, i + 1) for i in range(count - 1)])  12.3 us
    ppermute x3, starting transfers between devices, around(): return lax.ppermute(spread, line, pairs)  12.1 us
    pallas_call x1, Pallas kernels, first_iteration(): pl.pallas_call(first_kernel, in_specs=[ANY, ANY, ANY, *[VMEM] * 7, ANY],...  9.13 us
    pallas_call x1, Pallas kernels, stencil_matrix(): pl.pallas_call(stencil_kernel, in_specs=[SMEM, *[VMEM] * 5, ANY], out_spe...  5.57 us
  transfers between devices with their start and end apart: 19, of which 3 were waited for; matrix products, arithmetic and copies ran while one was open for 0% of the time, Pallas kernels for 12%

profile of v2, /device:TPU:7, one launch (start us, length us, event | category | flops | bytes accessed | tf_op | source)
XLA Modules:
  0.0 134.5 jit_solution(14531194537354609294)
XLA Ops:
  0.7 1.4 %copy.11 = f32[1,64,32]{2,1,0:T(8,128)} copy(f32[1,64,32]{1,2,0:T(8,128)} %param.12) | data formatting | bytes 16384 | tf_op args[3]
  2.1 1.4 %copy.12 = f32[1,64,32]{2,1,0:T(8,128)} copy(f32[1,64,32]{1,2,0:T(8,128)} %param.14) | data formatting | bytes 16384 | tf_op args[5]
  3.5 1.4 %copy.13 = s32[1,64,32]{2,1,0:T(8,128)} copy(s32[1,64,32]{1,2,0:T(8,128)} %param.15) | data formatting | bytes 16384 | tf_op args[6]
  4.9 0.6 pad_add_fusion.where
  5.5 3.1 %band_slabs.1 = (f32[32,512]{1,0:T(8,128)}, f32[32,512]{1,0:T(8,128)}) custom-call(s32[4]{0:T(128)} %pad_add_fusion.where, f32[64,32]{1,0:T(8,128)} %bitcast.30, f32[64,32]{1,0:T(8,128)} %bitcast.32, s32[64,32]{1,0:T(8,128)} %bitcast.34, f32[64,32,512]{2,1,0:T(8,128)} %bitcast.17, f32[64,32,512]{2,1,0:T(8,128)} %bitcast.22, f32[64,32,512]{2,1,0:T(8,128)} %bitcast.25), custom_call_target="tpu_custom_call" | custom-call | tf_op jit(solution)/shard_map/band_slabs/pallas_call | solution.py:95
  8.6 0.7 collective-permute-start.4
  9.3 0.7 collective-permute-start.5
  10.0 0.1 copy.14.index
  10.1 0.1 copy.15.weight
  10.3 0.0 copy-start
  10.3 2.2 %copy-done = f32[1,64,32,512]{3,2,1,0:T(8,128)S(1)} copy-done((f32[1,64,32,512]{3,2,1,0:T(8,128)S(1)}, f32[1,64,32,512]{3,2,1,0:T(8,128)}, u32[]{:S(2)}) %copy-start) | copy-done | bytes 4194328
  12.5 0.8 copy-done.11
  13.3 1.3 %prepare.1 = (f32[80,512]{1,0:T(8,128)S(1)}, f32[80,512]{1,0:T(8,128)S(1)}, f32[144,512]{1,0:T(8,128)S(1)}, f32[144,512]{1,0:T(8,128)S(1)}, f32[10,32,128]{2,1,0...) custom-call(f32[64,32,512]{2,1,0:T(8,128)S(1)} %bitcast.19, f32[64,32]{1,0:T(8,128)S(1)} %bitcast.31, ...), custom_call_target="tpu_custom_call" | custom-call | flops 1000000 | bytes 6291456 | tf_op jit(solution)/shard_map/prepare/pallas_call | solution.py:238
  14.7 0.0 collective-permute-done.4.left
  14.7 0.0 collective-permute-done.5.right
  14.7 0.8 copy-done.1
  15.5 2.2 %copy-done.2 = f32[1,64,32,512]{3,2,1,0:T(8,128)S(1)} copy-done((f32[1,64,32,512]{3,2,1,0:T(8,128)S(1)}, f32[1,64,32,512]{3,2,1,0:T(8,128)}, u32[]{:S(2)}) %copy-start.2) | copy-done | bytes 4194328
  17.7 2.2 %copy-done.3 = f32[1,64,32,512]{3,2,1,0:T(8,128)S(1)} copy-done((f32[1,64,32,512]{3,2,1,0:T(8,128)S(1)}, f32[1,64,32,512]{3,2,1,0:T(8,128)}, u32[]{:S(2)}) %copy-start.3) | copy-done | bytes 4194328
  19.9 0.6 both_bands.1.after
  20.4 0.7 collective-permute-start.11
  21.1 0.7 collective-permute-start.10
  21.8 0.0 collective-permute-done.11
  21.8 0.0 collective-permute-done.10
  21.9 0.7 collective-permute-start.14
  22.6 0.7 collective-permute-start.13
  23.2 1.3 collective-permute-start.12
  24.5 0.0 collective-permute-done.14
  24.6 0.0 collective-permute-done.13
  24.6 21.1 %collective-permute-done.12 = f32[128,512]{1,0:T(8,128)S(1)} collective-permute-done((f32[128,512]{1,0:T(8,128)S(1)}, f32[128,512]{1,0:T(8,128)S(1)}, u32[]{:S(2)}, u32[]{:S(2)}) %collective-permute-start.12) | collective-permute-done | bytes 262176 | tf_op jit(solution)/shard_map/ppermute | solution.py:628
  45.7 0.1 add_add_fusion
  45.8 3.6 %collective-permute-start.17 = (f32[128,512]{1,0:T(8,128)S(1)}, f32[128,512]{1,0:T(8,128)S(1)}, u32[]{:S(2)}, u32[]{:S(2)}) collective-permute-start(f32[128,512]{1,0:T(8,128)S(1)} %add_add_fusion), channel_id=1, source_target_pairs={{64,70},{65,71},{66,64},{67,65},{68,66},{69,67},{70,68},{71,69},{7... | collective-permute-start | bytes 786440 | tf_op jit(solution)/shard_map/ppermute | solution.py:640
  49.4 6.6 %collective-permute-start.16 = (f32[128,512]{1,0:T(8,128)S(1)}, f32[128,512]{1,0:T(8,128)S(1)}, u32[]{:S(2)}, u32[]{:S(2)}) collective-permute-start(f32[128,512]{1,0:T(8,128)S(1)} %add_add_fusion), channel_id=1, source_target_pairs={{64,68},{65,69},{66,70},{67,71},{68,64},{69,65},{70,66},{71,67},{7... | collective-permute-start | bytes 786440 | tf_op jit(solution)/shard_map/ppermute | solution.py:640
  55.9 1.9 %collective-permute-start.15 = (f32[128,512]{1,0:T(8,128)S(1)}, f32[128,512]{1,0:T(8,128)S(1)}, u32[]{:S(2)}, u32[]{:S(2)}) collective-permute-start(f32[128,512]{1,0:T(8,128)S(1)} %add_add_fusion), channel_id=1, source_target_pairs={{64,66},{65,67},{66,68},{67,69},{68,70},{69,71},{70,64},{71,65},{7... | collective-permute-start | bytes 786440 | tf_op jit(solution)/shard_map/ppermute | solution.py:640
  57.9 4.0 %collective-permute-start.2 = (f32[144,512]{1,0:T(8,128)S(1)}, f32[144,512]{1,0:T(8,128)S(1)}, u32[]{:S(2)}, u32[]{:S(2)}) collective-permute-start(f32[144,512]{1,0:T(8,128)S(1)} %get-tuple-element.26), channel_id=1, source_target_pairs={{0,1},{1,2},{2,3},{3,4},{4,5},{5,6},{6,7},{8,9},{9,10},{10,11},{11... | collective-permute-start | bytes 884744 | tf_op jit(solution)/shard_map/ppermute | solution.py:585
  61.9 1.9 %collective-permute-start.3 = (f32[144,512]{1,0:T(8,128)S(1)}, f32[144,512]{1,0:T(8,128)S(1)}, u32[]{:S(2)}, u32[]{:S(2)}) collective-permute-start(f32[144,512]{1,0:T(8,128)S(1)} %get-tuple-element.27), channel_id=1, source_target_pairs={{1,0},{2,1},{3,2},{4,3},{5,4},{6,5},{7,6},{9,8},{10,9},{11,10},{12... | collective-permute-start | bytes 884744 | tf_op jit(solution)/shard_map/ppermute | solution.py:586
  63.8 0.0 collective-permute-done.17
  63.8 2.1 %collective-permute-start = (f32[80,512]{1,0:T(8,128)S(1)}, f32[80,512]{1,0:T(8,128)S(1)}, u32[]{:S(2)}, u32[]{:S(2)}) collective-permute-start(f32[80,512]{1,0:T(8,128)S(1)} %get-tuple-element.24), channel_id=1, source_target_pairs={{0,8},{8,16},{16,24},{24,32},{32,40},{40,48},{48,56},{1,9},{9,17},... | collective-permute-start | bytes 491528 | tf_op jit(solution)/shard_map/ppermute | solution.py:585
  66.0 0.0 collective-permute-done.16
  66.0 6.8 %collective-permute-start.1 = (f32[80,512]{1,0:T(8,128)S(1)}, f32[80,512]{1,0:T(8,128)S(1)}, u32[]{:S(2)}, u32[]{:S(2)}) collective-permute-start(f32[80,512]{1,0:T(8,128)S(1)} %get-tuple-element.25), channel_id=1, source_target_pairs={{8,0},{16,8},{24,16},{32,24},{40,32},{48,40},{56,48},{9,1},{17,9},... | collective-permute-start | bytes 491528 | tf_op jit(solution)/shard_map/ppermute | solution.py:586
  72.7 0.0 collective-permute-done.15
  72.8 0.1 pad_maximum_fusion.own_table
  72.8 1.9 %collective-permute-start.18 = (f32[4,128,512]{2,1,0:T(8,128)S(1)}, f32[4,128,512]{2,1,0:T(8,128)S(1)}, u32[]{:S(2)}, u32[]{:S(2)}) collective-permute-start(f32[4,128,512]{2,1,0:T(8,128)S(1)} %pad_maximum_fusion.own_table), channel_id=1, source_target_pairs={{64,65},{65,64},{66,67},{67,66},{68,69},{69,68},{70,71},{71,70},{7... | collective-permute-start | bytes 3145736 | tf_op jit(solution)/shard_map/ppermute | solution.py:643
  74.8 0.1 collective-permute-done.up
  74.9 1.8 %collective-permute-done.1.down = f32[80,512]{1,0:T(8,128)S(1)} collective-permute-done((f32[80,512]{1,0:T(8,128)S(1)}, f32[80,512]{1,0:T(8,128)S(1)}, u32[]{:S(2)}, u32[]{:S(2)}) %collective-permute-start.1) | collective-permute-done | bytes 163872 | tf_op jit(solution)/shard_map/ppermute | solution.py:586
  76.7 0.0 collective-permute-done.2.left
  76.7 0.0 collective-permute-done.3.right
  76.7 9.1 %first_iteration.1 = (f32[64,32,512]{2,1,0:T(8,128)S(1)}, f32[64,512]{1,0:T(8,128)S(1)}, f32[64,512]{1,0:T(8,128)S(1)}, f32[128,512]{1,0:T(8,128)S(1)}, f32[128,512]{1,0:T(8,128)S(1)}) custom-call(f32[64,32,512]{2,1,0:T(8,128)S(1)} %bitcast.21, f32[64,32,512]{2,1,0:T(8,128)} %bitcast.23, f32[64,32,512]{2,1,0:T(8,128)} %bitcast.26, ...), custom_call_target="tpu_custom_call" | custom-call | flops 7000000000 | bytes 20971520 | tf_op jit(solution)/shard_map/first_iteration/pallas_call | solution.py:360
  85.9 1.9 %copy-done.17 = f32[64,32,512]{2,1,0:T(8,128)} copy-done((f32[64,32,512]{2,1,0:T(8,128)}, f32[64,32,512]{2,1,0:T(8,128)S(1)}, u32[]{:S(2)}) %copy-start.17) | copy-done | bytes 4194328
  87.8 3.3 %collective-permute-start.8 = (f32[128,512]{1,0:T(8,128)S(1)}, f32[128,512]{1,0:T(8,128)S(1)}, u32[]{:S(2)}, u32[]{:S(2)}) collective-permute-start(f32[128,512]{1,0:T(8,128)S(1)} %get-tuple-element.34), channel_id=1, source_target_pairs={{0,1},{1,2},{2,3},{3,4},{4,5},{5,6},{6,7},{8,9},{9,10},{10,11},{11... | collective-permute-start | bytes 786440 | tf_op jit(solution)/shard_map/ppermute | solution.py:585
  91.1 1.9 %collective-permute-start.9 = (f32[128,512]{1,0:T(8,128)S(1)}, f32[128,512]{1,0:T(8,128)S(1)}, u32[]{:S(2)}, u32[]{:S(2)}) collective-permute-start(f32[128,512]{1,0:T(8,128)S(1)} %get-tuple-element.35), channel_id=1, source_target_pairs={{1,0},{2,1},{3,2},{4,3},{5,4},{6,5},{7,6},{9,8},{10,9},{11,10},{12... | collective-permute-start | bytes 786440 | tf_op jit(solution)/shard_map/ppermute | solution.py:586
  93.1 2.9 %collective-permute-start.6 = (f32[64,512]{1,0:T(8,128)S(1)}, f32[64,512]{1,0:T(8,128)S(1)}, u32[]{:S(2)}, u32[]{:S(2)}) collective-permute-start(f32[64,512]{1,0:T(8,128)S(1)} %get-tuple-element.32), channel_id=1, source_target_pairs={{0,8},{8,16},{16,24},{24,32},{32,40},{40,48},{48,56},{1,9},{9,17},... | collective-permute-start | bytes 393224 | tf_op jit(solution)/shard_map/ppermute | solution.py:585
  95.9 6.8 %collective-permute-start.7 = (f32[64,512]{1,0:T(8,128)S(1)}, f32[64,512]{1,0:T(8,128)S(1)}, u32[]{:S(2)}, u32[]{:S(2)}) collective-permute-start(f32[64,512]{1,0:T(8,128)S(1)} %get-tuple-element.33), channel_id=1, source_target_pairs={{8,0},{16,8},{24,16},{32,24},{40,32},{48,40},{56,48},{9,1},{17,9},... | collective-permute-start | bytes 393224 | tf_op jit(solution)/shard_map/ppermute | solution.py:586
  102.7 5.6 %stencil_matrix.1 = (bf16[2048,512]{1,0:T(8,128)(2,1)S(1)}, bf16[2048,512]{1,0:T(8,128)(2,1)S(1)}, bf16[384,512]{1,0:T(8,128)(2,1)S(1)}, bf16[384,512]{1,0:T(8,128)(2,1)S(1)}) custom-call(s32[4]{0:T(128)S(1)} %copy-done.12, f32[10,32,128]{2,1,0:T(8,128)S(1)} %get-tuple-element.23.tables, f32[80,512]{1,0:T(8,128)S(1)} %collective-permute-done.up, ...), custom_call_target="tpu_custom_call" | custom-call | flops 15000000 | bytes 6291456 | tf_op jit(solution)/shard_map/stencil_matrix/pallas_call | solution.py:450
  108.3 1.3 %copy-done.13 = bf16[2048,512]{1,0:T(8,128)(2,1)} copy-done((bf16[2048,512]{1,0:T(8,128)(2,1)}, bf16[2048,512]{1,0:T(8,128)(2,1)S(1)}, u32[]{:S(2)}) %copy-start.13) | copy-done | bytes 2097176
  109.7 1.4 %copy-done.14 = bf16[2048,512]{1,0:T(8,128)(2,1)} copy-done((bf16[2048,512]{1,0:T(8,128)(2,1)}, bf16[2048,512]{1,0:T(8,128)(2,1)S(1)}, u32[]{:S(2)}) %copy-start.14) | copy-done | bytes 2097176
  111.1 0.8 copy-done.15
  111.8 0.8 copy-done.16
  112.6 0.0 collective-permute-done.7.down
  112.6 0.0 collective-permute-done.8.left
  112.7 0.0 collective-permute-done.18.other_table
  112.7 1.0 copy-done.21
  113.7 0.0 copy-done.22
  113.7 0.1 copy-done.23
  113.8 20.5 %last_iteration.1 = (f32[64,32,512]{2,1,0:T(8,128)}, f32[64,32,512]{2,1,0:T(8,128)}) custom-call(s32[4]{0:T(128)} %pad_add_fusion.where, f32[64,32,512]{2,1,0:T(8,128)} %copy-done.17, f32[64,32,512]{2,1,0:T(8,128)} %bitcast.18, f32[64,32,512]{2,1,0:T(8,128)} %bitcast.27, f32[10,32,128]{2,1,0:T(8,128)} %copy-done.5, f32[64,512]{1,0:T(8,128)} %copy-done.24, ...), custom_call_target="tpu_custom_call" | custom-call | flops 20000000000 | bytes 37748736 | tf_op jit(solution)/shard_map/last_iteration/pallas_call | solution.py:559
  (41 shorter events, 0.1 us)
Async XLA Ops:
  5.5 4.5 %copy-start.19 = (s32[4,64,32]{1,2,0:T(8,128)S(1)}, s32[4,64,32]{1,2,0:T(8,128)}, u32[]{:S(2)}) copy-start(s32[4,64,32]{1,2,0:T(8,128)} %param.16) | copy-start | bytes 98308
  5.5 4.6 %copy-start.20 = (f32[4,64,32]{1,2,0:T(8,128)S(1)}, f32[4,64,32]{1,2,0:T(8,128)}, u32[]{:S(2)}) copy-start(f32[4,64,32]{1,2,0:T(8,128)} %param.17) | copy-start | bytes 98308
  5.5 4.7 %copy-start.4 = (f32[1,512,512]{2,1,0:T(8,128)S(1)}, f32[1,512,512]{2,1,0:T(8,128)}, u32[]{:S(2)}) copy-start(f32[1,512,512]{2,1,0:T(8,128)} %param.13) | copy-start | bytes 3145732
  5.5 4.7 %copy-start.8 = (f32[1,64,32]{2,1,0:T(8,128)S(1)}, f32[1,64,32]{2,1,0:T(8,128)}, u32[]{:S(2)}) copy-start(f32[1,64,32]{2,1,0:T(8,128)} %copy.11) | copy-start | bytes 24580
  5.5 4.7 %copy-start.9 = (f32[1,64,32]{2,1,0:T(8,128)S(1)}, f32[1,64,32]{2,1,0:T(8,128)}, u32[]{:S(2)}) copy-start(f32[1,64,32]{2,1,0:T(8,128)} %copy.12) | copy-start | bytes 24580
  5.5 4.7 %copy-start.10 = (s32[1,64,32]{2,1,0:T(8,128)S(1)}, s32[1,64,32]{2,1,0:T(8,128)}, u32[]{:S(2)}) copy-start(s32[1,64,32]{2,1,0:T(8,128)} %copy.13) | copy-start | bytes 24580
  8.6 6.1 %copy-start.12 = (s32[4]{0:T(128)S(1)}, s32[4]{0:T(128)}, u32[]{:S(2)}) copy-start(s32[4]{0:T(128)} %pad_add_fusion.where) | copy-start | bytes 52
  8.6 6.0 %collective-permute-start.4 = (f32[32,512]{1,0:T(8,128)}, f32[32,512]{1,0:T(8,128)S(1)}, u32[]{:S(2)}, u32[]{:S(2)}) collective-permute-start(f32[32,512]{1,0:T(8,128)} %get-tuple-element.30), channel_id=1, source_target_pairs={{56,57},{57,58},{58,59},{59,60},{60,61},{61,62},{62,63}} | collective-permute-start | bytes 196616 | tf_op jit(solution)/shard_map/ppermute | solution.py:612
  9.3 5.4 %collective-permute-start.5 = (f32[32,512]{1,0:T(8,128)}, f32[32,512]{1,0:T(8,128)S(1)}, u32[]{:S(2)}, u32[]{:S(2)}) collective-permute-start(f32[32,512]{1,0:T(8,128)} %get-tuple-element.22.after), channel_id=1, source_target_pairs={{57,56},{58,57},{59,58},{60,59},{61,60},{62,61},{63,62}} | collective-permute-start | bytes 196616 | tf_op jit(solution)/shard_map/ppermute | solution.py:613
  10.3 2.2 %copy-start = (f32[1,64,32,512]{3,2,1,0:T(8,128)S(1)}, f32[1,64,32,512]{3,2,1,0:T(8,128)}, u32[]{:S(2)}) copy-start(f32[1,64,32,512]{3,2,1,0:T(8,128)} %param.9) | copy-start | bytes 12582916
  12.4 0.8 copy-start.11
  13.3 2.2 %copy-start.1 = (f32[1,64,32,512]{3,2,1,0:T(8,128)S(1)}, f32[1,64,32,512]{3,2,1,0:T(8,128)}, u32[]{:S(2)}) copy-start(f32[1,64,32,512]{3,2,1,0:T(8,128)} %param.9) | copy-start | bytes 12582916
  14.6 62.0 %copy-start.6 = (bf16[512,512]{1,0:T(8,128)(2,1)}, bf16[512,512]{1,0:T(8,128)(2,1)S(1)}, u32[]{:S(2)}) copy-start(bf16[512,512]{1,0:T(8,128)(2,1)S(1)} %get-tuple-element.28.high) | copy-start | bytes 1572868
  14.7 62.0 %copy-start.7 = (bf16[512,512]{1,0:T(8,128)(2,1)}, bf16[512,512]{1,0:T(8,128)(2,1)S(1)}, u32[]{:S(2)}) copy-start(bf16[512,512]{1,0:T(8,128)(2,1)S(1)} %get-tuple-element.29.low) | copy-start | bytes 1572868
  14.7 88.1 %copy-start.5 = (f32[10,32,128]{2,1,0:T(8,128)}, f32[10,32,128]{2,1,0:T(8,128)S(1)}, u32[]{:S(2)}) copy-start(f32[10,32,128]{2,1,0:T(8,128)S(1)} %get-tuple-element.23.tables) | copy-start | bytes 491524
  15.5 2.2 %copy-start.2 = (f32[1,64,32,512]{3,2,1,0:T(8,128)S(1)}, f32[1,64,32,512]{3,2,1,0:T(8,128)}, u32[]{:S(2)}) copy-start(f32[1,64,32,512]{3,2,1,0:T(8,128)} %param.10) | copy-start | bytes 12582916
  17.7 2.2 %copy-start.3 = (f32[1,64,32,512]{3,2,1,0:T(8,128)S(1)}, f32[1,64,32,512]{3,2,1,0:T(8,128)}, u32[]{:S(2)}) copy-start(f32[1,64,32,512]{3,2,1,0:T(8,128)} %param.11) | copy-start | bytes 12582916
  20.4 1.4 %collective-permute-start.11 = (f32[128,512]{1,0:T(8,128)S(1)}, f32[128,512]{1,0:T(8,128)S(1)}, u32[]{:S(2)}, u32[]{:S(2)}) collective-permute-start(f32[128,512]{1,0:T(8,128)S(1)} %both_bands.1.after), channel_id=1, source_target_pairs={{56,120},{57,121},{58,122},{59,123},{60,124},{61,125},{62,126},{63... | collective-permute-start | bytes 786440 | tf_op jit(solution)/shard_map/ppermute | solution.py:625
  21.1 0.7 collective-permute-start.10
  21.9 2.7 %collective-permute-start.14 = (f32[128,512]{1,0:T(8,128)S(1)}, f32[128,512]{1,0:T(8,128)S(1)}, u32[]{:S(2)}, u32[]{:S(2)}) collective-permute-start(f32[128,512]{1,0:T(8,128)S(1)} %add.18.after), channel_id=1, source_target_pairs={{88,72},{120,104},{89,73},{121,105},{90,74},{122,106},{91,75},{123... | collective-permute-start | bytes 786440 | tf_op jit(solution)/shard_map/ppermute | solution.py:628
  22.6 2.0 %collective-permute-start.13 = (f32[128,512]{1,0:T(8,128)S(1)}, f32[128,512]{1,0:T(8,128)S(1)}, u32[]{:S(2)}, u32[]{:S(2)}) collective-permute-start(f32[128,512]{1,0:T(8,128)S(1)} %add.18.after), channel_id=1, source_target_pairs={{88,80},{120,112},{89,81},{121,113},{90,82},{122,114},{91,83},{123... | collective-permute-start | bytes 786440 | tf_op jit(solution)/shard_map/ppermute | solution.py:628
  23.2 22.4 %collective-permute-start.12 = (f32[128,512]{1,0:T(8,128)S(1)}, f32[128,512]{1,0:T(8,128)S(1)}, u32[]{:S(2)}, u32[]{:S(2)}) collective-permute-start(f32[128,512]{1,0:T(8,128)S(1)} %add.18.after), channel_id=1, source_target_pairs={{88,64},{120,96},{89,65},{121,97},{90,66},{122,98},{91,67},{123,99... | collective-permute-start | bytes 786440 | tf_op jit(solution)/shard_map/ppermute | solution.py:628
  45.8 18.0 %collective-permute-start.17 = (f32[128,512]{1,0:T(8,128)S(1)}, f32[128,512]{1,0:T(8,128)S(1)}, u32[]{:S(2)}, u32[]{:S(2)}) collective-permute-start(f32[128,512]{1,0:T(8,128)S(1)} %add_add_fusion), channel_id=1, source_target_pairs={{64,70},{65,71},{66,64},{67,65},{68,66},{69,67},{70,68},{71,69},{7... | collective-permute-start | bytes 786440 | tf_op jit(solution)/shard_map/ppermute | solution.py:640
  49.4 16.6 %collective-permute-start.16 = (f32[128,512]{1,0:T(8,128)S(1)}, f32[128,512]{1,0:T(8,128)S(1)}, u32[]{:S(2)}, u32[]{:S(2)}) collective-permute-start(f32[128,512]{1,0:T(8,128)S(1)} %add_add_fusion), channel_id=1, source_target_pairs={{64,68},{65,69},{66,70},{67,71},{68,64},{69,65},{70,66},{71,67},{7... | collective-permute-start | bytes 786440 | tf_op jit(solution)/shard_map/ppermute | solution.py:640
  55.9 16.8 %collective-permute-start.15 = (f32[128,512]{1,0:T(8,128)S(1)}, f32[128,512]{1,0:T(8,128)S(1)}, u32[]{:S(2)}, u32[]{:S(2)}) collective-permute-start(f32[128,512]{1,0:T(8,128)S(1)} %add_add_fusion), channel_id=1, source_target_pairs={{64,66},{65,67},{66,68},{67,69},{68,70},{69,71},{70,64},{71,65},{7... | collective-permute-start | bytes 786440 | tf_op jit(solution)/shard_map/ppermute | solution.py:640
  57.9 18.8 %collective-permute-start.2 = (f32[144,512]{1,0:T(8,128)S(1)}, f32[144,512]{1,0:T(8,128)S(1)}, u32[]{:S(2)}, u32[]{:S(2)}) collective-permute-start(f32[144,512]{1,0:T(8,128)S(1)} %get-tuple-element.26), channel_id=1, source_target_pairs={{0,1},{1,2},{2,3},{3,4},{4,5},{5,6},{6,7},{8,9},{9,10},{10,11},{11... | collective-permute-start | bytes 884744 | tf_op jit(solution)/shard_map/ppermute | solution.py:585
  61.9 14.8 %collective-permute-start.3 = (f32[144,512]{1,0:T(8,128)S(1)}, f32[144,512]{1,0:T(8,128)S(1)}, u32[]{:S(2)}, u32[]{:S(2)}) collective-permute-start(f32[144,512]{1,0:T(8,128)S(1)} %get-tuple-element.27), channel_id=1, source_target_pairs={{1,0},{2,1},{3,2},{4,3},{5,4},{6,5},{7,6},{9,8},{10,9},{11,10},{12... | collective-permute-start | bytes 884744 | tf_op jit(solution)/shard_map/ppermute | solution.py:586
  63.8 11.0 %collective-permute-start = (f32[80,512]{1,0:T(8,128)S(1)}, f32[80,512]{1,0:T(8,128)S(1)}, u32[]{:S(2)}, u32[]{:S(2)}) collective-permute-start(f32[80,512]{1,0:T(8,128)S(1)} %get-tuple-element.24), channel_id=1, source_target_pairs={{0,8},{8,16},{16,24},{24,32},{32,40},{40,48},{48,56},{1,9},{9,17},... | collective-permute-start | bytes 491528 | tf_op jit(solution)/shard_map/ppermute | solution.py:585
  66.0 10.7 %collective-permute-start.1 = (f32[80,512]{1,0:T(8,128)S(1)}, f32[80,512]{1,0:T(8,128)S(1)}, u32[]{:S(2)}, u32[]{:S(2)}) collective-permute-start(f32[80,512]{1,0:T(8,128)S(1)} %get-tuple-element.25), channel_id=1, source_target_pairs={{8,0},{16,8},{24,16},{32,24},{40,32},{48,40},{56,48},{9,1},{17,9},... | collective-permute-start | bytes 491528 | tf_op jit(solution)/shard_map/ppermute | solution.py:586
  72.8 13.0 %copy-start.18 = (f32[4,128,512]{2,1,0:T(8,128)}, f32[4,128,512]{2,1,0:T(8,128)S(1)}, u32[]{:S(2)}) copy-start(f32[4,128,512]{2,1,0:T(8,128)S(1)} %pad_maximum_fusion.own_table) | copy-start | bytes 3145732
  72.8 39.8 %collective-permute-start.18 = (f32[4,128,512]{2,1,0:T(8,128)S(1)}, f32[4,128,512]{2,1,0:T(8,128)S(1)}, u32[]{:S(2)}, u32[]{:S(2)}) collective-permute-start(f32[4,128,512]{2,1,0:T(8,128)S(1)} %pad_maximum_fusion.own_table), channel_id=1, source_target_pairs={{64,65},{65,64},{66,67},{67,66},{68,69},{69,68},{70,71},{71,70},{7... | collective-permute-start | bytes 3145736 | tf_op jit(solution)/shard_map/ppermute | solution.py:643
  85.8 2.0 %copy-start.17 = (f32[64,32,512]{2,1,0:T(8,128)}, f32[64,32,512]{2,1,0:T(8,128)S(1)}, u32[]{:S(2)}) copy-start(f32[64,32,512]{2,1,0:T(8,128)S(1)} %get-tuple-element.31.one) | copy-start | bytes 12582916
  87.8 24.8 %collective-permute-start.8 = (f32[128,512]{1,0:T(8,128)S(1)}, f32[128,512]{1,0:T(8,128)S(1)}, u32[]{:S(2)}, u32[]{:S(2)}) collective-permute-start(f32[128,512]{1,0:T(8,128)S(1)} %get-tuple-element.34), channel_id=1, source_target_pairs={{0,1},{1,2},{2,3},{3,4},{4,5},{5,6},{6,7},{8,9},{9,10},{10,11},{11... | collective-permute-start | bytes 786440 | tf_op jit(solution)/shard_map/ppermute | solution.py:585
  91.1 21.5 %collective-permute-start.9 = (f32[128,512]{1,0:T(8,128)S(1)}, f32[128,512]{1,0:T(8,128)S(1)}, u32[]{:S(2)}, u32[]{:S(2)}) collective-permute-start(f32[128,512]{1,0:T(8,128)S(1)} %get-tuple-element.35), channel_id=1, source_target_pairs={{1,0},{2,1},{3,2},{4,3},{5,4},{6,5},{7,6},{9,8},{10,9},{11,10},{12... | collective-permute-start | bytes 786440 | tf_op jit(solution)/shard_map/ppermute | solution.py:586
  93.1 19.5 %collective-permute-start.6 = (f32[64,512]{1,0:T(8,128)S(1)}, f32[64,512]{1,0:T(8,128)S(1)}, u32[]{:S(2)}, u32[]{:S(2)}) collective-permute-start(f32[64,512]{1,0:T(8,128)S(1)} %get-tuple-element.32), channel_id=1, source_target_pairs={{0,8},{8,16},{16,24},{24,32},{32,40},{40,48},{48,56},{1,9},{9,17},... | collective-permute-start | bytes 393224 | tf_op jit(solution)/shard_map/ppermute | solution.py:585
  95.9 16.7 %collective-permute-start.7 = (f32[64,512]{1,0:T(8,128)S(1)}, f32[64,512]{1,0:T(8,128)S(1)}, u32[]{:S(2)}, u32[]{:S(2)}) collective-permute-start(f32[64,512]{1,0:T(8,128)S(1)} %get-tuple-element.33), channel_id=1, source_target_pairs={{8,0},{16,8},{24,16},{32,24},{40,32},{48,40},{56,48},{9,1},{17,9},... | collective-permute-start | bytes 393224 | tf_op jit(solution)/shard_map/ppermute | solution.py:586
  108.3 1.4 %copy-start.13 = (bf16[2048,512]{1,0:T(8,128)(2,1)}, bf16[2048,512]{1,0:T(8,128)(2,1)S(1)}, u32[]{:S(2)}) copy-start(bf16[2048,512]{1,0:T(8,128)(2,1)S(1)} %get-tuple-element.36.stencil_high) | copy-start | bytes 6291460
  109.7 1.4 %copy-start.14 = (bf16[2048,512]{1,0:T(8,128)(2,1)}, bf16[2048,512]{1,0:T(8,128)(2,1)S(1)}, u32[]{:S(2)}) copy-start(bf16[2048,512]{1,0:T(8,128)(2,1)S(1)} %get-tuple-element.37.stencil_low) | copy-start | bytes 6291460
  111.1 0.8 copy-start.15
  111.8 0.8 copy-start.16
  112.6 1.1 copy-start.24
  112.6 1.1 copy-start.25
  112.6 1.1 copy-start.22
  112.6 1.2 copy-start.23
  112.7 1.0 copy-start.21

commit v3 on v2

--- a/solution.py
+++ b/solution.py
@@ -12,17 +12,17 @@
 HALO = 2
 LANES = 128
 CHUNK = 16
-LAST = 8
+LAST = 16
 CORES = 2
 FAR = 2
-SOURCE, PRODUCT, CORE, CHIP = range(4)
 ROT, RET, INDEX, WEIGHT, TABLES = 0, 1, 2, 6, 10
 EXTRA = 2 * STENCILS * HALO
+AXES = ("sect", "rr", "row")
 MIB = 1 << 20
 F32 = jnp.float32
 BF16 = jnp.bfloat16
 ANY = pl.BlockSpec(memory_space=pl.ANY)
-SMEM = pl.BlockSpec(memory_space=pltpu.SMEM)
+HBM = pl.BlockSpec(memory_space=pltpu.HBM)
 VMEM = pl.BlockSpec(memory_space=pltpu.VMEM)
 
 SIDE1 = -16.0 / 96.0
@@ -58,58 +58,79 @@
     )
 
 
+def in_hbm(value):
+    return pltpu.with_memory_space_constraint(value, pltpu.HBM)
+
+
+def holds_bands():
+    return (lax.axis_index("sect") == 0) & (lax.axis_index("rr") == lax.axis_size("rr") - 1)
+
+
+def in_product():
+    return lax.axis_index("sect") == 1
+
+
 def retained_of(damping, absorber):
     return 1.0 - absorber.astype(F32) * (1.0 - damping)
 
 
-def band_slab_kernel(where, rotation, damping, absorber, packet, previous, potential, firsts, lasts, held, sems):
-    count_r, rows, width = packet.shape
-
-    @pl.when(where[SOURCE] == 1)
+def band_slab_kernel(rotation, damping, absorber, packet, previous, potential, firsts, lasts, held, factors, masks, sems):
+    count_r, rows, width = packet.shape
+
+    @pl.when(holds_bands())
     def _():
         copies = [
             pltpu.make_async_copy(ref.at[pl.ds(count_r - 4, 4)], held.at[n], sems.at[n])
             for n, ref in enumerate((packet, previous, potential))
         ]
+        copies += [
+            pltpu.make_async_copy(rotation, factors.at[0], sems.at[3]),
+            pltpu.make_async_copy(damping, factors.at[1], sems.at[4]),
+            pltpu.make_async_copy(absorber, masks, sems.at[5]),
+        ]
         for copy in copies:
             copy.start()
-        for out, near in ((firsts, 0), (lasts, rows - 2)):
-            for k in range(BAND):
-                for r in range(2):
-                    at = (count_r - BAND + k, near + r)
-                    ret = retained_of(damping[at], absorber[at])
-                    out[24 + 2 * k + r : 25 + 2 * k + r] = jnp.full((1, width), rotation[at], F32)
-                    out[28 + 2 * k + r : 29 + 2 * k + r] = jnp.full((1, width), ret, F32)
         for copy in copies:
             copy.wait()
+        retained = retained_of(factors[1], masks[...])
+        rotated = factors[0]
         for out, far, near in ((firsts, 0, 0), (lasts, rows - 4, rows - 2)):
             for k in range(4):
                 out[4 * k : 4 * k + 4] = held[0, k, far : far + 4]
             for k in range(BAND):
+                at = count_r - BAND + k
                 out[16 + 2 * k : 18 + 2 * k] = held[1, 2 + k, near : near + 2]
                 out[20 + 2 * k : 22 + 2 * k] = held[2, 2 + k, near : near + 2]
-
-
-def band_slabs(where, rotation, damping, absorber, packet, previous, potential):
-    _, rows, width = packet.shape
+                out[24 + 2 * k : 26 + 2 * k] = jnp.broadcast_to(rotated[near : near + 2, at : at + 1], (2, width))
+                out[28 + 2 * k : 30 + 2 * k] = jnp.broadcast_to(retained[near : near + 2, at : at + 1], (2, width))
+
+
+def band_slabs(rotation, damping, absorber, packet, previous, potential):
+    count_r, rows, width = packet.shape
     return pl.pallas_call(
         band_slab_kernel,
-        in_specs=[SMEM, SMEM, SMEM, SMEM, ANY, ANY, ANY],
+        in_specs=[ANY, ANY, ANY, HBM, HBM, HBM],
         out_specs=[VMEM, VMEM],
         out_shape=[jax.ShapeDtypeStruct((32, width), F32)] * 2,
-        scratch_shapes=[pltpu.VMEM((3, 4, rows, width), F32), pltpu.SemaphoreType.DMA((3,))],
+        scratch_shapes=[
+            pltpu.VMEM((3, 4, rows, width), F32),
+            pltpu.VMEM((2, rows, count_r), F32),
+            pltpu.VMEM((rows, count_r), jnp.int32),
+            pltpu.SemaphoreType.DMA((6,)),
+        ],
+        compiler_params=pltpu.CompilerParams(vmem_limit_bytes=8 * MIB),
         name="band_slabs",
-    )(where, rotation, damping, absorber, packet, previous, potential)
+    )(rotation, damping, absorber, packet, previous, potential)
 
 
 def band_kernel(
-    where, packet, previous, potential, tables, left, right, high, low, out, field, later, turned, held, sems
+    packet, previous, potential, tables, left, right, high, low, out, field, later, turned, held, sems
 ):
     count_r, rows, width = packet.shape
     base = 16
     wide = rows + 16
 
-    @pl.when(where[SOURCE] == 1)
+    @pl.when(holds_bands())
     def _():
         copies = [
             pltpu.make_async_copy(packet.at[pl.ds(count_r - 6, 6)], field.at[pl.ds(2, 6), pl.ds(base, rows)], sems.at[0]),
@@ -169,11 +190,11 @@
                 out[k * rows : (k + 1) * rows, lanes] = (1.0 - retained) * update
 
 
-def bands(where, packet, previous, potential, tables, left, right, high, low):
+def bands(packet, previous, potential, tables, left, right, high, low):
     _, rows, width = packet.shape
     return pl.pallas_call(
         band_kernel,
-        in_specs=[SMEM, ANY, ANY, ANY, VMEM, VMEM, VMEM, VMEM, VMEM],
+        in_specs=[HBM, HBM, HBM, VMEM, VMEM, VMEM, VMEM, VMEM],
         out_specs=VMEM,
         out_shape=jax.ShapeDtypeStruct((2 * BAND * rows, width), F32),
         scratch_shapes=[
@@ -186,12 +207,12 @@
         compiler_params=pltpu.CompilerParams(vmem_limit_bytes=16 * MIB),
         cost_estimate=pl.CostEstimate(flops=400_000_000, bytes_accessed=4 * MIB, transcendentals=0),
         name="both_bands",
-    )(where, packet, previous, potential, tables, left, right, high, low)
+    )(packet, previous, potential, tables, left, right, high, low)
 
 
 def prepare_kernel(
     packet, rotation, damping, absorber, index, weight, angular, after,
-    top, bottom, first, last, tables, high, low, ends, sides, square, sems,
+    top, bottom, first, last, tables, high, low, ends, sides, sems,
 ):
     count_r, rows, width = packet.shape
     copies = [
@@ -202,22 +223,26 @@
     ]
     for copy in copies:
         copy.start()
-    square[...] = jnp.zeros_like(square)
     values = [rotation[...], retained_of(damping[...], absorber[...])]
     values += [index[n].astype(F32) for n in range(STENCILS)]
     values += [weight[n] for n in range(STENCILS)]
     for n, value in enumerate(values):
-        square[0:count_r, 0:rows] = value
-        turned = square[...].T[0:rows]
-        tables[n] = turned
-        if n >= INDEX:
-            at = (n - INDEX) * HALO
-            edges = HALO * rows
-            columns = HALO * count_r
-            top[edges + at : edges + at + HALO, 0:rows] = value[0:HALO]
-            bottom[edges + at : edges + at + HALO, 0:rows] = value[count_r - HALO :]
-            first[columns + at : columns + at + HALO, 0:LANES] = turned[0:HALO]
-            last[columns + at : columns + at + HALO, 0:LANES] = turned[rows - HALO : rows]
+        tables[n] = jnp.concatenate([value, jnp.zeros((rows, LANES - count_r), F32)], axis=1)
+    edges = HALO * rows
+    columns = HALO * count_r
+    lane = lax.broadcasted_iota(jnp.int32, (rows, LANES), 1)
+    upper = jnp.zeros((rows, LANES), F32)
+    lower = jnp.zeros((rows, LANES), F32)
+    for n in range(2 * STENCILS):
+        value = tables[INDEX + n]
+        at = n * HALO
+        here = (lane >= at) & (lane < at + HALO)
+        upper = jnp.where(here, pltpu.roll(value, at, 1), upper)
+        lower = jnp.where(here, pltpu.roll(value, (at + LANES - (count_r - HALO)) % LANES, 1), lower)
+        first[columns + at : columns + at + HALO, 0:LANES] = value[0:HALO]
+        last[columns + at : columns + at + HALO, 0:LANES] = value[rows - HALO : rows]
+    top[edges : edges + rows, 0:LANES] = upper
+    bottom[edges : edges + rows, 0:LANES] = lower
     high[...], low[...] = halves(angular[...])
     for copy in copies:
         copy.wait()
@@ -232,18 +257,17 @@
 
 def prepare(packet, rotation, damping, absorber, index, weight, angular, after):
     count_r, rows, width = packet.shape
-    ends = jax.ShapeDtypeStruct((HALO * rows + EXTRA, width), F32)
+    ends = jax.ShapeDtypeStruct((HALO * rows + rows, width), F32)
     sides = jax.ShapeDtypeStruct((HALO * count_r + EXTRA, width), F32)
     part = jax.ShapeDtypeStruct(angular.shape, BF16)
     return pl.pallas_call(
         prepare_kernel,
-        in_specs=[ANY, VMEM, VMEM, VMEM, VMEM, VMEM, VMEM, ANY],
+        in_specs=[HBM, VMEM, VMEM, VMEM, VMEM, VMEM, VMEM, ANY],
         out_specs=[VMEM] * 7,
         out_shape=[ends, ends, sides, sides, jax.ShapeDtypeStruct((TABLES, rows, LANES), F32), part, part],
         scratch_shapes=[
             pltpu.VMEM((2, HALO, rows, width), F32),
             pltpu.VMEM((2, count_r, 8, width), F32),
-            pltpu.VMEM((LANES, LANES), F32),
             pltpu.SemaphoreType.DMA((4,)),
         ],
         compiler_params=pltpu.CompilerParams(vmem_limit_bytes=16 * MIB),
@@ -301,56 +325,52 @@
                 put(here + k, lanes, retained * update)
 
 
-def pieces(count, chunk):
-    return [pl.ds(n * chunk, chunk) for n in range(count // chunk)]
-
-
 def first_kernel(
     packet, previous, potential, tables, up, down, left, right, high, low, after,
-    out, top, bottom, first, last, field, prev, pot, done, sides, sems,
+    done, top, bottom, first, last, field, prev, pot, sides, sems,
 ):
     count_r, rows, width = packet.shape
     steps = count_r // CHUNK
-    into = []
-    for n, part in enumerate(pieces(count_r, CHUNK)):
-        into.append(
-            [
-                pltpu.make_async_copy(packet.at[part], field.at[pl.ds(HALO + n * CHUNK, CHUNK)], sems.at[0, n]),
-                pltpu.make_async_copy(previous.at[part], prev.at[part], sems.at[1, n]),
-                pltpu.make_async_copy(potential.at[part], pot.at[part], sems.at[2, n]),
-            ]
+
+    def copies(n):
+        part = pl.ds(n * CHUNK, CHUNK)
+        return (
+            pltpu.make_async_copy(packet.at[part], field.at[pl.ds(HALO + n * CHUNK, CHUNK)], sems.at[0, n]),
+            pltpu.make_async_copy(previous.at[part], prev.at[part], sems.at[1, n]),
+            pltpu.make_async_copy(potential.at[part], pot.at[part], sems.at[2, n]),
         )
-    for group in into:
-        for copy in group:
+
+    for n in range(steps):
+        for copy in copies(n):
             copy.start()
     for k in range(HALO):
         field[k] = up[k * rows : (k + 1) * rows]
         field[HALO + count_r + k] = down[k * rows : (k + 1) * rows]
     put_sides(sides, left, right, count_r)
-    into[0][0].wait()
-    outs = []
-    for step in range(steps):
-        if step + 1 < steps:
-            into[step + 1][0].wait()
-        into[step][1].wait()
-        into[step][2].wait()
-
-        def put(k, lanes, value):
-            done[k, :, lanes] = value
-
-        advance(step, CHUNK, field, sides, prev, pot, tables, high, low, put)
-        part = pl.ds(step * CHUNK, CHUNK)
-        outs.append(pltpu.make_async_copy(done.at[part], out.at[part], sems.at[3, step]))
-        outs[-1].start()
-        for k in range(step * CHUNK, (step + 1) * CHUNK):
+    copies(0)[0].wait()
+
+    def put(k, lanes, value):
+        done[k, :, lanes] = value
+
+    def body(n, carry):
+        @pl.when(n + 1 < steps)
+        def _():
+            copies(n + 1)[0].wait()
+
+        copies(n)[1].wait()
+        copies(n)[2].wait()
+        advance(n, CHUNK, field, sides, prev, pot, tables, high, low, put)
+        for k in range(CHUNK):
             for r in range(HALO):
-                first[r * count_r + k : r * count_r + k + 1] = done[k, r : r + 1]
-                last[r * count_r + k : r * count_r + k + 1] = done[k, rows - HALO + r : rows - HALO + r + 1]
+                at = pl.ds(r * count_r + n * CHUNK + k, 1)
+                first[at] = done[n * CHUNK + k, r : r + 1]
+                last[at] = done[n * CHUNK + k, rows - HALO + r : rows - HALO + r + 1]
+        return carry
+
+    lax.fori_loop(0, steps, body, 0)
     for k in range(HALO):
         top[k * rows : (k + 1) * rows] = done[k]
         bottom[k * rows : (k + 1) * rows] = done[count_r - HALO + k]
-    for copy in outs:
-        copy.wait()
 
 
 def first_iteration(packet, previous, potential, tables, halos, high, low, after):
@@ -359,24 +379,23 @@
     sides = jax.ShapeDtypeStruct((HALO * count_r, width), F32)
     return pl.pallas_call(
         first_kernel,
-        in_specs=[ANY, ANY, ANY, *[VMEM] * 7, ANY],
-        out_specs=[ANY, *[VMEM] * 4],
+        in_specs=[HBM, HBM, HBM, *[VMEM] * 7, ANY],
+        out_specs=[VMEM] * 5,
         out_shape=[jax.ShapeDtypeStruct(packet.shape, F32), ends, ends, sides, sides],
         scratch_shapes=[
             pltpu.VMEM((count_r + 2 * HALO, rows, width), F32),
             pltpu.VMEM(packet.shape, F32),
             pltpu.VMEM(packet.shape, F32),
-            pltpu.VMEM(packet.shape, F32),
             pltpu.VMEM((count_r, 8, width), F32),
-            pltpu.SemaphoreType.DMA((4, count_r // CHUNK)),
+            pltpu.SemaphoreType.DMA((3, count_r // CHUNK)),
         ],
-        compiler_params=pltpu.CompilerParams(vmem_limit_bytes=40 * MIB),
+        compiler_params=pltpu.CompilerParams(vmem_limit_bytes=28 * MIB),
         cost_estimate=pl.CostEstimate(flops=7_000_000_000, bytes_accessed=20 * MIB, transcendentals=0),
         name="first_iteration",
     )(packet, previous, potential, tables, *halos, high, low, after)
 
 
-def stencil_kernel(where, tables, up, down, left, right, after, high, low, edge_high, edge_low, square):
+def stencil_kernel(tables, up, down, left, right, after, high, low, edge_high, edge_low, square):
     _, rows, _ = tables.shape
     count_r = left.shape[0] // HALO - EXTRA // HALO
     width = high.shape[1]
@@ -388,8 +407,8 @@
         index = value.astype(jnp.int32)
         owner = index >> shift_owner
         inside = index & (per - 1)
-        core = (owner & 1) ^ where[CORE]
-        chip = (where[CHIP] - (owner >> 1)) & (chips - 1)
+        core = (owner & 1) ^ (lax.axis_index("row") & 1)
+        chip = ((lax.axis_index("row") >> 1) - (owner >> 1)) & (chips - 1)
         slot = ((core * chips + chip) << shift_owner) + (inside & 1) * rows + (inside >> 1)
         return slot.astype(F32)
 
@@ -407,7 +426,7 @@
             high_out[pl.ds(at, 32), tile : tile + LANES] = upper
             low_out[pl.ds(at, 32), tile : tile + LANES] = lower
 
-    @pl.when(where[PRODUCT] == 1)
+    @pl.when(in_product())
     def _():
         places = [place(tables[INDEX + n]) for n in range(STENCILS)]
         weights = [tables[WEIGHT + n] for n in range(STENCILS)]
@@ -424,83 +443,94 @@
 
         lax.fori_loop(0, count_r // group, body, 0)
 
+        edges = HALO * rows
+        at = 0
+        for side in (up, down):
+            value = side[edges : edges + rows, 0:LANES]
+            slots = place(value)
+            for e in range(HALO):
+                cut = [(slots if m < STENCILS else value)[:, HALO * m + e : HALO * m + e + 1] for m in range(2 * STENCILS)]
+                fill(at, cut[:STENCILS], cut[STENCILS:], edge_high, edge_low)
+                at += rows
         square[...] = jnp.zeros_like(square)
-        for n, side in enumerate((up, down, left, right)):
-            begin = side.shape[0] - EXTRA
+        for n, side in enumerate((left, right)):
+            begin = HALO * count_r
             square[n * EXTRA : n * EXTRA + EXTRA // 2] = place(side[begin : begin + EXTRA // 2, 0:LANES])
             square[n * EXTRA + EXTRA // 2 : (n + 1) * EXTRA] = side[begin + EXTRA // 2 : begin + EXTRA, 0:LANES]
         turned = square[...].T
-        at = 0
-        for n, length in enumerate((rows, rows, count_r, count_r)):
+        for n in range(2):
             for e in range(HALO):
-                for begin in range(0, length, 32):
+                for begin in range(0, count_r, rows):
                     cut = [
-                        turned[begin : begin + 32, n * EXTRA + HALO * m + e : n * EXTRA + HALO * m + e + 1]
+                        turned[begin : begin + rows, n * EXTRA + HALO * m + e : n * EXTRA + HALO * m + e + 1]
                         for m in range(2 * STENCILS)
                     ]
                     fill(at, cut[:STENCILS], cut[STENCILS:], edge_high, edge_low)
-                    at += 32
-
-
-def stencil_matrix(where, tables, halos, columns, after):
+                    at += rows
+
+
+def stencil_matrix(tables, halos, columns, after):
     rows = tables.shape[1]
     count_r = halos[2].shape[0] // HALO - EXTRA // HALO
     points = jax.ShapeDtypeStruct((count_r * rows, columns), BF16)
     edges = jax.ShapeDtypeStruct((2 * HALO * (rows + count_r), columns), BF16)
     return pl.pallas_call(
         stencil_kernel,
-        in_specs=[SMEM, *[VMEM] * 5, ANY],
+        in_specs=[*[VMEM] * 5, ANY],
         out_specs=[VMEM] * 4,
         out_shape=[points, points, edges, edges],
         scratch_shapes=[pltpu.VMEM((LANES, LANES), F32)],
         compiler_params=pltpu.CompilerParams(vmem_limit_bytes=16 * MIB),
         cost_estimate=pl.CostEstimate(flops=15_000_000, bytes_accessed=6 * MIB, transcendentals=0),
         name="stencil_matrix",
-    )(where, tables, *halos, after)
+    )(tables, *halos, after)
 
 
 def last_kernel(
-    where, one, packet, potential, tables, up, down, left, right, high, low,
-    stencil_high, stencil_low, edge_high, edge_low, own_table, other_table,
-    earlier, latest, field, prev, pot, done, sides, split_high, split_low, table, source, sems,
+    one, packet, potential, tables, up, down, left, right, high, low,
+    split_high, split_low, edge_high, edge_low, own_table, other_table,
+    earlier, latest, field, prev, pot, done, sides, table, source, sems,
 ):
     count_r, rows, width = packet.shape
     steps = count_r // LAST
-    is_product = where[PRODUCT] == 1
+    is_product = in_product()
     quarter = own_table.shape[1]
     half = quarter // 2
     chips = own_table.shape[0]
     size = LAST * rows
-    parts = pieces(count_r, LAST)
 
     def field_part(n):
         return field.at[pl.ds(HALO + n * LAST, LAST)]
 
-    ones, highs, lows, prevs, pots = [], [], [], [], []
-    for n, part in enumerate(parts):
-        cut = pl.ds(n * size, size)
-        ones.append(pltpu.make_async_copy(one.at[part], field_part(n), sems.at[0, n]))
-        highs.append(pltpu.make_async_copy(stencil_high.at[cut], split_high.at[cut], sems.at[1, n]))
-        lows.append(pltpu.make_async_copy(stencil_low.at[cut], split_low.at[cut], sems.at[2, n]))
-        prevs.append(pltpu.make_async_copy(packet.at[part], prev.at[part], sems.at[3, n]))
-        pots.append(pltpu.make_async_copy(potential.at[part], pot.at[part], sems.at[4, n]))
-    earliers = [pltpu.make_async_copy(field_part(n), earlier.at[part], sems.at[5, n]) for n, part in enumerate(parts)]
-    latests = [pltpu.make_async_copy(done.at[part], latest.at[part], sems.at[6, n]) for n, part in enumerate(parts)]
+    def part(n):
+        return pl.ds(n * LAST, LAST)
+
+    def cut(n):
+        return pl.ds(pl.multiple_of(n * size, size), size)
+
+    def locals_of(n):
+        return (
+            pltpu.make_async_copy(packet.at[part(n)], prev.at[part(n)], sems.at[0, n]),
+            pltpu.make_async_copy(potential.at[part(n)], pot.at[part(n)], sems.at[1, n]),
+        )
+
+    def earliers(n):
+        return pltpu.make_async_copy(field_part(n), earlier.at[part(n)], sems.at[2, n])
+
+    def latests(n):
+        return pltpu.make_async_copy(done.at[part(n)], latest.at[part(n)], sems.at[3, n])
 
     def put_ends(up_value, down_value):
         for k in range(HALO):
             field[k] = up_value[k * rows : (k + 1) * rows]
             field[HALO + count_r + k] = down_value[k * rows : (k + 1) * rows]
 
+    for n in range(steps):
+        for copy in locals_of(n):
+            copy.start()
+
     @pl.when(is_product)
     def _():
-        for n in range(steps):
-            ones[n].start()
-            highs[n].start()
-            lows[n].start()
-        for n in range(steps):
-            prevs[n].start()
-            pots[n].start()
         for side, ref in enumerate((own_table, other_table)):
             for k in range(chips):
                 at = (side * chips + k) * half
@@ -516,50 +546,51 @@
             sides, left, right, count_r,
             source.at[pl.ds(2 * edges, columns)], source.at[pl.ds(2 * edges + columns, columns)],
         )
-        for n in range(steps):
-            ones[n].wait()
-            highs[n].wait()
-            lows[n].wait()
-            cut = pl.ds(n * size, size)
-            weights = (split_high[cut], split_low[cut])
+
+        def body(n, carry):
+            matrix = (split_high[cut(n)], split_low[cut(n)])
             here = pl.ds(HALO + n * LAST, LAST)
-            field[here] = field[here] + product(weights, table[0], table[1]).reshape(LAST, rows, width)
-            done[parts[n]] = product(weights, table[2], table[3]).reshape(LAST, rows, width)
-            earliers[n].start()
+            field[here] = one[part(n)] + product(matrix, table[0], table[1]).reshape(LAST, rows, width)
+            done[part(n)] = product(matrix, table[2], table[3]).reshape(LAST, rows, width)
+            earliers(n).start()
+            return carry
+
+        lax.fori_loop(0, steps, body, 0)
 
     @pl.when(jnp.logical_not(is_product))
     def _():
-        for n in range(steps):
-            ones[n].start()
-            prevs[n].start()
-            pots[n].start()
         put_ends(up, down)
         put_sides(sides, left, right, count_r)
         done[...] = jnp.zeros_like(done)
         for n in range(steps):
-            ones[n].wait()
-            earliers[n].start()
+            here = pl.ds(HALO + n * LAST, LAST)
+            field[here] = one[part(n)]
+            earliers(n).start()
 
     def put(k, lanes, value):
         done[k, :, lanes] += value
 
+    def body(n, carry):
+        for copy in locals_of(n):
+            copy.wait()
+        advance(n, LAST, field, sides, prev, pot, tables, high, low, put)
+        latests(n).start()
+        return carry
+
+    lax.fori_loop(0, steps, body, 0)
     for n in range(steps):
-        prevs[n].wait()
-        pots[n].wait()
-        advance(n, LAST, field, sides, prev, pot, tables, high, low, put)
-        latests[n].start()
-    for copy in earliers + latests:
-        copy.wait()
-
-
-def last_iteration(where, one, packet, potential, tables, halos, high, low, matrices, band_tables):
+        earliers(n).wait()
+        latests(n).wait()
+
+
+def last_iteration(one, packet, potential, tables, halos, high, low, matrices, band_tables):
     count_r, rows, width = packet.shape
     steps = count_r // LAST
     columns = matrices[0].shape[1]
     return pl.pallas_call(
         last_kernel,
-        in_specs=[SMEM, ANY, ANY, ANY, *[VMEM] * 7, ANY, ANY, *[VMEM] * 4],
-        out_specs=[ANY, ANY],
+        in_specs=[VMEM, HBM, HBM, *[VMEM] * 13],
+        out_specs=[HBM, HBM],
         out_shape=[jax.ShapeDtypeStruct(packet.shape, F32)] * 2,
         scratch_shapes=[
             pltpu.VMEM((count_r + 2 * HALO, rows, width), F32),
@@ -567,16 +598,14 @@
             pltpu.VMEM(packet.shape, F32),
             pltpu.VMEM(packet.shape, F32),
             pltpu.VMEM((count_r, 8, width), F32),
-            pltpu.VMEM((count_r * rows, columns), BF16),
-            pltpu.VMEM((count_r * rows, columns), BF16),
             pltpu.VMEM((4, columns, width), BF16),
             pltpu.VMEM((2 * HALO * (rows + count_r), width), F32),
-            pltpu.SemaphoreType.DMA((7, steps)),
+            pltpu.SemaphoreType.DMA((4, steps)),
         ],
-        compiler_params=pltpu.CompilerParams(vmem_limit_bytes=56 * MIB),
+        compiler_params=pltpu.CompilerParams(vmem_limit_bytes=40 * MIB),
         cost_estimate=pl.CostEstimate(flops=20_000_000_000, bytes_accessed=36 * MIB, transcendentals=0),
         name="last_iteration",
-    )(where, one, packet, potential, tables, *halos, high, low, *matrices, *band_tables)
+    )(one, packet, potential, tables, *halos, high, low, *matrices, *band_tables)
 
 
 def neighbours(axis, upward, downward):
@@ -597,37 +626,40 @@
     packet, previous, potential = packet[0], previous[0], potential[0]
     rotation, angular, damping, absorber = rotation[0], angular[0], damping[0], absorber[0]
     count_r, rows, width = packet.shape
-    sect = lax.axis_index("sect")
-    rr = lax.axis_index("rr")
-    row = lax.axis_index("row")
     count_rr, count_row = (lax.axis_size(name) for name in ("rr", "row"))
     chips = count_row // CORES
-    where = jnp.stack(
-        [((sect == 0) & (rr == count_rr - 1)).astype(jnp.int32), sect, row % CORES, row // CORES]
-    ).astype(jnp.int32)
-
-    firsts, lasts = band_slabs(where, rotation, damping, absorber, packet, previous, potential)
-    axes = ("sect", "rr", "row")
+    packet, previous, potential = (in_hbm(value) for value in (packet, previous, potential))
+    rotation, damping, absorber = (jnp.swapaxes(value, 0, 1) for value in (rotation, damping, absorber))
+    stencil_index, stencil_weight = (jnp.swapaxes(value, 1, 2) for value in (stencil_index, stencil_weight))
+
+    firsts, lasts = band_slabs(rotation, damping, absorber, packet, previous, potential)
     sources = (count_rr - 1) * count_row
-    band_left = lax.ppermute(lasts, axes, [(sources + i, sources + i + 1) for i in range(count_row - 1)])
-    band_right = lax.ppermute(firsts, axes, [(sources + i + 1, sources + i) for i in range(count_row - 1)])
+    band_left = lax.ppermute(lasts, AXES, [(sources + i, sources + i + 1) for i in range(count_row - 1)])
+    band_right = lax.ppermute(firsts, AXES, [(sources + i + 1, sources + i) for i in range(count_row - 1)])
 
     top, bottom, first, last, tables, high, low = prepare(
         packet, rotation, damping, absorber, stencil_index, stencil_weight, angular, firsts
     )
-    table = bands(where, packet, previous, potential, tables, band_left, band_right, high, low)
+    table = bands(packet, previous, potential, tables, band_left, band_right, high, low)
+    top, bottom, first, last, table = lax.optimization_barrier((top, bottom, first, last, table))
     halos = exchange(top, bottom, first, last)
+
+    one, *edges = first_iteration(packet, previous, potential, tables, halos, high, low, table)
 
     plane = ("sect", "rr")
     half = count_rr // FAR
     start = count_rr - 1
     entries = [count_rr + (k + 1) * half - 1 for k in range(FAR)]
-    piece = sum(lax.ppermute(table, plane, [(start, entry)]) for entry in entries)
-    spread = piece
+    crossed = [lax.ppermute(table, plane, [(start, entry)]) for entry in entries]
+    *crossed, one = lax.optimization_barrier((*crossed, one))
+    piece = sum(crossed)
+    arrived = []
     for shift in (1, half - 1, 2):
-        spread = spread + lax.ppermute(
-            piece, plane, [(entry, entry - (half - 1) + (half - 1 + shift) % half) for entry in entries]
-        )
+        pairs = [(entry, entry - (half - 1) + (half - 1 + shift) % half) for entry in entries]
+        arrived.append(lax.ppermute(piece, plane, pairs))
+    matrices = stencil_matrix(tables, halos, count_row * rows * BAND, piece)
+    *arrived, matrices = lax.optimization_barrier((*arrived, matrices))
+    spread = piece + sum(arrived)
     line = ("sect", "row")
 
     def around(shift):
@@ -639,16 +671,15 @@
                 )
         return lax.ppermute(spread, line, pairs)
 
-    own = jnp.stack([spread, around(1), around(2), around(3)], axis=0)
+    rest = [around(1), around(2), around(3)]
+    later = exchange(*edges)
+    *rest, later = lax.optimization_barrier((*rest, later))
+    own = jnp.stack([spread, *rest], axis=0)
     other = lax.ppermute(
         own, line, [(count_row + i, count_row + i + 1 - 2 * (i % CORES)) for i in range(count_row)]
     )
-
-    one, *edges = first_iteration(packet, previous, potential, tables, halos, high, low, table)
-    matrices = stencil_matrix(where, tables, halos, count_row * rows * BAND, piece)
-    later = exchange(*edges)
     earlier, latest = last_iteration(
-        where, one, packet, potential, tables, later, high, low, matrices, (own, other)
+        one, packet, potential, tables, later, high, low, matrices, (own, other)
     )
     return latest[None], earlier[None]
 

time: 136 us -> 103 us (0.76)
  local copies, waits for them, and re-layouts: 20 us -> 2.17 us
  waiting for transfers between devices: 23.1 us -> 14.8 us
  Pallas kernels: 40.3 us -> 33.4 us
  starting transfers between devices: 49 us -> 51.1 us
    ppermute x5, waiting for transfers between devices: 21.1 us -> 0.01 us  [the longest x3 0.01 us: local(): arrived.append(lax.ppermute(piece, plane, pairs))]
    unnamed x57 -> x18, local copies, waits for them, and re-layouts: 20 us -> 2.17 us
    ppermute x3, waiting for transfers between devices: 0.01 us -> 10.8 us  [around(): return lax.ppermute(spread, line, pairs)]
    pallas_call x6, Pallas kernels: 40.3 us -> 33.4 us  [the longest x1 16.9 us: last_iteration(): pl.pallas_call(last_kernel, in_specs=[VMEM, HBM, HBM, *[VMEM] * 13], out_...]
    ppermute x3, starting transfers between devices: 12.1 us -> 8.8 us  [around(): return lax.ppermute(spread, line, pairs)]
    ppermute x4, starting transfers between devices: 17.4 us -> 19.9 us  [neighbours(): lax.ppermute(downward, axis, [(i + 1, i) for i in range(count - 1)])]
    ppermute x1, waiting for transfers between devices: 0.01 us -> 2.26 us  [local(): lax.ppermute(own, line, [(count_row + i, count_row + i + 1 - 2 * (i % COR...]
    ppermute x4, starting transfers between devices: 12.3 us -> 13.8 us  [neighbours(): lax.ppermute(upward, axis, [(i, i + 1) for i in range(count - 1)])]
  transfers between devices with their start and end apart: 19 -> 19, of which waited for: 3 -> 6; matrix products, arithmetic and copies ran while one was open for 0% -> 0% of each run, Pallas kernels for 12% -> 16%
where the time goes in v3:
time: 103 us
  starting transfers between devices  51.1 us (50%)
  Pallas kernels  33.4 us (32%)
  waiting for transfers between devices  14.8 us (14%)
  local copies, waits for them, and re-layouts  2.17 us (2%)
    ppermute x4, starting transfers between devices, neighbours(): lax.ppermute(downward, axis, [(i + 1, i) for i in range(count - 1)])  19.9 us
    pallas_call x1, Pallas kernels, last_iteration(): pl.pallas_call(last_kernel, in_specs=[VMEM, HBM, HBM, *[VMEM] * 13], out_...  16.9 us
    ppermute x4, starting transfers between devices, neighbours(): lax.ppermute(upward, axis, [(i, i + 1) for i in range(count - 1)])  13.8 us
    ppermute x3, waiting for transfers between devices, around(): return lax.ppermute(spread, line, pairs)  10.8 us
    pallas_call x1, Pallas kernels, first_iteration(): pl.pallas_call(first_kernel, in_specs=[HBM, HBM, HBM, *[VMEM] * 7, ANY],...  9.68 us
    ppermute x3, starting transfers between devices, around(): return lax.ppermute(spread, line, pairs)  8.8 us
    pallas_call x1, Pallas kernels, stencil_matrix(): pl.pallas_call(stencil_kernel, in_specs=[*[VMEM] * 5, ANY], out_specs=[VM...  4.82 us
    ppermute x1, starting transfers between devices, local(): lax.ppermute(own, line, [(count_row + i, count_row + i + 1 - 2 * (i % COR...  3.17 us
  transfers between devices with their start and end apart: 19, of which 6 were waited for; matrix products, arithmetic and copies ran while one was open for 0% of the time, Pallas kernels for 16%

profile of v3, /device:TPU:7, one launch (start us, length us, event | category | flops | bytes accessed | tf_op | source)
XLA Modules:
  0.0 102.7 jit_solution(17695853726593268725)
XLA Ops:
  0.6 0.0 copy-start.3
  0.6 0.7 copy-done.3
  1.4 0.0 copy-start.5
  1.4 0.7 copy-done.5
  2.1 0.0 copy-start.7
  2.1 0.7 copy-done.7
  2.8 0.0 copy-start
  2.8 0.0 copy-start.1
  2.8 0.0 copy-start.2
  2.8 0.0 copy-start.4
  2.8 0.0 copy-start.6
  2.8 0.0 copy-start.8
  2.8 0.1 band_slabs.1
  2.9 0.8 collective-permute-start
  3.7 0.7 collective-permute-start.1
  4.4 0.0 copy-done
  4.4 0.0 copy-done.1
  4.4 0.0 copy-done.2
  4.4 0.0 copy-done.4
  4.4 0.0 copy-done.6
  4.4 0.0 copy-done.8
  4.4 1.9 %prepare.1 = (f32[96,512]{1,0:T(8,128)S(1)}, f32[96,512]{1,0:T(8,128)S(1)}, f32[144,512]{1,0:T(8,128)S(1)}, f32[144,512]{1,0:T(8,128)S(1)}, f32[10,32,128]{2,1,0...) custom-call(f32[64,32,512]{2,1,0:T(8,128)} %bitcast.31, f32[32,64]{1,0:T(8,128)S(1)} %bitcast.25, ...), custom_call_target="tpu_custom_call" | custom-call | flops 1000000 | bytes 6291456 | tf_op jit(solution)/shard_map/prepare/pallas_call | solution.py:263
  6.3 0.0 collective-permute-done.left
  6.4 0.0 collective-permute-done.1.right
  6.4 4.1 %collective-permute-start.6 = (f32[144,512]{1,0:T(8,128)S(1)}, f32[144,512]{1,0:T(8,128)S(1)}, u32[]{:S(2)}, u32[]{:S(2)}) collective-permute-start(f32[144,512]{1,0:T(8,128)S(1)} %get-tuple-element.56), channel_id=1, source_target_pairs={{0,1},{1,2},{2,3},{3,4},{4,5},{5,6},{6,7},{8,9},{9,10},{10,11},{11... | collective-permute-start | bytes 884744 | tf_op jit(solution)/shard_map/ppermute | solution.py:614
  10.5 1.9 %collective-permute-start.7 = (f32[144,512]{1,0:T(8,128)S(1)}, f32[144,512]{1,0:T(8,128)S(1)}, u32[]{:S(2)}, u32[]{:S(2)}) collective-permute-start(f32[144,512]{1,0:T(8,128)S(1)} %get-tuple-element.57), channel_id=1, source_target_pairs={{1,0},{2,1},{3,2},{4,3},{5,4},{6,5},{7,6},{9,8},{10,9},{11,10},{12... | collective-permute-start | bytes 884744 | tf_op jit(solution)/shard_map/ppermute | solution.py:615
  12.5 3.2 %collective-permute-start.4 = (f32[96,512]{1,0:T(8,128)S(1)}, f32[96,512]{1,0:T(8,128)S(1)}, u32[]{:S(2)}, u32[]{:S(2)}) collective-permute-start(f32[96,512]{1,0:T(8,128)S(1)} %get-tuple-element.54), channel_id=1, source_target_pairs={{0,8},{8,16},{16,24},{24,32},{32,40},{40,48},{48,56},{1,9},{9,17},... | collective-permute-start | bytes 589832 | tf_op jit(solution)/shard_map/ppermute | solution.py:614
  15.7 5.7 %collective-permute-start.5 = (f32[96,512]{1,0:T(8,128)S(1)}, f32[96,512]{1,0:T(8,128)S(1)}, u32[]{:S(2)}, u32[]{:S(2)}) collective-permute-start(f32[96,512]{1,0:T(8,128)S(1)} %get-tuple-element.55), channel_id=1, source_target_pairs={{8,0},{16,8},{24,16},{32,24},{40,32},{48,40},{56,48},{9,1},{17,9},... | collective-permute-start | bytes 589832 | tf_op jit(solution)/shard_map/ppermute | solution.py:615
  21.4 0.7 collective-permute-start.3
  22.1 0.7 collective-permute-done.4.up
  22.8 0.7 collective-permute-start.2
  23.4 1.1 %collective-permute-done.5.down = f32[96,512]{1,0:T(8,128)S(1)} collective-permute-done((f32[96,512]{1,0:T(8,128)S(1)}, f32[96,512]{1,0:T(8,128)S(1)}, u32[]{:S(2)}, u32[]{:S(2)}) %collective-permute-start.5) | collective-permute-done | bytes 196640 | tf_op jit(solution)/shard_map/ppermute | solution.py:615
  24.5 0.0 collective-permute-done.6.left
  24.5 0.0 collective-permute-done.7.right
  24.5 9.7 %first_iteration.1 = (f32[64,32,512]{2,1,0:T(8,128)S(1)}, f32[64,512]{1,0:T(8,128)S(1)}, f32[64,512]{1,0:T(8,128)S(1)}, f32[128,512]{1,0:T(8,128)S(1)}, f32[128,512]{1,0:T(8,128)S(1)}) custom-call(f32[64,32,512]{2,1,0:T(8,128)} %bitcast.33, f32[64,32,512]{2,1,0:T(8,128)} %bitcast.37, f32[64,32,512]{2,1,0:T(8,128)} %bitcast.40, ...), custom_call_target="tpu_custom_call" | custom-call | flops 7000000000 | bytes 20971520 | tf_op jit(solution)/shard_map/first_iteration/pallas_call | solution.py:380
  34.2 0.0 collective-permute-done.3
  34.2 0.0 collective-permute-done.2
  34.3 0.7 collective-permute-start.10
  35.0 0.7 collective-permute-start.9
  35.6 1.3 %collective-permute-start.8 = (f32[128,512]{1,0:T(8,128)S(1)}, f32[128,512]{1,0:T(8,128)S(1)}, u32[]{:S(2)}, u32[]{:S(2)}) collective-permute-start(f32[128,512]{1,0:T(8,128)S(1)} %add.12.after), channel_id=1, source_target_pairs={{88,64},{120,96},{89,65},{121,97},{90,66},{122,98},{91,67},{123,99... | collective-permute-start | bytes 786440 | tf_op jit(solution)/shard_map/ppermute | solution.py:659
  36.9 1.9 %collective-permute-start.14 = (f32[64,512]{1,0:T(8,128)S(1)}, f32[64,512]{1,0:T(8,128)S(1)}, u32[]{:S(2)}, u32[]{:S(2)}) collective-permute-start(f32[64,512]{1,0:T(8,128)S(1)} %get-tuple-element.69), channel_id=1, source_target_pairs={{0,8},{8,16},{16,24},{24,32},{32,40},{40,48},{48,56},{1,9},{9,17},... | collective-permute-start | bytes 393224 | tf_op jit(solution)/shard_map/ppermute | solution.py:614
  38.9 10.3 %collective-permute-start.15 = (f32[64,512]{1,0:T(8,128)S(1)}, f32[64,512]{1,0:T(8,128)S(1)}, u32[]{:S(2)}, u32[]{:S(2)}) collective-permute-start(f32[64,512]{1,0:T(8,128)S(1)} %get-tuple-element.70), channel_id=1, source_target_pairs={{8,0},{16,8},{24,16},{32,24},{40,32},{48,40},{56,48},{9,1},{17,9},... | collective-permute-start | bytes 393224 | tf_op jit(solution)/shard_map/ppermute | solution.py:615
  49.2 4.8 %stencil_matrix.1 = (bf16[2048,512]{1,0:T(8,128)(2,1)S(1)}, bf16[2048,512]{1,0:T(8,128)(2,1)S(1)}, bf16[384,512]{1,0:T(8,128)(2,1)S(1)}, bf16[384,512]{1,0:T(8,128)(2,1)S(1)}) custom-call(f32[10,32,128]{2,1,0:T(8,128)S(1)} %get-tuple-element.49.tables, f32[96,512]{1,0:T(8,128)S(1)} %collective-permute-done.4.up, f32[96,512]{1,0:T(8,128)S(1)} %collective-permute-done.5.down, ...), custom_call_target="tpu_custom_call" | custom-call | flops 15000000 | bytes 6291456 | tf_op jit(solution)/shard_map/stencil_matrix/pallas_call | solution.py:477
  54.1 0.0 collective-permute-done.10
  54.1 4.5 %collective-permute-start.16 = (f32[128,512]{1,0:T(8,128)S(1)}, f32[128,512]{1,0:T(8,128)S(1)}, u32[]{:S(2)}, u32[]{:S(2)}) collective-permute-start(f32[128,512]{1,0:T(8,128)S(1)} %get-tuple-element.71), channel_id=1, source_target_pairs={{0,1},{1,2},{2,3},{3,4},{4,5},{5,6},{6,7},{8,9},{9,10},{10,11},{11... | collective-permute-start | bytes 786440 | tf_op jit(solution)/shard_map/ppermute | solution.py:614
  58.6 0.0 collective-permute-done.9
  58.6 1.9 %collective-permute-start.17 = (f32[128,512]{1,0:T(8,128)S(1)}, f32[128,512]{1,0:T(8,128)S(1)}, u32[]{:S(2)}, u32[]{:S(2)}) collective-permute-start(f32[128,512]{1,0:T(8,128)S(1)} %get-tuple-element.72), channel_id=1, source_target_pairs={{1,0},{2,1},{3,2},{4,3},{5,4},{6,5},{7,6},{9,8},{10,9},{11,10},{12... | collective-permute-start | bytes 786440 | tf_op jit(solution)/shard_map/ppermute | solution.py:615
  60.5 0.0 collective-permute-done.8
  60.5 0.1 add_add_fusion
  60.6 2.8 %collective-permute-start.13 = (f32[128,512]{1,0:T(8,128)S(1)}, f32[128,512]{1,0:T(8,128)S(1)}, u32[]{:S(2)}, u32[]{:S(2)}) collective-permute-start(f32[128,512]{1,0:T(8,128)S(1)} %add_add_fusion), channel_id=1, source_target_pairs={{64,70},{65,71},{66,64},{67,65},{68,66},{69,67},{70,68},{71,69},{7... | collective-permute-start | bytes 786440 | tf_op jit(solution)/shard_map/ppermute | solution.py:672
  63.4 0.0 collective-permute-done.14.up
  63.4 4.1 %collective-permute-start.12 = (f32[128,512]{1,0:T(8,128)S(1)}, f32[128,512]{1,0:T(8,128)S(1)}, u32[]{:S(2)}, u32[]{:S(2)}) collective-permute-start(f32[128,512]{1,0:T(8,128)S(1)} %add_add_fusion), channel_id=1, source_target_pairs={{64,68},{65,69},{66,70},{67,71},{68,64},{69,65},{70,66},{71,67},{7... | collective-permute-start | bytes 786440 | tf_op jit(solution)/shard_map/ppermute | solution.py:672
  67.5 0.0 collective-permute-done.15.down
  67.6 1.9 %collective-permute-start.11 = (f32[128,512]{1,0:T(8,128)S(1)}, f32[128,512]{1,0:T(8,128)S(1)}, u32[]{:S(2)}, u32[]{:S(2)}) collective-permute-start(f32[128,512]{1,0:T(8,128)S(1)} %add_add_fusion), channel_id=1, source_target_pairs={{64,66},{65,67},{66,68},{67,69},{68,70},{69,71},{70,64},{71,65},{7... | collective-permute-start | bytes 786440 | tf_op jit(solution)/shard_map/ppermute | solution.py:672
  69.5 0.0 collective-permute-done.16.left
  69.5 0.0 collective-permute-done.17.right
  69.5 1.4 %collective-permute-done.13 = f32[128,512]{1,0:T(8,128)S(1)} collective-permute-done((f32[128,512]{1,0:T(8,128)S(1)}, f32[128,512]{1,0:T(8,128)S(1)}, u32[]{:S(2)}, u32[]{:S(2)}) %collective-permute-start.13) | collective-permute-done | bytes 262176 | tf_op jit(solution)/shard_map/ppermute | solution.py:672
  70.9 1.7 %collective-permute-done.12 = f32[128,512]{1,0:T(8,128)S(1)} collective-permute-done((f32[128,512]{1,0:T(8,128)S(1)}, f32[128,512]{1,0:T(8,128)S(1)}, u32[]{:S(2)}, u32[]{:S(2)}) %collective-permute-start.12) | collective-permute-done | bytes 262176 | tf_op jit(solution)/shard_map/ppermute | solution.py:672
  72.6 7.6 %collective-permute-done.11 = f32[128,512]{1,0:T(8,128)S(1)} collective-permute-done((f32[128,512]{1,0:T(8,128)S(1)}, f32[128,512]{1,0:T(8,128)S(1)}, u32[]{:S(2)}, u32[]{:S(2)}) %collective-permute-start.11) | collective-permute-done | bytes 262176 | tf_op jit(solution)/shard_map/ppermute | solution.py:672
  80.3 0.1 pad_maximum_fusion.own_table
  80.3 3.2 %collective-permute-start.18 = (f32[4,128,512]{2,1,0:T(8,128)S(1)}, f32[4,128,512]{2,1,0:T(8,128)S(1)}, u32[]{:S(2)}, u32[]{:S(2)}) collective-permute-start(f32[4,128,512]{2,1,0:T(8,128)S(1)} %pad_maximum_fusion.own_table), channel_id=1, source_target_pairs={{64,65},{65,64},{66,67},{67,66},{68,69},{69,68},{70,71},{71,70},{7... | collective-permute-start | bytes 3145736 | tf_op jit(solution)/shard_map/ppermute | solution.py:678
  83.5 2.3 %collective-permute-done.18.other_table = f32[4,128,512]{2,1,0:T(8,128)S(1)} collective-permute-done((f32[4,128,512]{2,1,0:T(8,128)S(1)}, f32[4,128,512]{2,1,0:T(8,128)S(1)}, u32[]{:S(2)}, u32[]{:S(2)}) %collective-permute-start.18) | collective-permute-done | bytes 1048608 | tf_op jit(solution)/shard_map/ppermute | solution.py:678
  85.8 16.9 %last_iteration.1 = (f32[64,32,512]{2,1,0:T(8,128)}, f32[64,32,512]{2,1,0:T(8,128)}) custom-call(f32[64,32,512]{2,1,0:T(8,128)S(1)} %get-tuple-element.59.one, f32[64,32,512]{2,1,0:T(8,128)} %bitcast.34, f32[64,32,512]{2,1,0:T(8,128)} %bitcast.41, f32[10,32,128]{2,1,0:T(8,128)S(1)} %get-tuple-element.49.tables, f32[64,512]{1,0:T(8,128)S(1)} %collective-permute-done.14.up, ...), custom_call_target="tpu_custom_call" | custom-call | flops 20000000000 | bytes 37748736 | tf_op jit(solution)/shard_map/last_iteration/pallas_call | solution.py:590
  (2 shorter events, 0.1 us)
Async XLA Ops:
  0.6 0.7 copy-start.3
  1.4 0.7 copy-start.5
  2.1 0.7 copy-start.7
  2.8 1.6 %copy-start = (f32[1,512,512]{2,1,0:T(8,128)S(1)}, f32[1,512,512]{2,1,0:T(8,128)}, u32[]{:S(2)}) copy-start(f32[1,512,512]{2,1,0:T(8,128)} %param.13) | copy-start | bytes 3145732
  2.8 1.6 %copy-start.1 = (s32[4,64,32]{1,2,0:T(8,128)S(1)}, s32[4,64,32]{1,2,0:T(8,128)}, u32[]{:S(2)}) copy-start(s32[4,64,32]{1,2,0:T(8,128)} %param.16) | copy-start | bytes 98308
  2.8 1.6 %copy-start.2 = (f32[4,64,32]{1,2,0:T(8,128)S(1)}, f32[4,64,32]{1,2,0:T(8,128)}, u32[]{:S(2)}) copy-start(f32[4,64,32]{1,2,0:T(8,128)} %param.17) | copy-start | bytes 98308
  2.8 1.6 %copy-start.4 = (f32[1,64,32]{1,2,0:T(8,128)S(1)}, f32[1,64,32]{1,2,0:T(8,128)}, u32[]{:S(2)}) copy-start(f32[1,64,32]{1,2,0:T(8,128)} %param.12) | copy-start | bytes 24580
  2.8 1.6 %copy-start.6 = (f32[1,64,32]{1,2,0:T(8,128)S(1)}, f32[1,64,32]{1,2,0:T(8,128)}, u32[]{:S(2)}) copy-start(f32[1,64,32]{1,2,0:T(8,128)} %param.14) | copy-start | bytes 24580
  2.8 1.6 %copy-start.8 = (s32[1,64,32]{1,2,0:T(8,128)S(1)}, s32[1,64,32]{1,2,0:T(8,128)}, u32[]{:S(2)}) copy-start(s32[1,64,32]{1,2,0:T(8,128)} %param.15) | copy-start | bytes 24580
  2.9 3.5 %collective-permute-start = (f32[32,512]{1,0:T(8,128)S(1)}, f32[32,512]{1,0:T(8,128)S(1)}, u32[]{:S(2)}, u32[]{:S(2)}) collective-permute-start(f32[32,512]{1,0:T(8,128)S(1)} %get-tuple-element.50), channel_id=1, source_target_pairs={{56,57},{57,58},{58,59},{59,60},{60,61},{61,62},{62,63}} | collective-permute-start | bytes 196616 | tf_op jit(solution)/shard_map/ppermute | solution.py:637
  3.7 2.7 %collective-permute-start.1 = (f32[32,512]{1,0:T(8,128)S(1)}, f32[32,512]{1,0:T(8,128)S(1)}, u32[]{:S(2)}, u32[]{:S(2)}) collective-permute-start(f32[32,512]{1,0:T(8,128)S(1)} %get-tuple-element.44.after), channel_id=1, source_target_pairs={{57,56},{58,57},{59,58},{60,59},{61,60},{62,61},{63,62}} | collective-permute-start | bytes 196616 | tf_op jit(solution)/shard_map/ppermute | solution.py:638
  6.4 18.1 %collective-permute-start.6 = (f32[144,512]{1,0:T(8,128)S(1)}, f32[144,512]{1,0:T(8,128)S(1)}, u32[]{:S(2)}, u32[]{:S(2)}) collective-permute-start(f32[144,512]{1,0:T(8,128)S(1)} %get-tuple-element.56), channel_id=1, source_target_pairs={{0,1},{1,2},{2,3},{3,4},{4,5},{5,6},{6,7},{8,9},{9,10},{10,11},{11... | collective-permute-start | bytes 884744 | tf_op jit(solution)/shard_map/ppermute | solution.py:614
  10.5 14.0 %collective-permute-start.7 = (f32[144,512]{1,0:T(8,128)S(1)}, f32[144,512]{1,0:T(8,128)S(1)}, u32[]{:S(2)}, u32[]{:S(2)}) collective-permute-start(f32[144,512]{1,0:T(8,128)S(1)} %get-tuple-element.57), channel_id=1, source_target_pairs={{1,0},{2,1},{3,2},{4,3},{5,4},{6,5},{7,6},{9,8},{10,9},{11,10},{12... | collective-permute-start | bytes 884744 | tf_op jit(solution)/shard_map/ppermute | solution.py:615
  12.5 10.3 %collective-permute-start.4 = (f32[96,512]{1,0:T(8,128)S(1)}, f32[96,512]{1,0:T(8,128)S(1)}, u32[]{:S(2)}, u32[]{:S(2)}) collective-permute-start(f32[96,512]{1,0:T(8,128)S(1)} %get-tuple-element.54), channel_id=1, source_target_pairs={{0,8},{8,16},{16,24},{24,32},{32,40},{40,48},{48,56},{1,9},{9,17},... | collective-permute-start | bytes 589832 | tf_op jit(solution)/shard_map/ppermute | solution.py:614
  15.7 8.8 %collective-permute-start.5 = (f32[96,512]{1,0:T(8,128)S(1)}, f32[96,512]{1,0:T(8,128)S(1)}, u32[]{:S(2)}, u32[]{:S(2)}) collective-permute-start(f32[96,512]{1,0:T(8,128)S(1)} %get-tuple-element.55), channel_id=1, source_target_pairs={{8,0},{16,8},{24,16},{32,24},{40,32},{48,40},{56,48},{9,1},{17,9},... | collective-permute-start | bytes 589832 | tf_op jit(solution)/shard_map/ppermute | solution.py:615
  21.4 12.8 %collective-permute-start.3 = (f32[128,512]{1,0:T(8,128)S(1)}, f32[128,512]{1,0:T(8,128)S(1)}, u32[]{:S(2)}, u32[]{:S(2)}) collective-permute-start(f32[128,512]{1,0:T(8,128)S(1)} %both_bands.1.after), channel_id=1, source_target_pairs={{56,120},{57,121},{58,122},{59,123},{60,124},{61,125},{62,126},{63... | collective-permute-start | bytes 786440 | tf_op jit(solution)/shard_map/ppermute | solution.py:653
  22.8 11.5 %collective-permute-start.2 = (f32[128,512]{1,0:T(8,128)S(1)}, f32[128,512]{1,0:T(8,128)S(1)}, u32[]{:S(2)}, u32[]{:S(2)}) collective-permute-start(f32[128,512]{1,0:T(8,128)S(1)} %both_bands.1.after), channel_id=1, source_target_pairs={{56,88},{57,89},{58,90},{59,91},{60,92},{61,93},{62,94},{63,95}} | collective-permute-start | bytes 786440 | tf_op jit(solution)/shard_map/ppermute | solution.py:653
  34.3 19.8 %collective-permute-start.10 = (f32[128,512]{1,0:T(8,128)S(1)}, f32[128,512]{1,0:T(8,128)S(1)}, u32[]{:S(2)}, u32[]{:S(2)}) collective-permute-start(f32[128,512]{1,0:T(8,128)S(1)} %add.12.after), channel_id=1, source_target_pairs={{88,72},{120,104},{89,73},{121,105},{90,74},{122,106},{91,75},{123... | collective-permute-start | bytes 786440 | tf_op jit(solution)/shard_map/ppermute | solution.py:659
  35.0 23.6 %collective-permute-start.9 = (f32[128,512]{1,0:T(8,128)S(1)}, f32[128,512]{1,0:T(8,128)S(1)}, u32[]{:S(2)}, u32[]{:S(2)}) collective-permute-start(f32[128,512]{1,0:T(8,128)S(1)} %add.12.after), channel_id=1, source_target_pairs={{88,80},{120,112},{89,81},{121,113},{90,82},{122,114},{91,83},{123... | collective-permute-start | bytes 786440 | tf_op jit(solution)/shard_map/ppermute | solution.py:659
  35.6 24.9 %collective-permute-start.8 = (f32[128,512]{1,0:T(8,128)S(1)}, f32[128,512]{1,0:T(8,128)S(1)}, u32[]{:S(2)}, u32[]{:S(2)}) collective-permute-start(f32[128,512]{1,0:T(8,128)S(1)} %add.12.after), channel_id=1, source_target_pairs={{88,64},{120,96},{89,65},{121,97},{90,66},{122,98},{91,67},{123,99... | collective-permute-start | bytes 786440 | tf_op jit(solution)/shard_map/ppermute | solution.py:659
  36.9 26.5 %collective-permute-start.14 = (f32[64,512]{1,0:T(8,128)S(1)}, f32[64,512]{1,0:T(8,128)S(1)}, u32[]{:S(2)}, u32[]{:S(2)}) collective-permute-start(f32[64,512]{1,0:T(8,128)S(1)} %get-tuple-element.69), channel_id=1, source_target_pairs={{0,8},{8,16},{16,24},{24,32},{32,40},{40,48},{48,56},{1,9},{9,17},... | collective-permute-start | bytes 393224 | tf_op jit(solution)/shard_map/ppermute | solution.py:614
  38.9 28.7 %collective-permute-start.15 = (f32[64,512]{1,0:T(8,128)S(1)}, f32[64,512]{1,0:T(8,128)S(1)}, u32[]{:S(2)}, u32[]{:S(2)}) collective-permute-start(f32[64,512]{1,0:T(8,128)S(1)} %get-tuple-element.70), channel_id=1, source_target_pairs={{8,0},{16,8},{24,16},{32,24},{40,32},{48,40},{56,48},{9,1},{17,9},... | collective-permute-start | bytes 393224 | tf_op jit(solution)/shard_map/ppermute | solution.py:615
  54.1 15.4 %collective-permute-start.16 = (f32[128,512]{1,0:T(8,128)S(1)}, f32[128,512]{1,0:T(8,128)S(1)}, u32[]{:S(2)}, u32[]{:S(2)}) collective-permute-start(f32[128,512]{1,0:T(8,128)S(1)} %get-tuple-element.71), channel_id=1, source_target_pairs={{0,1},{1,2},{2,3},{3,4},{4,5},{5,6},{6,7},{8,9},{9,10},{10,11},{11... | collective-permute-start | bytes 786440 | tf_op jit(solution)/shard_map/ppermute | solution.py:614
  58.6 10.9 %collective-permute-start.17 = (f32[128,512]{1,0:T(8,128)S(1)}, f32[128,512]{1,0:T(8,128)S(1)}, u32[]{:S(2)}, u32[]{:S(2)}) collective-permute-start(f32[128,512]{1,0:T(8,128)S(1)} %get-tuple-element.72), channel_id=1, source_target_pairs={{1,0},{2,1},{3,2},{4,3},{5,4},{6,5},{7,6},{9,8},{10,9},{11,10},{12... | collective-permute-start | bytes 786440 | tf_op jit(solution)/shard_map/ppermute | solution.py:615
  60.6 10.3 %collective-permute-start.13 = (f32[128,512]{1,0:T(8,128)S(1)}, f32[128,512]{1,0:T(8,128)S(1)}, u32[]{:S(2)}, u32[]{:S(2)}) collective-permute-start(f32[128,512]{1,0:T(8,128)S(1)} %add_add_fusion), channel_id=1, source_target_pairs={{64,70},{65,71},{66,64},{67,65},{68,66},{69,67},{70,68},{71,69},{7... | collective-permute-start | bytes 786440 | tf_op jit(solution)/shard_map/ppermute | solution.py:672
  63.4 9.2 %collective-permute-start.12 = (f32[128,512]{1,0:T(8,128)S(1)}, f32[128,512]{1,0:T(8,128)S(1)}, u32[]{:S(2)}, u32[]{:S(2)}) collective-permute-start(f32[128,512]{1,0:T(8,128)S(1)} %add_add_fusion), channel_id=1, source_target_pairs={{64,68},{65,69},{66,70},{67,71},{68,64},{69,65},{70,66},{71,67},{7... | collective-permute-start | bytes 786440 | tf_op jit(solution)/shard_map/ppermute | solution.py:672
  67.6 12.7 %collective-permute-start.11 = (f32[128,512]{1,0:T(8,128)S(1)}, f32[128,512]{1,0:T(8,128)S(1)}, u32[]{:S(2)}, u32[]{:S(2)}) collective-permute-start(f32[128,512]{1,0:T(8,128)S(1)} %add_add_fusion), channel_id=1, source_target_pairs={{64,66},{65,67},{66,68},{67,69},{68,70},{69,71},{70,64},{71,65},{7... | collective-permute-start | bytes 786440 | tf_op jit(solution)/shard_map/ppermute | solution.py:672
  80.3 5.4 %collective-permute-start.18 = (f32[4,128,512]{2,1,0:T(8,128)S(1)}, f32[4,128,512]{2,1,0:T(8,128)S(1)}, u32[]{:S(2)}, u32[]{:S(2)}) collective-permute-start(f32[4,128,512]{2,1,0:T(8,128)S(1)} %pad_maximum_fusion.own_table), channel_id=1, source_target_pairs={{64,65},{65,64},{66,67},{67,66},{68,69},{69,68},{70,71},{71,70},{7... | collective-permute-start | bytes 3145736 | tf_op jit(solution)/shard_map/ppermute | solution.py:678

commit v4 on v3

--- a/solution.py
+++ b/solution.py
@@ -17,7 +17,7 @@
 FAR = 2
 ROT, RET, INDEX, WEIGHT, TABLES = 0, 1, 2, 6, 10
 EXTRA = 2 * STENCILS * HALO
-AXES = ("sect", "rr", "row")
+OFBAND = 32
 MIB = 1 << 20
 F32 = jnp.float32
 BF16 = jnp.bfloat16
@@ -74,61 +74,13 @@
     return 1.0 - absorber.astype(F32) * (1.0 - damping)
 
 
-def band_slab_kernel(rotation, damping, absorber, packet, previous, potential, firsts, lasts, held, factors, masks, sems):
-    count_r, rows, width = packet.shape
-
-    @pl.when(holds_bands())
-    def _():
-        copies = [
-            pltpu.make_async_copy(ref.at[pl.ds(count_r - 4, 4)], held.at[n], sems.at[n])
-            for n, ref in enumerate((packet, previous, potential))
-        ]
-        copies += [
-            pltpu.make_async_copy(rotation, factors.at[0], sems.at[3]),
-            pltpu.make_async_copy(damping, factors.at[1], sems.at[4]),
-            pltpu.make_async_copy(absorber, masks, sems.at[5]),
-        ]
-        for copy in copies:
-            copy.start()
-        for copy in copies:
-            copy.wait()
-        retained = retained_of(factors[1], masks[...])
-        rotated = factors[0]
-        for out, far, near in ((firsts, 0, 0), (lasts, rows - 4, rows - 2)):
-            for k in range(4):
-                out[4 * k : 4 * k + 4] = held[0, k, far : far + 4]
-            for k in range(BAND):
-                at = count_r - BAND + k
-                out[16 + 2 * k : 18 + 2 * k] = held[1, 2 + k, near : near + 2]
-                out[20 + 2 * k : 22 + 2 * k] = held[2, 2 + k, near : near + 2]
-                out[24 + 2 * k : 26 + 2 * k] = jnp.broadcast_to(rotated[near : near + 2, at : at + 1], (2, width))
-                out[28 + 2 * k : 30 + 2 * k] = jnp.broadcast_to(retained[near : near + 2, at : at + 1], (2, width))
-
-
-def band_slabs(rotation, damping, absorber, packet, previous, potential):
-    count_r, rows, width = packet.shape
-    return pl.pallas_call(
-        band_slab_kernel,
-        in_specs=[ANY, ANY, ANY, HBM, HBM, HBM],
-        out_specs=[VMEM, VMEM],
-        out_shape=[jax.ShapeDtypeStruct((32, width), F32)] * 2,
-        scratch_shapes=[
-            pltpu.VMEM((3, 4, rows, width), F32),
-            pltpu.VMEM((2, rows, count_r), F32),
-            pltpu.VMEM((rows, count_r), jnp.int32),
-            pltpu.SemaphoreType.DMA((6,)),
-        ],
-        compiler_params=pltpu.CompilerParams(vmem_limit_bytes=8 * MIB),
-        name="band_slabs",
-    )(rotation, damping, absorber, packet, previous, potential)
-
-
 def band_kernel(
     packet, previous, potential, tables, left, right, high, low, out, field, later, turned, held, sems
 ):
     count_r, rows, width = packet.shape
     base = 16
     wide = rows + 16
+    begin = left.shape[0] - OFBAND
 
     @pl.when(holds_bands())
     def _():
@@ -146,8 +98,9 @@
         for copy in copies:
             copy.start()
         for k in range(4):
-            field[4 + k, base - 4 : base] = left[4 * k : 4 * k + 4]
-            field[4 + k, base + rows : base + rows + 4] = right[4 * k : 4 * k + 4]
+            at = begin + 4 * k
+            field[4 + k, base - 4 : base] = left[at : at + 4]
+            field[4 + k, base + rows : base + rows + 4] = right[at : at + 4]
         columns = [
             (tables[ROT, :, count_r - 4 + k : count_r - 3 + k], tables[RET, :, count_r - 4 + k : count_r - 3 + k])
             for k in range(4)
@@ -170,7 +123,7 @@
                     out[(k - 2) * rows : (k - 1) * rows, lanes] = (1.0 - retained) * update
         for k in range(2, 4):
             for slab, place, inside in ((left, base - 8, 6), (right, base + rows, 0)):
-                at = 16 + 2 * (k - 2)
+                at = begin + 16 + 2 * (k - 2)
                 prev, pot, rot, ret = (slab[at + 4 * n : at + 4 * n + 2] for n in range(4))
                 update = doubled_hamilton(
                     field, 4 + k, place + inside, 2, slice(None),
@@ -211,21 +164,34 @@
 
 
 def prepare_kernel(
-    packet, rotation, damping, absorber, index, weight, angular, after,
-    top, bottom, first, last, tables, high, low, ends, sides, sems,
+    packet, previous, potential, rotation, damping, absorber, index, weight, angular,
+    top, bottom, first, last, tables, high, low,
+    ends, sides, others, factors, masks, indices, weights, matrix, sems,
 ):
     count_r, rows, width = packet.shape
+    small = [
+        pltpu.make_async_copy(rotation, factors.at[0], sems.at[0]),
+        pltpu.make_async_copy(damping, factors.at[1], sems.at[1]),
+        pltpu.make_async_copy(absorber, masks, sems.at[2]),
+        pltpu.make_async_copy(index, indices, sems.at[3]),
+        pltpu.make_async_copy(weight, weights, sems.at[4]),
+    ]
     copies = [
-        pltpu.make_async_copy(packet.at[pl.ds(0, HALO)], ends.at[0], sems.at[0]),
-        pltpu.make_async_copy(packet.at[pl.ds(count_r - HALO, HALO)], ends.at[1], sems.at[1]),
-        pltpu.make_async_copy(packet.at[:, pl.ds(0, 8)], sides.at[0], sems.at[2]),
-        pltpu.make_async_copy(packet.at[:, pl.ds(rows - 8, 8)], sides.at[1], sems.at[3]),
+        pltpu.make_async_copy(packet.at[:, pl.ds(0, 8)], sides.at[0], sems.at[5]),
+        pltpu.make_async_copy(packet.at[:, pl.ds(rows - 8, 8)], sides.at[1], sems.at[6]),
+        pltpu.make_async_copy(packet.at[pl.ds(0, HALO)], ends.at[0], sems.at[7]),
+        pltpu.make_async_copy(packet.at[pl.ds(count_r - HALO, HALO)], ends.at[1], sems.at[8]),
+        pltpu.make_async_copy(previous.at[pl.ds(count_r - BAND, BAND)], others.at[0], sems.at[9]),
+        pltpu.make_async_copy(potential.at[pl.ds(count_r - BAND, BAND)], others.at[1], sems.at[10]),
+        pltpu.make_async_copy(angular, matrix, sems.at[11]),
     ]
-    for copy in copies:
+    for copy in small + copies:
         copy.start()
-    values = [rotation[...], retained_of(damping[...], absorber[...])]
-    values += [index[n].astype(F32) for n in range(STENCILS)]
-    values += [weight[n] for n in range(STENCILS)]
+    for copy in small:
+        copy.wait()
+    values = [factors[0], retained_of(factors[1], masks[...])]
+    values += [indices[n].astype(F32) for n in range(STENCILS)]
+    values += [weights[n] for n in range(STENCILS)]
     for n, value in enumerate(values):
         tables[n] = jnp.concatenate([value, jnp.zeros((rows, LANES - count_r), F32)], axis=1)
     edges = HALO * rows
@@ -243,37 +209,55 @@
         last[columns + at : columns + at + HALO, 0:LANES] = value[rows - HALO : rows]
     top[edges : edges + rows, 0:LANES] = upper
     bottom[edges : edges + rows, 0:LANES] = lower
-    high[...], low[...] = halves(angular[...])
+    begin = columns + EXTRA
     for copy in copies:
         copy.wait()
-    for out, n in ((top, 0), (bottom, 1)):
-        for k in range(HALO):
-            out[k * rows : (k + 1) * rows] = ends[n, k]
+    for out, n, far, near in ((first, 0, 0, 0), (last, 1, 4, rows - 2)):
+        for k in range(4):
+            out[begin + 4 * k : begin + 4 * k + 4] = sides[n, count_r - 4 + k, far : far + 4]
+        for k in range(BAND):
+            at = begin + 16 + 2 * k
+            column = count_r - BAND + k
+            out[at : at + 2] = others[0, k, near : near + 2]
+            out[at + 4 : at + 6] = others[1, k, near : near + 2]
+            for m in (ROT, RET):
+                value = tables[m, near : near + 2, column : column + 1]
+                out[at + 8 + 4 * m : at + 10 + 4 * m] = jnp.broadcast_to(value, (2, width))
     for out, n, near in ((first, 0, 0), (last, 1, 8 - HALO)):
         for k in range(count_r):
             for r in range(HALO):
                 out[r * count_r + k : r * count_r + k + 1] = sides[n, k, near + r : near + r + 1]
-
-
-def prepare(packet, rotation, damping, absorber, index, weight, angular, after):
+    for out, n in ((top, 0), (bottom, 1)):
+        for k in range(HALO):
+            out[k * rows : (k + 1) * rows] = ends[n, k]
+    high[...], low[...] = halves(matrix[...])
+
+
+def prepare(packet, previous, potential, rotation, damping, absorber, index, weight, angular):
     count_r, rows, width = packet.shape
     ends = jax.ShapeDtypeStruct((HALO * rows + rows, width), F32)
-    sides = jax.ShapeDtypeStruct((HALO * count_r + EXTRA, width), F32)
+    sides = jax.ShapeDtypeStruct((HALO * count_r + EXTRA + OFBAND, width), F32)
     part = jax.ShapeDtypeStruct(angular.shape, BF16)
     return pl.pallas_call(
         prepare_kernel,
-        in_specs=[HBM, VMEM, VMEM, VMEM, VMEM, VMEM, VMEM, ANY],
+        in_specs=[HBM] * 9,
         out_specs=[VMEM] * 7,
         out_shape=[ends, ends, sides, sides, jax.ShapeDtypeStruct((TABLES, rows, LANES), F32), part, part],
         scratch_shapes=[
             pltpu.VMEM((2, HALO, rows, width), F32),
             pltpu.VMEM((2, count_r, 8, width), F32),
-            pltpu.SemaphoreType.DMA((4,)),
+            pltpu.VMEM((2, BAND, rows, width), F32),
+            pltpu.VMEM((2, rows, count_r), F32),
+            pltpu.VMEM((rows, count_r), jnp.int32),
+            pltpu.VMEM((STENCILS, rows, count_r), jnp.int32),
+            pltpu.VMEM((STENCILS, rows, count_r), F32),
+            pltpu.VMEM(angular.shape, F32),
+            pltpu.SemaphoreType.DMA((12,)),
         ],
         compiler_params=pltpu.CompilerParams(vmem_limit_bytes=16 * MIB),
         cost_estimate=pl.CostEstimate(flops=1_000_000, bytes_accessed=6 * MIB, transcendentals=0),
         name="prepare",
-    )(packet, rotation, damping, absorber, index, weight, angular, after)
+    )(packet, previous, potential, rotation, damping, absorber, index, weight, angular)
 
 
 def put_sides(sides, left, right, count_r, left_more=None, right_more=None):
@@ -397,7 +381,7 @@
 
 def stencil_kernel(tables, up, down, left, right, after, high, low, edge_high, edge_low, square):
     _, rows, _ = tables.shape
-    count_r = left.shape[0] // HALO - EXTRA // HALO
+    count_r = high.shape[0] // rows
     width = high.shape[1]
     per = rows * BAND
     shift_owner = per.bit_length() - 1
@@ -469,9 +453,8 @@
                     at += rows
 
 
-def stencil_matrix(tables, halos, columns, after):
+def stencil_matrix(tables, halos, count_r, columns, after):
     rows = tables.shape[1]
-    count_r = halos[2].shape[0] // HALO - EXTRA // HALO
     points = jax.ShapeDtypeStruct((count_r * rows, columns), BF16)
     edges = jax.ShapeDtypeStruct((2 * HALO * (rows + count_r), columns), BF16)
     return pl.pallas_call(
@@ -628,22 +611,20 @@
     count_r, rows, width = packet.shape
     count_rr, count_row = (lax.axis_size(name) for name in ("rr", "row"))
     chips = count_row // CORES
-    packet, previous, potential = (in_hbm(value) for value in (packet, previous, potential))
     rotation, damping, absorber = (jnp.swapaxes(value, 0, 1) for value in (rotation, damping, absorber))
     stencil_index, stencil_weight = (jnp.swapaxes(value, 1, 2) for value in (stencil_index, stencil_weight))
-
-    firsts, lasts = band_slabs(rotation, damping, absorber, packet, previous, potential)
-    sources = (count_rr - 1) * count_row
-    band_left = lax.ppermute(lasts, AXES, [(sources + i, sources + i + 1) for i in range(count_row - 1)])
-    band_right = lax.ppermute(firsts, AXES, [(sources + i + 1, sources + i) for i in range(count_row - 1)])
+    packet, previous, potential, rotation, damping, absorber, stencil_index, stencil_weight, angular = (
+        in_hbm(value)
+        for value in (
+            packet, previous, potential, rotation, damping, absorber, stencil_index, stencil_weight, angular
+        )
+    )
 
     top, bottom, first, last, tables, high, low = prepare(
-        packet, rotation, damping, absorber, stencil_index, stencil_weight, angular, firsts
+        packet, previous, potential, rotation, damping, absorber, stencil_index, stencil_weight, angular
     )
-    table = bands(packet, previous, potential, tables, band_left, band_right, high, low)
-    top, bottom, first, last, table = lax.optimization_barrier((top, bottom, first, last, table))
     halos = exchange(top, bottom, first, last)
-
+    table = bands(packet, previous, potential, tables, *halos[2:], high, low)
     one, *edges = first_iteration(packet, previous, potential, tables, halos, high, low, table)
 
     plane = ("sect", "rr")
@@ -657,8 +638,6 @@
     for shift in (1, half - 1, 2):
         pairs = [(entry, entry - (half - 1) + (half - 1 + shift) % half) for entry in entries]
         arrived.append(lax.ppermute(piece, plane, pairs))
-    matrices = stencil_matrix(tables, halos, count_row * rows * BAND, piece)
-    *arrived, matrices = lax.optimization_barrier((*arrived, matrices))
     spread = piece + sum(arrived)
     line = ("sect", "row")
 
@@ -673,7 +652,8 @@
 
     rest = [around(1), around(2), around(3)]
     later = exchange(*edges)
-    *rest, later = lax.optimization_barrier((*rest, later))
+    matrices = stencil_matrix(tables, halos, count_r, count_row * rows * BAND, spread)
+    *rest, later, matrices = lax.optimization_barrier((*rest, later, matrices))
     own = jnp.stack([spread, *rest], axis=0)
     other = lax.ppermute(
         own, line, [(count_row + i, count_row + i + 1 - 2 * (i % CORES)) for i in range(count_row)]

time: 103 us -> 95.2 us (0.924)
  waiting for transfers between devices: 14.8 us -> 10 us
  local copies, waits for them, and re-layouts: 2.17 us -> 0 us
  starting transfers between devices: 51.1 us -> 49.4 us
    ppermute x3, waiting for transfers between devices: 10.8 us -> 6.05 us  [around(): return lax.ppermute(spread, line, pairs)]
    unnamed x18 -> x0, local copies, waits for them, and re-layouts: 2.17 us -> none
    ppermute x4, starting transfers between devices: 19.9 us -> 18.2 us  [neighbours(): lax.ppermute(downward, axis, [(i + 1, i) for i in range(count - 1)])]
    ppermute x2 -> x0, starting transfers between devices: 1.46 us -> none  [the longest x1 0.8 us: local(): lax.ppermute(lasts, AXES, [(sources + i, sources + i + 1) for i in range(...]
    ppermute x4, starting transfers between devices: 13.8 us -> 15.2 us  [neighbours(): lax.ppermute(upward, axis, [(i, i + 1) for i in range(count - 1)])]
    pallas_call x2 -> x1, Pallas kernels: 1.98 us -> 2.69 us  [prepare(): pl.pallas_call(prepare_kernel, in_specs=[HBM] * 9, out_specs=[VMEM] * 7,...]
  transfers between devices with their start and end apart: 19 -> 17, of which waited for: 6 -> 3; matrix products, arithmetic and copies ran while one was open for 0% -> 0% of each run, Pallas kernels for 16% -> 15%
where the time goes in v4:
time: 95.2 us; the launch traced here: 94.7 us
  starting transfers between devices  49.4 us (52%)
  Pallas kernels  34.1 us (36%)
  waiting for transfers between devices  10 us (11%)
    ppermute x4, starting transfers between devices, neighbours(): lax.ppermute(downward, axis, [(i + 1, i) for i in range(count - 1)])  18.2 us
    pallas_call x1, Pallas kernels, last_iteration(): pl.pallas_call(last_kernel, in_specs=[VMEM, HBM, HBM, *[VMEM] * 13], out_...  16.9 us
    ppermute x4, starting transfers between devices, neighbours(): lax.ppermute(upward, axis, [(i, i + 1) for i in range(count - 1)])  15.2 us
    pallas_call x1, Pallas kernels, first_iteration(): pl.pallas_call(first_kernel, in_specs=[HBM, HBM, HBM, *[VMEM] * 7, ANY],...  9.67 us
    ppermute x3, starting transfers between devices, around(): return lax.ppermute(spread, line, pairs)  8.88 us
    ppermute x3, waiting for transfers between devices, around(): return lax.ppermute(spread, line, pairs)  6.05 us
    pallas_call x1, Pallas kernels, stencil_matrix(): pl.pallas_call(stencil_kernel, in_specs=[*[VMEM] * 5, ANY], out_specs=[VM...  4.82 us
    ppermute x1, starting transfers between devices, local(): lax.ppermute(own, line, [(count_row + i, count_row + i + 1 - 2 * (i % COR...  3.13 us
  transfers between devices with their start and end apart: 17, of which 3 were waited for; matrix products, arithmetic and copies ran while one was open for 0% of the time, Pallas kernels for 15%

profile of v4, /device:TPU:7, one launch (start us, length us, event | category | flops | bytes accessed | tf_op | source)
XLA Modules:
  0.0 94.7 jit_solution(5926524658172792986)
XLA Ops:
  0.6 2.7 %prepare.1 = (f32[96,512]{1,0:T(8,128)S(1)}, f32[96,512]{1,0:T(8,128)S(1)}, f32[176,512]{1,0:T(8,128)S(1)}, f32[176,512]{1,0:T(8,128)S(1)}, f32[10,32,128]{2,1,0...) custom-call(f32[64,32,512]{2,1,0:T(8,128)} %bitcast.25, f32[64,32,512]{2,1,0:T(8,128)} %bitcast.22, ...), custom_call_target="tpu_custom_call" | custom-call | flops 1000000 | bytes 6291456 | tf_op jit(solution)/shard_map/prepare/pallas_call | solution.py:241
  3.3 4.1 %collective-permute-start = (f32[176,512]{1,0:T(8,128)S(1)}, f32[176,512]{1,0:T(8,128)S(1)}, u32[]{:S(2)}, u32[]{:S(2)}) collective-permute-start(f32[176,512]{1,0:T(8,128)S(1)} %get-tuple-element.35), channel_id=1, source_target_pairs={{0,1},{1,2},{2,3},{3,4},{4,5},{5,6},{6,7},{8,9},{9,10},{10,11},{11... | collective-permute-start | bytes 1081352 | tf_op jit(solution)/shard_map/ppermute | solution.py:597
  7.4 1.9 %collective-permute-start.1 = (f32[176,512]{1,0:T(8,128)S(1)}, f32[176,512]{1,0:T(8,128)S(1)}, u32[]{:S(2)}, u32[]{:S(2)}) collective-permute-start(f32[176,512]{1,0:T(8,128)S(1)} %get-tuple-element.36), channel_id=1, source_target_pairs={{1,0},{2,1},{3,2},{4,3},{5,4},{6,5},{7,6},{9,8},{10,9},{11,10},{12... | collective-permute-start | bytes 1081352 | tf_op jit(solution)/shard_map/ppermute | solution.py:598
  9.4 3.2 %collective-permute-start.4 = (f32[96,512]{1,0:T(8,128)S(1)}, f32[96,512]{1,0:T(8,128)S(1)}, u32[]{:S(2)}, u32[]{:S(2)}) collective-permute-start(f32[96,512]{1,0:T(8,128)S(1)} %get-tuple-element.39), channel_id=1, source_target_pairs={{0,8},{8,16},{16,24},{24,32},{32,40},{40,48},{48,56},{1,9},{9,17},... | collective-permute-start | bytes 589832 | tf_op jit(solution)/shard_map/ppermute | solution.py:597
  12.6 5.7 %collective-permute-start.5 = (f32[96,512]{1,0:T(8,128)S(1)}, f32[96,512]{1,0:T(8,128)S(1)}, u32[]{:S(2)}, u32[]{:S(2)}) collective-permute-start(f32[96,512]{1,0:T(8,128)S(1)} %get-tuple-element.40), channel_id=1, source_target_pairs={{8,0},{16,8},{24,16},{32,24},{40,32},{48,40},{56,48},{9,1},{17,9},... | collective-permute-start | bytes 589832 | tf_op jit(solution)/shard_map/ppermute | solution.py:598
  18.3 0.0 collective-permute-done.left
  18.3 0.0 collective-permute-done.1.right
  18.4 0.7 collective-permute-start.3
  19.0 0.7 collective-permute-start.2
  19.7 0.0 collective-permute-done.4.up
  19.7 1.7 %collective-permute-done.5.down = f32[96,512]{1,0:T(8,128)S(1)} collective-permute-done((f32[96,512]{1,0:T(8,128)S(1)}, f32[96,512]{1,0:T(8,128)S(1)}, u32[]{:S(2)}, u32[]{:S(2)}) %collective-permute-start.5) | collective-permute-done | bytes 196640 | tf_op jit(solution)/shard_map/ppermute | solution.py:598
  21.4 9.7 %first_iteration.1 = (f32[64,32,512]{2,1,0:T(8,128)S(1)}, f32[64,512]{1,0:T(8,128)S(1)}, f32[64,512]{1,0:T(8,128)S(1)}, f32[128,512]{1,0:T(8,128)S(1)}, f32[128,512]{1,0:T(8,128)S(1)}) custom-call(f32[64,32,512]{2,1,0:T(8,128)} %bitcast.27, f32[64,32,512]{2,1,0:T(8,128)} %bitcast.24, f32[64,32,512]{2,1,0:T(8,128)} %bitcast.31, ...), custom_call_target="tpu_custom_call" | custom-call | flops 7000000000 | bytes 20971520 | tf_op jit(solution)/shard_map/first_iteration/pallas_call | solution.py:364
  31.1 0.0 collective-permute-done.3
  31.1 0.0 collective-permute-done.2
  31.2 0.7 collective-permute-start.8
  31.9 0.7 collective-permute-start.7
  32.5 1.3 %collective-permute-start.6 = (f32[128,512]{1,0:T(8,128)S(1)}, f32[128,512]{1,0:T(8,128)S(1)}, u32[]{:S(2)}, u32[]{:S(2)}) collective-permute-start(f32[128,512]{1,0:T(8,128)S(1)} %add.12), channel_id=1, source_target_pairs={{88,64},{120,96},{89,65},{121,97},{90,66},{122,98},{91,67},{123,99... | collective-permute-start | bytes 786440 | tf_op jit(solution)/shard_map/ppermute | solution.py:640
  33.8 1.9 %collective-permute-start.12 = (f32[64,512]{1,0:T(8,128)S(1)}, f32[64,512]{1,0:T(8,128)S(1)}, u32[]{:S(2)}, u32[]{:S(2)}) collective-permute-start(f32[64,512]{1,0:T(8,128)S(1)} %get-tuple-element.45), channel_id=1, source_target_pairs={{0,8},{8,16},{16,24},{24,32},{32,40},{40,48},{48,56},{1,9},{9,17},... | collective-permute-start | bytes 393224 | tf_op jit(solution)/shard_map/ppermute | solution.py:597
  35.8 8.7 %collective-permute-start.13 = (f32[64,512]{1,0:T(8,128)S(1)}, f32[64,512]{1,0:T(8,128)S(1)}, u32[]{:S(2)}, u32[]{:S(2)}) collective-permute-start(f32[64,512]{1,0:T(8,128)S(1)} %get-tuple-element.46), channel_id=1, source_target_pairs={{8,0},{16,8},{24,16},{32,24},{40,32},{48,40},{56,48},{9,1},{17,9},... | collective-permute-start | bytes 393224 | tf_op jit(solution)/shard_map/ppermute | solution.py:598
  44.5 0.0 collective-permute-done.8
  44.5 6.0 %collective-permute-start.14 = (f32[128,512]{1,0:T(8,128)S(1)}, f32[128,512]{1,0:T(8,128)S(1)}, u32[]{:S(2)}, u32[]{:S(2)}) collective-permute-start(f32[128,512]{1,0:T(8,128)S(1)} %get-tuple-element.47), channel_id=1, source_target_pairs={{0,1},{1,2},{2,3},{3,4},{4,5},{5,6},{6,7},{8,9},{9,10},{10,11},{11... | collective-permute-start | bytes 786440 | tf_op jit(solution)/shard_map/ppermute | solution.py:597
  50.5 0.0 collective-permute-done.7
  50.5 1.9 %collective-permute-start.15 = (f32[128,512]{1,0:T(8,128)S(1)}, f32[128,512]{1,0:T(8,128)S(1)}, u32[]{:S(2)}, u32[]{:S(2)}) collective-permute-start(f32[128,512]{1,0:T(8,128)S(1)} %get-tuple-element.48), channel_id=1, source_target_pairs={{1,0},{2,1},{3,2},{4,3},{5,4},{6,5},{7,6},{9,8},{10,9},{11,10},{12... | collective-permute-start | bytes 786440 | tf_op jit(solution)/shard_map/ppermute | solution.py:598
  52.4 0.0 collective-permute-done.6
  52.4 0.1 add_add_fusion.after
  52.5 3.0 %collective-permute-start.11 = (f32[128,512]{1,0:T(8,128)S(1)}, f32[128,512]{1,0:T(8,128)S(1)}, u32[]{:S(2)}, u32[]{:S(2)}) collective-permute-start(f32[128,512]{1,0:T(8,128)S(1)} %add_add_fusion.after), channel_id=1, source_target_pairs={{64,70},{65,71},{66,64},{67,65},{68,66},{69,67},{70,68},{71,69},{7... | collective-permute-start | bytes 786440 | tf_op jit(solution)/shard_map/ppermute | solution.py:651
  55.5 0.0 collective-permute-done.12.up
  55.5 4.0 %collective-permute-start.10 = (f32[128,512]{1,0:T(8,128)S(1)}, f32[128,512]{1,0:T(8,128)S(1)}, u32[]{:S(2)}, u32[]{:S(2)}) collective-permute-start(f32[128,512]{1,0:T(8,128)S(1)} %add_add_fusion.after), channel_id=1, source_target_pairs={{64,68},{65,69},{66,70},{67,71},{68,64},{69,65},{70,66},{71,67},{7... | collective-permute-start | bytes 786440 | tf_op jit(solution)/shard_map/ppermute | solution.py:651
  59.5 0.0 collective-permute-done.13.down
  59.5 1.9 %collective-permute-start.9 = (f32[128,512]{1,0:T(8,128)S(1)}, f32[128,512]{1,0:T(8,128)S(1)}, u32[]{:S(2)}, u32[]{:S(2)}) collective-permute-start(f32[128,512]{1,0:T(8,128)S(1)} %add_add_fusion.after), channel_id=1, source_target_pairs={{64,66},{65,67},{66,68},{67,69},{68,70},{69,71},{70,64},{71,65},{7... | collective-permute-start | bytes 786440 | tf_op jit(solution)/shard_map/ppermute | solution.py:651
  61.4 4.8 %stencil_matrix.1 = (bf16[2048,512]{1,0:T(8,128)(2,1)S(1)}, bf16[2048,512]{1,0:T(8,128)(2,1)S(1)}, bf16[384,512]{1,0:T(8,128)(2,1)S(1)}, bf16[384,512]{1,0:T(8,128)(2,1)S(1)}) custom-call(f32[10,32,128]{2,1,0:T(8,128)S(1)} %get-tuple-element.34.tables, f32[96,512]{1,0:T(8,128)S(1)} %collective-permute-done.4.up, f32[96,512]{1,0:T(8,128)S(1)} %collective-permute-done.5.down, ...), custom_call_target="tpu_custom_call" | custom-call | flops 15000000 | bytes 6291456 | tf_op jit(solution)/shard_map/stencil_matrix/pallas_call | solution.py:460
  66.3 0.0 collective-permute-done.14.left
  66.3 0.0 collective-permute-done.15.right
  66.3 0.0 collective-permute-done.11
  66.3 0.0 collective-permute-done.10
  66.3 6.0 %collective-permute-done.9 = f32[128,512]{1,0:T(8,128)S(1)} collective-permute-done((f32[128,512]{1,0:T(8,128)S(1)}, f32[128,512]{1,0:T(8,128)S(1)}, u32[]{:S(2)}, u32[]{:S(2)}) %collective-permute-start.9) | collective-permute-done | bytes 262176 | tf_op jit(solution)/shard_map/ppermute | solution.py:651
  72.3 0.1 pad_maximum_fusion.own_table
  72.4 3.1 %collective-permute-start.16 = (f32[4,128,512]{2,1,0:T(8,128)S(1)}, f32[4,128,512]{2,1,0:T(8,128)S(1)}, u32[]{:S(2)}, u32[]{:S(2)}) collective-permute-start(f32[4,128,512]{2,1,0:T(8,128)S(1)} %pad_maximum_fusion.own_table), channel_id=1, source_target_pairs={{64,65},{65,64},{66,67},{67,66},{68,69},{69,68},{70,71},{71,70},{7... | collective-permute-start | bytes 3145736 | tf_op jit(solution)/shard_map/ppermute | solution.py:658
  75.5 2.3 %collective-permute-done.16.other_table = f32[4,128,512]{2,1,0:T(8,128)S(1)} collective-permute-done((f32[4,128,512]{2,1,0:T(8,128)S(1)}, f32[4,128,512]{2,1,0:T(8,128)S(1)}, u32[]{:S(2)}, u32[]{:S(2)}) %collective-permute-start.16) | collective-permute-done | bytes 1048608 | tf_op jit(solution)/shard_map/ppermute | solution.py:658
  77.8 16.9 %last_iteration.1 = (f32[64,32,512]{2,1,0:T(8,128)}, f32[64,32,512]{2,1,0:T(8,128)}) custom-call(f32[64,32,512]{2,1,0:T(8,128)S(1)} %get-tuple-element.42.one, f32[64,32,512]{2,1,0:T(8,128)} %bitcast.28, f32[64,32,512]{2,1,0:T(8,128)} %bitcast.32, f32[10,32,128]{2,1,0:T(8,128)S(1)} %get-tuple-element.34.tables, f32[64,512]{1,0:T(8,128)S(1)} %collective-permute-done.12.up, ...), custom_call_target="tpu_custom_call" | custom-call | flops 20000000000 | bytes 37748736 | tf_op jit(solution)/shard_map/last_iteration/pallas_call | solution.py:573
  (2 shorter events, 0.1 us)
Async XLA Ops:
  3.3 15.0 %collective-permute-start = (f32[176,512]{1,0:T(8,128)S(1)}, f32[176,512]{1,0:T(8,128)S(1)}, u32[]{:S(2)}, u32[]{:S(2)}) collective-permute-start(f32[176,512]{1,0:T(8,128)S(1)} %get-tuple-element.35), channel_id=1, source_target_pairs={{0,1},{1,2},{2,3},{3,4},{4,5},{5,6},{6,7},{8,9},{9,10},{10,11},{11... | collective-permute-start | bytes 1081352 | tf_op jit(solution)/shard_map/ppermute | solution.py:597
  7.4 10.9 %collective-permute-start.1 = (f32[176,512]{1,0:T(8,128)S(1)}, f32[176,512]{1,0:T(8,128)S(1)}, u32[]{:S(2)}, u32[]{:S(2)}) collective-permute-start(f32[176,512]{1,0:T(8,128)S(1)} %get-tuple-element.36), channel_id=1, source_target_pairs={{1,0},{2,1},{3,2},{4,3},{5,4},{6,5},{7,6},{9,8},{10,9},{11,10},{12... | collective-permute-start | bytes 1081352 | tf_op jit(solution)/shard_map/ppermute | solution.py:598
  9.4 10.4 %collective-permute-start.4 = (f32[96,512]{1,0:T(8,128)S(1)}, f32[96,512]{1,0:T(8,128)S(1)}, u32[]{:S(2)}, u32[]{:S(2)}) collective-permute-start(f32[96,512]{1,0:T(8,128)S(1)} %get-tuple-element.39), channel_id=1, source_target_pairs={{0,8},{8,16},{16,24},{24,32},{32,40},{40,48},{48,56},{1,9},{9,17},... | collective-permute-start | bytes 589832 | tf_op jit(solution)/shard_map/ppermute | solution.py:597
  12.6 8.8 %collective-permute-start.5 = (f32[96,512]{1,0:T(8,128)S(1)}, f32[96,512]{1,0:T(8,128)S(1)}, u32[]{:S(2)}, u32[]{:S(2)}) collective-permute-start(f32[96,512]{1,0:T(8,128)S(1)} %get-tuple-element.40), channel_id=1, source_target_pairs={{8,0},{16,8},{24,16},{32,24},{40,32},{48,40},{56,48},{9,1},{17,9},... | collective-permute-start | bytes 589832 | tf_op jit(solution)/shard_map/ppermute | solution.py:598
  18.4 12.8 %collective-permute-start.3 = (f32[128,512]{1,0:T(8,128)S(1)}, f32[128,512]{1,0:T(8,128)S(1)}, u32[]{:S(2)}, u32[]{:S(2)}) collective-permute-start(f32[128,512]{1,0:T(8,128)S(1)} %both_bands.1.after), channel_id=1, source_target_pairs={{56,120},{57,121},{58,122},{59,123},{60,124},{61,125},{62,126},{63... | collective-permute-start | bytes 786440 | tf_op jit(solution)/shard_map/ppermute | solution.py:634
  19.0 12.1 %collective-permute-start.2 = (f32[128,512]{1,0:T(8,128)S(1)}, f32[128,512]{1,0:T(8,128)S(1)}, u32[]{:S(2)}, u32[]{:S(2)}) collective-permute-start(f32[128,512]{1,0:T(8,128)S(1)} %both_bands.1.after), channel_id=1, source_target_pairs={{56,88},{57,89},{58,90},{59,91},{60,92},{61,93},{62,94},{63,95}} | collective-permute-start | bytes 786440 | tf_op jit(solution)/shard_map/ppermute | solution.py:634
  31.2 13.3 %collective-permute-start.8 = (f32[128,512]{1,0:T(8,128)S(1)}, f32[128,512]{1,0:T(8,128)S(1)}, u32[]{:S(2)}, u32[]{:S(2)}) collective-permute-start(f32[128,512]{1,0:T(8,128)S(1)} %add.12), channel_id=1, source_target_pairs={{88,72},{120,104},{89,73},{121,105},{90,74},{122,106},{91,75},{123... | collective-permute-start | bytes 786440 | tf_op jit(solution)/shard_map/ppermute | solution.py:640
  31.9 18.6 %collective-permute-start.7 = (f32[128,512]{1,0:T(8,128)S(1)}, f32[128,512]{1,0:T(8,128)S(1)}, u32[]{:S(2)}, u32[]{:S(2)}) collective-permute-start(f32[128,512]{1,0:T(8,128)S(1)} %add.12), channel_id=1, source_target_pairs={{88,80},{120,112},{89,81},{121,113},{90,82},{122,114},{91,83},{123... | collective-permute-start | bytes 786440 | tf_op jit(solution)/shard_map/ppermute | solution.py:640
  32.5 19.9 %collective-permute-start.6 = (f32[128,512]{1,0:T(8,128)S(1)}, f32[128,512]{1,0:T(8,128)S(1)}, u32[]{:S(2)}, u32[]{:S(2)}) collective-permute-start(f32[128,512]{1,0:T(8,128)S(1)} %add.12), channel_id=1, source_target_pairs={{88,64},{120,96},{89,65},{121,97},{90,66},{122,98},{91,67},{123,99... | collective-permute-start | bytes 786440 | tf_op jit(solution)/shard_map/ppermute | solution.py:640
  33.8 21.7 %collective-permute-start.12 = (f32[64,512]{1,0:T(8,128)S(1)}, f32[64,512]{1,0:T(8,128)S(1)}, u32[]{:S(2)}, u32[]{:S(2)}) collective-permute-start(f32[64,512]{1,0:T(8,128)S(1)} %get-tuple-element.45), channel_id=1, source_target_pairs={{0,8},{8,16},{16,24},{24,32},{32,40},{40,48},{48,56},{1,9},{9,17},... | collective-permute-start | bytes 393224 | tf_op jit(solution)/shard_map/ppermute | solution.py:597
  35.8 23.7 %collective-permute-start.13 = (f32[64,512]{1,0:T(8,128)S(1)}, f32[64,512]{1,0:T(8,128)S(1)}, u32[]{:S(2)}, u32[]{:S(2)}) collective-permute-start(f32[64,512]{1,0:T(8,128)S(1)} %get-tuple-element.46), channel_id=1, source_target_pairs={{8,0},{16,8},{24,16},{32,24},{40,32},{48,40},{56,48},{9,1},{17,9},... | collective-permute-start | bytes 393224 | tf_op jit(solution)/shard_map/ppermute | solution.py:598
  44.5 21.8 %collective-permute-start.14 = (f32[128,512]{1,0:T(8,128)S(1)}, f32[128,512]{1,0:T(8,128)S(1)}, u32[]{:S(2)}, u32[]{:S(2)}) collective-permute-start(f32[128,512]{1,0:T(8,128)S(1)} %get-tuple-element.47), channel_id=1, source_target_pairs={{0,1},{1,2},{2,3},{3,4},{4,5},{5,6},{6,7},{8,9},{9,10},{10,11},{11... | collective-permute-start | bytes 786440 | tf_op jit(solution)/shard_map/ppermute | solution.py:597
  50.5 15.8 %collective-permute-start.15 = (f32[128,512]{1,0:T(8,128)S(1)}, f32[128,512]{1,0:T(8,128)S(1)}, u32[]{:S(2)}, u32[]{:S(2)}) collective-permute-start(f32[128,512]{1,0:T(8,128)S(1)} %get-tuple-element.48), channel_id=1, source_target_pairs={{1,0},{2,1},{3,2},{4,3},{5,4},{6,5},{7,6},{9,8},{10,9},{11,10},{12... | collective-permute-start | bytes 786440 | tf_op jit(solution)/shard_map/ppermute | solution.py:598
  52.5 13.8 %collective-permute-start.11 = (f32[128,512]{1,0:T(8,128)S(1)}, f32[128,512]{1,0:T(8,128)S(1)}, u32[]{:S(2)}, u32[]{:S(2)}) collective-permute-start(f32[128,512]{1,0:T(8,128)S(1)} %add_add_fusion.after), channel_id=1, source_target_pairs={{64,70},{65,71},{66,64},{67,65},{68,66},{69,67},{70,68},{71,69},{7... | collective-permute-start | bytes 786440 | tf_op jit(solution)/shard_map/ppermute | solution.py:651
  55.5 10.8 %collective-permute-start.10 = (f32[128,512]{1,0:T(8,128)S(1)}, f32[128,512]{1,0:T(8,128)S(1)}, u32[]{:S(2)}, u32[]{:S(2)}) collective-permute-start(f32[128,512]{1,0:T(8,128)S(1)} %add_add_fusion.after), channel_id=1, source_target_pairs={{64,68},{65,69},{66,70},{67,71},{68,64},{69,65},{70,66},{71,67},{7... | collective-permute-start | bytes 786440 | tf_op jit(solution)/shard_map/ppermute | solution.py:651
  59.5 12.8 %collective-permute-start.9 = (f32[128,512]{1,0:T(8,128)S(1)}, f32[128,512]{1,0:T(8,128)S(1)}, u32[]{:S(2)}, u32[]{:S(2)}) collective-permute-start(f32[128,512]{1,0:T(8,128)S(1)} %add_add_fusion.after), channel_id=1, source_target_pairs={{64,66},{65,67},{66,68},{67,69},{68,70},{69,71},{70,64},{71,65},{7... | collective-permute-start | bytes 786440 | tf_op jit(solution)/shard_map/ppermute | solution.py:651
  72.4 5.4 %collective-permute-start.16 = (f32[4,128,512]{2,1,0:T(8,128)S(1)}, f32[4,128,512]{2,1,0:T(8,128)S(1)}, u32[]{:S(2)}, u32[]{:S(2)}) collective-permute-start(f32[4,128,512]{2,1,0:T(8,128)S(1)} %pad_maximum_fusion.own_table), channel_id=1, source_target_pairs={{64,65},{65,64},{66,67},{67,66},{68,69},{69,68},{70,71},{71,70},{7... | collective-permute-start | bytes 3145736 | tf_op jit(solution)/shard_map/ppermute | solution.py:658

commit v5 on v4

--- a/solution.py
+++ b/solution.py
@@ -379,68 +379,89 @@
     )(packet, previous, potential, tables, *halos, high, low, after)
 
 
-def stencil_kernel(tables, up, down, left, right, after, high, low, edge_high, edge_low, square):
-    _, rows, _ = tables.shape
-    count_r = high.shape[0] // rows
-    width = high.shape[1]
+def slot_of(value, rows, width):
     per = rows * BAND
     shift_owner = per.bit_length() - 1
     chips = width // per // CORES
-
-    def place(value):
-        index = value.astype(jnp.int32)
-        owner = index >> shift_owner
-        inside = index & (per - 1)
-        core = (owner & 1) ^ (lax.axis_index("row") & 1)
-        chip = ((lax.axis_index("row") >> 1) - (owner >> 1)) & (chips - 1)
-        slot = ((core * chips + chip) << shift_owner) + (inside & 1) * rows + (inside >> 1)
-        return slot.astype(F32)
-
-    column = lax.broadcasted_iota(jnp.int32, (32, LANES), 1).astype(F32)
-
-    def fill(at, places, weights, high_out, low_out):
-        places = [jnp.broadcast_to(p, (32, LANES)) for p in places]
-        weights = [jnp.broadcast_to(w, (32, LANES)) for w in weights]
-        for tile in range(0, width, LANES):
-            here = column + float(tile)
-            total = jnp.where(here == places[0], weights[0], 0.0)
-            for n in range(1, STENCILS):
-                total += jnp.where(here == places[n], weights[n], 0.0)
-            upper, lower = halves(total)
-            high_out[pl.ds(at, 32), tile : tile + LANES] = upper
-            low_out[pl.ds(at, 32), tile : tile + LANES] = lower
+    row = lax.axis_index("row")
+    index = value.astype(jnp.int32)
+    owner = index >> shift_owner
+    inside = index & (per - 1)
+    core = (owner & 1) ^ (row & 1)
+    chip = ((row >> 1) - (owner >> 1)) & (chips - 1)
+    slot = ((core * chips + chip) << shift_owner) + (inside & 1) * rows + (inside >> 1)
+    return slot.astype(F32)
+
+
+def fill_rows(at, cut, rows, high, low):
+    column = lax.broadcasted_iota(jnp.int32, (rows, LANES), 1).astype(F32)
+    cut = [jnp.broadcast_to(value, (rows, LANES)) for value in cut]
+    for tile in range(0, high.shape[1], LANES):
+        here = column + float(tile)
+        total = jnp.where(here == cut[0], cut[STENCILS], 0.0)
+        for n in range(1, STENCILS):
+            total += jnp.where(here == cut[n], cut[STENCILS + n], 0.0)
+        upper, lower = halves(total)
+        high[pl.ds(at, rows), tile : tile + LANES] = upper
+        low[pl.ds(at, rows), tile : tile + LANES] = lower
+
+
+def stencil_kernel(tables, after, high, low):
+    _, rows, _ = tables.shape
+    count_r = high.shape[0] // rows
+    group = 8
 
     @pl.when(in_product())
     def _():
-        places = [place(tables[INDEX + n]) for n in range(STENCILS)]
-        weights = [tables[WEIGHT + n] for n in range(STENCILS)]
-        group = 8
+        values = [slot_of(tables[INDEX + n], rows, high.shape[1]) for n in range(STENCILS)]
+        values += [tables[WEIGHT + n] for n in range(STENCILS)]
 
         def body(step, carry):
             shift = lax.rem(LANES - step * group, LANES)
-            moved = [pltpu.roll(value, shift, 1) for value in places + weights]
+            moved = [pltpu.roll(value, shift, 1) for value in values]
             for k in range(group):
-                cut = [value[:, k : k + 1] for value in moved]
                 at = pl.multiple_of((step * group + k) * rows, rows)
-                fill(at, cut[:STENCILS], cut[STENCILS:], high, low)
+                fill_rows(at, [value[:, k : k + 1] for value in moved], rows, high, low)
             return carry
 
         lax.fori_loop(0, count_r // group, body, 0)
 
+
+def stencil_matrix(tables, count_r, columns, after):
+    rows = tables.shape[1]
+    points = jax.ShapeDtypeStruct((count_r * rows, columns), BF16)
+    return pl.pallas_call(
+        stencil_kernel,
+        in_specs=[VMEM, ANY],
+        out_specs=[VMEM] * 2,
+        out_shape=[points, points],
+        compiler_params=pltpu.CompilerParams(vmem_limit_bytes=16 * MIB),
+        cost_estimate=pl.CostEstimate(flops=15_000_000, bytes_accessed=6 * MIB, transcendentals=0),
+        name="stencil_matrix",
+    )(tables, after)
+
+
+def stencil_edge_kernel(up, down, left, right, after, high, low, square, *, rows, count_r):
+    @pl.when(in_product())
+    def _():
         edges = HALO * rows
         at = 0
         for side in (up, down):
             value = side[edges : edges + rows, 0:LANES]
-            slots = place(value)
+            slots = slot_of(value, rows, high.shape[1])
             for e in range(HALO):
-                cut = [(slots if m < STENCILS else value)[:, HALO * m + e : HALO * m + e + 1] for m in range(2 * STENCILS)]
-                fill(at, cut[:STENCILS], cut[STENCILS:], edge_high, edge_low)
+                cut = [
+                    (slots if m < STENCILS else value)[:, HALO * m + e : HALO * m + e + 1]
+                    for m in range(2 * STENCILS)
+                ]
+                fill_rows(at, cut, rows, high, low)
                 at += rows
         square[...] = jnp.zeros_like(square)
+        part = EXTRA // 2
         for n, side in enumerate((left, right)):
             begin = HALO * count_r
-            square[n * EXTRA : n * EXTRA + EXTRA // 2] = place(side[begin : begin + EXTRA // 2, 0:LANES])
-            square[n * EXTRA + EXTRA // 2 : (n + 1) * EXTRA] = side[begin + EXTRA // 2 : begin + EXTRA, 0:LANES]
+            square[n * EXTRA : n * EXTRA + part] = slot_of(side[begin : begin + part, 0:LANES], rows, high.shape[1])
+            square[n * EXTRA + part : (n + 1) * EXTRA] = side[begin + part : begin + EXTRA, 0:LANES]
         turned = square[...].T
         for n in range(2):
             for e in range(HALO):
@@ -449,24 +470,22 @@
                         turned[begin : begin + rows, n * EXTRA + HALO * m + e : n * EXTRA + HALO * m + e + 1]
                         for m in range(2 * STENCILS)
                     ]
-                    fill(at, cut[:STENCILS], cut[STENCILS:], edge_high, edge_low)
+                    fill_rows(at, cut, rows, high, low)
                     at += rows
 
 
-def stencil_matrix(tables, halos, count_r, columns, after):
-    rows = tables.shape[1]
-    points = jax.ShapeDtypeStruct((count_r * rows, columns), BF16)
-    edges = jax.ShapeDtypeStruct((2 * HALO * (rows + count_r), columns), BF16)
+def stencil_edges(halos, rows, count_r, columns, after):
+    points = jax.ShapeDtypeStruct((2 * HALO * (rows + count_r), columns), BF16)
     return pl.pallas_call(
-        stencil_kernel,
-        in_specs=[*[VMEM] * 5, ANY],
-        out_specs=[VMEM] * 4,
-        out_shape=[points, points, edges, edges],
+        functools.partial(stencil_edge_kernel, rows=rows, count_r=count_r),
+        in_specs=[*[VMEM] * 4, ANY],
+        out_specs=[VMEM] * 2,
+        out_shape=[points, points],
         scratch_shapes=[pltpu.VMEM((LANES, LANES), F32)],
         compiler_params=pltpu.CompilerParams(vmem_limit_bytes=16 * MIB),
-        cost_estimate=pl.CostEstimate(flops=15_000_000, bytes_accessed=6 * MIB, transcendentals=0),
-        name="stencil_matrix",
-    )(tables, *halos, after)
+        cost_estimate=pl.CostEstimate(flops=2_000_000, bytes_accessed=2 * MIB, transcendentals=0),
+        name="stencil_edges",
+    )(*halos, after)
 
 
 def last_kernel(
@@ -625,19 +644,22 @@
     )
     halos = exchange(top, bottom, first, last)
     table = bands(packet, previous, potential, tables, *halos[2:], high, low)
-    one, *edges = first_iteration(packet, previous, potential, tables, halos, high, low, table)
-
+
+    columns = count_row * rows * BAND
     plane = ("sect", "rr")
     half = count_rr // FAR
     start = count_rr - 1
     entries = [count_rr + (k + 1) * half - 1 for k in range(FAR)]
     crossed = [lax.ppermute(table, plane, [(start, entry)]) for entry in entries]
-    *crossed, one = lax.optimization_barrier((*crossed, one))
+    matrix = stencil_matrix(tables, count_r, columns, table)
+    *crossed, matrix = lax.optimization_barrier((*crossed, matrix))
     piece = sum(crossed)
     arrived = []
     for shift in (1, half - 1, 2):
         pairs = [(entry, entry - (half - 1) + (half - 1 + shift) % half) for entry in entries]
         arrived.append(lax.ppermute(piece, plane, pairs))
+    one, *edges = first_iteration(packet, previous, potential, tables, halos, high, low, piece)
+    *arrived, one, edges = lax.optimization_barrier((*arrived, one, edges))
     spread = piece + sum(arrived)
     line = ("sect", "row")
 
@@ -651,15 +673,16 @@
         return lax.ppermute(spread, line, pairs)
 
     rest = [around(1), around(2), around(3)]
+    edge_matrix = stencil_edges(halos, rows, count_r, columns, spread)
+    rest[-1], edge_matrix, edges = lax.optimization_barrier((rest[-1], edge_matrix, edges))
     later = exchange(*edges)
-    matrices = stencil_matrix(tables, halos, count_r, count_row * rows * BAND, spread)
-    *rest, later, matrices = lax.optimization_barrier((*rest, later, matrices))
+    *rest, later = lax.optimization_barrier((*rest, later))
     own = jnp.stack([spread, *rest], axis=0)
     other = lax.ppermute(
         own, line, [(count_row + i, count_row + i + 1 - 2 * (i % CORES)) for i in range(count_row)]
     )
     earlier, latest = last_iteration(
-        one, packet, potential, tables, later, high, low, matrices, (own, other)
+        one, packet, potential, tables, later, high, low, (*matrix, *edge_matrix), (own, other)
     )
     return latest[None], earlier[None]
 

time: 95.2 us -> 95.9 us (level)
  the two profiles are of different devices: /device:TPU:7 before, /device:TPU:59 now
where the time goes in v5:
time: 95.9 us; the launch traced here: 95.3 us
  starting transfers between devices  42.1 us (44%)
  Pallas kernels  34.1 us (36%)
  waiting for transfers between devices  18.1 us (19%)
    pallas_call x1, Pallas kernels, last_iteration(): pl.pallas_call(last_kernel, in_specs=[VMEM, HBM, HBM, *[VMEM] * 13], out_...  16.9 us
    ppermute x4, starting transfers between devices, neighbours(): lax.ppermute(upward, axis, [(i, i + 1) for i in range(count - 1)])  15.3 us
    ppermute x4, waiting for transfers between devices, neighbours(): lax.ppermute(downward, axis, [(i + 1, i) for i in range(count - 1)])  11.8 us
    pallas_call x1, Pallas kernels, first_iteration(): pl.pallas_call(first_kernel, in_specs=[HBM, HBM, HBM, *[VMEM] * 7, ANY],...  9.68 us
    ppermute x3, starting transfers between devices, around(): return lax.ppermute(spread, line, pairs)  8.25 us
    ppermute x4, starting transfers between devices, neighbours(): lax.ppermute(downward, axis, [(i + 1, i) for i in range(count - 1)])  8.25 us
    ppermute x3, starting transfers between devices, local(): arrived.append(lax.ppermute(piece, plane, pairs))  4.88 us
    pallas_call x1, Pallas kernels, stencil_matrix(): pl.pallas_call(stencil_kernel, in_specs=[VMEM, ANY], out_specs=[VMEM] * 2...  4.04 us
  transfers between devices with their start and end apart: 17, of which 6 were waited for; matrix products, arithmetic and copies ran while one was open for 0% of the time, Pallas kernels for 15%

profile of v5, /device:TPU:59, one launch (start us, length us, event | category | flops | bytes accessed | tf_op | source)
XLA Modules:
  0.0 95.3 jit_solution(12106116501066376851)
XLA Ops:
  0.6 2.7 %prepare.1 = (f32[96,512]{1,0:T(8,128)S(1)}, f32[96,512]{1,0:T(8,128)S(1)}, f32[176,512]{1,0:T(8,128)S(1)}, f32[176,512]{1,0:T(8,128)S(1)}, f32[10,32,128]{2,1,0...) custom-call(f32[64,32,512]{2,1,0:T(8,128)} %bitcast.25, f32[64,32,512]{2,1,0:T(8,128)} %bitcast.22, ...), custom_call_target="tpu_custom_call" | custom-call | flops 1000000 | bytes 6291456 | tf_op jit(solution)/shard_map/prepare/pallas_call | solution.py:241
  3.3 4.1 %collective-permute-start = (f32[176,512]{1,0:T(8,128)S(1)}, f32[176,512]{1,0:T(8,128)S(1)}, u32[]{:S(2)}, u32[]{:S(2)}) collective-permute-start(f32[176,512]{1,0:T(8,128)S(1)} %get-tuple-element.47), channel_id=1, source_target_pairs={{0,1},{1,2},{2,3},{3,4},{4,5},{5,6},{6,7},{8,9},{9,10},{10,11},{11... | collective-permute-start | bytes 1081352 | tf_op jit(solution)/shard_map/ppermute | solution.py:616
  7.4 1.9 %collective-permute-start.1 = (f32[176,512]{1,0:T(8,128)S(1)}, f32[176,512]{1,0:T(8,128)S(1)}, u32[]{:S(2)}, u32[]{:S(2)}) collective-permute-start(f32[176,512]{1,0:T(8,128)S(1)} %get-tuple-element.48), channel_id=1, source_target_pairs={{1,0},{2,1},{3,2},{4,3},{5,4},{6,5},{7,6},{9,8},{10,9},{11,10},{12... | collective-permute-start | bytes 1081352 | tf_op jit(solution)/shard_map/ppermute | solution.py:617
  9.4 2.4 %collective-permute-done.left = f32[176,512]{1,0:T(8,128)S(1)} collective-permute-done((f32[176,512]{1,0:T(8,128)S(1)}, f32[176,512]{1,0:T(8,128)S(1)}, u32[]{:S(2)}, u32[]{:S(2)}) %collective-permute-start) | collective-permute-done | bytes 360480 | tf_op jit(solution)/shard_map/ppermute | solution.py:616
  11.8 4.4 %collective-permute-done.1.right = f32[176,512]{1,0:T(8,128)S(1)} collective-permute-done((f32[176,512]{1,0:T(8,128)S(1)}, f32[176,512]{1,0:T(8,128)S(1)}, u32[]{:S(2)}, u32[]{:S(2)}) %collective-permute-start.1) | collective-permute-done | bytes 360480 | tf_op jit(solution)/shard_map/ppermute | solution.py:617
  16.2 0.7 collective-permute-start.3
  16.9 1.3 %collective-permute-start.2 = (f32[128,512]{1,0:T(8,128)S(1)}, f32[128,512]{1,0:T(8,128)S(1)}, u32[]{:S(2)}, u32[]{:S(2)}) collective-permute-start(f32[128,512]{1,0:T(8,128)S(1)} %both_bands.1.after), channel_id=1, source_target_pairs={{56,88},{57,89},{58,90},{59,91},{60,92},{61,93},{62,94},{63,95}} | collective-permute-start | bytes 786440 | tf_op jit(solution)/shard_map/ppermute | solution.py:653
  18.2 2.8 %collective-permute-start.7 = (f32[96,512]{1,0:T(8,128)S(1)}, f32[96,512]{1,0:T(8,128)S(1)}, u32[]{:S(2)}, u32[]{:S(2)}) collective-permute-start(f32[96,512]{1,0:T(8,128)S(1)} %get-tuple-element.55), channel_id=1, source_target_pairs={{0,8},{8,16},{16,24},{24,32},{32,40},{40,48},{48,56},{1,9},{9,17},... | collective-permute-start | bytes 589832 | tf_op jit(solution)/shard_map/ppermute | solution.py:616
  21.0 2.5 %collective-permute-start.8 = (f32[96,512]{1,0:T(8,128)S(1)}, f32[96,512]{1,0:T(8,128)S(1)}, u32[]{:S(2)}, u32[]{:S(2)}) collective-permute-start(f32[96,512]{1,0:T(8,128)S(1)} %get-tuple-element.56), channel_id=1, source_target_pairs={{8,0},{16,8},{24,16},{32,24},{40,32},{48,40},{56,48},{9,1},{17,9},... | collective-permute-start | bytes 589832 | tf_op jit(solution)/shard_map/ppermute | solution.py:617
  23.5 4.0 %stencil_matrix.1 = (bf16[2048,512]{1,0:T(8,128)(2,1)S(1)}, bf16[2048,512]{1,0:T(8,128)(2,1)S(1)}) custom-call(f32[10,32,128]{2,1,0:T(8,128)S(1)} %get-tuple-element.46.tables, f32[128,512]{1,0:T(8,128)S(1)} %both_bands.1.after), custom_call_target="tpu_custom_call" | custom-call | flops 15000000 | bytes 6291456 | tf_op jit(solution)/shard_map/stencil_matrix/pallas_call | solution.py:433
  27.6 0.0 collective-permute-done.3
  27.6 0.0 collective-permute-done.2
  27.6 2.3 %collective-permute-start.6 = (f32[128,512]{1,0:T(8,128)S(1)}, f32[128,512]{1,0:T(8,128)S(1)}, u32[]{:S(2)}, u32[]{:S(2)}) collective-permute-start(f32[128,512]{1,0:T(8,128)S(1)} %add.12.after), channel_id=1, source_target_pairs={{88,72},{120,104},{89,73},{121,105},{90,74},{122,106},{91,75},{123... | collective-permute-start | bytes 786440 | tf_op jit(solution)/shard_map/ppermute | solution.py:660
  29.9 1.3 %collective-permute-start.5 = (f32[128,512]{1,0:T(8,128)S(1)}, f32[128,512]{1,0:T(8,128)S(1)}, u32[]{:S(2)}, u32[]{:S(2)}) collective-permute-start(f32[128,512]{1,0:T(8,128)S(1)} %add.12.after), channel_id=1, source_target_pairs={{88,80},{120,112},{89,81},{121,113},{90,82},{122,114},{91,83},{123... | collective-permute-start | bytes 786440 | tf_op jit(solution)/shard_map/ppermute | solution.py:660
  31.2 1.3 %collective-permute-start.4 = (f32[128,512]{1,0:T(8,128)S(1)}, f32[128,512]{1,0:T(8,128)S(1)}, u32[]{:S(2)}, u32[]{:S(2)}) collective-permute-start(f32[128,512]{1,0:T(8,128)S(1)} %add.12.after), channel_id=1, source_target_pairs={{88,64},{120,96},{89,65},{121,97},{90,66},{122,98},{91,67},{123,99... | collective-permute-start | bytes 786440 | tf_op jit(solution)/shard_map/ppermute | solution.py:660
  32.5 0.0 collective-permute-done.7.up
  32.5 0.0 collective-permute-done.8.down
  32.5 9.7 %first_iteration.1 = (f32[64,32,512]{2,1,0:T(8,128)S(1)}, f32[64,512]{1,0:T(8,128)S(1)}, f32[64,512]{1,0:T(8,128)S(1)}, f32[128,512]{1,0:T(8,128)S(1)}, f32[128,512]{1,0:T(8,128)S(1)}) custom-call(f32[64,32,512]{2,1,0:T(8,128)} %bitcast.27, f32[64,32,512]{2,1,0:T(8,128)} %bitcast.24, f32[64,32,512]{2,1,0:T(8,128)} %bitcast.31, ...), custom_call_target="tpu_custom_call" | custom-call | flops 7000000000 | bytes 20971520 | tf_op jit(solution)/shard_map/first_iteration/pallas_call | solution.py:364
  42.2 0.0 collective-permute-done.6
  42.2 0.0 collective-permute-done.5
  42.3 0.0 collective-permute-done.4
  42.3 0.1 add_add_fusion.after
  42.4 1.9 %collective-permute-start.11 = (f32[128,512]{1,0:T(8,128)S(1)}, f32[128,512]{1,0:T(8,128)S(1)}, u32[]{:S(2)}, u32[]{:S(2)}) collective-permute-start(f32[128,512]{1,0:T(8,128)S(1)} %add_add_fusion.after), channel_id=1, source_target_pairs={{64,70},{65,71},{66,64},{67,65},{68,66},{69,67},{70,68},{71,69},{7... | collective-permute-start | bytes 786440 | tf_op jit(solution)/shard_map/ppermute | solution.py:673
  44.3 4.4 %collective-permute-start.10 = (f32[128,512]{1,0:T(8,128)S(1)}, f32[128,512]{1,0:T(8,128)S(1)}, u32[]{:S(2)}, u32[]{:S(2)}) collective-permute-start(f32[128,512]{1,0:T(8,128)S(1)} %add_add_fusion.after), channel_id=1, source_target_pairs={{64,68},{65,69},{66,70},{67,71},{68,64},{69,65},{70,66},{71,67},{7... | collective-permute-start | bytes 786440 | tf_op jit(solution)/shard_map/ppermute | solution.py:673
  48.7 1.9 %collective-permute-start.9 = (f32[128,512]{1,0:T(8,128)S(1)}, f32[128,512]{1,0:T(8,128)S(1)}, u32[]{:S(2)}, u32[]{:S(2)}) collective-permute-start(f32[128,512]{1,0:T(8,128)S(1)} %add_add_fusion.after), channel_id=1, source_target_pairs={{64,66},{65,67},{66,68},{67,69},{68,70},{69,71},{70,64},{71,65},{7... | collective-permute-start | bytes 786440 | tf_op jit(solution)/shard_map/ppermute | solution.py:673
  50.6 0.8 stencil_edges.1
  51.4 1.0 %collective-permute-done.11 = f32[128,512]{1,0:T(8,128)S(1)} collective-permute-done((f32[128,512]{1,0:T(8,128)S(1)}, f32[128,512]{1,0:T(8,128)S(1)}, u32[]{:S(2)}, u32[]{:S(2)}) %collective-permute-start.11) | collective-permute-done | bytes 262176 | tf_op jit(solution)/shard_map/ppermute | solution.py:673
  52.5 4.0 %collective-permute-start.14 = (f32[128,512]{1,0:T(8,128)S(1)}, f32[128,512]{1,0:T(8,128)S(1)}, u32[]{:S(2)}, u32[]{:S(2)}) collective-permute-start(f32[128,512]{1,0:T(8,128)S(1)} %get-tuple-element.75), channel_id=1, source_target_pairs={{0,1},{1,2},{2,3},{3,4},{4,5},{5,6},{6,7},{8,9},{9,10},{10,11},{11... | collective-permute-start | bytes 786440 | tf_op jit(solution)/shard_map/ppermute | solution.py:616
  56.5 1.9 %collective-permute-start.15 = (f32[128,512]{1,0:T(8,128)S(1)}, f32[128,512]{1,0:T(8,128)S(1)}, u32[]{:S(2)}, u32[]{:S(2)}) collective-permute-start(f32[128,512]{1,0:T(8,128)S(1)} %get-tuple-element.76), channel_id=1, source_target_pairs={{1,0},{2,1},{3,2},{4,3},{5,4},{6,5},{7,6},{9,8},{10,9},{11,10},{12... | collective-permute-start | bytes 786440 | tf_op jit(solution)/shard_map/ppermute | solution.py:617
  58.5 4.3 %collective-permute-start.12 = (f32[64,512]{1,0:T(8,128)S(1)}, f32[64,512]{1,0:T(8,128)S(1)}, u32[]{:S(2)}, u32[]{:S(2)}) collective-permute-start(f32[64,512]{1,0:T(8,128)S(1)} %get-tuple-element.73), channel_id=1, source_target_pairs={{0,8},{8,16},{16,24},{24,32},{32,40},{40,48},{48,56},{1,9},{9,17},... | collective-permute-start | bytes 393224 | tf_op jit(solution)/shard_map/ppermute | solution.py:616
  62.8 0.0 collective-permute-done.10
  62.8 1.9 %collective-permute-start.13 = (f32[64,512]{1,0:T(8,128)S(1)}, f32[64,512]{1,0:T(8,128)S(1)}, u32[]{:S(2)}, u32[]{:S(2)}) collective-permute-start(f32[64,512]{1,0:T(8,128)S(1)} %get-tuple-element.74), channel_id=1, source_target_pairs={{8,0},{16,8},{24,16},{32,24},{40,32},{48,40},{56,48},{9,1},{17,9},... | collective-permute-start | bytes 393224 | tf_op jit(solution)/shard_map/ppermute | solution.py:617
  64.7 0.0 collective-permute-done.9
  64.7 0.5 collective-permute-done.12.up
  65.2 7.4 %collective-permute-done.13.down = f32[64,512]{1,0:T(8,128)S(1)} collective-permute-done((f32[64,512]{1,0:T(8,128)S(1)}, f32[64,512]{1,0:T(8,128)S(1)}, u32[]{:S(2)}, u32[]{:S(2)}) %collective-permute-start.13) | collective-permute-done | bytes 131104 | tf_op jit(solution)/shard_map/ppermute | solution.py:617
  72.7 0.0 collective-permute-done.14.left
  72.7 0.0 collective-permute-done.15.right
  72.7 0.1 pad_maximum_fusion.own_table
  72.7 3.5 %collective-permute-start.16 = (f32[4,128,512]{2,1,0:T(8,128)S(1)}, f32[4,128,512]{2,1,0:T(8,128)S(1)}, u32[]{:S(2)}, u32[]{:S(2)}) collective-permute-start(f32[4,128,512]{2,1,0:T(8,128)S(1)} %pad_maximum_fusion.own_table), channel_id=1, source_target_pairs={{64,65},{65,64},{66,67},{67,66},{68,69},{69,68},{70,71},{71,70},{7... | collective-permute-start | bytes 3145736 | tf_op jit(solution)/shard_map/ppermute | solution.py:681
  76.2 2.3 %collective-permute-done.16.other_table = f32[4,128,512]{2,1,0:T(8,128)S(1)} collective-permute-done((f32[4,128,512]{2,1,0:T(8,128)S(1)}, f32[4,128,512]{2,1,0:T(8,128)S(1)}, u32[]{:S(2)}, u32[]{:S(2)}) %collective-permute-start.16) | collective-permute-done | bytes 1048608 | tf_op jit(solution)/shard_map/ppermute | solution.py:681
  78.5 16.9 %last_iteration.1 = (f32[64,32,512]{2,1,0:T(8,128)}, f32[64,32,512]{2,1,0:T(8,128)}) custom-call(f32[64,32,512]{2,1,0:T(8,128)S(1)} %get-tuple-element.62.one, f32[64,32,512]{2,1,0:T(8,128)} %bitcast.28, f32[64,32,512]{2,1,0:T(8,128)} %bitcast.32, f32[10,32,128]{2,1,0:T(8,128)S(1)} %get-tuple-element.46.tables, f32[64,512]{1,0:T(8,128)S(1)} %collective-permute-done.12.up, ...), custom_call_target="tpu_custom_call" | custom-call | flops 20000000000 | bytes 37748736 | tf_op jit(solution)/shard_map/last_iteration/pallas_call | solution.py:592
  (2 shorter events, 0.1 us)
Async XLA Ops:
  3.3 8.5 %collective-permute-start = (f32[176,512]{1,0:T(8,128)S(1)}, f32[176,512]{1,0:T(8,128)S(1)}, u32[]{:S(2)}, u32[]{:S(2)}) collective-permute-start(f32[176,512]{1,0:T(8,128)S(1)} %get-tuple-element.47), channel_id=1, source_target_pairs={{0,1},{1,2},{2,3},{3,4},{4,5},{5,6},{6,7},{8,9},{9,10},{10,11},{11... | collective-permute-start | bytes 1081352 | tf_op jit(solution)/shard_map/ppermute | solution.py:616
  7.4 8.7 %collective-permute-start.1 = (f32[176,512]{1,0:T(8,128)S(1)}, f32[176,512]{1,0:T(8,128)S(1)}, u32[]{:S(2)}, u32[]{:S(2)}) collective-permute-start(f32[176,512]{1,0:T(8,128)S(1)} %get-tuple-element.48), channel_id=1, source_target_pairs={{1,0},{2,1},{3,2},{4,3},{5,4},{6,5},{7,6},{9,8},{10,9},{11,10},{12... | collective-permute-start | bytes 1081352 | tf_op jit(solution)/shard_map/ppermute | solution.py:617
  16.2 11.3 %collective-permute-start.3 = (f32[128,512]{1,0:T(8,128)S(1)}, f32[128,512]{1,0:T(8,128)S(1)}, u32[]{:S(2)}, u32[]{:S(2)}) collective-permute-start(f32[128,512]{1,0:T(8,128)S(1)} %both_bands.1.after), channel_id=1, source_target_pairs={{56,120},{57,121},{58,122},{59,123},{60,124},{61,125},{62,126},{63... | collective-permute-start | bytes 786440 | tf_op jit(solution)/shard_map/ppermute | solution.py:653
  16.9 10.7 %collective-permute-start.2 = (f32[128,512]{1,0:T(8,128)S(1)}, f32[128,512]{1,0:T(8,128)S(1)}, u32[]{:S(2)}, u32[]{:S(2)}) collective-permute-start(f32[128,512]{1,0:T(8,128)S(1)} %both_bands.1.after), channel_id=1, source_target_pairs={{56,88},{57,89},{58,90},{59,91},{60,92},{61,93},{62,94},{63,95}} | collective-permute-start | bytes 786440 | tf_op jit(solution)/shard_map/ppermute | solution.py:653
  18.2 14.3 %collective-permute-start.7 = (f32[96,512]{1,0:T(8,128)S(1)}, f32[96,512]{1,0:T(8,128)S(1)}, u32[]{:S(2)}, u32[]{:S(2)}) collective-permute-start(f32[96,512]{1,0:T(8,128)S(1)} %get-tuple-element.55), channel_id=1, source_target_pairs={{0,8},{8,16},{16,24},{24,32},{32,40},{40,48},{48,56},{1,9},{9,17},... | collective-permute-start | bytes 589832 | tf_op jit(solution)/shard_map/ppermute | solution.py:616
  21.0 11.5 %collective-permute-start.8 = (f32[96,512]{1,0:T(8,128)S(1)}, f32[96,512]{1,0:T(8,128)S(1)}, u32[]{:S(2)}, u32[]{:S(2)}) collective-permute-start(f32[96,512]{1,0:T(8,128)S(1)} %get-tuple-element.56), channel_id=1, source_target_pairs={{8,0},{16,8},{24,16},{32,24},{40,32},{48,40},{56,48},{9,1},{17,9},... | collective-permute-start | bytes 589832 | tf_op jit(solution)/shard_map/ppermute | solution.py:617
  27.6 14.6 %collective-permute-start.6 = (f32[128,512]{1,0:T(8,128)S(1)}, f32[128,512]{1,0:T(8,128)S(1)}, u32[]{:S(2)}, u32[]{:S(2)}) collective-permute-start(f32[128,512]{1,0:T(8,128)S(1)} %add.12.after), channel_id=1, source_target_pairs={{88,72},{120,104},{89,73},{121,105},{90,74},{122,106},{91,75},{123... | collective-permute-start | bytes 786440 | tf_op jit(solution)/shard_map/ppermute | solution.py:660
  29.9 12.4 %collective-permute-start.5 = (f32[128,512]{1,0:T(8,128)S(1)}, f32[128,512]{1,0:T(8,128)S(1)}, u32[]{:S(2)}, u32[]{:S(2)}) collective-permute-start(f32[128,512]{1,0:T(8,128)S(1)} %add.12.after), channel_id=1, source_target_pairs={{88,80},{120,112},{89,81},{121,113},{90,82},{122,114},{91,83},{123... | collective-permute-start | bytes 786440 | tf_op jit(solution)/shard_map/ppermute | solution.py:660
  31.2 11.0 %collective-permute-start.4 = (f32[128,512]{1,0:T(8,128)S(1)}, f32[128,512]{1,0:T(8,128)S(1)}, u32[]{:S(2)}, u32[]{:S(2)}) collective-permute-start(f32[128,512]{1,0:T(8,128)S(1)} %add.12.after), channel_id=1, source_target_pairs={{88,64},{120,96},{89,65},{121,97},{90,66},{122,98},{91,67},{123,99... | collective-permute-start | bytes 786440 | tf_op jit(solution)/shard_map/ppermute | solution.py:660
  42.4 10.1 %collective-permute-start.11 = (f32[128,512]{1,0:T(8,128)S(1)}, f32[128,512]{1,0:T(8,128)S(1)}, u32[]{:S(2)}, u32[]{:S(2)}) collective-permute-start(f32[128,512]{1,0:T(8,128)S(1)} %add_add_fusion.after), channel_id=1, source_target_pairs={{64,70},{65,71},{66,64},{67,65},{68,66},{69,67},{70,68},{71,69},{7... | collective-permute-start | bytes 786440 | tf_op jit(solution)/shard_map/ppermute | solution.py:673
  44.3 18.5 %collective-permute-start.10 = (f32[128,512]{1,0:T(8,128)S(1)}, f32[128,512]{1,0:T(8,128)S(1)}, u32[]{:S(2)}, u32[]{:S(2)}) collective-permute-start(f32[128,512]{1,0:T(8,128)S(1)} %add_add_fusion.after), channel_id=1, source_target_pairs={{64,68},{65,69},{66,70},{67,71},{68,64},{69,65},{70,66},{71,67},{7... | collective-permute-start | bytes 786440 | tf_op jit(solution)/shard_map/ppermute | solution.py:673
  48.7 16.0 %collective-permute-start.9 = (f32[128,512]{1,0:T(8,128)S(1)}, f32[128,512]{1,0:T(8,128)S(1)}, u32[]{:S(2)}, u32[]{:S(2)}) collective-permute-start(f32[128,512]{1,0:T(8,128)S(1)} %add_add_fusion.after), channel_id=1, source_target_pairs={{64,66},{65,67},{66,68},{67,69},{68,70},{69,71},{70,64},{71,65},{7... | collective-permute-start | bytes 786440 | tf_op jit(solution)/shard_map/ppermute | solution.py:673
  52.5 20.2 %collective-permute-start.14 = (f32[128,512]{1,0:T(8,128)S(1)}, f32[128,512]{1,0:T(8,128)S(1)}, u32[]{:S(2)}, u32[]{:S(2)}) collective-permute-start(f32[128,512]{1,0:T(8,128)S(1)} %get-tuple-element.75), channel_id=1, source_target_pairs={{0,1},{1,2},{2,3},{3,4},{4,5},{5,6},{6,7},{8,9},{9,10},{10,11},{11... | collective-permute-start | bytes 786440 | tf_op jit(solution)/shard_map/ppermute | solution.py:616
  56.5 16.1 %collective-permute-start.15 = (f32[128,512]{1,0:T(8,128)S(1)}, f32[128,512]{1,0:T(8,128)S(1)}, u32[]{:S(2)}, u32[]{:S(2)}) collective-permute-start(f32[128,512]{1,0:T(8,128)S(1)} %get-tuple-element.76), channel_id=1, source_target_pairs={{1,0},{2,1},{3,2},{4,3},{5,4},{6,5},{7,6},{9,8},{10,9},{11,10},{12... | collective-permute-start | bytes 786440 | tf_op jit(solution)/shard_map/ppermute | solution.py:617
  58.5 6.8 %collective-permute-start.12 = (f32[64,512]{1,0:T(8,128)S(1)}, f32[64,512]{1,0:T(8,128)S(1)}, u32[]{:S(2)}, u32[]{:S(2)}) collective-permute-start(f32[64,512]{1,0:T(8,128)S(1)} %get-tuple-element.73), channel_id=1, source_target_pairs={{0,8},{8,16},{16,24},{24,32},{32,40},{40,48},{48,56},{1,9},{9,17},... | collective-permute-start | bytes 393224 | tf_op jit(solution)/shard_map/ppermute | solution.py:616
  62.8 9.9 %collective-permute-start.13 = (f32[64,512]{1,0:T(8,128)S(1)}, f32[64,512]{1,0:T(8,128)S(1)}, u32[]{:S(2)}, u32[]{:S(2)}) collective-permute-start(f32[64,512]{1,0:T(8,128)S(1)} %get-tuple-element.74), channel_id=1, source_target_pairs={{8,0},{16,8},{24,16},{32,24},{40,32},{48,40},{56,48},{9,1},{17,9},... | collective-permute-start | bytes 393224 | tf_op jit(solution)/shard_map/ppermute | solution.py:617
  72.7 5.7 %collective-permute-start.16 = (f32[4,128,512]{2,1,0:T(8,128)S(1)}, f32[4,128,512]{2,1,0:T(8,128)S(1)}, u32[]{:S(2)}, u32[]{:S(2)}) collective-permute-start(f32[4,128,512]{2,1,0:T(8,128)S(1)} %pad_maximum_fusion.own_table), channel_id=1, source_target_pairs={{64,65},{65,64},{66,67},{67,66},{68,69},{69,68},{70,71},{71,70},{7... | collective-permute-start | bytes 3145736 | tf_op jit(solution)/shard_map/ppermute | solution.py:681

commit v6 on v5

--- a/solution.py
+++ b/solution.py
@@ -406,7 +406,7 @@
         low[pl.ds(at, rows), tile : tile + LANES] = lower
 
 
-def stencil_kernel(tables, after, high, low):
+def stencil_kernel(tables, high, low):
     _, rows, _ = tables.shape
     count_r = high.shape[0] // rows
     group = 8
@@ -427,18 +427,18 @@
         lax.fori_loop(0, count_r // group, body, 0)
 
 
-def stencil_matrix(tables, count_r, columns, after):
+def stencil_matrix(tables, count_r, columns):
     rows = tables.shape[1]
     points = jax.ShapeDtypeStruct((count_r * rows, columns), BF16)
     return pl.pallas_call(
         stencil_kernel,
-        in_specs=[VMEM, ANY],
+        in_specs=[VMEM],
         out_specs=[VMEM] * 2,
         out_shape=[points, points],
         compiler_params=pltpu.CompilerParams(vmem_limit_bytes=16 * MIB),
         cost_estimate=pl.CostEstimate(flops=15_000_000, bytes_accessed=6 * MIB, transcendentals=0),
         name="stencil_matrix",
-    )(tables, after)
+    )(tables)
 
 
 def stencil_edge_kernel(up, down, left, right, after, high, low, square, *, rows, count_r):
@@ -618,12 +618,6 @@
     )
 
 
-def exchange(top, bottom, first, last):
-    left, right = neighbours("row", last, first)
-    up, down = neighbours("rr", bottom, top)
-    return up, down, left, right
-
-
 def local(packet, previous, potential, rotation, angular, damping, absorber, stencil_index, stencil_weight):
     packet, previous, potential = packet[0], previous[0], potential[0]
     rotation, angular, damping, absorber = rotation[0], angular[0], damping[0], absorber[0]
@@ -642,24 +636,25 @@
     top, bottom, first, last, tables, high, low = prepare(
         packet, previous, potential, rotation, damping, absorber, stencil_index, stencil_weight, angular
     )
-    halos = exchange(top, bottom, first, last)
-    table = bands(packet, previous, potential, tables, *halos[2:], high, low)
-
     columns = count_row * rows * BAND
+    left, right = neighbours("row", last, first)
+    matrix = stencil_matrix(tables, count_r, columns)
+    left, right, matrix = lax.optimization_barrier((left, right, matrix))
+    table = bands(packet, previous, potential, tables, left, right, high, low)
+    up, down = neighbours("rr", bottom, top)
+
     plane = ("sect", "rr")
     half = count_rr // FAR
     start = count_rr - 1
     entries = [count_rr + (k + 1) * half - 1 for k in range(FAR)]
     crossed = [lax.ppermute(table, plane, [(start, entry)]) for entry in entries]
-    matrix = stencil_matrix(tables, count_r, columns, table)
-    *crossed, matrix = lax.optimization_barrier((*crossed, matrix))
+    *crossed, up, down = lax.optimization_barrier((*crossed, up, down))
+    halos = (up, down, left, right)
     piece = sum(crossed)
     arrived = []
     for shift in (1, half - 1, 2):
         pairs = [(entry, entry - (half - 1) + (half - 1 + shift) % half) for entry in entries]
         arrived.append(lax.ppermute(piece, plane, pairs))
-    one, *edges = first_iteration(packet, previous, potential, tables, halos, high, low, piece)
-    *arrived, one, edges = lax.optimization_barrier((*arrived, one, edges))
     spread = piece + sum(arrived)
     line = ("sect", "row")
 
@@ -673,10 +668,13 @@
         return lax.ppermute(spread, line, pairs)
 
     rest = [around(1), around(2), around(3)]
-    edge_matrix = stencil_edges(halos, rows, count_r, columns, spread)
-    rest[-1], edge_matrix, edges = lax.optimization_barrier((rest[-1], edge_matrix, edges))
-    later = exchange(*edges)
-    *rest, later = lax.optimization_barrier((*rest, later))
+    one, *edges = first_iteration(packet, previous, potential, tables, halos, high, low, spread)
+    edge_matrix = stencil_edges(halos, rows, count_r, columns, one)
+    top, bottom, first, last = edges
+    left, right = neighbours("row", last, first)
+    *rest, edge_matrix, left, right = lax.optimization_barrier((*rest, edge_matrix, left, right))
+    up, down = neighbours("rr", bottom, top)
+    later = (up, down, left, right)
     own = jnp.stack([spread, *rest], axis=0)
     other = lax.ppermute(
         own, line, [(count_row + i, count_row + i + 1 - 2 * (i % CORES)) for i in range(count_row)]

time: 95.9 us -> 108 us (1.13)
  the two profiles are of different devices: /device:TPU:59 before, /device:TPU:26 now
where the time goes in v6:
time: 108 us; the launch traced here: 107 us
  starting transfers between devices  49.4 us (46%)
  Pallas kernels  34.1 us (32%)
  waiting for transfers between devices  22.6 us (21%)
    ppermute x3, starting transfers between devices, around(): return lax.ppermute(spread, line, pairs)  19.1 us
    pallas_call x1, Pallas kernels, last_iteration(): pl.pallas_call(last_kernel, in_specs=[VMEM, HBM, HBM, *[VMEM] * 13], out_...  16.9 us
    ppermute x4, waiting for transfers between devices, neighbours(): lax.ppermute(downward, axis, [(i + 1, i) for i in range(count - 1)])  13 us
    ppermute x4, starting transfers between devices, neighbours(): lax.ppermute(downward, axis, [(i + 1, i) for i in range(count - 1)])  9.74 us
    pallas_call x1, Pallas kernels, first_iteration(): pl.pallas_call(first_kernel, in_specs=[HBM, HBM, HBM, *[VMEM] * 7, ANY],...  9.67 us
    ppermute x4, starting transfers between devices, neighbours(): lax.ppermute(upward, axis, [(i, i + 1) for i in range(count - 1)])  8.07 us
    ppermute x1, starting transfers between devices, local(): lax.ppermute(own, line, [(count_row + i, count_row + i + 1 - 2 * (i % COR...  6.67 us
    ppermute x3, waiting for transfers between devices, local(): arrived.append(lax.ppermute(piece, plane, pairs))  6.17 us
  transfers between devices with their start and end apart: 17, of which 7 were waited for; matrix products, arithmetic and copies ran while one was open for 0% of the time, Pallas kernels for 14%

profile of v6, /device:TPU:26, one launch (start us, length us, event | category | flops | bytes accessed | tf_op | source)
XLA Modules:
  0.0 107.3 jit_solution(16402328271656397629)
XLA Ops:
  0.6 2.7 %prepare.1 = (f32[96,512]{1,0:T(8,128)S(1)}, f32[96,512]{1,0:T(8,128)S(1)}, f32[176,512]{1,0:T(8,128)S(1)}, f32[176,512]{1,0:T(8,128)S(1)}, f32[10,32,128]{2,1,0...) custom-call(f32[64,32,512]{2,1,0:T(8,128)} %bitcast.25, f32[64,32,512]{2,1,0:T(8,128)} %bitcast.22, ...), custom_call_target="tpu_custom_call" | custom-call | flops 1000000 | bytes 6291456 | tf_op jit(solution)/shard_map/prepare/pallas_call | solution.py:241
  3.3 1.8 %collective-permute-start = (f32[176,512]{1,0:T(8,128)S(1)}, f32[176,512]{1,0:T(8,128)S(1)}, u32[]{:S(2)}, u32[]{:S(2)}) collective-permute-start(f32[176,512]{1,0:T(8,128)S(1)} %get-tuple-element.36), channel_id=1, source_target_pairs={{0,1},{1,2},{2,3},{3,4},{4,5},{5,6},{6,7},{8,9},{9,10},{10,11},{11... | collective-permute-start | bytes 1081352 | tf_op jit(solution)/shard_map/ppermute | solution.py:616
  5.1 1.3 %collective-permute-start.1 = (f32[176,512]{1,0:T(8,128)S(1)}, f32[176,512]{1,0:T(8,128)S(1)}, u32[]{:S(2)}, u32[]{:S(2)}) collective-permute-start(f32[176,512]{1,0:T(8,128)S(1)} %get-tuple-element.37), channel_id=1, source_target_pairs={{1,0},{2,1},{3,2},{4,3},{5,4},{6,5},{7,6},{9,8},{10,9},{11,10},{12... | collective-permute-start | bytes 1081352 | tf_op jit(solution)/shard_map/ppermute | solution.py:617
  6.4 4.0 %stencil_matrix.1 = (bf16[2048,512]{1,0:T(8,128)(2,1)S(1)}, bf16[2048,512]{1,0:T(8,128)(2,1)S(1)}) custom-call(f32[10,32,128]{2,1,0:T(8,128)S(1)} %get-tuple-element.35.tables), custom_call_target="tpu_custom_call" | custom-call | flops 15000000 | bytes 6291456 | tf_op jit(solution)/shard_map/stencil_matrix/pallas_call | solution.py:433
  10.4 0.0 collective-permute-done.left
  10.5 0.0 collective-permute-done.1.right
  10.5 0.7 collective-permute-start.3
  11.2 1.3 %collective-permute-start.2 = (f32[128,512]{1,0:T(8,128)S(1)}, f32[128,512]{1,0:T(8,128)S(1)}, u32[]{:S(2)}, u32[]{:S(2)}) collective-permute-start(f32[128,512]{1,0:T(8,128)S(1)} %both_bands.1), channel_id=1, source_target_pairs={{56,88},{57,89},{58,90},{59,91},{60,92},{61,93},{62,94},{63,95}} | collective-permute-start | bytes 786440 | tf_op jit(solution)/shard_map/ppermute | solution.py:650
  12.5 3.1 %collective-permute-start.4 = (f32[96,512]{1,0:T(8,128)S(1)}, f32[96,512]{1,0:T(8,128)S(1)}, u32[]{:S(2)}, u32[]{:S(2)}) collective-permute-start(f32[96,512]{1,0:T(8,128)S(1)} %get-tuple-element.44), channel_id=1, source_target_pairs={{0,8},{8,16},{16,24},{24,32},{32,40},{40,48},{48,56},{1,9},{9,17},... | collective-permute-start | bytes 589832 | tf_op jit(solution)/shard_map/ppermute | solution.py:616
  15.6 2.8 %collective-permute-start.5 = (f32[96,512]{1,0:T(8,128)S(1)}, f32[96,512]{1,0:T(8,128)S(1)}, u32[]{:S(2)}, u32[]{:S(2)}) collective-permute-start(f32[96,512]{1,0:T(8,128)S(1)} %get-tuple-element.45), channel_id=1, source_target_pairs={{8,0},{16,8},{24,16},{32,24},{40,32},{48,40},{56,48},{9,1},{17,9},... | collective-permute-start | bytes 589832 | tf_op jit(solution)/shard_map/ppermute | solution.py:617
  18.4 1.7 %collective-permute-done.4.up = f32[96,512]{1,0:T(8,128)S(1)} collective-permute-done((f32[96,512]{1,0:T(8,128)S(1)}, f32[96,512]{1,0:T(8,128)S(1)}, u32[]{:S(2)}, u32[]{:S(2)}) %collective-permute-start.4) | collective-permute-done | bytes 196640 | tf_op jit(solution)/shard_map/ppermute | solution.py:616
  20.1 6.7 %collective-permute-done.5.down = f32[96,512]{1,0:T(8,128)S(1)} collective-permute-done((f32[96,512]{1,0:T(8,128)S(1)}, f32[96,512]{1,0:T(8,128)S(1)}, u32[]{:S(2)}, u32[]{:S(2)}) %collective-permute-start.5) | collective-permute-done | bytes 196640 | tf_op jit(solution)/shard_map/ppermute | solution.py:617
  26.8 0.0 collective-permute-done.3
  26.8 0.0 collective-permute-done.2
  26.8 1.3 %collective-permute-start.8 = (f32[128,512]{1,0:T(8,128)S(1)}, f32[128,512]{1,0:T(8,128)S(1)}, u32[]{:S(2)}, u32[]{:S(2)}) collective-permute-start(f32[128,512]{1,0:T(8,128)S(1)} %add.12), channel_id=1, source_target_pairs={{88,72},{120,104},{89,73},{121,105},{90,74},{122,106},{91,75},{123... | collective-permute-start | bytes 786440 | tf_op jit(solution)/shard_map/ppermute | solution.py:657
  28.1 1.3 %collective-permute-start.7 = (f32[128,512]{1,0:T(8,128)S(1)}, f32[128,512]{1,0:T(8,128)S(1)}, u32[]{:S(2)}, u32[]{:S(2)}) collective-permute-start(f32[128,512]{1,0:T(8,128)S(1)} %add.12), channel_id=1, source_target_pairs={{88,80},{120,112},{89,81},{121,113},{90,82},{122,114},{91,83},{123... | collective-permute-start | bytes 786440 | tf_op jit(solution)/shard_map/ppermute | solution.py:657
  29.4 1.3 %collective-permute-start.6 = (f32[128,512]{1,0:T(8,128)S(1)}, f32[128,512]{1,0:T(8,128)S(1)}, u32[]{:S(2)}, u32[]{:S(2)}) collective-permute-start(f32[128,512]{1,0:T(8,128)S(1)} %add.12), channel_id=1, source_target_pairs={{88,64},{120,96},{89,65},{121,97},{90,66},{122,98},{91,67},{123,99... | collective-permute-start | bytes 786440 | tf_op jit(solution)/shard_map/ppermute | solution.py:657
  30.8 1.2 %collective-permute-done.8 = f32[128,512]{1,0:T(8,128)S(1)} collective-permute-done((f32[128,512]{1,0:T(8,128)S(1)}, f32[128,512]{1,0:T(8,128)S(1)}, u32[]{:S(2)}, u32[]{:S(2)}) %collective-permute-start.8) | collective-permute-done | bytes 262176 | tf_op jit(solution)/shard_map/ppermute | solution.py:657
  32.0 4.9 %collective-permute-done.7 = f32[128,512]{1,0:T(8,128)S(1)} collective-permute-done((f32[128,512]{1,0:T(8,128)S(1)}, f32[128,512]{1,0:T(8,128)S(1)}, u32[]{:S(2)}, u32[]{:S(2)}) %collective-permute-start.7) | collective-permute-done | bytes 262176 | tf_op jit(solution)/shard_map/ppermute | solution.py:657
  36.9 0.0 collective-permute-done.6
  36.9 0.1 add_add_fusion.after
  37.0 8.6 %collective-permute-start.13 = (f32[128,512]{1,0:T(8,128)S(1)}, f32[128,512]{1,0:T(8,128)S(1)}, u32[]{:S(2)}, u32[]{:S(2)}) collective-permute-start(f32[128,512]{1,0:T(8,128)S(1)} %add_add_fusion.after), channel_id=1, source_target_pairs={{64,70},{65,71},{66,64},{67,65},{68,66},{69,67},{70,68},{71,69},{7... | collective-permute-start | bytes 786440 | tf_op jit(solution)/shard_map/ppermute | solution.py:668
  45.6 7.2 %collective-permute-start.12 = (f32[128,512]{1,0:T(8,128)S(1)}, f32[128,512]{1,0:T(8,128)S(1)}, u32[]{:S(2)}, u32[]{:S(2)}) collective-permute-start(f32[128,512]{1,0:T(8,128)S(1)} %add_add_fusion.after), channel_id=1, source_target_pairs={{64,68},{65,69},{66,70},{67,71},{68,64},{69,65},{70,66},{71,67},{7... | collective-permute-start | bytes 786440 | tf_op jit(solution)/shard_map/ppermute | solution.py:668
  52.8 3.3 %collective-permute-start.11 = (f32[128,512]{1,0:T(8,128)S(1)}, f32[128,512]{1,0:T(8,128)S(1)}, u32[]{:S(2)}, u32[]{:S(2)}) collective-permute-start(f32[128,512]{1,0:T(8,128)S(1)} %add_add_fusion.after), channel_id=1, source_target_pairs={{64,66},{65,67},{66,68},{67,69},{68,70},{69,71},{70,64},{71,65},{7... | collective-permute-start | bytes 786440 | tf_op jit(solution)/shard_map/ppermute | solution.py:668
  56.1 9.7 %first_iteration.1 = (f32[64,32,512]{2,1,0:T(8,128)S(1)}, f32[64,512]{1,0:T(8,128)S(1)}, f32[64,512]{1,0:T(8,128)S(1)}, f32[128,512]{1,0:T(8,128)S(1)}, f32[128,512]{1,0:T(8,128)S(1)}) custom-call(f32[64,32,512]{2,1,0:T(8,128)} %bitcast.27, f32[64,32,512]{2,1,0:T(8,128)} %bitcast.24, f32[64,32,512]{2,1,0:T(8,128)} %bitcast.31, ...), custom_call_target="tpu_custom_call" | custom-call | flops 7000000000 | bytes 20971520 | tf_op jit(solution)/shard_map/first_iteration/pallas_call | solution.py:364
  65.8 1.3 %collective-permute-start.14 = (f32[128,512]{1,0:T(8,128)S(1)}, f32[128,512]{1,0:T(8,128)S(1)}, u32[]{:S(2)}, u32[]{:S(2)}) collective-permute-start(f32[128,512]{1,0:T(8,128)S(1)} %get-tuple-element.55), channel_id=1, source_target_pairs={{0,1},{1,2},{2,3},{3,4},{4,5},{5,6},{6,7},{8,9},{9,10},{10,11},{11... | collective-permute-start | bytes 786440 | tf_op jit(solution)/shard_map/ppermute | solution.py:616
  67.1 1.3 %collective-permute-start.15 = (f32[128,512]{1,0:T(8,128)S(1)}, f32[128,512]{1,0:T(8,128)S(1)}, u32[]{:S(2)}, u32[]{:S(2)}) collective-permute-start(f32[128,512]{1,0:T(8,128)S(1)} %get-tuple-element.56), channel_id=1, source_target_pairs={{1,0},{2,1},{3,2},{4,3},{5,4},{6,5},{7,6},{9,8},{10,9},{11,10},{12... | collective-permute-start | bytes 786440 | tf_op jit(solution)/shard_map/ppermute | solution.py:617
  68.4 0.8 stencil_edges.1
  69.2 0.0 collective-permute-done.13
  69.2 0.0 collective-permute-done.12
  69.2 0.0 collective-permute-done.11
  69.3 0.0 collective-permute-done.14.left
  69.3 1.5 %collective-permute-done.15.right = f32[128,512]{1,0:T(8,128)S(1)} collective-permute-done((f32[128,512]{1,0:T(8,128)S(1)}, f32[128,512]{1,0:T(8,128)S(1)}, u32[]{:S(2)}, u32[]{:S(2)}) %collective-permute-start.15) | collective-permute-done | bytes 262176 | tf_op jit(solution)/shard_map/ppermute | solution.py:617
  70.8 0.1 pad_maximum_fusion.own_table
  70.9 6.7 %collective-permute-start.16 = (f32[4,128,512]{2,1,0:T(8,128)S(1)}, f32[4,128,512]{2,1,0:T(8,128)S(1)}, u32[]{:S(2)}, u32[]{:S(2)}) collective-permute-start(f32[4,128,512]{2,1,0:T(8,128)S(1)} %pad_maximum_fusion.own_table), channel_id=1, source_target_pairs={{64,65},{65,64},{66,67},{67,66},{68,69},{69,68},{70,71},{71,70},{7... | collective-permute-start | bytes 3145736 | tf_op jit(solution)/shard_map/ppermute | solution.py:679
  77.5 1.9 %collective-permute-start.9 = (f32[64,512]{1,0:T(8,128)S(1)}, f32[64,512]{1,0:T(8,128)S(1)}, u32[]{:S(2)}, u32[]{:S(2)}) collective-permute-start(f32[64,512]{1,0:T(8,128)S(1)} %get-tuple-element.51), channel_id=1, source_target_pairs={{0,8},{8,16},{16,24},{24,32},{32,40},{40,48},{48,56},{1,9},{9,17},... | collective-permute-start | bytes 393224 | tf_op jit(solution)/shard_map/ppermute | solution.py:616
  79.5 4.4 %collective-permute-start.10 = (f32[64,512]{1,0:T(8,128)S(1)}, f32[64,512]{1,0:T(8,128)S(1)}, u32[]{:S(2)}, u32[]{:S(2)}) collective-permute-start(f32[64,512]{1,0:T(8,128)S(1)} %get-tuple-element.52), channel_id=1, source_target_pairs={{8,0},{16,8},{24,16},{32,24},{40,32},{48,40},{56,48},{9,1},{17,9},... | collective-permute-start | bytes 393224 | tf_op jit(solution)/shard_map/ppermute | solution.py:617
  83.9 1.7 %collective-permute-done.9.up = f32[64,512]{1,0:T(8,128)S(1)} collective-permute-done((f32[64,512]{1,0:T(8,128)S(1)}, f32[64,512]{1,0:T(8,128)S(1)}, u32[]{:S(2)}, u32[]{:S(2)}) %collective-permute-start.9) | collective-permute-done | bytes 131104 | tf_op jit(solution)/shard_map/ppermute | solution.py:616
  85.6 4.8 %collective-permute-done.10.down = f32[64,512]{1,0:T(8,128)S(1)} collective-permute-done((f32[64,512]{1,0:T(8,128)S(1)}, f32[64,512]{1,0:T(8,128)S(1)}, u32[]{:S(2)}, u32[]{:S(2)}) %collective-permute-start.10) | collective-permute-done | bytes 131104 | tf_op jit(solution)/shard_map/ppermute | solution.py:617
  90.4 0.0 collective-permute-done.16.other_table
  90.4 16.9 %last_iteration.1 = (f32[64,32,512]{2,1,0:T(8,128)}, f32[64,32,512]{2,1,0:T(8,128)}) custom-call(f32[64,32,512]{2,1,0:T(8,128)S(1)} %get-tuple-element.50.after.one, f32[64,32,512]{2,1,0:T(8,128)} %bitcast.28, f32[64,32,512]{2,1,0:T(8,128)} %bitcast.32, f32[10,32,128]{2,1,0:T(8,128)S(1)} %get-tuple-element.35.tables, ...), custom_call_target="tpu_custom_call" | custom-call | flops 20000000000 | bytes 37748736 | tf_op jit(solution)/shard_map/last_iteration/pallas_call | solution.py:592
  (2 shorter events, 0.1 us)
Async XLA Ops:
  3.3 7.1 %collective-permute-start = (f32[176,512]{1,0:T(8,128)S(1)}, f32[176,512]{1,0:T(8,128)S(1)}, u32[]{:S(2)}, u32[]{:S(2)}) collective-permute-start(f32[176,512]{1,0:T(8,128)S(1)} %get-tuple-element.36), channel_id=1, source_target_pairs={{0,1},{1,2},{2,3},{3,4},{4,5},{5,6},{6,7},{8,9},{9,10},{10,11},{11... | collective-permute-start | bytes 1081352 | tf_op jit(solution)/shard_map/ppermute | solution.py:616
  5.1 5.4 %collective-permute-start.1 = (f32[176,512]{1,0:T(8,128)S(1)}, f32[176,512]{1,0:T(8,128)S(1)}, u32[]{:S(2)}, u32[]{:S(2)}) collective-permute-start(f32[176,512]{1,0:T(8,128)S(1)} %get-tuple-element.37), channel_id=1, source_target_pairs={{1,0},{2,1},{3,2},{4,3},{5,4},{6,5},{7,6},{9,8},{10,9},{11,10},{12... | collective-permute-start | bytes 1081352 | tf_op jit(solution)/shard_map/ppermute | solution.py:617
  10.5 16.3 %collective-permute-start.3 = (f32[128,512]{1,0:T(8,128)S(1)}, f32[128,512]{1,0:T(8,128)S(1)}, u32[]{:S(2)}, u32[]{:S(2)}) collective-permute-start(f32[128,512]{1,0:T(8,128)S(1)} %both_bands.1), channel_id=1, source_target_pairs={{56,120},{57,121},{58,122},{59,123},{60,124},{61,125},{62,126},{63... | collective-permute-start | bytes 786440 | tf_op jit(solution)/shard_map/ppermute | solution.py:650
  11.2 15.6 %collective-permute-start.2 = (f32[128,512]{1,0:T(8,128)S(1)}, f32[128,512]{1,0:T(8,128)S(1)}, u32[]{:S(2)}, u32[]{:S(2)}) collective-permute-start(f32[128,512]{1,0:T(8,128)S(1)} %both_bands.1), channel_id=1, source_target_pairs={{56,88},{57,89},{58,90},{59,91},{60,92},{61,93},{62,94},{63,95}} | collective-permute-start | bytes 786440 | tf_op jit(solution)/shard_map/ppermute | solution.py:650
  12.5 7.6 %collective-permute-start.4 = (f32[96,512]{1,0:T(8,128)S(1)}, f32[96,512]{1,0:T(8,128)S(1)}, u32[]{:S(2)}, u32[]{:S(2)}) collective-permute-start(f32[96,512]{1,0:T(8,128)S(1)} %get-tuple-element.44), channel_id=1, source_target_pairs={{0,8},{8,16},{16,24},{24,32},{32,40},{40,48},{48,56},{1,9},{9,17},... | collective-permute-start | bytes 589832 | tf_op jit(solution)/shard_map/ppermute | solution.py:616
  15.6 11.2 %collective-permute-start.5 = (f32[96,512]{1,0:T(8,128)S(1)}, f32[96,512]{1,0:T(8,128)S(1)}, u32[]{:S(2)}, u32[]{:S(2)}) collective-permute-start(f32[96,512]{1,0:T(8,128)S(1)} %get-tuple-element.45), channel_id=1, source_target_pairs={{8,0},{16,8},{24,16},{32,24},{40,32},{48,40},{56,48},{9,1},{17,9},... | collective-permute-start | bytes 589832 | tf_op jit(solution)/shard_map/ppermute | solution.py:617
  26.8 5.2 %collective-permute-start.8 = (f32[128,512]{1,0:T(8,128)S(1)}, f32[128,512]{1,0:T(8,128)S(1)}, u32[]{:S(2)}, u32[]{:S(2)}) collective-permute-start(f32[128,512]{1,0:T(8,128)S(1)} %add.12), channel_id=1, source_target_pairs={{88,72},{120,104},{89,73},{121,105},{90,74},{122,106},{91,75},{123... | collective-permute-start | bytes 786440 | tf_op jit(solution)/shard_map/ppermute | solution.py:657
  28.1 8.8 %collective-permute-start.7 = (f32[128,512]{1,0:T(8,128)S(1)}, f32[128,512]{1,0:T(8,128)S(1)}, u32[]{:S(2)}, u32[]{:S(2)}) collective-permute-start(f32[128,512]{1,0:T(8,128)S(1)} %add.12), channel_id=1, source_target_pairs={{88,80},{120,112},{89,81},{121,113},{90,82},{122,114},{91,83},{123... | collective-permute-start | bytes 786440 | tf_op jit(solution)/shard_map/ppermute | solution.py:657
  29.4 7.5 %collective-permute-start.6 = (f32[128,512]{1,0:T(8,128)S(1)}, f32[128,512]{1,0:T(8,128)S(1)}, u32[]{:S(2)}, u32[]{:S(2)}) collective-permute-start(f32[128,512]{1,0:T(8,128)S(1)} %add.12), channel_id=1, source_target_pairs={{88,64},{120,96},{89,65},{121,97},{90,66},{122,98},{91,67},{123,99... | collective-permute-start | bytes 786440 | tf_op jit(solution)/shard_map/ppermute | solution.py:657
  37.0 32.2 %collective-permute-start.13 = (f32[128,512]{1,0:T(8,128)S(1)}, f32[128,512]{1,0:T(8,128)S(1)}, u32[]{:S(2)}, u32[]{:S(2)}) collective-permute-start(f32[128,512]{1,0:T(8,128)S(1)} %add_add_fusion.after), channel_id=1, source_target_pairs={{64,70},{65,71},{66,64},{67,65},{68,66},{69,67},{70,68},{71,69},{7... | collective-permute-start | bytes 786440 | tf_op jit(solution)/shard_map/ppermute | solution.py:668
  45.6 23.6 %collective-permute-start.12 = (f32[128,512]{1,0:T(8,128)S(1)}, f32[128,512]{1,0:T(8,128)S(1)}, u32[]{:S(2)}, u32[]{:S(2)}) collective-permute-start(f32[128,512]{1,0:T(8,128)S(1)} %add_add_fusion.after), channel_id=1, source_target_pairs={{64,68},{65,69},{66,70},{67,71},{68,64},{69,65},{70,66},{71,67},{7... | collective-permute-start | bytes 786440 | tf_op jit(solution)/shard_map/ppermute | solution.py:668
  52.8 16.4 %collective-permute-start.11 = (f32[128,512]{1,0:T(8,128)S(1)}, f32[128,512]{1,0:T(8,128)S(1)}, u32[]{:S(2)}, u32[]{:S(2)}) collective-permute-start(f32[128,512]{1,0:T(8,128)S(1)} %add_add_fusion.after), channel_id=1, source_target_pairs={{64,66},{65,67},{66,68},{67,69},{68,70},{69,71},{70,64},{71,65},{7... | collective-permute-start | bytes 786440 | tf_op jit(solution)/shard_map/ppermute | solution.py:668
  65.8 3.4 %collective-permute-start.14 = (f32[128,512]{1,0:T(8,128)S(1)}, f32[128,512]{1,0:T(8,128)S(1)}, u32[]{:S(2)}, u32[]{:S(2)}) collective-permute-start(f32[128,512]{1,0:T(8,128)S(1)} %get-tuple-element.55), channel_id=1, source_target_pairs={{0,1},{1,2},{2,3},{3,4},{4,5},{5,6},{6,7},{8,9},{9,10},{10,11},{11... | collective-permute-start | bytes 786440 | tf_op jit(solution)/shard_map/ppermute | solution.py:616
  67.1 3.7 %collective-permute-start.15 = (f32[128,512]{1,0:T(8,128)S(1)}, f32[128,512]{1,0:T(8,128)S(1)}, u32[]{:S(2)}, u32[]{:S(2)}) collective-permute-start(f32[128,512]{1,0:T(8,128)S(1)} %get-tuple-element.56), channel_id=1, source_target_pairs={{1,0},{2,1},{3,2},{4,3},{5,4},{6,5},{7,6},{9,8},{10,9},{11,10},{12... | collective-permute-start | bytes 786440 | tf_op jit(solution)/shard_map/ppermute | solution.py:617
  70.9 19.5 %collective-permute-start.16 = (f32[4,128,512]{2,1,0:T(8,128)S(1)}, f32[4,128,512]{2,1,0:T(8,128)S(1)}, u32[]{:S(2)}, u32[]{:S(2)}) collective-permute-start(f32[4,128,512]{2,1,0:T(8,128)S(1)} %pad_maximum_fusion.own_table), channel_id=1, source_target_pairs={{64,65},{65,64},{66,67},{67,66},{68,69},{69,68},{70,71},{71,70},{7... | collective-permute-start | bytes 3145736 | tf_op jit(solution)/shard_map/ppermute | solution.py:679
  77.5 8.1 %collective-permute-start.9 = (f32[64,512]{1,0:T(8,128)S(1)}, f32[64,512]{1,0:T(8,128)S(1)}, u32[]{:S(2)}, u32[]{:S(2)}) collective-permute-start(f32[64,512]{1,0:T(8,128)S(1)} %get-tuple-element.51), channel_id=1, source_target_pairs={{0,8},{8,16},{16,24},{24,32},{32,40},{40,48},{48,56},{1,9},{9,17},... | collective-permute-start | bytes 393224 | tf_op jit(solution)/shard_map/ppermute | solution.py:616
  79.5 10.9 %collective-permute-start.10 = (f32[64,512]{1,0:T(8,128)S(1)}, f32[64,512]{1,0:T(8,128)S(1)}, u32[]{:S(2)}, u32[]{:S(2)}) collective-permute-start(f32[64,512]{1,0:T(8,128)S(1)} %get-tuple-element.52), channel_id=1, source_target_pairs={{8,0},{16,8},{24,16},{32,24},{40,32},{48,40},{56,48},{9,1},{17,9},... | collective-permute-start | bytes 393224 | tf_op jit(solution)/shard_map/ppermute | solution.py:617

commit v7 on v6

--- a/solution.py
+++ b/solution.py
@@ -274,7 +274,7 @@
     lax.fori_loop(0, count_r, body, 0, unroll=8)
 
 
-def advance(step, chunk, field, sides, previous, potential, tables, high, low, put):
+def advance(step, chunk, field, sides, previous, potential, tables, high, low, put, more=None):
     rows = previous.shape[1]
     width = previous.shape[2]
     here = step * chunk
@@ -285,6 +285,7 @@
     wide = 2 * LANES
     for tile in range(0, width, wide):
         turned = product(split, high[:, tile : tile + wide], low[:, tile : tile + wide])
+        source = None if more is None else more(slice(tile, tile + wide))
         for k in range(chunk):
             rotation = jnp.broadcast_to(0.25 * columns[0][:, k : k + 1], (rows, LANES))
             retained = jnp.broadcast_to(columns[1][:, k : k + 1], (rows, LANES))
@@ -306,7 +307,10 @@
                     + rotation * turned[k * rows : (k + 1) * rows, at - tile : at - tile + LANES]
                     - retained * previous[here + k, :, lanes]
                 )
-                put(here + k, lanes, retained * update)
+                value = retained * update
+                if source is not None:
+                    value += source[k * rows : (k + 1) * rows, at - tile : at - tile + LANES]
+                put(here + k, lanes, value)
 
 
 def first_kernel(
@@ -488,21 +492,69 @@
     )(*halos, after)
 
 
+def split_table(pieces, table):
+    half = pieces.shape[1] // 2
+    for k in range(pieces.shape[0]):
+        for band in range(2):
+            upper, lower = halves(pieces[k, band * half : (band + 1) * half])
+            table[2 * band, k * half : (k + 1) * half] = upper
+            table[2 * band + 1, k * half : (k + 1) * half] = lower
+
+
+def own_source_kernel(one, stencil_high, stencil_low, edge_high, edge_low, own, sum_one, source, edge_source, table):
+    count_r, rows, width = one.shape
+    columns = table.shape[1]
+    size = LAST * rows
+
+    @pl.when(in_product())
+    def _():
+        split_table(own, table)
+
+        def body(n, carry):
+            cut = pl.ds(pl.multiple_of(n * size, size), size)
+            part = pl.ds(n * LAST, LAST)
+            weights = (stencil_high[cut, 0:columns], stencil_low[cut, 0:columns])
+            sum_one[part] = one[part] + product(weights, table[0], table[1]).reshape(LAST, rows, width)
+            source[cut] = product(weights, table[2], table[3])
+            return carry
+
+        lax.fori_loop(0, count_r // LAST, body, 0)
+        edge_source[...] = product((edge_high[:, 0:columns], edge_low[:, 0:columns]), table[0], table[1])
+
+    @pl.when(jnp.logical_not(in_product()))
+    def _():
+        sum_one[...] = one[...]
+
+
+def own_source(one, matrices, own):
+    count_r, rows, width = one.shape
+    points = count_r * rows
+    return pl.pallas_call(
+        own_source_kernel,
+        in_specs=[VMEM] * 6,
+        out_specs=[VMEM] * 3,
+        out_shape=[
+            jax.ShapeDtypeStruct(one.shape, F32),
+            jax.ShapeDtypeStruct((points, width), F32),
+            jax.ShapeDtypeStruct((matrices[2].shape[0], width), F32),
+        ],
+        scratch_shapes=[pltpu.VMEM((4, own.shape[0] * own.shape[1] // 2, width), BF16)],
+        compiler_params=pltpu.CompilerParams(vmem_limit_bytes=16 * MIB),
+        cost_estimate=pl.CostEstimate(flops=7_000_000_000, bytes_accessed=20 * MIB, transcendentals=0),
+        name="own_source",
+    )(one, *matrices, own)
+
+
 def last_kernel(
-    one, packet, potential, tables, up, down, left, right, high, low,
-    split_high, split_low, edge_high, edge_low, own_table, other_table,
-    earlier, latest, field, prev, pot, done, sides, table, source, sems,
+    one, source, edge_source, packet, potential, tables, up, down, left, right, high, low,
+    stencil_high, stencil_low, edge_high, edge_low, other,
+    earlier, latest, field, prev, pot, done, sides, table, ends, sems,
 ):
     count_r, rows, width = packet.shape
     steps = count_r // LAST
+    size = LAST * rows
+    columns = table.shape[1]
     is_product = in_product()
-    quarter = own_table.shape[1]
-    half = quarter // 2
-    chips = own_table.shape[0]
-    size = LAST * rows
-
-    def field_part(n):
-        return field.at[pl.ds(HALO + n * LAST, LAST)]
 
     def part(n):
         return pl.ds(n * LAST, LAST)
@@ -517,7 +569,7 @@
         )
 
     def earliers(n):
-        return pltpu.make_async_copy(field_part(n), earlier.at[part(n)], sems.at[2, n])
+        return pltpu.make_async_copy(field.at[pl.ds(HALO + n * LAST, LAST)], earlier.at[part(n)], sems.at[2, n])
 
     def latests(n):
         return pltpu.make_async_copy(done.at[part(n)], latest.at[part(n)], sems.at[3, n])
@@ -527,34 +579,47 @@
             field[k] = up_value[k * rows : (k + 1) * rows]
             field[HALO + count_r + k] = down_value[k * rows : (k + 1) * rows]
 
+    def put(k, lanes, value):
+        done[k, :, lanes] = value
+
     for n in range(steps):
         for copy in locals_of(n):
             copy.start()
 
     @pl.when(is_product)
     def _():
-        for side, ref in enumerate((own_table, other_table)):
-            for k in range(chips):
-                at = (side * chips + k) * half
-                for band in range(2):
-                    upper, lower = halves(ref[k, band * half : (band + 1) * half])
-                    table[2 * band, at : at + half] = upper
-                    table[2 * band + 1, at : at + half] = lower
-        source[...] = product((edge_high[...], edge_low[...]), table[0], table[1])
+        split_table(other, table)
+        ends[...] = edge_source[...] + product(
+            (edge_high[:, columns : 2 * columns], edge_low[:, columns : 2 * columns]), table[0], table[1]
+        )
         edges = HALO * rows
-        columns = HALO * count_r
-        put_ends(up[...] + source[:edges], down[...] + source[edges : 2 * edges])
+        long = HALO * count_r
+        put_ends(up[...] + ends[:edges], down[...] + ends[edges : 2 * edges])
         put_sides(
-            sides, left, right, count_r,
-            source.at[pl.ds(2 * edges, columns)], source.at[pl.ds(2 * edges + columns, columns)],
+            sides, left, right, count_r, ends.at[pl.ds(2 * edges, long)], ends.at[pl.ds(2 * edges + long, long)]
         )
 
+        def weights(n):
+            return stencil_high[cut(n), columns : 2 * columns], stencil_low[cut(n), columns : 2 * columns]
+
+        def add(n, carry):
+            more = product(weights(n), table[0], table[1]).reshape(LAST, rows, width)
+            field[pl.ds(HALO + n * LAST, LAST)] = one[part(n)] + more
+            earliers(n).start()
+            return carry
+
+        lax.fori_loop(0, steps, add, 0)
+
         def body(n, carry):
-            matrix = (split_high[cut(n)], split_low[cut(n)])
-            here = pl.ds(HALO + n * LAST, LAST)
-            field[here] = one[part(n)] + product(matrix, table[0], table[1]).reshape(LAST, rows, width)
-            done[part(n)] = product(matrix, table[2], table[3]).reshape(LAST, rows, width)
-            earliers(n).start()
+            for copy in locals_of(n):
+                copy.wait()
+            matrix = weights(n)
+
+            def more(lanes):
+                return source[cut(n), lanes] + product(matrix, table[2, :, lanes], table[3, :, lanes])
+
+            advance(n, LAST, field, sides, prev, pot, tables, high, low, put, more)
+            latests(n).start()
             return carry
 
         lax.fori_loop(0, steps, body, 0)
@@ -563,35 +628,30 @@
     def _():
         put_ends(up, down)
         put_sides(sides, left, right, count_r)
-        done[...] = jnp.zeros_like(done)
         for n in range(steps):
-            here = pl.ds(HALO + n * LAST, LAST)
-            field[here] = one[part(n)]
+            field[pl.ds(HALO + n * LAST, LAST)] = one[part(n)]
             earliers(n).start()
 
-    def put(k, lanes, value):
-        done[k, :, lanes] += value
-
-    def body(n, carry):
-        for copy in locals_of(n):
-            copy.wait()
-        advance(n, LAST, field, sides, prev, pot, tables, high, low, put)
-        latests(n).start()
-        return carry
-
-    lax.fori_loop(0, steps, body, 0)
+        def body(n, carry):
+            for copy in locals_of(n):
+                copy.wait()
+            advance(n, LAST, field, sides, prev, pot, tables, high, low, put)
+            latests(n).start()
+            return carry
+
+        lax.fori_loop(0, steps, body, 0)
+
     for n in range(steps):
         earliers(n).wait()
         latests(n).wait()
 
 
-def last_iteration(one, packet, potential, tables, halos, high, low, matrices, band_tables):
+def last_iteration(own_sums, packet, potential, tables, halos, high, low, matrices, other):
     count_r, rows, width = packet.shape
     steps = count_r // LAST
-    columns = matrices[0].shape[1]
     return pl.pallas_call(
         last_kernel,
-        in_specs=[VMEM, HBM, HBM, *[VMEM] * 13],
+        in_specs=[VMEM, VMEM, VMEM, HBM, HBM, *[VMEM] * 12],
         out_specs=[HBM, HBM],
         out_shape=[jax.ShapeDtypeStruct(packet.shape, F32)] * 2,
         scratch_shapes=[
@@ -600,14 +660,14 @@
             pltpu.VMEM(packet.shape, F32),
             pltpu.VMEM(packet.shape, F32),
             pltpu.VMEM((count_r, 8, width), F32),
-            pltpu.VMEM((4, columns, width), BF16),
+            pltpu.VMEM((4, other.shape[0] * other.shape[1] // 2, width), BF16),
             pltpu.VMEM((2 * HALO * (rows + count_r), width), F32),
             pltpu.SemaphoreType.DMA((4, steps)),
         ],
-        compiler_params=pltpu.CompilerParams(vmem_limit_bytes=40 * MIB),
-        cost_estimate=pl.CostEstimate(flops=20_000_000_000, bytes_accessed=36 * MIB, transcendentals=0),
+        compiler_params=pltpu.CompilerParams(vmem_limit_bytes=32 * MIB),
+        cost_estimate=pl.CostEstimate(flops=14_000_000_000, bytes_accessed=36 * MIB, transcendentals=0),
         name="last_iteration",
-    )(one, packet, potential, tables, *halos, high, low, *matrices, *band_tables)
+    )(*own_sums, packet, potential, tables, *halos, high, low, *matrices, other)
 
 
 def neighbours(axis, upward, downward):
@@ -616,6 +676,12 @@
         lax.ppermute(upward, axis, [(i, i + 1) for i in range(count - 1)]),
         lax.ppermute(downward, axis, [(i + 1, i) for i in range(count - 1)]),
     )
+
+
+def exchange(top, bottom, first, last):
+    up, down = neighbours("rr", bottom, top)
+    left, right = neighbours("row", last, first)
+    return up, down, left, right
 
 
 def local(packet, previous, potential, rotation, angular, damping, absorber, stencil_index, stencil_weight):
@@ -648,13 +714,14 @@
     start = count_rr - 1
     entries = [count_rr + (k + 1) * half - 1 for k in range(FAR)]
     crossed = [lax.ppermute(table, plane, [(start, entry)]) for entry in entries]
-    *crossed, up, down = lax.optimization_barrier((*crossed, up, down))
     halos = (up, down, left, right)
     piece = sum(crossed)
     arrived = []
     for shift in (1, half - 1, 2):
         pairs = [(entry, entry - (half - 1) + (half - 1 + shift) % half) for entry in entries]
         arrived.append(lax.ppermute(piece, plane, pairs))
+    one, *edges = first_iteration(packet, previous, potential, tables, halos, high, low, piece)
+    *arrived, one, edges = lax.optimization_barrier((*arrived, one, edges))
     spread = piece + sum(arrived)
     line = ("sect", "row")
 
@@ -667,21 +734,19 @@
                 )
         return lax.ppermute(spread, line, pairs)
 
-    rest = [around(1), around(2), around(3)]
-    one, *edges = first_iteration(packet, previous, potential, tables, halos, high, low, spread)
-    edge_matrix = stencil_edges(halos, rows, count_r, columns, one)
-    top, bottom, first, last = edges
-    left, right = neighbours("row", last, first)
-    *rest, edge_matrix, left, right = lax.optimization_barrier((*rest, edge_matrix, left, right))
-    up, down = neighbours("rr", bottom, top)
-    later = (up, down, left, right)
-    own = jnp.stack([spread, *rest], axis=0)
+    rest = [around(1), around(3), around(2)]
+    edge_matrix = stencil_edges(halos, rows, count_r, columns, spread)
+    rest[1], edge_matrix, edges = lax.optimization_barrier((rest[1], edge_matrix, edges))
+    later = exchange(*edges)
+    *rest, later = lax.optimization_barrier((*rest, later))
+    own = jnp.stack([spread, rest[0], rest[2], rest[1]], axis=0)
     other = lax.ppermute(
         own, line, [(count_row + i, count_row + i + 1 - 2 * (i % CORES)) for i in range(count_row)]
     )
-    earlier, latest = last_iteration(
-        one, packet, potential, tables, later, high, low, (*matrix, *edge_matrix), (own, other)
-    )
+    matrices = (*matrix, *edge_matrix)
+    own_sums = own_source(one, matrices, own)
+    other, own_sums = lax.optimization_barrier((other, own_sums))
+    earlier, latest = last_iteration(own_sums, packet, potential, tables, later, high, low, matrices, other)
     return latest[None], earlier[None]
 
 

time: 108 us -> 91.3 us (0.85)
  the two profiles are of different devices: /device:TPU:26 before, /device:TPU:59 now
where the time goes in v7:
time: 91.3 us; the launch traced here: 90.8 us
  starting transfers between devices  39.9 us (44%)
  Pallas kernels  34.2 us (37%)
  waiting for transfers between devices  15.6 us (17%)
    ppermute x4, starting transfers between devices, neighbours(): lax.ppermute(upward, axis, [(i, i + 1) for i in range(count - 1)])  13.2 us
    pallas_call x1, Pallas kernels, last_iteration(): pl.pallas_call(last_kernel, in_specs=[VMEM, VMEM, VMEM, HBM, HBM, *[VMEM]...  12.4 us
    ppermute x4, starting transfers between devices, neighbours(): lax.ppermute(downward, axis, [(i + 1, i) for i in range(count - 1)])  9.69 us
    pallas_call x1, Pallas kernels, first_iteration(): pl.pallas_call(first_kernel, in_specs=[HBM, HBM, HBM, *[VMEM] * 7, ANY],...  9.69 us
    ppermute x4, waiting for transfers between devices, neighbours(): lax.ppermute(downward, axis, [(i + 1, i) for i in range(count - 1)])  9.22 us
    ppermute x3, starting transfers between devices, around(): return lax.ppermute(spread, line, pairs)  8.56 us
    pallas_call x1, Pallas kernels, own_source(): pl.pallas_call(own_source_kernel, in_specs=[VMEM] * 6, out_specs=[VMEM] *...  4.49 us
    pallas_call x1, Pallas kernels, stencil_matrix(): pl.pallas_call(stencil_kernel, in_specs=[VMEM], out_specs=[VMEM] * 2, out...  4.04 us
  transfers between devices with their start and end apart: 17, of which 6 were waited for; matrix products, arithmetic and copies ran while one was open for 0% of the time, Pallas kernels for 21%

profile of v7, /device:TPU:59, one launch (start us, length us, event | category | flops | bytes accessed | tf_op | source)
XLA Modules:
  0.0 90.8 jit_solution(15727567703330934644)
XLA Ops:
  0.6 2.7 %prepare.1 = (f32[96,512]{1,0:T(8,128)S(1)}, f32[96,512]{1,0:T(8,128)S(1)}, f32[176,512]{1,0:T(8,128)S(1)}, f32[176,512]{1,0:T(8,128)S(1)}, f32[10,32,128]{2,1,0...) custom-call(f32[64,32,512]{2,1,0:T(8,128)} %bitcast.25, f32[64,32,512]{2,1,0:T(8,128)} %bitcast.22, ...), custom_call_target="tpu_custom_call" | custom-call | flops 1000000 | bytes 6291456 | tf_op jit(solution)/shard_map/prepare/pallas_call | solution.py:241
  3.3 4.1 %collective-permute-start = (f32[176,512]{1,0:T(8,128)S(1)}, f32[176,512]{1,0:T(8,128)S(1)}, u32[]{:S(2)}, u32[]{:S(2)}) collective-permute-start(f32[176,512]{1,0:T(8,128)S(1)} %get-tuple-element.54), channel_id=1, source_target_pairs={{0,1},{1,2},{2,3},{3,4},{4,5},{5,6},{6,7},{8,9},{9,10},{10,11},{11... | collective-permute-start | bytes 1081352 | tf_op jit(solution)/shard_map/ppermute | solution.py:676
  7.4 1.9 %collective-permute-start.1 = (f32[176,512]{1,0:T(8,128)S(1)}, f32[176,512]{1,0:T(8,128)S(1)}, u32[]{:S(2)}, u32[]{:S(2)}) collective-permute-start(f32[176,512]{1,0:T(8,128)S(1)} %get-tuple-element.55), channel_id=1, source_target_pairs={{1,0},{2,1},{3,2},{4,3},{5,4},{6,5},{7,6},{9,8},{10,9},{11,10},{12... | collective-permute-start | bytes 1081352 | tf_op jit(solution)/shard_map/ppermute | solution.py:677
  9.4 4.0 %stencil_matrix.1 = (bf16[2048,512]{1,0:T(8,128)(2,1)S(1)}, bf16[2048,512]{1,0:T(8,128)(2,1)S(1)}) custom-call(f32[10,32,128]{2,1,0:T(8,128)S(1)} %get-tuple-element.53.tables), custom_call_target="tpu_custom_call" | custom-call | flops 15000000 | bytes 6291456 | tf_op jit(solution)/shard_map/stencil_matrix/pallas_call | solution.py:437
  13.4 0.0 collective-permute-done.left
  13.4 2.8 %collective-permute-done.1.right = f32[176,512]{1,0:T(8,128)S(1)} collective-permute-done((f32[176,512]{1,0:T(8,128)S(1)}, f32[176,512]{1,0:T(8,128)S(1)}, u32[]{:S(2)}, u32[]{:S(2)}) %collective-permute-start.1) | collective-permute-done | bytes 360480 | tf_op jit(solution)/shard_map/ppermute | solution.py:677
  16.2 0.7 collective-permute-start.3
  16.9 1.3 %collective-permute-start.2 = (f32[128,512]{1,0:T(8,128)S(1)}, f32[128,512]{1,0:T(8,128)S(1)}, u32[]{:S(2)}, u32[]{:S(2)}) collective-permute-start(f32[128,512]{1,0:T(8,128)S(1)} %both_bands.1), channel_id=1, source_target_pairs={{56,88},{57,89},{58,90},{59,91},{60,92},{61,93},{62,94},{63,95}} | collective-permute-start | bytes 786440 | tf_op jit(solution)/shard_map/ppermute | solution.py:716
  18.2 2.8 %collective-permute-start.7 = (f32[96,512]{1,0:T(8,128)S(1)}, f32[96,512]{1,0:T(8,128)S(1)}, u32[]{:S(2)}, u32[]{:S(2)}) collective-permute-start(f32[96,512]{1,0:T(8,128)S(1)} %get-tuple-element.62), channel_id=1, source_target_pairs={{0,8},{8,16},{16,24},{24,32},{32,40},{40,48},{48,56},{1,9},{9,17},... | collective-permute-start | bytes 589832 | tf_op jit(solution)/shard_map/ppermute | solution.py:676
  21.0 2.5 %collective-permute-start.8 = (f32[96,512]{1,0:T(8,128)S(1)}, f32[96,512]{1,0:T(8,128)S(1)}, u32[]{:S(2)}, u32[]{:S(2)}) collective-permute-start(f32[96,512]{1,0:T(8,128)S(1)} %get-tuple-element.63), channel_id=1, source_target_pairs={{8,0},{16,8},{24,16},{32,24},{40,32},{48,40},{56,48},{9,1},{17,9},... | collective-permute-start | bytes 589832 | tf_op jit(solution)/shard_map/ppermute | solution.py:677
  23.5 0.0 collective-permute-done.3
  23.5 3.8 %collective-permute-done.2 = f32[128,512]{1,0:T(8,128)S(1)} collective-permute-done((f32[128,512]{1,0:T(8,128)S(1)}, f32[128,512]{1,0:T(8,128)S(1)}, u32[]{:S(2)}, u32[]{:S(2)}) %collective-permute-start.2) | collective-permute-done | bytes 262176 | tf_op jit(solution)/shard_map/ppermute | solution.py:716
  27.3 1.3 %collective-permute-start.6 = (f32[128,512]{1,0:T(8,128)S(1)}, f32[128,512]{1,0:T(8,128)S(1)}, u32[]{:S(2)}, u32[]{:S(2)}) collective-permute-start(f32[128,512]{1,0:T(8,128)S(1)} %add.12.after), channel_id=1, source_target_pairs={{88,72},{120,104},{89,73},{121,105},{90,74},{122,106},{91,75},{123... | collective-permute-start | bytes 786440 | tf_op jit(solution)/shard_map/ppermute | solution.py:722
  28.7 1.3 %collective-permute-start.5 = (f32[128,512]{1,0:T(8,128)S(1)}, f32[128,512]{1,0:T(8,128)S(1)}, u32[]{:S(2)}, u32[]{:S(2)}) collective-permute-start(f32[128,512]{1,0:T(8,128)S(1)} %add.12.after), channel_id=1, source_target_pairs={{88,80},{120,112},{89,81},{121,113},{90,82},{122,114},{91,83},{123... | collective-permute-start | bytes 786440 | tf_op jit(solution)/shard_map/ppermute | solution.py:722
  30.0 1.3 %collective-permute-start.4 = (f32[128,512]{1,0:T(8,128)S(1)}, f32[128,512]{1,0:T(8,128)S(1)}, u32[]{:S(2)}, u32[]{:S(2)}) collective-permute-start(f32[128,512]{1,0:T(8,128)S(1)} %add.12.after), channel_id=1, source_target_pairs={{88,64},{120,96},{89,65},{121,97},{90,66},{122,98},{91,67},{123,99... | collective-permute-start | bytes 786440 | tf_op jit(solution)/shard_map/ppermute | solution.py:722
  31.3 0.0 collective-permute-done.7.up
  31.3 0.9 %collective-permute-done.8.down = f32[96,512]{1,0:T(8,128)S(1)} collective-permute-done((f32[96,512]{1,0:T(8,128)S(1)}, f32[96,512]{1,0:T(8,128)S(1)}, u32[]{:S(2)}, u32[]{:S(2)}) %collective-permute-start.8) | collective-permute-done | bytes 196640 | tf_op jit(solution)/shard_map/ppermute | solution.py:677
  32.2 9.7 %first_iteration.1 = (f32[64,32,512]{2,1,0:T(8,128)S(1)}, f32[64,512]{1,0:T(8,128)S(1)}, f32[64,512]{1,0:T(8,128)S(1)}, f32[128,512]{1,0:T(8,128)S(1)}, f32[128,512]{1,0:T(8,128)S(1)}) custom-call(f32[64,32,512]{2,1,0:T(8,128)} %bitcast.27, f32[64,32,512]{2,1,0:T(8,128)} %bitcast.24, f32[64,32,512]{2,1,0:T(8,128)} %bitcast.31, ...), custom_call_target="tpu_custom_call" | custom-call | flops 7000000000 | bytes 20971520 | tf_op jit(solution)/shard_map/first_iteration/pallas_call | solution.py:368
  41.9 0.0 collective-permute-done.6
  41.9 0.0 collective-permute-done.5
  41.9 0.0 collective-permute-done.4
  41.9 0.1 add_add_fusion.after
  42.0 1.9 %collective-permute-start.10 = (f32[128,512]{1,0:T(8,128)S(1)}, f32[128,512]{1,0:T(8,128)S(1)}, u32[]{:S(2)}, u32[]{:S(2)}) collective-permute-start(f32[128,512]{1,0:T(8,128)S(1)} %add_add_fusion.after), channel_id=1, source_target_pairs={{64,70},{65,71},{66,64},{67,65},{68,66},{69,67},{70,68},{71,69},{7... | collective-permute-start | bytes 786440 | tf_op jit(solution)/shard_map/ppermute | solution.py:735
  44.0 4.7 %collective-permute-start.11 = (f32[128,512]{1,0:T(8,128)S(1)}, f32[128,512]{1,0:T(8,128)S(1)}, u32[]{:S(2)}, u32[]{:S(2)}) collective-permute-start(f32[128,512]{1,0:T(8,128)S(1)} %add_add_fusion.after), channel_id=1, source_target_pairs={{64,68},{65,69},{66,70},{67,71},{68,64},{69,65},{70,66},{71,67},{7... | collective-permute-start | bytes 786440 | tf_op jit(solution)/shard_map/ppermute | solution.py:735
  48.7 1.9 %collective-permute-start.9 = (f32[128,512]{1,0:T(8,128)S(1)}, f32[128,512]{1,0:T(8,128)S(1)}, u32[]{:S(2)}, u32[]{:S(2)}) collective-permute-start(f32[128,512]{1,0:T(8,128)S(1)} %add_add_fusion.after), channel_id=1, source_target_pairs={{64,66},{65,67},{66,68},{67,69},{68,70},{69,71},{70,64},{71,65},{7... | collective-permute-start | bytes 786440 | tf_op jit(solution)/shard_map/ppermute | solution.py:735
  50.6 0.8 stencil_edges.1
  51.4 0.7 collective-permute-done.10
  52.1 4.4 %collective-permute-start.14 = (f32[128,512]{1,0:T(8,128)S(1)}, f32[128,512]{1,0:T(8,128)S(1)}, u32[]{:S(2)}, u32[]{:S(2)}) collective-permute-start(f32[128,512]{1,0:T(8,128)S(1)} %get-tuple-element.81), channel_id=1, source_target_pairs={{0,1},{1,2},{2,3},{3,4},{4,5},{5,6},{6,7},{8,9},{9,10},{10,11},{11... | collective-permute-start | bytes 786440 | tf_op jit(solution)/shard_map/ppermute | solution.py:676
  56.5 1.9 %collective-permute-start.15 = (f32[128,512]{1,0:T(8,128)S(1)}, f32[128,512]{1,0:T(8,128)S(1)}, u32[]{:S(2)}, u32[]{:S(2)}) collective-permute-start(f32[128,512]{1,0:T(8,128)S(1)} %get-tuple-element.82), channel_id=1, source_target_pairs={{1,0},{2,1},{3,2},{4,3},{5,4},{6,5},{7,6},{9,8},{10,9},{11,10},{12... | collective-permute-start | bytes 786440 | tf_op jit(solution)/shard_map/ppermute | solution.py:677
  58.5 1.9 %collective-permute-start.12 = (f32[64,512]{1,0:T(8,128)S(1)}, f32[64,512]{1,0:T(8,128)S(1)}, u32[]{:S(2)}, u32[]{:S(2)}) collective-permute-start(f32[64,512]{1,0:T(8,128)S(1)} %get-tuple-element.79), channel_id=1, source_target_pairs={{0,8},{8,16},{16,24},{24,32},{32,40},{40,48},{48,56},{1,9},{9,17},... | collective-permute-start | bytes 393224 | tf_op jit(solution)/shard_map/ppermute | solution.py:676
  60.4 0.0 collective-permute-done.11
  60.4 3.4 %collective-permute-start.13 = (f32[64,512]{1,0:T(8,128)S(1)}, f32[64,512]{1,0:T(8,128)S(1)}, u32[]{:S(2)}, u32[]{:S(2)}) collective-permute-start(f32[64,512]{1,0:T(8,128)S(1)} %get-tuple-element.80), channel_id=1, source_target_pairs={{8,0},{16,8},{24,16},{32,24},{40,32},{48,40},{56,48},{9,1},{17,9},... | collective-permute-start | bytes 393224 | tf_op jit(solution)/shard_map/ppermute | solution.py:677
  63.8 0.0 collective-permute-done.9
  63.8 1.8 %collective-permute-done.12.up = f32[64,512]{1,0:T(8,128)S(1)} collective-permute-done((f32[64,512]{1,0:T(8,128)S(1)}, f32[64,512]{1,0:T(8,128)S(1)}, u32[]{:S(2)}, u32[]{:S(2)}) %collective-permute-start.12) | collective-permute-done | bytes 131104 | tf_op jit(solution)/shard_map/ppermute | solution.py:676
  65.6 5.6 %collective-permute-done.13.down = f32[64,512]{1,0:T(8,128)S(1)} collective-permute-done((f32[64,512]{1,0:T(8,128)S(1)}, f32[64,512]{1,0:T(8,128)S(1)}, u32[]{:S(2)}, u32[]{:S(2)}) %collective-permute-start.13) | collective-permute-done | bytes 131104 | tf_op jit(solution)/shard_map/ppermute | solution.py:677
  71.1 0.0 collective-permute-done.14.left
  71.1 0.0 collective-permute-done.15.right
  71.1 0.1 pad_maximum_fusion.own
  71.2 2.6 %collective-permute-start.16 = (f32[4,128,512]{2,1,0:T(8,128)S(1)}, f32[4,128,512]{2,1,0:T(8,128)S(1)}, u32[]{:S(2)}, u32[]{:S(2)}) collective-permute-start(f32[4,128,512]{2,1,0:T(8,128)S(1)} %pad_maximum_fusion.own), channel_id=1, source_target_pairs={{64,65},{65,64},{66,67},{67,66},{68,69},{69,68},{70,71},{71,70},{7... | collective-permute-start | bytes 3145736 | tf_op jit(solution)/shard_map/ppermute | solution.py:743
  73.8 4.5 %own_source.1 = (f32[64,32,512]{2,1,0:T(8,128)S(1)}, f32[2048,512]{1,0:T(8,128)S(1)}, f32[384,512]{1,0:T(8,128)S(1)}) custom-call(f32[64,32,512]{2,1,0:T(8,128)S(1)} %get-tuple-element.86.one, bf16[2048,512]{1,0:T(8,128)(2,1)S(1)} %get-tuple-element.87.stencil_high, bf16[2048,512]{1,0:T(8,128)(2,1)S(1)} %get-tuple-element.88.stencil_low, ...), custom_call_target="tpu_custom_call" | custom-call | flops 7000000000 | bytes 20971520 | tf_op jit(solution)/shard_map/own_source/pallas_call | solution.py:532
  78.3 0.0 collective-permute-done.16.other
  78.3 12.4 %last_iteration.1 = (f32[64,32,512]{2,1,0:T(8,128)}, f32[64,32,512]{2,1,0:T(8,128)}) custom-call(f32[64,32,512]{2,1,0:T(8,128)S(1)} %get-tuple-element.94.one, f32[2048,512]{1,0:T(8,128)S(1)} %get-tuple-element.95.source, f32[384,512]{1,0:T(8,128)S(1)} %get-tuple-element.96.edge_source, f32[64,32,512]{2,1,0:T(8,128)} %bitcast.28, f32[64,32,512]{2,1,0:T(8,128)} %bitcast.32, ...), custom_call_target="tpu_custom_call" | custom-call | flops 14000000000 | bytes 37748736 | tf_op jit(solution)/shard_map/last_iteration/pallas_call | solution.py:652
  (2 shorter events, 0.1 us)
Async XLA Ops:
  3.3 10.1 %collective-permute-start = (f32[176,512]{1,0:T(8,128)S(1)}, f32[176,512]{1,0:T(8,128)S(1)}, u32[]{:S(2)}, u32[]{:S(2)}) collective-permute-start(f32[176,512]{1,0:T(8,128)S(1)} %get-tuple-element.54), channel_id=1, source_target_pairs={{0,1},{1,2},{2,3},{3,4},{4,5},{5,6},{6,7},{8,9},{9,10},{10,11},{11... | collective-permute-start | bytes 1081352 | tf_op jit(solution)/shard_map/ppermute | solution.py:676
  7.4 8.7 %collective-permute-start.1 = (f32[176,512]{1,0:T(8,128)S(1)}, f32[176,512]{1,0:T(8,128)S(1)}, u32[]{:S(2)}, u32[]{:S(2)}) collective-permute-start(f32[176,512]{1,0:T(8,128)S(1)} %get-tuple-element.55), channel_id=1, source_target_pairs={{1,0},{2,1},{3,2},{4,3},{5,4},{6,5},{7,6},{9,8},{10,9},{11,10},{12... | collective-permute-start | bytes 1081352 | tf_op jit(solution)/shard_map/ppermute | solution.py:677
  16.2 7.3 %collective-permute-start.3 = (f32[128,512]{1,0:T(8,128)S(1)}, f32[128,512]{1,0:T(8,128)S(1)}, u32[]{:S(2)}, u32[]{:S(2)}) collective-permute-start(f32[128,512]{1,0:T(8,128)S(1)} %both_bands.1), channel_id=1, source_target_pairs={{56,120},{57,121},{58,122},{59,123},{60,124},{61,125},{62,126},{63... | collective-permute-start | bytes 786440 | tf_op jit(solution)/shard_map/ppermute | solution.py:716
  16.9 10.4 %collective-permute-start.2 = (f32[128,512]{1,0:T(8,128)S(1)}, f32[128,512]{1,0:T(8,128)S(1)}, u32[]{:S(2)}, u32[]{:S(2)}) collective-permute-start(f32[128,512]{1,0:T(8,128)S(1)} %both_bands.1), channel_id=1, source_target_pairs={{56,88},{57,89},{58,90},{59,91},{60,92},{61,93},{62,94},{63,95}} | collective-permute-start | bytes 786440 | tf_op jit(solution)/shard_map/ppermute | solution.py:716
  18.2 13.1 %collective-permute-start.7 = (f32[96,512]{1,0:T(8,128)S(1)}, f32[96,512]{1,0:T(8,128)S(1)}, u32[]{:S(2)}, u32[]{:S(2)}) collective-permute-start(f32[96,512]{1,0:T(8,128)S(1)} %get-tuple-element.62), channel_id=1, source_target_pairs={{0,8},{8,16},{16,24},{24,32},{32,40},{40,48},{48,56},{1,9},{9,17},... | collective-permute-start | bytes 589832 | tf_op jit(solution)/shard_map/ppermute | solution.py:676
  21.0 11.2 %collective-permute-start.8 = (f32[96,512]{1,0:T(8,128)S(1)}, f32[96,512]{1,0:T(8,128)S(1)}, u32[]{:S(2)}, u32[]{:S(2)}) collective-permute-start(f32[96,512]{1,0:T(8,128)S(1)} %get-tuple-element.63), channel_id=1, source_target_pairs={{8,0},{16,8},{24,16},{32,24},{40,32},{48,40},{56,48},{9,1},{17,9},... | collective-permute-start | bytes 589832 | tf_op jit(solution)/shard_map/ppermute | solution.py:677
  27.3 14.6 %collective-permute-start.6 = (f32[128,512]{1,0:T(8,128)S(1)}, f32[128,512]{1,0:T(8,128)S(1)}, u32[]{:S(2)}, u32[]{:S(2)}) collective-permute-start(f32[128,512]{1,0:T(8,128)S(1)} %add.12.after), channel_id=1, source_target_pairs={{88,72},{120,104},{89,73},{121,105},{90,74},{122,106},{91,75},{123... | collective-permute-start | bytes 786440 | tf_op jit(solution)/shard_map/ppermute | solution.py:722
  28.7 13.3 %collective-permute-start.5 = (f32[128,512]{1,0:T(8,128)S(1)}, f32[128,512]{1,0:T(8,128)S(1)}, u32[]{:S(2)}, u32[]{:S(2)}) collective-permute-start(f32[128,512]{1,0:T(8,128)S(1)} %add.12.after), channel_id=1, source_target_pairs={{88,80},{120,112},{89,81},{121,113},{90,82},{122,114},{91,83},{123... | collective-permute-start | bytes 786440 | tf_op jit(solution)/shard_map/ppermute | solution.py:722
  30.0 12.0 %collective-permute-start.4 = (f32[128,512]{1,0:T(8,128)S(1)}, f32[128,512]{1,0:T(8,128)S(1)}, u32[]{:S(2)}, u32[]{:S(2)}) collective-permute-start(f32[128,512]{1,0:T(8,128)S(1)} %add.12.after), channel_id=1, source_target_pairs={{88,64},{120,96},{89,65},{121,97},{90,66},{122,98},{91,67},{123,99... | collective-permute-start | bytes 786440 | tf_op jit(solution)/shard_map/ppermute | solution.py:722
  42.0 10.1 %collective-permute-start.10 = (f32[128,512]{1,0:T(8,128)S(1)}, f32[128,512]{1,0:T(8,128)S(1)}, u32[]{:S(2)}, u32[]{:S(2)}) collective-permute-start(f32[128,512]{1,0:T(8,128)S(1)} %add_add_fusion.after), channel_id=1, source_target_pairs={{64,70},{65,71},{66,64},{67,65},{68,66},{69,67},{70,68},{71,69},{7... | collective-permute-start | bytes 786440 | tf_op jit(solution)/shard_map/ppermute | solution.py:735
  44.0 16.4 %collective-permute-start.11 = (f32[128,512]{1,0:T(8,128)S(1)}, f32[128,512]{1,0:T(8,128)S(1)}, u32[]{:S(2)}, u32[]{:S(2)}) collective-permute-start(f32[128,512]{1,0:T(8,128)S(1)} %add_add_fusion.after), channel_id=1, source_target_pairs={{64,68},{65,69},{66,70},{67,71},{68,64},{69,65},{70,66},{71,67},{7... | collective-permute-start | bytes 786440 | tf_op jit(solution)/shard_map/ppermute | solution.py:735
  48.7 15.1 %collective-permute-start.9 = (f32[128,512]{1,0:T(8,128)S(1)}, f32[128,512]{1,0:T(8,128)S(1)}, u32[]{:S(2)}, u32[]{:S(2)}) collective-permute-start(f32[128,512]{1,0:T(8,128)S(1)} %add_add_fusion.after), channel_id=1, source_target_pairs={{64,66},{65,67},{66,68},{67,69},{68,70},{69,71},{70,64},{71,65},{7... | collective-permute-start | bytes 786440 | tf_op jit(solution)/shard_map/ppermute | solution.py:735
  52.1 19.0 %collective-permute-start.14 = (f32[128,512]{1,0:T(8,128)S(1)}, f32[128,512]{1,0:T(8,128)S(1)}, u32[]{:S(2)}, u32[]{:S(2)}) collective-permute-start(f32[128,512]{1,0:T(8,128)S(1)} %get-tuple-element.81), channel_id=1, source_target_pairs={{0,1},{1,2},{2,3},{3,4},{4,5},{5,6},{6,7},{8,9},{9,10},{10,11},{11... | collective-permute-start | bytes 786440 | tf_op jit(solution)/shard_map/ppermute | solution.py:676
  56.5 14.6 %collective-permute-start.15 = (f32[128,512]{1,0:T(8,128)S(1)}, f32[128,512]{1,0:T(8,128)S(1)}, u32[]{:S(2)}, u32[]{:S(2)}) collective-permute-start(f32[128,512]{1,0:T(8,128)S(1)} %get-tuple-element.82), channel_id=1, source_target_pairs={{1,0},{2,1},{3,2},{4,3},{5,4},{6,5},{7,6},{9,8},{10,9},{11,10},{12... | collective-permute-start | bytes 786440 | tf_op jit(solution)/shard_map/ppermute | solution.py:677
  58.5 7.1 %collective-permute-start.12 = (f32[64,512]{1,0:T(8,128)S(1)}, f32[64,512]{1,0:T(8,128)S(1)}, u32[]{:S(2)}, u32[]{:S(2)}) collective-permute-start(f32[64,512]{1,0:T(8,128)S(1)} %get-tuple-element.79), channel_id=1, source_target_pairs={{0,8},{8,16},{16,24},{24,32},{32,40},{40,48},{48,56},{1,9},{9,17},... | collective-permute-start | bytes 393224 | tf_op jit(solution)/shard_map/ppermute | solution.py:676
  60.4 10.7 %collective-permute-start.13 = (f32[64,512]{1,0:T(8,128)S(1)}, f32[64,512]{1,0:T(8,128)S(1)}, u32[]{:S(2)}, u32[]{:S(2)}) collective-permute-start(f32[64,512]{1,0:T(8,128)S(1)} %get-tuple-element.80), channel_id=1, source_target_pairs={{8,0},{16,8},{24,16},{32,24},{40,32},{48,40},{56,48},{9,1},{17,9},... | collective-permute-start | bytes 393224 | tf_op jit(solution)/shard_map/ppermute | solution.py:677
  71.2 7.1 %collective-permute-start.16 = (f32[4,128,512]{2,1,0:T(8,128)S(1)}, f32[4,128,512]{2,1,0:T(8,128)S(1)}, u32[]{:S(2)}, u32[]{:S(2)}) collective-permute-start(f32[4,128,512]{2,1,0:T(8,128)S(1)} %pad_maximum_fusion.own), channel_id=1, source_target_pairs={{64,65},{65,64},{66,67},{67,66},{68,69},{69,68},{70,71},{71,70},{7... | collective-permute-start | bytes 3145736 | tf_op jit(solution)/shard_map/ppermute | solution.py:743

commit v8 on v7

--- a/solution.py
+++ b/solution.py
@@ -14,7 +14,7 @@
 CHUNK = 16
 LAST = 16
 CORES = 2
-FAR = 2
+PLANES = 2
 ROT, RET, INDEX, WEIGHT, TABLES = 0, 1, 2, 6, 10
 EXTRA = 2 * STENCILS * HALO
 OFBAND = 32
@@ -314,7 +314,7 @@
 
 
 def first_kernel(
-    packet, previous, potential, tables, up, down, left, right, high, low, after,
+    packet, previous, potential, tables, left, right, high, low, after,
     done, top, bottom, first, last, field, prev, pot, sides, sems,
 ):
     count_r, rows, width = packet.shape
@@ -331,9 +331,8 @@
     for n in range(steps):
         for copy in copies(n):
             copy.start()
-    for k in range(HALO):
-        field[k] = up[k * rows : (k + 1) * rows]
-        field[HALO + count_r + k] = down[k * rows : (k + 1) * rows]
+    field[0:HALO] = jnp.zeros((HALO, rows, width), F32)
+    field[HALO + count_r :] = jnp.zeros((HALO, rows, width), F32)
     put_sides(sides, left, right, count_r)
     copies(0)[0].wait()
 
@@ -361,13 +360,13 @@
         bottom[k * rows : (k + 1) * rows] = done[count_r - HALO + k]
 
 
-def first_iteration(packet, previous, potential, tables, halos, high, low, after):
+def first_iteration(packet, previous, potential, tables, left, right, high, low, after):
     count_r, rows, width = packet.shape
     ends = jax.ShapeDtypeStruct((HALO * rows, width), F32)
     sides = jax.ShapeDtypeStruct((HALO * count_r, width), F32)
     return pl.pallas_call(
         first_kernel,
-        in_specs=[HBM, HBM, HBM, *[VMEM] * 7, ANY],
+        in_specs=[HBM, HBM, HBM, *[VMEM] * 5, ANY],
         out_specs=[VMEM] * 5,
         out_shape=[jax.ShapeDtypeStruct(packet.shape, F32), ends, ends, sides, sides],
         scratch_shapes=[
@@ -380,7 +379,7 @@
         compiler_params=pltpu.CompilerParams(vmem_limit_bytes=28 * MIB),
         cost_estimate=pl.CostEstimate(flops=7_000_000_000, bytes_accessed=20 * MIB, transcendentals=0),
         name="first_iteration",
-    )(packet, previous, potential, tables, *halos, high, low, after)
+    )(packet, previous, potential, tables, left, right, high, low, after)
 
 
 def slot_of(value, rows, width):
@@ -397,11 +396,11 @@
     return slot.astype(F32)
 
 
-def fill_rows(at, cut, rows, high, low):
+def fill_rows(at, cut, rows, high, low, begin=0):
     column = lax.broadcasted_iota(jnp.int32, (rows, LANES), 1).astype(F32)
     cut = [jnp.broadcast_to(value, (rows, LANES)) for value in cut]
     for tile in range(0, high.shape[1], LANES):
-        here = column + float(tile)
+        here = column + float(begin + tile)
         total = jnp.where(here == cut[0], cut[STENCILS], 0.0)
         for n in range(1, STENCILS):
             total += jnp.where(here == cut[n], cut[STENCILS + n], 0.0)
@@ -410,14 +409,15 @@
         low[pl.ds(at, rows), tile : tile + LANES] = lower
 
 
-def stencil_kernel(tables, high, low):
+def stencil_kernel(tables, after, high, low, *, side):
     _, rows, _ = tables.shape
     count_r = high.shape[0] // rows
     group = 8
+    half = high.shape[1]
 
     @pl.when(in_product())
     def _():
-        values = [slot_of(tables[INDEX + n], rows, high.shape[1]) for n in range(STENCILS)]
+        values = [slot_of(tables[INDEX + n], rows, CORES * half) for n in range(STENCILS)]
         values += [tables[WEIGHT + n] for n in range(STENCILS)]
 
         def body(step, carry):
@@ -425,30 +425,54 @@
             moved = [pltpu.roll(value, shift, 1) for value in values]
             for k in range(group):
                 at = pl.multiple_of((step * group + k) * rows, rows)
-                fill_rows(at, [value[:, k : k + 1] for value in moved], rows, high, low)
+                fill_rows(at, [value[:, k : k + 1] for value in moved], rows, high, low, side * half)
             return carry
 
         lax.fori_loop(0, count_r // group, body, 0)
 
 
-def stencil_matrix(tables, count_r, columns):
+def stencil_matrix(tables, count_r, columns, side, after):
     rows = tables.shape[1]
-    points = jax.ShapeDtypeStruct((count_r * rows, columns), BF16)
+    points = jax.ShapeDtypeStruct((count_r * rows, columns // CORES), BF16)
     return pl.pallas_call(
-        stencil_kernel,
-        in_specs=[VMEM],
+        functools.partial(stencil_kernel, side=side),
+        in_specs=[VMEM, ANY],
         out_specs=[VMEM] * 2,
         out_shape=[points, points],
         compiler_params=pltpu.CompilerParams(vmem_limit_bytes=16 * MIB),
-        cost_estimate=pl.CostEstimate(flops=15_000_000, bytes_accessed=6 * MIB, transcendentals=0),
+        cost_estimate=pl.CostEstimate(flops=8_000_000, bytes_accessed=6 * MIB, transcendentals=0),
         name="stencil_matrix",
-    )(tables)
-
-
-def stencil_edge_kernel(up, down, left, right, after, high, low, square, *, rows, count_r):
+    )(tables, after)
+
+
+def edge_kernel(
+    up, down, left, right, tables, top, bottom, first, last, after,
+    high, low, new_top, new_bottom, new_first, new_last, added, square, *, rows, count_r,
+):
+    width = up.shape[1]
+    edges = HALO * rows
+
+    def retained(k):
+        return jnp.broadcast_to(tables[RET, :, k : k + 1], (rows, width))
+
+    added[0] = retained(0) * (SIDE1 * up[rows:edges] + SIDE2 * up[0:rows])
+    added[1] = retained(1) * (SIDE2 * up[rows:edges])
+    added[2] = retained(count_r - 2) * (SIDE2 * down[0:rows])
+    added[3] = retained(count_r - 1) * (SIDE1 * down[0:rows] + SIDE2 * down[rows:edges])
+    new_first[...] = first[...]
+    new_last[...] = last[...]
+    for k in range(HALO):
+        here = slice(k * rows, (k + 1) * rows)
+        new_top[here] = top[here] + added[k]
+        new_bottom[here] = bottom[here] + added[HALO + k]
+        for n, r_row in ((k, k), (HALO + k, count_r - HALO + k)):
+            for r in range(HALO):
+                at = r * count_r + r_row
+                new_first[at : at + 1] = first[at : at + 1] + added[n, r : r + 1]
+                new_last[at : at + 1] = last[at : at + 1] + added[n, rows - HALO + r : rows - HALO + r + 1]
+
     @pl.when(in_product())
     def _():
-        edges = HALO * rows
         at = 0
         for side in (up, down):
             value = side[edges : edges + rows, 0:LANES]
@@ -478,18 +502,23 @@
                     at += rows
 
 
-def stencil_edges(halos, rows, count_r, columns, after):
+def finish_edges(halos, tables, edges, rows, count_r, columns, after):
     points = jax.ShapeDtypeStruct((2 * HALO * (rows + count_r), columns), BF16)
+    width = edges[0].shape[1]
     return pl.pallas_call(
-        functools.partial(stencil_edge_kernel, rows=rows, count_r=count_r),
-        in_specs=[*[VMEM] * 4, ANY],
-        out_specs=[VMEM] * 2,
-        out_shape=[points, points],
+        functools.partial(edge_kernel, rows=rows, count_r=count_r),
+        in_specs=[*[VMEM] * 9, ANY],
+        out_specs=[VMEM] * 7,
+        out_shape=[
+            points, points,
+            *[jax.ShapeDtypeStruct(edge.shape, F32) for edge in edges],
+            jax.ShapeDtypeStruct((2 * HALO, rows, width), F32),
+        ],
         scratch_shapes=[pltpu.VMEM((LANES, LANES), F32)],
         compiler_params=pltpu.CompilerParams(vmem_limit_bytes=16 * MIB),
-        cost_estimate=pl.CostEstimate(flops=2_000_000, bytes_accessed=2 * MIB, transcendentals=0),
-        name="stencil_edges",
-    )(*halos, after)
+        cost_estimate=pl.CostEstimate(flops=2_000_000, bytes_accessed=3 * MIB, transcendentals=0),
+        name="finish_edges",
+    )(*halos, tables, *edges, after)
 
 
 def split_table(pieces, table):
@@ -501,7 +530,9 @@
             table[2 * band + 1, k * half : (k + 1) * half] = lower
 
 
-def own_source_kernel(one, stencil_high, stencil_low, edge_high, edge_low, own, sum_one, source, edge_source, table):
+def own_source_kernel(
+    one, added, stencil_high, stencil_low, edge_high, edge_low, own, sum_one, source, edge_source, table
+):
     count_r, rows, width = one.shape
     columns = table.shape[1]
     size = LAST * rows
@@ -513,7 +544,7 @@
         def body(n, carry):
             cut = pl.ds(pl.multiple_of(n * size, size), size)
             part = pl.ds(n * LAST, LAST)
-            weights = (stencil_high[cut, 0:columns], stencil_low[cut, 0:columns])
+            weights = (stencil_high[cut], stencil_low[cut])
             sum_one[part] = one[part] + product(weights, table[0], table[1]).reshape(LAST, rows, width)
             source[cut] = product(weights, table[2], table[3])
             return carry
@@ -525,13 +556,17 @@
     def _():
         sum_one[...] = one[...]
 
-
-def own_source(one, matrices, own):
+    for k in range(HALO):
+        sum_one[k] += added[k]
+        sum_one[count_r - HALO + k] += added[HALO + k]
+
+
+def own_source(one, added, matrices, own):
     count_r, rows, width = one.shape
     points = count_r * rows
     return pl.pallas_call(
         own_source_kernel,
-        in_specs=[VMEM] * 6,
+        in_specs=[VMEM] * 7,
         out_specs=[VMEM] * 3,
         out_shape=[
             jax.ShapeDtypeStruct(one.shape, F32),
@@ -542,7 +577,7 @@
         compiler_params=pltpu.CompilerParams(vmem_limit_bytes=16 * MIB),
         cost_estimate=pl.CostEstimate(flops=7_000_000_000, bytes_accessed=20 * MIB, transcendentals=0),
         name="own_source",
-    )(one, *matrices, own)
+    )(one, added, *matrices, own)
 
 
 def last_kernel(
@@ -600,7 +635,7 @@
         )
 
         def weights(n):
-            return stencil_high[cut(n), columns : 2 * columns], stencil_low[cut(n), columns : 2 * columns]
+            return stencil_high[cut(n)], stencil_low[cut(n)]
 
         def add(n, carry):
             more = product(weights(n), table[0], table[1]).reshape(LAST, rows, width)
@@ -678,12 +713,6 @@
     )
 
 
-def exchange(top, bottom, first, last):
-    up, down = neighbours("rr", bottom, top)
-    left, right = neighbours("row", last, first)
-    return up, down, left, right
-
-
 def local(packet, previous, potential, rotation, angular, damping, absorber, stencil_index, stencil_weight):
     packet, previous, potential = packet[0], previous[0], potential[0]
     rotation, angular, damping, absorber = rotation[0], angular[0], damping[0], absorber[0]
@@ -704,24 +733,28 @@
     )
     columns = count_row * rows * BAND
     left, right = neighbours("row", last, first)
-    matrix = stencil_matrix(tables, count_r, columns)
-    left, right, matrix = lax.optimization_barrier((left, right, matrix))
+    own_matrix = stencil_matrix(tables, count_r, columns, 0, first)
+    left, right, own_matrix = lax.optimization_barrier((left, right, own_matrix))
     table = bands(packet, previous, potential, tables, left, right, high, low)
+
+    half = count_rr // PLANES
+    start = count_rr - 1
+    plane = ("sect", "rr")
+    low_side, high_side = start - half + 1, start - 1
+    relays = [low_side, high_side, count_rr + half - 1, count_rr + start]
+    crossed = [lax.ppermute(table, plane, [(start, relay)]) for relay in relays]
+    one, *edges = first_iteration(packet, previous, potential, tables, left, right, high, low, table)
+    *crossed, one, edges = lax.optimization_barrier((*crossed, one, edges))
+    piece = sum(crossed)
+    near = [(low_side, count_rr), (high_side, count_rr + half - 2)]
+    near += [(count_rr + half - 1, count_rr + half - 3), (count_rr + start, count_rr + start - 2)]
+    opposite = [(low_side, count_rr + low_side), (high_side, count_rr + high_side)]
+    arrived = [lax.ppermute(piece, plane, near), lax.ppermute(piece, plane, opposite)]
+    top, bottom, piece = lax.optimization_barrier((top, bottom, piece))
     up, down = neighbours("rr", bottom, top)
-
-    plane = ("sect", "rr")
-    half = count_rr // FAR
-    start = count_rr - 1
-    entries = [count_rr + (k + 1) * half - 1 for k in range(FAR)]
-    crossed = [lax.ppermute(table, plane, [(start, entry)]) for entry in entries]
+    other_matrix = stencil_matrix(tables, count_r, columns, 1, piece)
+    *arrived, other_matrix, up, down = lax.optimization_barrier((*arrived, other_matrix, up, down))
     halos = (up, down, left, right)
-    piece = sum(crossed)
-    arrived = []
-    for shift in (1, half - 1, 2):
-        pairs = [(entry, entry - (half - 1) + (half - 1 + shift) % half) for entry in entries]
-        arrived.append(lax.ppermute(piece, plane, pairs))
-    one, *edges = first_iteration(packet, previous, potential, tables, halos, high, low, piece)
-    *arrived, one, edges = lax.optimization_barrier((*arrived, one, edges))
     spread = piece + sum(arrived)
     line = ("sect", "row")
 
@@ -735,18 +768,21 @@
         return lax.ppermute(spread, line, pairs)
 
     rest = [around(1), around(3), around(2)]
-    edge_matrix = stencil_edges(halos, rows, count_r, columns, spread)
-    rest[1], edge_matrix, edges = lax.optimization_barrier((rest[1], edge_matrix, edges))
-    later = exchange(*edges)
-    *rest, later = lax.optimization_barrier((*rest, later))
+    *edge_matrix, top, bottom, first, last, added = finish_edges(halos, tables, edges, rows, count_r, columns, spread)
+    rest[0], edge_matrix, top, bottom = lax.optimization_barrier((rest[0], edge_matrix, top, bottom))
+    up, down = neighbours("rr", bottom, top)
+    rest[0], rest[1], first, last = lax.optimization_barrier((rest[0], rest[1], first, last))
+    left, right = neighbours("row", last, first)
+    *rest, up, down, left, right = lax.optimization_barrier((*rest, up, down, left, right))
     own = jnp.stack([spread, rest[0], rest[2], rest[1]], axis=0)
     other = lax.ppermute(
         own, line, [(count_row + i, count_row + i + 1 - 2 * (i % CORES)) for i in range(count_row)]
     )
-    matrices = (*matrix, *edge_matrix)
-    own_sums = own_source(one, matrices, own)
+    own_sums = own_source(one, added, (*own_matrix, *edge_matrix), own)
     other, own_sums = lax.optimization_barrier((other, own_sums))
-    earlier, latest = last_iteration(own_sums, packet, potential, tables, later, high, low, matrices, other)
+    earlier, latest = last_iteration(
+        own_sums, packet, potential, tables, (up, down, left, right), high, low, (*other_matrix, *edge_matrix), other
+    )
     return latest[None], earlier[None]
 
 

time: 91.3 us -> 103 us (1.13)
  starting transfers between devices: 39.9 us -> 46.8 us
  Pallas kernels: 34.2 us -> 37.2 us
  waiting for transfers between devices: 15.6 us -> 17.2 us
    ppermute x4, waiting for transfers between devices: 9.22 us -> 13.2 us  [neighbours(): lax.ppermute(downward, axis, [(i + 1, i) for i in range(count - 1)])]
    ppermute x5 -> x6, waiting for transfers between devices: 3.79 us -> 0.02 us  [the longest x4 0.01 us: local(): crossed = [lax.ppermute(table, plane, [(start, relay)]) for relay in relays]]
    pallas_call x4 -> x5, Pallas kernels: 19 us -> 22 us  [the longest x1 9.68 us: first_iteration(): pl.pallas_call(first_kernel, in_specs=[HBM, HBM, HBM, *[VMEM] * 5, ANY],...]
    ppermute x3, waiting for transfers between devices: 0.75 us -> 3.59 us  [around(): return lax.ppermute(spread, line, pairs)]
    ppermute x4, starting transfers between devices: 13.2 us -> 15.8 us  [neighbours(): lax.ppermute(upward, axis, [(i, i + 1) for i in range(count - 1)])]
    ppermute x1, starting transfers between devices: 2.59 us -> 4.79 us  [local(): lax.ppermute(own, line, [(count_row + i, count_row + i + 1 - 2 * (i % COR...]
    ppermute x4, starting transfers between devices: 9.69 us -> 11.4 us  [neighbours(): lax.ppermute(downward, axis, [(i + 1, i) for i in range(count - 1)])]
    ppermute x4, waiting for transfers between devices: 1.81 us -> 0.41 us  [neighbours(): lax.ppermute(upward, axis, [(i, i + 1) for i in range(count - 1)])]
  transfers between devices with their start and end apart: 17 -> 18, of which waited for: 6 -> 6; matrix products, arithmetic and copies ran while one was open for 0% -> 0% of each run, Pallas kernels for 21% -> 22%
where the time goes in v8:
time: 103 us; the launch traced here: 102 us
  starting transfers between devices  46.8 us (45%)
  Pallas kernels  37.2 us (36%)
  waiting for transfers between devices  17.2 us (17%)
    ppermute x4, starting transfers between devices, neighbours(): lax.ppermute(upward, axis, [(i, i + 1) for i in range(count - 1)])  15.8 us
    ppermute x4, waiting for transfers between devices, neighbours(): lax.ppermute(downward, axis, [(i + 1, i) for i in range(count - 1)])  13.2 us
    pallas_call x1, Pallas kernels, last_iteration(): pl.pallas_call(last_kernel, in_specs=[VMEM, VMEM, VMEM, HBM, HBM, *[VMEM]...  12.4 us
    ppermute x4, starting transfers between devices, neighbours(): lax.ppermute(downward, axis, [(i + 1, i) for i in range(count - 1)])  11.4 us
    pallas_call x1, Pallas kernels, first_iteration(): pl.pallas_call(first_kernel, in_specs=[HBM, HBM, HBM, *[VMEM] * 5, ANY],...  9.68 us
    ppermute x3, starting transfers between devices, around(): return lax.ppermute(spread, line, pairs)  8.58 us
    pallas_call x2, Pallas kernels, stencil_matrix(): pl.pallas_call(functools.partial(stencil_kernel, side=side), in_specs=[VM...  6.94 us
    ppermute x1, starting transfers between devices, local(): lax.ppermute(own, line, [(count_row + i, count_row + i + 1 - 2 * (i % COR...  4.79 us
  transfers between devices with their start and end apart: 18, of which 6 were waited for; matrix products, arithmetic and copies ran while one was open for 0% of the time, Pallas kernels for 22%

profile of v8, /device:TPU:59, one launch (start us, length us, event | category | flops | bytes accessed | tf_op | source)
XLA Modules:
  0.0 102.3 jit_solution(2485473360522378621)
XLA Ops:
  0.6 2.7 %prepare.1 = (f32[96,512]{1,0:T(8,128)S(1)}, f32[96,512]{1,0:T(8,128)S(1)}, f32[176,512]{1,0:T(8,128)S(1)}, f32[176,512]{1,0:T(8,128)S(1)}, f32[10,32,128]{2,1,0...) custom-call(f32[64,32,512]{2,1,0:T(8,128)} %bitcast.25, f32[64,32,512]{2,1,0:T(8,128)} %bitcast.22, ...), custom_call_target="tpu_custom_call" | custom-call | flops 1000000 | bytes 6291456 | tf_op jit(solution)/shard_map/prepare/pallas_call | solution.py:241
  3.3 4.1 %collective-permute-start = (f32[176,512]{1,0:T(8,128)S(1)}, f32[176,512]{1,0:T(8,128)S(1)}, u32[]{:S(2)}, u32[]{:S(2)}) collective-permute-start(f32[176,512]{1,0:T(8,128)S(1)} %get-tuple-element.75), channel_id=1, source_target_pairs={{0,1},{1,2},{2,3},{3,4},{4,5},{5,6},{6,7},{8,9},{9,10},{10,11},{11... | collective-permute-start | bytes 1081352 | tf_op jit(solution)/shard_map/ppermute | solution.py:711
  7.4 1.9 %collective-permute-start.1 = (f32[176,512]{1,0:T(8,128)S(1)}, f32[176,512]{1,0:T(8,128)S(1)}, u32[]{:S(2)}, u32[]{:S(2)}) collective-permute-start(f32[176,512]{1,0:T(8,128)S(1)} %get-tuple-element.76.after), channel_id=1, source_target_pairs={{1,0},{2,1},{3,2},{4,3},{5,4},{6,5},{7,6},{9,8},{10,9},{11,10},{12... | collective-permute-start | bytes 1081352 | tf_op jit(solution)/shard_map/ppermute | solution.py:712
  9.4 3.5 %stencil_matrix.2 = (bf16[2048,256]{1,0:T(8,128)(2,1)S(1)}, bf16[2048,256]{1,0:T(8,128)(2,1)S(1)}) custom-call(f32[10,32,128]{2,1,0:T(8,128)S(1)} %get-tuple-element.74.tables, f32[176,512]{1,0:T(8,128)S(1)} %get-tuple-element.76.after), custom_call_target="tpu_custom_call" | custom-call | flops 8000000 | bytes 6291456 | tf_op jit(solution)/shard_map/stencil_matrix/pallas_call | solution.py:437
  12.9 0.0 collective-permute-done.left
  12.9 3.3 %collective-permute-done.1.right = f32[176,512]{1,0:T(8,128)S(1)} collective-permute-done((f32[176,512]{1,0:T(8,128)S(1)}, f32[176,512]{1,0:T(8,128)S(1)}, u32[]{:S(2)}, u32[]{:S(2)}) %collective-permute-start.1) | collective-permute-done | bytes 360480 | tf_op jit(solution)/shard_map/ppermute | solution.py:712
  16.2 0.7 collective-permute-start.5
  16.9 1.3 %collective-permute-start.4 = (f32[128,512]{1,0:T(8,128)S(1)}, f32[128,512]{1,0:T(8,128)S(1)}, u32[]{:S(2)}, u32[]{:S(2)}) collective-permute-start(f32[128,512]{1,0:T(8,128)S(1)} %both_bands.1.after), channel_id=1, source_target_pairs={{56,88},{57,89},{58,90},{59,91},{60,92},{61,93},{62,94},{63,95}} | collective-permute-start | bytes 786440 | tf_op jit(solution)/shard_map/ppermute | solution.py:745
  18.2 0.7 collective-permute-start.3
  18.9 0.7 collective-permute-start.2
  19.6 9.7 %first_iteration.1 = (f32[64,32,512]{2,1,0:T(8,128)S(1)}, f32[64,512]{1,0:T(8,128)S(1)}, f32[64,512]{1,0:T(8,128)S(1)}, f32[128,512]{1,0:T(8,128)S(1)}, f32[128,512]{1,0:T(8,128)S(1)}) custom-call(f32[64,32,512]{2,1,0:T(8,128)} %bitcast.27, f32[64,32,512]{2,1,0:T(8,128)} %bitcast.24, f32[64,32,512]{2,1,0:T(8,128)} %bitcast.31, ...), custom_call_target="tpu_custom_call" | custom-call | flops 7000000000 | bytes 20971520 | tf_op jit(solution)/shard_map/first_iteration/pallas_call | solution.py:367
  29.3 0.0 collective-permute-done.5
  29.3 0.0 collective-permute-done.4
  29.3 0.0 collective-permute-done.3
  29.3 0.0 collective-permute-done.2
  29.3 0.1 add_add_fusion.1.after
  29.4 0.7 collective-permute-start.7
  30.1 2.3 %collective-permute-start.6 = (f32[128,512]{1,0:T(8,128)S(1)}, f32[128,512]{1,0:T(8,128)S(1)}, u32[]{:S(2)}, u32[]{:S(2)}) collective-permute-start(f32[128,512]{1,0:T(8,128)S(1)} %add_add_fusion.1.after), channel_id=1, source_target_pairs={{32,64},{48,80},{88,72},{120,104},{33,65},{49,81},{89,73},{121,105... | collective-permute-start | bytes 786440 | tf_op jit(solution)/shard_map/ppermute | solution.py:752
  32.4 1.9 %collective-permute-start.8 = (f32[96,512]{1,0:T(8,128)S(1)}, f32[96,512]{1,0:T(8,128)S(1)}, u32[]{:S(2)}, u32[]{:S(2)}) collective-permute-start(f32[96,512]{1,0:T(8,128)S(1)} %get-tuple-element.95), channel_id=1, source_target_pairs={{0,8},{8,16},{16,24},{24,32},{32,40},{40,48},{48,56},{1,9},{9,17},... | collective-permute-start | bytes 589832 | tf_op jit(solution)/shard_map/ppermute | solution.py:711
  34.3 3.4 %collective-permute-start.9 = (f32[96,512]{1,0:T(8,128)S(1)}, f32[96,512]{1,0:T(8,128)S(1)}, u32[]{:S(2)}, u32[]{:S(2)}) collective-permute-start(f32[96,512]{1,0:T(8,128)S(1)} %get-tuple-element.96), channel_id=1, source_target_pairs={{8,0},{16,8},{24,16},{32,24},{40,32},{48,40},{56,48},{9,1},{17,9},... | collective-permute-start | bytes 589832 | tf_op jit(solution)/shard_map/ppermute | solution.py:712
  37.7 3.5 %stencil_matrix.3 = (bf16[2048,256]{1,0:T(8,128)(2,1)S(1)}, bf16[2048,256]{1,0:T(8,128)(2,1)S(1)}) custom-call(f32[10,32,128]{2,1,0:T(8,128)S(1)} %get-tuple-element.74.tables, f32[128,512]{1,0:T(8,128)S(1)} %add_add_fusion.1.after), custom_call_target="tpu_custom_call" | custom-call | flops 8000000 | bytes 6291456 | tf_op jit(solution)/shard_map/stencil_matrix/pallas_call | solution.py:437
  41.1 0.0 collective-permute-done.8.up
  41.1 4.3 %collective-permute-done.9.down = f32[96,512]{1,0:T(8,128)S(1)} collective-permute-done((f32[96,512]{1,0:T(8,128)S(1)}, f32[96,512]{1,0:T(8,128)S(1)}, u32[]{:S(2)}, u32[]{:S(2)}) %collective-permute-start.9) | collective-permute-done | bytes 196640 | tf_op jit(solution)/shard_map/ppermute | solution.py:712
  45.5 0.0 collective-permute-done.7
  45.5 0.0 collective-permute-done.6
  45.5 0.1 add_add_fusion.after
  45.5 3.6 %collective-permute-start.10 = (f32[128,512]{1,0:T(8,128)S(1)}, f32[128,512]{1,0:T(8,128)S(1)}, u32[]{:S(2)}, u32[]{:S(2)}) collective-permute-start(f32[128,512]{1,0:T(8,128)S(1)} %add_add_fusion.after), channel_id=1, source_target_pairs={{64,66},{65,67},{66,68},{67,69},{68,70},{69,71},{70,64},{71,65},{7... | collective-permute-start | bytes 786440 | tf_op jit(solution)/shard_map/ppermute | solution.py:768
  49.1 1.9 %collective-permute-start.11 = (f32[128,512]{1,0:T(8,128)S(1)}, f32[128,512]{1,0:T(8,128)S(1)}, u32[]{:S(2)}, u32[]{:S(2)}) collective-permute-start(f32[128,512]{1,0:T(8,128)S(1)} %add_add_fusion.after), channel_id=1, source_target_pairs={{64,70},{65,71},{66,64},{67,65},{68,66},{69,67},{70,68},{71,69},{7... | collective-permute-start | bytes 786440 | tf_op jit(solution)/shard_map/ppermute | solution.py:768
  51.1 3.1 %collective-permute-start.12 = (f32[128,512]{1,0:T(8,128)S(1)}, f32[128,512]{1,0:T(8,128)S(1)}, u32[]{:S(2)}, u32[]{:S(2)}) collective-permute-start(f32[128,512]{1,0:T(8,128)S(1)} %add_add_fusion.after), channel_id=1, source_target_pairs={{64,68},{65,69},{66,70},{67,71},{68,64},{69,65},{70,66},{71,67},{7... | collective-permute-start | bytes 786440 | tf_op jit(solution)/shard_map/ppermute | solution.py:768
  54.1 0.9 finish_edges.1
  55.0 0.5 collective-permute-done.10
  55.5 3.1 %collective-permute-done.11 = f32[128,512]{1,0:T(8,128)S(1)} collective-permute-done((f32[128,512]{1,0:T(8,128)S(1)}, f32[128,512]{1,0:T(8,128)S(1)}, u32[]{:S(2)}, u32[]{:S(2)}) %collective-permute-start.11) | collective-permute-done | bytes 262176 | tf_op jit(solution)/shard_map/ppermute | solution.py:768
  58.6 7.8 %collective-permute-start.15 = (f32[128,512]{1,0:T(8,128)S(1)}, f32[128,512]{1,0:T(8,128)S(1)}, u32[]{:S(2)}, u32[]{:S(2)}) collective-permute-start(f32[128,512]{1,0:T(8,128)S(1)} %get-tuple-element.116), channel_id=1, source_target_pairs={{0,1},{1,2},{2,3},{3,4},{4,5},{5,6},{6,7},{8,9},{9,10},{10,11},{11... | collective-permute-start | bytes 786440 | tf_op jit(solution)/shard_map/ppermute | solution.py:711
  66.5 2.7 %collective-permute-start.16 = (f32[128,512]{1,0:T(8,128)S(1)}, f32[128,512]{1,0:T(8,128)S(1)}, u32[]{:S(2)}, u32[]{:S(2)}) collective-permute-start(f32[128,512]{1,0:T(8,128)S(1)} %get-tuple-element.117), channel_id=1, source_target_pairs={{1,0},{2,1},{3,2},{4,3},{5,4},{6,5},{7,6},{9,8},{10,9},{11,10},{12... | collective-permute-start | bytes 786440 | tf_op jit(solution)/shard_map/ppermute | solution.py:712
  69.2 1.9 %collective-permute-start.13 = (f32[64,512]{1,0:T(8,128)S(1)}, f32[64,512]{1,0:T(8,128)S(1)}, u32[]{:S(2)}, u32[]{:S(2)}) collective-permute-start(f32[64,512]{1,0:T(8,128)S(1)} %get-tuple-element.114), channel_id=1, source_target_pairs={{0,8},{8,16},{16,24},{24,32},{32,40},{40,48},{48,56},{1,9},{9,17},... | collective-permute-start | bytes 393224 | tf_op jit(solution)/shard_map/ppermute | solution.py:711
  71.1 3.4 %collective-permute-start.14 = (f32[64,512]{1,0:T(8,128)S(1)}, f32[64,512]{1,0:T(8,128)S(1)}, u32[]{:S(2)}, u32[]{:S(2)}) collective-permute-start(f32[64,512]{1,0:T(8,128)S(1)} %get-tuple-element.115), channel_id=1, source_target_pairs={{8,0},{16,8},{24,16},{32,24},{40,32},{48,40},{56,48},{9,1},{17,9},... | collective-permute-start | bytes 393224 | tf_op jit(solution)/shard_map/ppermute | solution.py:712
  74.5 0.0 collective-permute-done.12
  74.5 0.4 collective-permute-done.13.up
  74.9 5.5 %collective-permute-done.14.down = f32[64,512]{1,0:T(8,128)S(1)} collective-permute-done((f32[64,512]{1,0:T(8,128)S(1)}, f32[64,512]{1,0:T(8,128)S(1)}, u32[]{:S(2)}, u32[]{:S(2)}) %collective-permute-start.14) | collective-permute-done | bytes 131104 | tf_op jit(solution)/shard_map/ppermute | solution.py:712
  80.5 0.0 collective-permute-done.15.left
  80.5 0.0 collective-permute-done.16.right
  80.5 0.1 pad_maximum_fusion.own
  80.5 4.8 %collective-permute-start.17 = (f32[4,128,512]{2,1,0:T(8,128)S(1)}, f32[4,128,512]{2,1,0:T(8,128)S(1)}, u32[]{:S(2)}, u32[]{:S(2)}) collective-permute-start(f32[4,128,512]{2,1,0:T(8,128)S(1)} %pad_maximum_fusion.own), channel_id=1, source_target_pairs={{64,65},{65,64},{66,67},{67,66},{68,69},{69,68},{70,71},{71,70},{7... | collective-permute-start | bytes 3145736 | tf_op jit(solution)/shard_map/ppermute | solution.py:778
  85.3 4.5 %own_source.1 = (f32[64,32,512]{2,1,0:T(8,128)S(1)}, f32[2048,512]{1,0:T(8,128)S(1)}, f32[384,512]{1,0:T(8,128)S(1)}) custom-call(f32[64,32,512]{2,1,0:T(8,128)S(1)} %get-tuple-element.121.one, f32[4,32,512]{2,1,0:T(8,128)S(1)} %get-tuple-element.122.added, bf16[2048,256]{1,0:T(8,128)(2,1)S(1)} %get-tuple-element.123.stencil_high, ...), custom_call_target="tpu_custom_call" | custom-call | flops 7000000000 | bytes 20971520 | tf_op jit(solution)/shard_map/own_source/pallas_call | solution.py:567
  89.9 0.0 collective-permute-done.17.other
  89.9 12.4 %last_iteration.1 = (f32[64,32,512]{2,1,0:T(8,128)}, f32[64,32,512]{2,1,0:T(8,128)}) custom-call(f32[64,32,512]{2,1,0:T(8,128)S(1)} %get-tuple-element.130.one, f32[2048,512]{1,0:T(8,128)S(1)} %get-tuple-element.131.source, f32[384,512]{1,0:T(8,128)S(1)} %get-tuple-element.132.edge_source, f32[64,32,512]{2,1,0:T(8,128)} %bitcast.28, ...), custom_call_target="tpu_custom_call" | custom-call | flops 14000000000 | bytes 37748736 | tf_op jit(solution)/shard_map/last_iteration/pallas_call | solution.py:687
  (1 shorter events, 0.0 us)
Async XLA Ops:
  3.3 9.5 %collective-permute-start = (f32[176,512]{1,0:T(8,128)S(1)}, f32[176,512]{1,0:T(8,128)S(1)}, u32[]{:S(2)}, u32[]{:S(2)}) collective-permute-start(f32[176,512]{1,0:T(8,128)S(1)} %get-tuple-element.75), channel_id=1, source_target_pairs={{0,1},{1,2},{2,3},{3,4},{4,5},{5,6},{6,7},{8,9},{9,10},{10,11},{11... | collective-permute-start | bytes 1081352 | tf_op jit(solution)/shard_map/ppermute | solution.py:711
  7.4 8.7 %collective-permute-start.1 = (f32[176,512]{1,0:T(8,128)S(1)}, f32[176,512]{1,0:T(8,128)S(1)}, u32[]{:S(2)}, u32[]{:S(2)}) collective-permute-start(f32[176,512]{1,0:T(8,128)S(1)} %get-tuple-element.76.after), channel_id=1, source_target_pairs={{1,0},{2,1},{3,2},{4,3},{5,4},{6,5},{7,6},{9,8},{10,9},{11,10},{12... | collective-permute-start | bytes 1081352 | tf_op jit(solution)/shard_map/ppermute | solution.py:712
  16.2 13.0 %collective-permute-start.5 = (f32[128,512]{1,0:T(8,128)S(1)}, f32[128,512]{1,0:T(8,128)S(1)}, u32[]{:S(2)}, u32[]{:S(2)}) collective-permute-start(f32[128,512]{1,0:T(8,128)S(1)} %both_bands.1.after), channel_id=1, source_target_pairs={{56,120},{57,121},{58,122},{59,123},{60,124},{61,125},{62,126},{63... | collective-permute-start | bytes 786440 | tf_op jit(solution)/shard_map/ppermute | solution.py:745
  16.9 12.4 %collective-permute-start.4 = (f32[128,512]{1,0:T(8,128)S(1)}, f32[128,512]{1,0:T(8,128)S(1)}, u32[]{:S(2)}, u32[]{:S(2)}) collective-permute-start(f32[128,512]{1,0:T(8,128)S(1)} %both_bands.1.after), channel_id=1, source_target_pairs={{56,88},{57,89},{58,90},{59,91},{60,92},{61,93},{62,94},{63,95}} | collective-permute-start | bytes 786440 | tf_op jit(solution)/shard_map/ppermute | solution.py:745
  18.2 11.1 %collective-permute-start.3 = (f32[128,512]{1,0:T(8,128)S(1)}, f32[128,512]{1,0:T(8,128)S(1)}, u32[]{:S(2)}, u32[]{:S(2)}) collective-permute-start(f32[128,512]{1,0:T(8,128)S(1)} %both_bands.1.after), channel_id=1, source_target_pairs={{56,48},{57,49},{58,50},{59,51},{60,52},{61,53},{62,54},{63,55}} | collective-permute-start | bytes 786440 | tf_op jit(solution)/shard_map/ppermute | solution.py:745
  18.9 10.4 %collective-permute-start.2 = (f32[128,512]{1,0:T(8,128)S(1)}, f32[128,512]{1,0:T(8,128)S(1)}, u32[]{:S(2)}, u32[]{:S(2)}) collective-permute-start(f32[128,512]{1,0:T(8,128)S(1)} %both_bands.1.after), channel_id=1, source_target_pairs={{56,32},{57,33},{58,34},{59,35},{60,36},{61,37},{62,38},{63,39}} | collective-permute-start | bytes 786440 | tf_op jit(solution)/shard_map/ppermute | solution.py:745
  29.4 16.1 %collective-permute-start.7 = (f32[128,512]{1,0:T(8,128)S(1)}, f32[128,512]{1,0:T(8,128)S(1)}, u32[]{:S(2)}, u32[]{:S(2)}) collective-permute-start(f32[128,512]{1,0:T(8,128)S(1)} %add_add_fusion.1.after), channel_id=1, source_target_pairs={{32,96},{48,112},{33,97},{49,113},{34,98},{50,114},{35,99},{51,115... | collective-permute-start | bytes 786440 | tf_op jit(solution)/shard_map/ppermute | solution.py:752
  30.1 15.4 %collective-permute-start.6 = (f32[128,512]{1,0:T(8,128)S(1)}, f32[128,512]{1,0:T(8,128)S(1)}, u32[]{:S(2)}, u32[]{:S(2)}) collective-permute-start(f32[128,512]{1,0:T(8,128)S(1)} %add_add_fusion.1.after), channel_id=1, source_target_pairs={{32,64},{48,80},{88,72},{120,104},{33,65},{49,81},{89,73},{121,105... | collective-permute-start | bytes 786440 | tf_op jit(solution)/shard_map/ppermute | solution.py:752
  32.4 8.8 %collective-permute-start.8 = (f32[96,512]{1,0:T(8,128)S(1)}, f32[96,512]{1,0:T(8,128)S(1)}, u32[]{:S(2)}, u32[]{:S(2)}) collective-permute-start(f32[96,512]{1,0:T(8,128)S(1)} %get-tuple-element.95), channel_id=1, source_target_pairs={{0,8},{8,16},{16,24},{24,32},{32,40},{40,48},{48,56},{1,9},{9,17},... | collective-permute-start | bytes 589832 | tf_op jit(solution)/shard_map/ppermute | solution.py:711
  34.3 11.2 %collective-permute-start.9 = (f32[96,512]{1,0:T(8,128)S(1)}, f32[96,512]{1,0:T(8,128)S(1)}, u32[]{:S(2)}, u32[]{:S(2)}) collective-permute-start(f32[96,512]{1,0:T(8,128)S(1)} %get-tuple-element.96), channel_id=1, source_target_pairs={{8,0},{16,8},{24,16},{32,24},{40,32},{48,40},{56,48},{9,1},{17,9},... | collective-permute-start | bytes 589832 | tf_op jit(solution)/shard_map/ppermute | solution.py:712
  45.5 10.0 %collective-permute-start.10 = (f32[128,512]{1,0:T(8,128)S(1)}, f32[128,512]{1,0:T(8,128)S(1)}, u32[]{:S(2)}, u32[]{:S(2)}) collective-permute-start(f32[128,512]{1,0:T(8,128)S(1)} %add_add_fusion.after), channel_id=1, source_target_pairs={{64,66},{65,67},{66,68},{67,69},{68,70},{69,71},{70,64},{71,65},{7... | collective-permute-start | bytes 786440 | tf_op jit(solution)/shard_map/ppermute | solution.py:768
  49.1 9.5 %collective-permute-start.11 = (f32[128,512]{1,0:T(8,128)S(1)}, f32[128,512]{1,0:T(8,128)S(1)}, u32[]{:S(2)}, u32[]{:S(2)}) collective-permute-start(f32[128,512]{1,0:T(8,128)S(1)} %add_add_fusion.after), channel_id=1, source_target_pairs={{64,70},{65,71},{66,64},{67,65},{68,66},{69,67},{70,68},{71,69},{7... | collective-permute-start | bytes 786440 | tf_op jit(solution)/shard_map/ppermute | solution.py:768
  51.1 23.4 %collective-permute-start.12 = (f32[128,512]{1,0:T(8,128)S(1)}, f32[128,512]{1,0:T(8,128)S(1)}, u32[]{:S(2)}, u32[]{:S(2)}) collective-permute-start(f32[128,512]{1,0:T(8,128)S(1)} %add_add_fusion.after), channel_id=1, source_target_pairs={{64,68},{65,69},{66,70},{67,71},{68,64},{69,65},{70,66},{71,67},{7... | collective-permute-start | bytes 786440 | tf_op jit(solution)/shard_map/ppermute | solution.py:768
  58.6 21.8 %collective-permute-start.15 = (f32[128,512]{1,0:T(8,128)S(1)}, f32[128,512]{1,0:T(8,128)S(1)}, u32[]{:S(2)}, u32[]{:S(2)}) collective-permute-start(f32[128,512]{1,0:T(8,128)S(1)} %get-tuple-element.116), channel_id=1, source_target_pairs={{0,1},{1,2},{2,3},{3,4},{4,5},{5,6},{6,7},{8,9},{9,10},{10,11},{11... | collective-permute-start | bytes 786440 | tf_op jit(solution)/shard_map/ppermute | solution.py:711
  66.5 14.0 %collective-permute-start.16 = (f32[128,512]{1,0:T(8,128)S(1)}, f32[128,512]{1,0:T(8,128)S(1)}, u32[]{:S(2)}, u32[]{:S(2)}) collective-permute-start(f32[128,512]{1,0:T(8,128)S(1)} %get-tuple-element.117), channel_id=1, source_target_pairs={{1,0},{2,1},{3,2},{4,3},{5,4},{6,5},{7,6},{9,8},{10,9},{11,10},{12... | collective-permute-start | bytes 786440 | tf_op jit(solution)/shard_map/ppermute | solution.py:712
  69.2 5.7 %collective-permute-start.13 = (f32[64,512]{1,0:T(8,128)S(1)}, f32[64,512]{1,0:T(8,128)S(1)}, u32[]{:S(2)}, u32[]{:S(2)}) collective-permute-start(f32[64,512]{1,0:T(8,128)S(1)} %get-tuple-element.114), channel_id=1, source_target_pairs={{0,8},{8,16},{16,24},{24,32},{32,40},{40,48},{48,56},{1,9},{9,17},... | collective-permute-start | bytes 393224 | tf_op jit(solution)/shard_map/ppermute | solution.py:711
  71.1 9.3 %collective-permute-start.14 = (f32[64,512]{1,0:T(8,128)S(1)}, f32[64,512]{1,0:T(8,128)S(1)}, u32[]{:S(2)}, u32[]{:S(2)}) collective-permute-start(f32[64,512]{1,0:T(8,128)S(1)} %get-tuple-element.115), channel_id=1, source_target_pairs={{8,0},{16,8},{24,16},{32,24},{40,32},{48,40},{56,48},{9,1},{17,9},... | collective-permute-start | bytes 393224 | tf_op jit(solution)/shard_map/ppermute | solution.py:712
  80.5 9.3 %collective-permute-start.17 = (f32[4,128,512]{2,1,0:T(8,128)S(1)}, f32[4,128,512]{2,1,0:T(8,128)S(1)}, u32[]{:S(2)}, u32[]{:S(2)}) collective-permute-start(f32[4,128,512]{2,1,0:T(8,128)S(1)} %pad_maximum_fusion.own), channel_id=1, source_target_pairs={{64,65},{65,64},{66,67},{67,66},{68,69},{69,68},{70,71},{71,70},{7... | collective-permute-start | bytes 3145736 | tf_op jit(solution)/shard_map/ppermute | solution.py:778

commit v9 on v8

--- a/solution.py
+++ b/solution.py
@@ -165,8 +165,8 @@
 
 def prepare_kernel(
     packet, previous, potential, rotation, damping, absorber, index, weight, angular,
-    top, bottom, first, last, tables, high, low,
-    ends, sides, others, factors, masks, indices, weights, matrix, sems,
+    upper, lower, first, last, tables, high, low,
+    sides, others, factors, masks, indices, weights, matrix, sems,
 ):
     count_r, rows, width = packet.shape
     small = [
@@ -179,11 +179,9 @@
     copies = [
         pltpu.make_async_copy(packet.at[:, pl.ds(0, 8)], sides.at[0], sems.at[5]),
         pltpu.make_async_copy(packet.at[:, pl.ds(rows - 8, 8)], sides.at[1], sems.at[6]),
-        pltpu.make_async_copy(packet.at[pl.ds(0, HALO)], ends.at[0], sems.at[7]),
-        pltpu.make_async_copy(packet.at[pl.ds(count_r - HALO, HALO)], ends.at[1], sems.at[8]),
-        pltpu.make_async_copy(previous.at[pl.ds(count_r - BAND, BAND)], others.at[0], sems.at[9]),
-        pltpu.make_async_copy(potential.at[pl.ds(count_r - BAND, BAND)], others.at[1], sems.at[10]),
-        pltpu.make_async_copy(angular, matrix, sems.at[11]),
+        pltpu.make_async_copy(previous.at[pl.ds(count_r - BAND, BAND)], others.at[0], sems.at[7]),
+        pltpu.make_async_copy(potential.at[pl.ds(count_r - BAND, BAND)], others.at[1], sems.at[8]),
+        pltpu.make_async_copy(angular, matrix, sems.at[9]),
     ]
     for copy in small + copies:
         copy.start()
@@ -194,21 +192,21 @@
     values += [weights[n] for n in range(STENCILS)]
     for n, value in enumerate(values):
         tables[n] = jnp.concatenate([value, jnp.zeros((rows, LANES - count_r), F32)], axis=1)
-    edges = HALO * rows
     columns = HALO * count_r
     lane = lax.broadcasted_iota(jnp.int32, (rows, LANES), 1)
-    upper = jnp.zeros((rows, LANES), F32)
-    lower = jnp.zeros((rows, LANES), F32)
-    for n in range(2 * STENCILS):
-        value = tables[INDEX + n]
+    at_top = jnp.zeros((rows, LANES), F32)
+    at_bottom = jnp.zeros((rows, LANES), F32)
+    for n, table in enumerate([*range(INDEX, TABLES), RET]):
+        value = tables[table]
         at = n * HALO
         here = (lane >= at) & (lane < at + HALO)
-        upper = jnp.where(here, pltpu.roll(value, at, 1), upper)
-        lower = jnp.where(here, pltpu.roll(value, (at + LANES - (count_r - HALO)) % LANES, 1), lower)
-        first[columns + at : columns + at + HALO, 0:LANES] = value[0:HALO]
-        last[columns + at : columns + at + HALO, 0:LANES] = value[rows - HALO : rows]
-    top[edges : edges + rows, 0:LANES] = upper
-    bottom[edges : edges + rows, 0:LANES] = lower
+        at_top = jnp.where(here, pltpu.roll(value, at, 1), at_top)
+        at_bottom = jnp.where(here, pltpu.roll(value, (at + LANES - (count_r - HALO)) % LANES, 1), at_bottom)
+        if table != RET:
+            first[columns + at : columns + at + HALO, 0:LANES] = value[0:HALO]
+            last[columns + at : columns + at + HALO, 0:LANES] = value[rows - HALO : rows]
+    upper[...] = at_top
+    lower[...] = at_bottom
     begin = columns + EXTRA
     for copy in copies:
         copy.wait()
@@ -227,15 +225,12 @@
         for k in range(count_r):
             for r in range(HALO):
                 out[r * count_r + k : r * count_r + k + 1] = sides[n, k, near + r : near + r + 1]
-    for out, n in ((top, 0), (bottom, 1)):
-        for k in range(HALO):
-            out[k * rows : (k + 1) * rows] = ends[n, k]
     high[...], low[...] = halves(matrix[...])
 
 
 def prepare(packet, previous, potential, rotation, damping, absorber, index, weight, angular):
     count_r, rows, width = packet.shape
-    ends = jax.ShapeDtypeStruct((HALO * rows + rows, width), F32)
+    ends = jax.ShapeDtypeStruct((rows, LANES), F32)
     sides = jax.ShapeDtypeStruct((HALO * count_r + EXTRA + OFBAND, width), F32)
     part = jax.ShapeDtypeStruct(angular.shape, BF16)
     return pl.pallas_call(
@@ -244,7 +239,6 @@
         out_specs=[VMEM] * 7,
         out_shape=[ends, ends, sides, sides, jax.ShapeDtypeStruct((TABLES, rows, LANES), F32), part, part],
         scratch_shapes=[
-            pltpu.VMEM((2, HALO, rows, width), F32),
             pltpu.VMEM((2, count_r, 8, width), F32),
             pltpu.VMEM((2, BAND, rows, width), F32),
             pltpu.VMEM((2, rows, count_r), F32),
@@ -252,7 +246,7 @@
             pltpu.VMEM((STENCILS, rows, count_r), jnp.int32),
             pltpu.VMEM((STENCILS, rows, count_r), F32),
             pltpu.VMEM(angular.shape, F32),
-            pltpu.SemaphoreType.DMA((12,)),
+            pltpu.SemaphoreType.DMA((10,)),
         ],
         compiler_params=pltpu.CompilerParams(vmem_limit_bytes=16 * MIB),
         cost_estimate=pl.CostEstimate(flops=1_000_000, bytes_accessed=6 * MIB, transcendentals=0),
@@ -314,7 +308,7 @@
 
 
 def first_kernel(
-    packet, previous, potential, tables, left, right, high, low, after,
+    packet, previous, potential, tables, upper, lower, left, right, high, low, after,
     done, top, bottom, first, last, field, prev, pot, sides, sems,
 ):
     count_r, rows, width = packet.shape
@@ -355,18 +349,25 @@
         return carry
 
     lax.fori_loop(0, steps, body, 0)
+    edges = HALO * rows
     for k in range(HALO):
-        top[k * rows : (k + 1) * rows] = done[k]
-        bottom[k * rows : (k + 1) * rows] = done[count_r - HALO + k]
-
-
-def first_iteration(packet, previous, potential, tables, left, right, high, low, after):
+        here = slice(k * rows, (k + 1) * rows)
+        beside = slice(edges + k * rows, edges + (k + 1) * rows)
+        top[here] = done[k]
+        bottom[here] = done[count_r - HALO + k]
+        top[beside] = field[HALO + k]
+        bottom[beside] = field[count_r + k]
+    top[2 * edges : 2 * edges + rows, 0:LANES] = upper[...]
+    bottom[2 * edges : 2 * edges + rows, 0:LANES] = lower[...]
+
+
+def first_iteration(packet, previous, potential, tables, upper, lower, left, right, high, low, after):
     count_r, rows, width = packet.shape
-    ends = jax.ShapeDtypeStruct((HALO * rows, width), F32)
+    ends = jax.ShapeDtypeStruct((2 * HALO * rows + rows, width), F32)
     sides = jax.ShapeDtypeStruct((HALO * count_r, width), F32)
     return pl.pallas_call(
         first_kernel,
-        in_specs=[HBM, HBM, HBM, *[VMEM] * 5, ANY],
+        in_specs=[HBM, HBM, HBM, *[VMEM] * 7, ANY],
         out_specs=[VMEM] * 5,
         out_shape=[jax.ShapeDtypeStruct(packet.shape, F32), ends, ends, sides, sides],
         scratch_shapes=[
@@ -379,7 +380,7 @@
         compiler_params=pltpu.CompilerParams(vmem_limit_bytes=28 * MIB),
         cost_estimate=pl.CostEstimate(flops=7_000_000_000, bytes_accessed=20 * MIB, transcendentals=0),
         name="first_iteration",
-    )(packet, previous, potential, tables, left, right, high, low, after)
+    )(packet, previous, potential, tables, upper, lower, left, right, high, low, after)
 
 
 def slot_of(value, rows, width):
@@ -409,7 +410,7 @@
         low[pl.ds(at, rows), tile : tile + LANES] = lower
 
 
-def stencil_kernel(tables, after, high, low, *, side):
+def stencil_kernel(tables, after, high, low, other_high, other_low):
     _, rows, _ = tables.shape
     count_r = high.shape[0] // rows
     group = 8
@@ -425,29 +426,31 @@
             moved = [pltpu.roll(value, shift, 1) for value in values]
             for k in range(group):
                 at = pl.multiple_of((step * group + k) * rows, rows)
-                fill_rows(at, [value[:, k : k + 1] for value in moved], rows, high, low, side * half)
+                cut = [jnp.broadcast_to(value[:, k : k + 1], (rows, LANES)) for value in moved]
+                fill_rows(at, cut, rows, high, low)
+                fill_rows(at, cut, rows, other_high, other_low, half)
             return carry
 
         lax.fori_loop(0, count_r // group, body, 0)
 
 
-def stencil_matrix(tables, count_r, columns, side, after):
+def stencil_matrix(tables, count_r, columns, after):
     rows = tables.shape[1]
     points = jax.ShapeDtypeStruct((count_r * rows, columns // CORES), BF16)
     return pl.pallas_call(
-        functools.partial(stencil_kernel, side=side),
+        stencil_kernel,
         in_specs=[VMEM, ANY],
-        out_specs=[VMEM] * 2,
-        out_shape=[points, points],
+        out_specs=[VMEM] * 4,
+        out_shape=[points] * 4,
         compiler_params=pltpu.CompilerParams(vmem_limit_bytes=16 * MIB),
-        cost_estimate=pl.CostEstimate(flops=8_000_000, bytes_accessed=6 * MIB, transcendentals=0),
+        cost_estimate=pl.CostEstimate(flops=15_000_000, bytes_accessed=6 * MIB, transcendentals=0),
         name="stencil_matrix",
     )(tables, after)
 
 
 def edge_kernel(
     up, down, left, right, tables, top, bottom, first, last, after,
-    high, low, new_top, new_bottom, new_first, new_last, added, square, *, rows, count_r,
+    high, low, whole_up, whole_down, new_first, new_last, added, square, *, rows, count_r,
 ):
     width = up.shape[1]
     edges = HALO * rows
@@ -455,16 +458,24 @@
     def retained(k):
         return jnp.broadcast_to(tables[RET, :, k : k + 1], (rows, width))
 
-    added[0] = retained(0) * (SIDE1 * up[rows:edges] + SIDE2 * up[0:rows])
-    added[1] = retained(1) * (SIDE2 * up[rows:edges])
-    added[2] = retained(count_r - 2) * (SIDE2 * down[0:rows])
-    added[3] = retained(count_r - 1) * (SIDE1 * down[0:rows] + SIDE2 * down[rows:edges])
+    def there(side, k):
+        at = 2 * STENCILS * HALO + k
+        return jnp.broadcast_to(side[2 * edges : 2 * edges + rows, at : at + 1], (rows, width))
+
+    def packet_row(slab, k):
+        return slab[edges + k * rows : edges + (k + 1) * rows]
+
+    added[0] = retained(0) * (SIDE1 * packet_row(up, 1) + SIDE2 * packet_row(up, 0))
+    added[1] = retained(1) * (SIDE2 * packet_row(up, 1))
+    added[2] = retained(count_r - 2) * (SIDE2 * packet_row(down, 0))
+    added[3] = retained(count_r - 1) * (SIDE1 * packet_row(down, 0) + SIDE2 * packet_row(down, 1))
+    whole_up[0:rows] = up[0:rows] + there(up, 0) * (SIDE2 * packet_row(top, 0))
+    whole_up[rows:edges] = up[rows:edges] + there(up, 1) * (SIDE1 * packet_row(top, 0) + SIDE2 * packet_row(top, 1))
+    whole_down[0:rows] = down[0:rows] + there(down, 0) * (SIDE1 * packet_row(bottom, 1) + SIDE2 * packet_row(bottom, 0))
+    whole_down[rows:edges] = down[rows:edges] + there(down, 1) * (SIDE2 * packet_row(bottom, 1))
     new_first[...] = first[...]
     new_last[...] = last[...]
     for k in range(HALO):
-        here = slice(k * rows, (k + 1) * rows)
-        new_top[here] = top[here] + added[k]
-        new_bottom[here] = bottom[here] + added[HALO + k]
         for n, r_row in ((k, k), (HALO + k, count_r - HALO + k)):
             for r in range(HALO):
                 at = r * count_r + r_row
@@ -475,7 +486,7 @@
     def _():
         at = 0
         for side in (up, down):
-            value = side[edges : edges + rows, 0:LANES]
+            value = side[2 * edges : 2 * edges + rows, 0:LANES]
             slots = slot_of(value, rows, high.shape[1])
             for e in range(HALO):
                 cut = [
@@ -511,7 +522,7 @@
         out_specs=[VMEM] * 7,
         out_shape=[
             points, points,
-            *[jax.ShapeDtypeStruct(edge.shape, F32) for edge in edges],
+            *[jax.ShapeDtypeStruct((HALO * length, width), F32) for length in (rows, rows, count_r, count_r)],
             jax.ShapeDtypeStruct((2 * HALO, rows, width), F32),
         ],
         scratch_shapes=[pltpu.VMEM((LANES, LANES), F32)],
@@ -728,13 +739,13 @@
         )
     )
 
-    top, bottom, first, last, tables, high, low = prepare(
+    upper, lower, first, last, tables, high, low = prepare(
         packet, previous, potential, rotation, damping, absorber, stencil_index, stencil_weight, angular
     )
     columns = count_row * rows * BAND
     left, right = neighbours("row", last, first)
-    own_matrix = stencil_matrix(tables, count_r, columns, 0, first)
-    left, right, own_matrix = lax.optimization_barrier((left, right, own_matrix))
+    matrix = stencil_matrix(tables, count_r, columns, first)
+    left, right, matrix = lax.optimization_barrier((left, right, matrix))
     table = bands(packet, previous, potential, tables, left, right, high, low)
 
     half = count_rr // PLANES
@@ -743,18 +754,18 @@
     low_side, high_side = start - half + 1, start - 1
     relays = [low_side, high_side, count_rr + half - 1, count_rr + start]
     crossed = [lax.ppermute(table, plane, [(start, relay)]) for relay in relays]
-    one, *edges = first_iteration(packet, previous, potential, tables, left, right, high, low, table)
+    one, *edges = first_iteration(
+        packet, previous, potential, tables, upper, lower, left, right, high, low, table
+    )
     *crossed, one, edges = lax.optimization_barrier((*crossed, one, edges))
     piece = sum(crossed)
     near = [(low_side, count_rr), (high_side, count_rr + half - 2)]
     near += [(count_rr + half - 1, count_rr + half - 3), (count_rr + start, count_rr + start - 2)]
     opposite = [(low_side, count_rr + low_side), (high_side, count_rr + high_side)]
     arrived = [lax.ppermute(piece, plane, near), lax.ppermute(piece, plane, opposite)]
+    top, bottom, first, last = edges
     top, bottom, piece = lax.optimization_barrier((top, bottom, piece))
     up, down = neighbours("rr", bottom, top)
-    other_matrix = stencil_matrix(tables, count_r, columns, 1, piece)
-    *arrived, other_matrix, up, down = lax.optimization_barrier((*arrived, other_matrix, up, down))
-    halos = (up, down, left, right)
     spread = piece + sum(arrived)
     line = ("sect", "row")
 
@@ -768,20 +779,21 @@
         return lax.ppermute(spread, line, pairs)
 
     rest = [around(1), around(3), around(2)]
-    *edge_matrix, top, bottom, first, last, added = finish_edges(halos, tables, edges, rows, count_r, columns, spread)
-    rest[0], edge_matrix, top, bottom = lax.optimization_barrier((rest[0], edge_matrix, top, bottom))
-    up, down = neighbours("rr", bottom, top)
-    rest[0], rest[1], first, last = lax.optimization_barrier((rest[0], rest[1], first, last))
+    edge_matrix_and_ends = finish_edges(
+        (up, down, left, right), tables, (top, bottom, first, last), rows, count_r, columns, spread
+    )
+    *edge_matrix, up, down, first, last, added = edge_matrix_and_ends
+    rest[1], edge_matrix, first, last = lax.optimization_barrier((rest[1], edge_matrix, first, last))
     left, right = neighbours("row", last, first)
-    *rest, up, down, left, right = lax.optimization_barrier((*rest, up, down, left, right))
+    *rest, left, right = lax.optimization_barrier((*rest, left, right))
     own = jnp.stack([spread, rest[0], rest[2], rest[1]], axis=0)
     other = lax.ppermute(
         own, line, [(count_row + i, count_row + i + 1 - 2 * (i % CORES)) for i in range(count_row)]
     )
-    own_sums = own_source(one, added, (*own_matrix, *edge_matrix), own)
+    own_sums = own_source(one, added, (*matrix[:2], *edge_matrix), own)
     other, own_sums = lax.optimization_barrier((other, own_sums))
     earlier, latest = last_iteration(
-        own_sums, packet, potential, tables, (up, down, left, right), high, low, (*other_matrix, *edge_matrix), other
+        own_sums, packet, potential, tables, (up, down, left, right), high, low, (*matrix[2:], *edge_matrix), other
     )
     return latest[None], earlier[None]
 

time: 103 us -> 84.3 us (0.82)
  the two profiles are of different devices: /device:TPU:59 before, /device:TPU:35 now
where the time goes in v9:
time: 84.3 us; the launch traced here: 83.7 us
  Pallas kernels  34.2 us (41%)
  starting transfers between devices  32.9 us (39%)
  waiting for transfers between devices  15.6 us (19%)
  between operations  0.89 us (1%)
    pallas_call x1, Pallas kernels, last_iteration(): pl.pallas_call(last_kernel, in_specs=[VMEM, VMEM, VMEM, HBM, HBM, *[VMEM]...  12.4 us
    ppermute x3, starting transfers between devices, neighbours(): lax.ppermute(upward, axis, [(i, i + 1) for i in range(count - 1)])  11.8 us
    pallas_call x1, Pallas kernels, first_iteration(): pl.pallas_call(first_kernel, in_specs=[HBM, HBM, HBM, *[VMEM] * 7, ANY],...  9.69 us
    ppermute x3, starting transfers between devices, around(): return lax.ppermute(spread, line, pairs)  8.92 us
    ppermute x1, waiting for transfers between devices, local(): lax.ppermute(piece, plane, near)  6.18 us
    ppermute x3, starting transfers between devices, neighbours(): lax.ppermute(downward, axis, [(i + 1, i) for i in range(count - 1)])  5.13 us
    pallas_call x1, Pallas kernels, own_source(): pl.pallas_call(own_source_kernel, in_specs=[VMEM] * 7, out_specs=[VMEM] *...  4.52 us
    pallas_call x1, Pallas kernels, stencil_matrix(): pl.pallas_call(stencil_kernel, in_specs=[VMEM, ANY], out_specs=[VMEM] * 4...  4.04 us
  transfers between devices with their start and end apart: 16, of which 7 were waited for; matrix products, arithmetic and copies ran while one was open for 0% of the time, Pallas kernels for 23%

profile of v9, /device:TPU:35, one launch (start us, length us, event | category | flops | bytes accessed | tf_op | source)
XLA Modules:
  0.0 83.7 jit_solution(10423108843023631676)
XLA Ops:
  0.6 2.6 %prepare.1 = (f32[32,128]{1,0:T(8,128)S(1)}, f32[32,128]{1,0:T(8,128)S(1)}, f32[176,512]{1,0:T(8,128)S(1)}, f32[176,512]{1,0:T(8,128)S(1)}, f32[10,32,128]{2,1,0...) custom-call(f32[64,32,512]{2,1,0:T(8,128)} %bitcast.25, f32[64,32,512]{2,1,0:T(8,128)} %bitcast.22, ...), custom_call_target="tpu_custom_call" | custom-call | flops 1000000 | bytes 6291456 | tf_op jit(solution)/shard_map/prepare/pallas_call | solution.py:236
  3.2 4.1 %collective-permute-start = (f32[176,512]{1,0:T(8,128)S(1)}, f32[176,512]{1,0:T(8,128)S(1)}, u32[]{:S(2)}, u32[]{:S(2)}) collective-permute-start(f32[176,512]{1,0:T(8,128)S(1)} %get-tuple-element.63), channel_id=1, source_target_pairs={{0,1},{1,2},{2,3},{3,4},{4,5},{5,6},{6,7},{8,9},{9,10},{10,11},{11... | collective-permute-start | bytes 1081352 | tf_op jit(solution)/shard_map/ppermute | solution.py:722
  7.3 1.9 %collective-permute-start.1 = (f32[176,512]{1,0:T(8,128)S(1)}, f32[176,512]{1,0:T(8,128)S(1)}, u32[]{:S(2)}, u32[]{:S(2)}) collective-permute-start(f32[176,512]{1,0:T(8,128)S(1)} %get-tuple-element.64.after), channel_id=1, source_target_pairs={{1,0},{2,1},{3,2},{4,3},{5,4},{6,5},{7,6},{9,8},{10,9},{11,10},{12... | collective-permute-start | bytes 1081352 | tf_op jit(solution)/shard_map/ppermute | solution.py:723
  9.3 4.0 %stencil_matrix.1 = (bf16[2048,256]{1,0:T(8,128)(2,1)S(1)}, bf16[2048,256]{1,0:T(8,128)(2,1)S(1)}, bf16[2048,256]{1,0:T(8,128)(2,1)S(1)}, bf16[2048,256]{1,0:T(8,128)(2,1)S(1)}) custom-call(f32[10,32,128]{2,1,0:T(8,128)S(1)} %get-tuple-element.62.tables, f32[176,512]{1,0:T(8,128)S(1)} %get-tuple-element.64.after), custom_call_target="tpu_custom_call" | custom-call | flops 15000000 | bytes 6291456 | tf_op jit(solution)/shard_map/stencil_matrix/pallas_call | solution.py:440
  13.3 0.0 collective-permute-done.left
  13.3 2.8 %collective-permute-done.1.right = f32[176,512]{1,0:T(8,128)S(1)} collective-permute-done((f32[176,512]{1,0:T(8,128)S(1)}, f32[176,512]{1,0:T(8,128)S(1)}, u32[]{:S(2)}, u32[]{:S(2)}) %collective-permute-start.1) | collective-permute-done | bytes 360480 | tf_op jit(solution)/shard_map/ppermute | solution.py:723
  16.1 0.7 collective-permute-start.5
  16.8 0.7 collective-permute-start.4
  17.5 0.7 collective-permute-start.3
  18.2 0.7 collective-permute-start.2
  18.8 9.7 %first_iteration.1 = (f32[64,32,512]{2,1,0:T(8,128)S(1)}, f32[160,512]{1,0:T(8,128)S(1)}, f32[160,512]{1,0:T(8,128)S(1)}, f32[128,512]{1,0:T(8,128)S(1)}, f32[128,512]{1,0:T(8,128)S(1)}) custom-call(f32[64,32,512]{2,1,0:T(8,128)} %bitcast.27, f32[64,32,512]{2,1,0:T(8,128)} %bitcast.24, f32[64,32,512]{2,1,0:T(8,128)} %bitcast.31, ...), custom_call_target="tpu_custom_call" | custom-call | flops 7000000000 | bytes 20971520 | tf_op jit(solution)/shard_map/first_iteration/pallas_call | solution.py:368
  28.5 0.0 collective-permute-done.5
  28.6 0.0 collective-permute-done.4
  28.6 0.0 collective-permute-done.3
  28.6 0.0 collective-permute-done.2
  28.6 0.1 add_add_fusion.1
  28.7 0.7 collective-permute-start.7
  29.4 1.3 %collective-permute-start.6 = (f32[128,512]{1,0:T(8,128)S(1)}, f32[128,512]{1,0:T(8,128)S(1)}, u32[]{:S(2)}, u32[]{:S(2)}) collective-permute-start(f32[128,512]{1,0:T(8,128)S(1)} %add_add_fusion.1), channel_id=1, source_target_pairs={{32,64},{48,80},{88,72},{120,104},{33,65},{49,81},{89,73},{121,105... | collective-permute-start | bytes 786440 | tf_op jit(solution)/shard_map/ppermute | solution.py:765
  30.7 3.2 %collective-permute-start.10 = (f32[160,512]{1,0:T(8,128)S(1)}, f32[160,512]{1,0:T(8,128)S(1)}, u32[]{:S(2)}, u32[]{:S(2)}) collective-permute-start(f32[160,512]{1,0:T(8,128)S(1)} %get-tuple-element.87.bottom), channel_id=1, source_target_pairs={{0,8},{8,16},{16,24},{24,32},{32,40},{40,48},{48,56},{1,9},{9,17},... | collective-permute-start | bytes 983048 | tf_op jit(solution)/shard_map/ppermute | solution.py:722
  33.9 1.3 %collective-permute-start.11 = (f32[160,512]{1,0:T(8,128)S(1)}, f32[160,512]{1,0:T(8,128)S(1)}, u32[]{:S(2)}, u32[]{:S(2)}) collective-permute-start(f32[160,512]{1,0:T(8,128)S(1)} %get-tuple-element.88.top), channel_id=1, source_target_pairs={{8,0},{16,8},{24,16},{32,24},{40,32},{48,40},{56,48},{9,1},{17,9},... | collective-permute-start | bytes 983048 | tf_op jit(solution)/shard_map/ppermute | solution.py:723
  35.2 0.0 collective-permute-done.7
  35.2 6.2 %collective-permute-done.6 = f32[128,512]{1,0:T(8,128)S(1)} collective-permute-done((f32[128,512]{1,0:T(8,128)S(1)}, f32[128,512]{1,0:T(8,128)S(1)}, u32[]{:S(2)}, u32[]{:S(2)}) %collective-permute-start.6) | collective-permute-done | bytes 262176 | tf_op jit(solution)/shard_map/ppermute | solution.py:765
  41.4 0.1 add_add_fusion.after
  41.4 1.9 %collective-permute-start.9 = (f32[128,512]{1,0:T(8,128)S(1)}, f32[128,512]{1,0:T(8,128)S(1)}, u32[]{:S(2)}, u32[]{:S(2)}) collective-permute-start(f32[128,512]{1,0:T(8,128)S(1)} %add_add_fusion.after), channel_id=1, source_target_pairs={{64,70},{65,71},{66,64},{67,65},{68,66},{69,67},{70,68},{71,69},{7... | collective-permute-start | bytes 786440 | tf_op jit(solution)/shard_map/ppermute | solution.py:779
  43.4 5.1 %collective-permute-start.12 = (f32[128,512]{1,0:T(8,128)S(1)}, f32[128,512]{1,0:T(8,128)S(1)}, u32[]{:S(2)}, u32[]{:S(2)}) collective-permute-start(f32[128,512]{1,0:T(8,128)S(1)} %add_add_fusion.after), channel_id=1, source_target_pairs={{64,68},{65,69},{66,70},{67,71},{68,64},{69,65},{70,66},{71,67},{7... | collective-permute-start | bytes 786440 | tf_op jit(solution)/shard_map/ppermute | solution.py:779
  48.5 1.9 %collective-permute-start.8 = (f32[128,512]{1,0:T(8,128)S(1)}, f32[128,512]{1,0:T(8,128)S(1)}, u32[]{:S(2)}, u32[]{:S(2)}) collective-permute-start(f32[128,512]{1,0:T(8,128)S(1)} %add_add_fusion.after), channel_id=1, source_target_pairs={{64,66},{65,67},{66,68},{67,69},{68,70},{69,71},{70,64},{71,65},{7... | collective-permute-start | bytes 786440 | tf_op jit(solution)/shard_map/ppermute | solution.py:779
  50.4 0.0 collective-permute-done.10.up
  50.4 0.0 collective-permute-done.11.down
  50.4 0.9 %finish_edges.1 = (bf16[384,512]{1,0:T(8,128)(2,1)S(1)}, bf16[384,512]{1,0:T(8,128)(2,1)S(1)}, f32[64,512]{1,0:T(8,128)S(1)}, f32[64,512]{1,0:T(8,128)S(1)}, f32...) custom-call(f32[160,512]{1,0:T(8,128)S(1)} %collective-permute-done.10.up, ...), custom_call_target="tpu_custom_call" | custom-call | flops 2000000 | bytes 3145728 | tf_op jit(solution)/shard_map/finish_edges/pallas_call | solution.py:519
  51.4 0.5 collective-permute-done.9
  51.9 4.4 %collective-permute-start.13 = (f32[128,512]{1,0:T(8,128)S(1)}, f32[128,512]{1,0:T(8,128)S(1)}, u32[]{:S(2)}, u32[]{:S(2)}) collective-permute-start(f32[128,512]{1,0:T(8,128)S(1)} %get-tuple-element.96), channel_id=1, source_target_pairs={{0,1},{1,2},{2,3},{3,4},{4,5},{5,6},{6,7},{8,9},{9,10},{10,11},{11... | collective-permute-start | bytes 786440 | tf_op jit(solution)/shard_map/ppermute | solution.py:722
  56.3 1.9 %collective-permute-start.14 = (f32[128,512]{1,0:T(8,128)S(1)}, f32[128,512]{1,0:T(8,128)S(1)}, u32[]{:S(2)}, u32[]{:S(2)}) collective-permute-start(f32[128,512]{1,0:T(8,128)S(1)} %get-tuple-element.97), channel_id=1, source_target_pairs={{1,0},{2,1},{3,2},{4,3},{5,4},{6,5},{7,6},{9,8},{10,9},{11,10},{12... | collective-permute-start | bytes 786440 | tf_op jit(solution)/shard_map/ppermute | solution.py:723
  58.2 0.3 collective-permute-done.12
  58.5 2.6 %collective-permute-done.8 = f32[128,512]{1,0:T(8,128)S(1)} collective-permute-done((f32[128,512]{1,0:T(8,128)S(1)}, f32[128,512]{1,0:T(8,128)S(1)}, u32[]{:S(2)}, u32[]{:S(2)}) %collective-permute-start.8) | collective-permute-done | bytes 262176 | tf_op jit(solution)/shard_map/ppermute | solution.py:779
  61.1 2.2 %collective-permute-done.13.left = f32[128,512]{1,0:T(8,128)S(1)} collective-permute-done((f32[128,512]{1,0:T(8,128)S(1)}, f32[128,512]{1,0:T(8,128)S(1)}, u32[]{:S(2)}, u32[]{:S(2)}) %collective-permute-start.13) | collective-permute-done | bytes 262176 | tf_op jit(solution)/shard_map/ppermute | solution.py:722
  63.3 1.0 %collective-permute-done.14.right = f32[128,512]{1,0:T(8,128)S(1)} collective-permute-done((f32[128,512]{1,0:T(8,128)S(1)}, f32[128,512]{1,0:T(8,128)S(1)}, u32[]{:S(2)}, u32[]{:S(2)}) %collective-permute-start.14) | collective-permute-done | bytes 262176 | tf_op jit(solution)/shard_map/ppermute | solution.py:723
  64.3 0.1 pad_maximum_fusion.own
  64.4 2.4 %collective-permute-start.15 = (f32[4,128,512]{2,1,0:T(8,128)S(1)}, f32[4,128,512]{2,1,0:T(8,128)S(1)}, u32[]{:S(2)}, u32[]{:S(2)}) collective-permute-start(f32[4,128,512]{2,1,0:T(8,128)S(1)} %pad_maximum_fusion.own), channel_id=1, source_target_pairs={{64,65},{65,64},{66,67},{67,66},{68,69},{69,68},{70,71},{71,70},{7... | collective-permute-start | bytes 3145736 | tf_op jit(solution)/shard_map/ppermute | solution.py:790
  66.8 4.5 %own_source.1 = (f32[64,32,512]{2,1,0:T(8,128)S(1)}, f32[2048,512]{1,0:T(8,128)S(1)}, f32[384,512]{1,0:T(8,128)S(1)}) custom-call(f32[64,32,512]{2,1,0:T(8,128)S(1)} %get-tuple-element.101.one, f32[4,32,512]{2,1,0:T(8,128)S(1)} %get-tuple-element.102.added, bf16[2048,256]{1,0:T(8,128)(2,1)S(1)} %get-tuple-element.103.stencil_high, ...), custom_call_target="tpu_custom_call" | custom-call | flops 7000000000 | bytes 20971520 | tf_op jit(solution)/shard_map/own_source/pallas_call | solution.py:578
  71.3 0.0 collective-permute-done.15.other
  71.3 12.4 %last_iteration.1 = (f32[64,32,512]{2,1,0:T(8,128)}, f32[64,32,512]{2,1,0:T(8,128)}) custom-call(f32[64,32,512]{2,1,0:T(8,128)S(1)} %get-tuple-element.110.one, f32[2048,512]{1,0:T(8,128)S(1)} %get-tuple-element.111.source, f32[384,512]{1,0:T(8,128)S(1)} %get-tuple-element.112.edge_source, f32[64,32,512]{2,1,0:T(8,128)} %bitcast.28, ...), custom_call_target="tpu_custom_call" | custom-call | flops 14000000000 | bytes 37748736 | tf_op jit(solution)/shard_map/last_iteration/pallas_call | solution.py:698
  (1 shorter events, 0.0 us)
Async XLA Ops:
  3.2 10.1 %collective-permute-start = (f32[176,512]{1,0:T(8,128)S(1)}, f32[176,512]{1,0:T(8,128)S(1)}, u32[]{:S(2)}, u32[]{:S(2)}) collective-permute-start(f32[176,512]{1,0:T(8,128)S(1)} %get-tuple-element.63), channel_id=1, source_target_pairs={{0,1},{1,2},{2,3},{3,4},{4,5},{5,6},{6,7},{8,9},{9,10},{10,11},{11... | collective-permute-start | bytes 1081352 | tf_op jit(solution)/shard_map/ppermute | solution.py:722
  7.3 8.7 %collective-permute-start.1 = (f32[176,512]{1,0:T(8,128)S(1)}, f32[176,512]{1,0:T(8,128)S(1)}, u32[]{:S(2)}, u32[]{:S(2)}) collective-permute-start(f32[176,512]{1,0:T(8,128)S(1)} %get-tuple-element.64.after), channel_id=1, source_target_pairs={{1,0},{2,1},{3,2},{4,3},{5,4},{6,5},{7,6},{9,8},{10,9},{11,10},{12... | collective-permute-start | bytes 1081352 | tf_op jit(solution)/shard_map/ppermute | solution.py:723
  16.1 12.4 %collective-permute-start.5 = (f32[128,512]{1,0:T(8,128)S(1)}, f32[128,512]{1,0:T(8,128)S(1)}, u32[]{:S(2)}, u32[]{:S(2)}) collective-permute-start(f32[128,512]{1,0:T(8,128)S(1)} %both_bands.1.after), channel_id=1, source_target_pairs={{56,120},{57,121},{58,122},{59,123},{60,124},{61,125},{62,126},{63... | collective-permute-start | bytes 786440 | tf_op jit(solution)/shard_map/ppermute | solution.py:756
  16.8 11.8 %collective-permute-start.4 = (f32[128,512]{1,0:T(8,128)S(1)}, f32[128,512]{1,0:T(8,128)S(1)}, u32[]{:S(2)}, u32[]{:S(2)}) collective-permute-start(f32[128,512]{1,0:T(8,128)S(1)} %both_bands.1.after), channel_id=1, source_target_pairs={{56,88},{57,89},{58,90},{59,91},{60,92},{61,93},{62,94},{63,95}} | collective-permute-start | bytes 786440 | tf_op jit(solution)/shard_map/ppermute | solution.py:756
  17.5 11.1 %collective-permute-start.3 = (f32[128,512]{1,0:T(8,128)S(1)}, f32[128,512]{1,0:T(8,128)S(1)}, u32[]{:S(2)}, u32[]{:S(2)}) collective-permute-start(f32[128,512]{1,0:T(8,128)S(1)} %both_bands.1.after), channel_id=1, source_target_pairs={{56,48},{57,49},{58,50},{59,51},{60,52},{61,53},{62,54},{63,55}} | collective-permute-start | bytes 786440 | tf_op jit(solution)/shard_map/ppermute | solution.py:756
  18.2 10.4 %collective-permute-start.2 = (f32[128,512]{1,0:T(8,128)S(1)}, f32[128,512]{1,0:T(8,128)S(1)}, u32[]{:S(2)}, u32[]{:S(2)}) collective-permute-start(f32[128,512]{1,0:T(8,128)S(1)} %both_bands.1.after), channel_id=1, source_target_pairs={{56,32},{57,33},{58,34},{59,35},{60,36},{61,37},{62,38},{63,39}} | collective-permute-start | bytes 786440 | tf_op jit(solution)/shard_map/ppermute | solution.py:756
  28.7 6.5 %collective-permute-start.7 = (f32[128,512]{1,0:T(8,128)S(1)}, f32[128,512]{1,0:T(8,128)S(1)}, u32[]{:S(2)}, u32[]{:S(2)}) collective-permute-start(f32[128,512]{1,0:T(8,128)S(1)} %add_add_fusion.1), channel_id=1, source_target_pairs={{32,96},{48,112},{33,97},{49,113},{34,98},{50,114},{35,99},{51,115... | collective-permute-start | bytes 786440 | tf_op jit(solution)/shard_map/ppermute | solution.py:765
  29.4 12.0 %collective-permute-start.6 = (f32[128,512]{1,0:T(8,128)S(1)}, f32[128,512]{1,0:T(8,128)S(1)}, u32[]{:S(2)}, u32[]{:S(2)}) collective-permute-start(f32[128,512]{1,0:T(8,128)S(1)} %add_add_fusion.1), channel_id=1, source_target_pairs={{32,64},{48,80},{88,72},{120,104},{33,65},{49,81},{89,73},{121,105... | collective-permute-start | bytes 786440 | tf_op jit(solution)/shard_map/ppermute | solution.py:765
  30.7 19.7 %collective-permute-start.10 = (f32[160,512]{1,0:T(8,128)S(1)}, f32[160,512]{1,0:T(8,128)S(1)}, u32[]{:S(2)}, u32[]{:S(2)}) collective-permute-start(f32[160,512]{1,0:T(8,128)S(1)} %get-tuple-element.87.bottom), channel_id=1, source_target_pairs={{0,8},{8,16},{16,24},{24,32},{32,40},{40,48},{48,56},{1,9},{9,17},... | collective-permute-start | bytes 983048 | tf_op jit(solution)/shard_map/ppermute | solution.py:722
  33.9 16.5 %collective-permute-start.11 = (f32[160,512]{1,0:T(8,128)S(1)}, f32[160,512]{1,0:T(8,128)S(1)}, u32[]{:S(2)}, u32[]{:S(2)}) collective-permute-start(f32[160,512]{1,0:T(8,128)S(1)} %get-tuple-element.88.top), channel_id=1, source_target_pairs={{8,0},{16,8},{24,16},{32,24},{40,32},{48,40},{56,48},{9,1},{17,9},... | collective-permute-start | bytes 983048 | tf_op jit(solution)/shard_map/ppermute | solution.py:723
  41.4 10.4 %collective-permute-start.9 = (f32[128,512]{1,0:T(8,128)S(1)}, f32[128,512]{1,0:T(8,128)S(1)}, u32[]{:S(2)}, u32[]{:S(2)}) collective-permute-start(f32[128,512]{1,0:T(8,128)S(1)} %add_add_fusion.after), channel_id=1, source_target_pairs={{64,70},{65,71},{66,64},{67,65},{68,66},{69,67},{70,68},{71,69},{7... | collective-permute-start | bytes 786440 | tf_op jit(solution)/shard_map/ppermute | solution.py:779
  43.4 15.1 %collective-permute-start.12 = (f32[128,512]{1,0:T(8,128)S(1)}, f32[128,512]{1,0:T(8,128)S(1)}, u32[]{:S(2)}, u32[]{:S(2)}) collective-permute-start(f32[128,512]{1,0:T(8,128)S(1)} %add_add_fusion.after), channel_id=1, source_target_pairs={{64,68},{65,69},{66,70},{67,71},{68,64},{69,65},{70,66},{71,67},{7... | collective-permute-start | bytes 786440 | tf_op jit(solution)/shard_map/ppermute | solution.py:779
  48.5 12.6 %collective-permute-start.8 = (f32[128,512]{1,0:T(8,128)S(1)}, f32[128,512]{1,0:T(8,128)S(1)}, u32[]{:S(2)}, u32[]{:S(2)}) collective-permute-start(f32[128,512]{1,0:T(8,128)S(1)} %add_add_fusion.after), channel_id=1, source_target_pairs={{64,66},{65,67},{66,68},{67,69},{68,70},{69,71},{70,64},{71,65},{7... | collective-permute-start | bytes 786440 | tf_op jit(solution)/shard_map/ppermute | solution.py:779
  51.9 11.4 %collective-permute-start.13 = (f32[128,512]{1,0:T(8,128)S(1)}, f32[128,512]{1,0:T(8,128)S(1)}, u32[]{:S(2)}, u32[]{:S(2)}) collective-permute-start(f32[128,512]{1,0:T(8,128)S(1)} %get-tuple-element.96), channel_id=1, source_target_pairs={{0,1},{1,2},{2,3},{3,4},{4,5},{5,6},{6,7},{8,9},{9,10},{10,11},{11... | collective-permute-start | bytes 786440 | tf_op jit(solution)/shard_map/ppermute | solution.py:722
  56.3 8.0 %collective-permute-start.14 = (f32[128,512]{1,0:T(8,128)S(1)}, f32[128,512]{1,0:T(8,128)S(1)}, u32[]{:S(2)}, u32[]{:S(2)}) collective-permute-start(f32[128,512]{1,0:T(8,128)S(1)} %get-tuple-element.97), channel_id=1, source_target_pairs={{1,0},{2,1},{3,2},{4,3},{5,4},{6,5},{7,6},{9,8},{10,9},{11,10},{12... | collective-permute-start | bytes 786440 | tf_op jit(solution)/shard_map/ppermute | solution.py:723
  64.4 6.9 %collective-permute-start.15 = (f32[4,128,512]{2,1,0:T(8,128)S(1)}, f32[4,128,512]{2,1,0:T(8,128)S(1)}, u32[]{:S(2)}, u32[]{:S(2)}) collective-permute-start(f32[4,128,512]{2,1,0:T(8,128)S(1)} %pad_maximum_fusion.own), channel_id=1, source_target_pairs={{64,65},{65,64},{66,67},{67,66},{68,69},{69,68},{70,71},{71,70},{7... | collective-permute-start | bytes 3145736 | tf_op jit(solution)/shard_map/ppermute | solution.py:790

commit v10 on v9

--- a/solution.py
+++ b/solution.py
@@ -309,26 +309,21 @@
 
 def first_kernel(
     packet, previous, potential, tables, upper, lower, left, right, high, low, after,
-    done, top, bottom, first, last, field, prev, pot, sides, sems,
+    done, top, bottom, first, last, field, sides, sems,
 ):
     count_r, rows, width = packet.shape
     steps = count_r // CHUNK
 
     def copies(n):
         part = pl.ds(n * CHUNK, CHUNK)
-        return (
-            pltpu.make_async_copy(packet.at[part], field.at[pl.ds(HALO + n * CHUNK, CHUNK)], sems.at[0, n]),
-            pltpu.make_async_copy(previous.at[part], prev.at[part], sems.at[1, n]),
-            pltpu.make_async_copy(potential.at[part], pot.at[part], sems.at[2, n]),
-        )
+        return pltpu.make_async_copy(packet.at[part], field.at[pl.ds(HALO + n * CHUNK, CHUNK)], sems.at[n])
 
     for n in range(steps):
-        for copy in copies(n):
-            copy.start()
+        copies(n).start()
     field[0:HALO] = jnp.zeros((HALO, rows, width), F32)
     field[HALO + count_r :] = jnp.zeros((HALO, rows, width), F32)
     put_sides(sides, left, right, count_r)
-    copies(0)[0].wait()
+    copies(0).wait()
 
     def put(k, lanes, value):
         done[k, :, lanes] = value
@@ -336,11 +331,9 @@
     def body(n, carry):
         @pl.when(n + 1 < steps)
         def _():
-            copies(n + 1)[0].wait()
-
-        copies(n)[1].wait()
-        copies(n)[2].wait()
-        advance(n, CHUNK, field, sides, prev, pot, tables, high, low, put)
+            copies(n + 1).wait()
+
+        advance(n, CHUNK, field, sides, previous, potential, tables, high, low, put)
         for k in range(CHUNK):
             for r in range(HALO):
                 at = pl.ds(r * count_r + n * CHUNK + k, 1)
@@ -367,17 +360,15 @@
     sides = jax.ShapeDtypeStruct((HALO * count_r, width), F32)
     return pl.pallas_call(
         first_kernel,
-        in_specs=[HBM, HBM, HBM, *[VMEM] * 7, ANY],
+        in_specs=[HBM, *[VMEM] * 9, ANY],
         out_specs=[VMEM] * 5,
         out_shape=[jax.ShapeDtypeStruct(packet.shape, F32), ends, ends, sides, sides],
         scratch_shapes=[
             pltpu.VMEM((count_r + 2 * HALO, rows, width), F32),
-            pltpu.VMEM(packet.shape, F32),
-            pltpu.VMEM(packet.shape, F32),
             pltpu.VMEM((count_r, 8, width), F32),
-            pltpu.SemaphoreType.DMA((3, count_r // CHUNK)),
+            pltpu.SemaphoreType.DMA((count_r // CHUNK,)),
         ],
-        compiler_params=pltpu.CompilerParams(vmem_limit_bytes=28 * MIB),
+        compiler_params=pltpu.CompilerParams(vmem_limit_bytes=14 * MIB),
         cost_estimate=pl.CostEstimate(flops=7_000_000_000, bytes_accessed=20 * MIB, transcendentals=0),
         name="first_iteration",
     )(packet, previous, potential, tables, upper, lower, left, right, high, low, after)
@@ -594,7 +585,7 @@
 def last_kernel(
     one, source, edge_source, packet, potential, tables, up, down, left, right, high, low,
     stencil_high, stencil_low, edge_high, edge_low, other,
-    earlier, latest, field, prev, pot, done, sides, table, ends, sems,
+    earlier, latest, field, done, sides, table, ends, sems,
 ):
     count_r, rows, width = packet.shape
     steps = count_r // LAST
@@ -608,17 +599,11 @@
     def cut(n):
         return pl.ds(pl.multiple_of(n * size, size), size)
 
-    def locals_of(n):
-        return (
-            pltpu.make_async_copy(packet.at[part(n)], prev.at[part(n)], sems.at[0, n]),
-            pltpu.make_async_copy(potential.at[part(n)], pot.at[part(n)], sems.at[1, n]),
-        )
-
     def earliers(n):
-        return pltpu.make_async_copy(field.at[pl.ds(HALO + n * LAST, LAST)], earlier.at[part(n)], sems.at[2, n])
+        return pltpu.make_async_copy(field.at[pl.ds(HALO + n * LAST, LAST)], earlier.at[part(n)], sems.at[0, n])
 
     def latests(n):
-        return pltpu.make_async_copy(done.at[part(n)], latest.at[part(n)], sems.at[3, n])
+        return pltpu.make_async_copy(done.at[part(n)], latest.at[part(n)], sems.at[1, n])
 
     def put_ends(up_value, down_value):
         for k in range(HALO):
@@ -627,10 +612,6 @@
 
     def put(k, lanes, value):
         done[k, :, lanes] = value
-
-    for n in range(steps):
-        for copy in locals_of(n):
-            copy.start()
 
     @pl.when(is_product)
     def _():
@@ -657,14 +638,12 @@
         lax.fori_loop(0, steps, add, 0)
 
         def body(n, carry):
-            for copy in locals_of(n):
-                copy.wait()
             matrix = weights(n)
 
             def more(lanes):
                 return source[cut(n), lanes] + product(matrix, table[2, :, lanes], table[3, :, lanes])
 
-            advance(n, LAST, field, sides, prev, pot, tables, high, low, put, more)
+            advance(n, LAST, field, sides, packet, potential, tables, high, low, put, more)
             latests(n).start()
             return carry
 
@@ -679,9 +658,7 @@
             earliers(n).start()
 
         def body(n, carry):
-            for copy in locals_of(n):
-                copy.wait()
-            advance(n, LAST, field, sides, prev, pot, tables, high, low, put)
+            advance(n, LAST, field, sides, packet, potential, tables, high, low, put)
             latests(n).start()
             return carry
 
@@ -697,20 +674,18 @@
     steps = count_r // LAST
     return pl.pallas_call(
         last_kernel,
-        in_specs=[VMEM, VMEM, VMEM, HBM, HBM, *[VMEM] * 12],
+        in_specs=[VMEM] * 17,
         out_specs=[HBM, HBM],
         out_shape=[jax.ShapeDtypeStruct(packet.shape, F32)] * 2,
         scratch_shapes=[
             pltpu.VMEM((count_r + 2 * HALO, rows, width), F32),
             pltpu.VMEM(packet.shape, F32),
-            pltpu.VMEM(packet.shape, F32),
-            pltpu.VMEM(packet.shape, F32),
             pltpu.VMEM((count_r, 8, width), F32),
             pltpu.VMEM((4, other.shape[0] * other.shape[1] // 2, width), BF16),
             pltpu.VMEM((2 * HALO * (rows + count_r), width), F32),
-            pltpu.SemaphoreType.DMA((4, steps)),
+            pltpu.SemaphoreType.DMA((2, steps)),
         ],
-        compiler_params=pltpu.CompilerParams(vmem_limit_bytes=32 * MIB),
+        compiler_params=pltpu.CompilerParams(vmem_limit_bytes=20 * MIB),
         cost_estimate=pl.CostEstimate(flops=14_000_000_000, bytes_accessed=36 * MIB, transcendentals=0),
         name="last_iteration",
     )(*own_sums, packet, potential, tables, *halos, high, low, *matrices, other)
@@ -732,6 +707,7 @@
     chips = count_row // CORES
     rotation, damping, absorber = (jnp.swapaxes(value, 0, 1) for value in (rotation, damping, absorber))
     stencil_index, stencil_weight = (jnp.swapaxes(value, 1, 2) for value in (stencil_index, stencil_weight))
+    near_packet, near_previous, near_potential = packet, previous, potential
     packet, previous, potential, rotation, damping, absorber, stencil_index, stencil_weight, angular = (
         in_hbm(value)
         for value in (
@@ -752,10 +728,10 @@
     start = count_rr - 1
     plane = ("sect", "rr")
     low_side, high_side = start - half + 1, start - 1
-    relays = [low_side, high_side, count_rr + half - 1, count_rr + start]
+    relays = [count_rr + half - 1, count_rr + start, high_side, low_side]
     crossed = [lax.ppermute(table, plane, [(start, relay)]) for relay in relays]
     one, *edges = first_iteration(
-        packet, previous, potential, tables, upper, lower, left, right, high, low, table
+        packet, near_previous, near_potential, tables, upper, lower, left, right, high, low, table
     )
     *crossed, one, edges = lax.optimization_barrier((*crossed, one, edges))
     piece = sum(crossed)
@@ -793,7 +769,7 @@
     own_sums = own_source(one, added, (*matrix[:2], *edge_matrix), own)
     other, own_sums = lax.optimization_barrier((other, own_sums))
     earlier, latest = last_iteration(
-        own_sums, packet, potential, tables, (up, down, left, right), high, low, (*matrix[2:], *edge_matrix), other
+        own_sums, near_packet, near_potential, tables, (up, down, left, right), high, low, (*matrix[2:], *edge_matrix), other
     )
     return latest[None], earlier[None]
 

time: 84.3 us -> 82.9 us (0.983)
  the two profiles are of different devices: /device:TPU:35 before, /device:TPU:43 now
where the time goes in v10:
time: 82.9 us; the launch traced here: 82.4 us
  starting transfers between devices  34.5 us (42%)
  Pallas kernels  33.4 us (40%)
  waiting for transfers between devices  13.1 us (16%)
  between operations  0.93 us (1%)
    pallas_call x1, Pallas kernels, last_iteration(): pl.pallas_call(last_kernel, in_specs=[VMEM] * 17, out_specs=[HBM, HBM], o...  12.3 us
    ppermute x3, starting transfers between devices, neighbours(): lax.ppermute(upward, axis, [(i, i + 1) for i in range(count - 1)])  12.3 us
    pallas_call x1, Pallas kernels, first_iteration(): pl.pallas_call(first_kernel, in_specs=[HBM, *[VMEM] * 9, ANY], out_specs=...  8.95 us
    ppermute x3, starting transfers between devices, around(): return lax.ppermute(spread, line, pairs)  8.89 us
    ppermute x3, starting transfers between devices, neighbours(): lax.ppermute(downward, axis, [(i + 1, i) for i in range(count - 1)])  5.92 us
    pallas_call x1, Pallas kernels, own_source(): pl.pallas_call(own_source_kernel, in_specs=[VMEM] * 7, out_specs=[VMEM] *...  4.52 us
    ppermute x1, waiting for transfers between devices, local(): lax.ppermute(piece, plane, near)  4.2 us
    pallas_call x1, Pallas kernels, stencil_matrix(): pl.pallas_call(stencil_kernel, in_specs=[VMEM, ANY], out_specs=[VMEM] * 4...  4.04 us
  transfers between devices with their start and end apart: 16, of which 6 were waited for; matrix products, arithmetic and copies ran while one was open for 0% of the time, Pallas kernels for 22%

profile of v10, /device:TPU:43, one launch (start us, length us, event | category | flops | bytes accessed | tf_op | source)
XLA Modules:
  0.0 82.4 jit_solution(12438441437315281657)
XLA Ops:
  0.6 2.6 %prepare.1 = (f32[32,128]{1,0:T(8,128)S(1)}, f32[32,128]{1,0:T(8,128)S(1)}, f32[176,512]{1,0:T(8,128)S(1)}, f32[176,512]{1,0:T(8,128)S(1)}, f32[10,32,128]{2,1,0...) custom-call(f32[64,32,512]{2,1,0:T(8,128)} %bitcast.24, f32[64,32,512]{2,1,0:T(8,128)} %bitcast.21, ...), custom_call_target="tpu_custom_call" | custom-call | flops 1000000 | bytes 6291456 | tf_op jit(solution)/shard_map/prepare/pallas_call | solution.py:236
  3.2 4.1 %collective-permute-start = (f32[176,512]{1,0:T(8,128)S(1)}, f32[176,512]{1,0:T(8,128)S(1)}, u32[]{:S(2)}, u32[]{:S(2)}) collective-permute-start(f32[176,512]{1,0:T(8,128)S(1)} %get-tuple-element.63), channel_id=1, source_target_pairs={{0,1},{1,2},{2,3},{3,4},{4,5},{5,6},{6,7},{8,9},{9,10},{10,11},{11... | collective-permute-start | bytes 1081352 | tf_op jit(solution)/shard_map/ppermute | solution.py:697
  7.3 1.9 %collective-permute-start.1 = (f32[176,512]{1,0:T(8,128)S(1)}, f32[176,512]{1,0:T(8,128)S(1)}, u32[]{:S(2)}, u32[]{:S(2)}) collective-permute-start(f32[176,512]{1,0:T(8,128)S(1)} %get-tuple-element.64.after), channel_id=1, source_target_pairs={{1,0},{2,1},{3,2},{4,3},{5,4},{6,5},{7,6},{9,8},{10,9},{11,10},{12... | collective-permute-start | bytes 1081352 | tf_op jit(solution)/shard_map/ppermute | solution.py:698
  9.3 4.0 %stencil_matrix.1 = (bf16[2048,256]{1,0:T(8,128)(2,1)S(1)}, bf16[2048,256]{1,0:T(8,128)(2,1)S(1)}, bf16[2048,256]{1,0:T(8,128)(2,1)S(1)}, bf16[2048,256]{1,0:T(8,128)(2,1)S(1)}) custom-call(f32[10,32,128]{2,1,0:T(8,128)S(1)} %get-tuple-element.62.tables, f32[176,512]{1,0:T(8,128)S(1)} %get-tuple-element.64.after), custom_call_target="tpu_custom_call" | custom-call | flops 15000000 | bytes 6291456 | tf_op jit(solution)/shard_map/stencil_matrix/pallas_call | solution.py:431
  13.3 0.0 collective-permute-done.left
  13.3 2.8 %collective-permute-done.1.right = f32[176,512]{1,0:T(8,128)S(1)} collective-permute-done((f32[176,512]{1,0:T(8,128)S(1)}, f32[176,512]{1,0:T(8,128)S(1)}, u32[]{:S(2)}, u32[]{:S(2)}) %collective-permute-start.1) | collective-permute-done | bytes 360480 | tf_op jit(solution)/shard_map/ppermute | solution.py:698
  16.1 0.0 copy-start
  16.1 0.0 copy-start.2
  16.1 0.8 collective-permute-start.5
  16.9 0.8 collective-permute-start.4
  17.7 0.8 collective-permute-start.3
  18.6 0.7 collective-permute-start.2
  19.2 0.0 copy-done
  19.3 0.3 copy-done.2
  19.5 9.0 %first_iteration.1 = (f32[64,32,512]{2,1,0:T(8,128)S(1)}, f32[160,512]{1,0:T(8,128)S(1)}, f32[160,512]{1,0:T(8,128)S(1)}, f32[128,512]{1,0:T(8,128)S(1)}, f32[128,512]{1,0:T(8,128)S(1)}) custom-call(f32[64,32,512]{2,1,0:T(8,128)} %bitcast.26, f32[64,32,512]{2,1,0:T(8,128)S(1)} %bitcast.23, f32[64,32,512]{2,1,0:T(8,128)S(1)} %bitcast.30, ...), custom_call_target="tpu_custom_call" | custom-call | flops 7000000000 | bytes 20971520 | tf_op jit(solution)/shard_map/first_iteration/pallas_call | solution.py:361
  28.5 0.0 collective-permute-done.5
  28.5 0.0 collective-permute-done.4
  28.5 0.0 collective-permute-done.3
  28.5 0.0 collective-permute-done.2
  28.5 0.1 add_add_fusion.1
  28.6 0.7 collective-permute-start.7
  29.3 1.3 %collective-permute-start.6 = (f32[128,512]{1,0:T(8,128)S(1)}, f32[128,512]{1,0:T(8,128)S(1)}, u32[]{:S(2)}, u32[]{:S(2)}) collective-permute-start(f32[128,512]{1,0:T(8,128)S(1)} %add_add_fusion.1), channel_id=1, source_target_pairs={{32,64},{48,80},{88,72},{120,104},{33,65},{49,81},{89,73},{121,105... | collective-permute-start | bytes 786440 | tf_op jit(solution)/shard_map/ppermute | solution.py:741
  30.6 3.2 %collective-permute-start.10 = (f32[160,512]{1,0:T(8,128)S(1)}, f32[160,512]{1,0:T(8,128)S(1)}, u32[]{:S(2)}, u32[]{:S(2)}) collective-permute-start(f32[160,512]{1,0:T(8,128)S(1)} %get-tuple-element.87.bottom), channel_id=1, source_target_pairs={{0,8},{8,16},{16,24},{24,32},{32,40},{40,48},{48,56},{1,9},{9,17},... | collective-permute-start | bytes 983048 | tf_op jit(solution)/shard_map/ppermute | solution.py:697
  33.8 2.1 %collective-permute-start.11 = (f32[160,512]{1,0:T(8,128)S(1)}, f32[160,512]{1,0:T(8,128)S(1)}, u32[]{:S(2)}, u32[]{:S(2)}) collective-permute-start(f32[160,512]{1,0:T(8,128)S(1)} %get-tuple-element.88.top), channel_id=1, source_target_pairs={{8,0},{16,8},{24,16},{32,24},{40,32},{48,40},{56,48},{9,1},{17,9},... | collective-permute-start | bytes 983048 | tf_op jit(solution)/shard_map/ppermute | solution.py:698
  35.9 0.0 collective-permute-done.7
  35.9 4.2 %collective-permute-done.6 = f32[128,512]{1,0:T(8,128)S(1)} collective-permute-done((f32[128,512]{1,0:T(8,128)S(1)}, f32[128,512]{1,0:T(8,128)S(1)}, u32[]{:S(2)}, u32[]{:S(2)}) %collective-permute-start.6) | collective-permute-done | bytes 262176 | tf_op jit(solution)/shard_map/ppermute | solution.py:741
  40.1 0.1 add_add_fusion.after
  40.2 1.9 %collective-permute-start.9 = (f32[128,512]{1,0:T(8,128)S(1)}, f32[128,512]{1,0:T(8,128)S(1)}, u32[]{:S(2)}, u32[]{:S(2)}) collective-permute-start(f32[128,512]{1,0:T(8,128)S(1)} %add_add_fusion.after), channel_id=1, source_target_pairs={{64,70},{65,71},{66,64},{67,65},{68,66},{69,67},{70,68},{71,69},{7... | collective-permute-start | bytes 786440 | tf_op jit(solution)/shard_map/ppermute | solution.py:755
  42.1 5.0 %collective-permute-start.12 = (f32[128,512]{1,0:T(8,128)S(1)}, f32[128,512]{1,0:T(8,128)S(1)}, u32[]{:S(2)}, u32[]{:S(2)}) collective-permute-start(f32[128,512]{1,0:T(8,128)S(1)} %add_add_fusion.after), channel_id=1, source_target_pairs={{64,68},{65,69},{66,70},{67,71},{68,64},{69,65},{70,66},{71,67},{7... | collective-permute-start | bytes 786440 | tf_op jit(solution)/shard_map/ppermute | solution.py:755
  47.2 1.9 %collective-permute-start.8 = (f32[128,512]{1,0:T(8,128)S(1)}, f32[128,512]{1,0:T(8,128)S(1)}, u32[]{:S(2)}, u32[]{:S(2)}) collective-permute-start(f32[128,512]{1,0:T(8,128)S(1)} %add_add_fusion.after), channel_id=1, source_target_pairs={{64,66},{65,67},{66,68},{67,69},{68,70},{69,71},{70,64},{71,65},{7... | collective-permute-start | bytes 786440 | tf_op jit(solution)/shard_map/ppermute | solution.py:755
  49.1 0.0 collective-permute-done.10.up
  49.1 0.0 collective-permute-done.11.down
  49.1 0.9 %finish_edges.1 = (bf16[384,512]{1,0:T(8,128)(2,1)S(1)}, bf16[384,512]{1,0:T(8,128)(2,1)S(1)}, f32[64,512]{1,0:T(8,128)S(1)}, f32[64,512]{1,0:T(8,128)S(1)}, f32...) custom-call(f32[160,512]{1,0:T(8,128)S(1)} %collective-permute-done.10.up, ...), custom_call_target="tpu_custom_call" | custom-call | flops 2000000 | bytes 3145728 | tf_op jit(solution)/shard_map/finish_edges/pallas_call | solution.py:510
  50.1 0.3 collective-permute-done.9
  50.4 5.0 %collective-permute-start.13 = (f32[128,512]{1,0:T(8,128)S(1)}, f32[128,512]{1,0:T(8,128)S(1)}, u32[]{:S(2)}, u32[]{:S(2)}) collective-permute-start(f32[128,512]{1,0:T(8,128)S(1)} %get-tuple-element.96), channel_id=1, source_target_pairs={{0,1},{1,2},{2,3},{3,4},{4,5},{5,6},{6,7},{8,9},{9,10},{10,11},{11... | collective-permute-start | bytes 786440 | tf_op jit(solution)/shard_map/ppermute | solution.py:697
  55.4 1.9 %collective-permute-start.14 = (f32[128,512]{1,0:T(8,128)S(1)}, f32[128,512]{1,0:T(8,128)S(1)}, u32[]{:S(2)}, u32[]{:S(2)}) collective-permute-start(f32[128,512]{1,0:T(8,128)S(1)} %get-tuple-element.97), channel_id=1, source_target_pairs={{1,0},{2,1},{3,2},{4,3},{5,4},{6,5},{7,6},{9,8},{10,9},{11,10},{12... | collective-permute-start | bytes 786440 | tf_op jit(solution)/shard_map/ppermute | solution.py:698
  57.3 0.0 collective-permute-done.12
  57.3 2.1 %collective-permute-done.8 = f32[128,512]{1,0:T(8,128)S(1)} collective-permute-done((f32[128,512]{1,0:T(8,128)S(1)}, f32[128,512]{1,0:T(8,128)S(1)}, u32[]{:S(2)}, u32[]{:S(2)}) %collective-permute-start.8) | collective-permute-done | bytes 262176 | tf_op jit(solution)/shard_map/ppermute | solution.py:755
  59.5 2.6 %collective-permute-done.13.left = f32[128,512]{1,0:T(8,128)S(1)} collective-permute-done((f32[128,512]{1,0:T(8,128)S(1)}, f32[128,512]{1,0:T(8,128)S(1)}, u32[]{:S(2)}, u32[]{:S(2)}) %collective-permute-start.13) | collective-permute-done | bytes 262176 | tf_op jit(solution)/shard_map/ppermute | solution.py:697
  62.0 1.1 %collective-permute-done.14.right = f32[128,512]{1,0:T(8,128)S(1)} collective-permute-done((f32[128,512]{1,0:T(8,128)S(1)}, f32[128,512]{1,0:T(8,128)S(1)}, u32[]{:S(2)}, u32[]{:S(2)}) %collective-permute-start.14) | collective-permute-done | bytes 262176 | tf_op jit(solution)/shard_map/ppermute | solution.py:698
  63.1 0.1 pad_maximum_fusion.own
  63.2 2.3 %collective-permute-start.15 = (f32[4,128,512]{2,1,0:T(8,128)S(1)}, f32[4,128,512]{2,1,0:T(8,128)S(1)}, u32[]{:S(2)}, u32[]{:S(2)}) collective-permute-start(f32[4,128,512]{2,1,0:T(8,128)S(1)} %pad_maximum_fusion.own), channel_id=1, source_target_pairs={{64,65},{65,64},{66,67},{67,66},{68,69},{69,68},{70,71},{71,70},{7... | collective-permute-start | bytes 3145736 | tf_op jit(solution)/shard_map/ppermute | solution.py:766
  65.5 0.0 copy-start.1
  65.5 4.5 %own_source.1 = (f32[64,32,512]{2,1,0:T(8,128)S(1)}, f32[2048,512]{1,0:T(8,128)S(1)}, f32[384,512]{1,0:T(8,128)S(1)}) custom-call(f32[64,32,512]{2,1,0:T(8,128)S(1)} %get-tuple-element.101.one, f32[4,32,512]{2,1,0:T(8,128)S(1)} %get-tuple-element.102.added, bf16[2048,256]{1,0:T(8,128)(2,1)S(1)} %get-tuple-element.103.stencil_high, ...), custom_call_target="tpu_custom_call" | custom-call | flops 7000000000 | bytes 20971520 | tf_op jit(solution)/shard_map/own_source/pallas_call | solution.py:569
  70.0 0.0 collective-permute-done.15.other
  70.0 0.0 copy-done.1
  70.1 12.3 %last_iteration.1 = (f32[64,32,512]{2,1,0:T(8,128)}, f32[64,32,512]{2,1,0:T(8,128)}) custom-call(f32[64,32,512]{2,1,0:T(8,128)S(1)} %get-tuple-element.110.one, f32[2048,512]{1,0:T(8,128)S(1)} %get-tuple-element.111.source, f32[384,512]{1,0:T(8,128)S(1)} %get-tuple-element.112.edge_source, f32[64,32,512]{2,1,0:T(8,128)S(1)} %bitcast.27, ...), custom_call_target="tpu_custom_call" | custom-call | flops 14000000000 | bytes 37748736 | tf_op jit(solution)/shard_map/last_iteration/pallas_call | solution.py:675
  (1 shorter events, 0.0 us)
Async XLA Ops:
  3.2 10.1 %collective-permute-start = (f32[176,512]{1,0:T(8,128)S(1)}, f32[176,512]{1,0:T(8,128)S(1)}, u32[]{:S(2)}, u32[]{:S(2)}) collective-permute-start(f32[176,512]{1,0:T(8,128)S(1)} %get-tuple-element.63), channel_id=1, source_target_pairs={{0,1},{1,2},{2,3},{3,4},{4,5},{5,6},{6,7},{8,9},{9,10},{10,11},{11... | collective-permute-start | bytes 1081352 | tf_op jit(solution)/shard_map/ppermute | solution.py:697
  7.3 8.7 %collective-permute-start.1 = (f32[176,512]{1,0:T(8,128)S(1)}, f32[176,512]{1,0:T(8,128)S(1)}, u32[]{:S(2)}, u32[]{:S(2)}) collective-permute-start(f32[176,512]{1,0:T(8,128)S(1)} %get-tuple-element.64.after), channel_id=1, source_target_pairs={{1,0},{2,1},{3,2},{4,3},{5,4},{6,5},{7,6},{9,8},{10,9},{11,10},{12... | collective-permute-start | bytes 1081352 | tf_op jit(solution)/shard_map/ppermute | solution.py:698
  16.1 3.2 %copy-start = (f32[1,64,32,512]{3,2,1,0:T(8,128)S(1)}, f32[1,64,32,512]{3,2,1,0:T(8,128)}, u32[]{:S(2)}) copy-start(f32[1,64,32,512]{3,2,1,0:T(8,128)} %param.10) | copy-start | bytes 12582916
  16.1 3.5 %copy-start.2 = (f32[1,64,32,512]{3,2,1,0:T(8,128)S(1)}, f32[1,64,32,512]{3,2,1,0:T(8,128)}, u32[]{:S(2)}) copy-start(f32[1,64,32,512]{3,2,1,0:T(8,128)} %param.11) | copy-start | bytes 12582916
  16.1 12.4 %collective-permute-start.5 = (f32[128,512]{1,0:T(8,128)S(1)}, f32[128,512]{1,0:T(8,128)S(1)}, u32[]{:S(2)}, u32[]{:S(2)}) collective-permute-start(f32[128,512]{1,0:T(8,128)S(1)} %both_bands.1.after), channel_id=1, source_target_pairs={{56,32},{57,33},{58,34},{59,35},{60,36},{61,37},{62,38},{63,39}} | collective-permute-start | bytes 786440 | tf_op jit(solution)/shard_map/ppermute | solution.py:732
  16.9 11.6 %collective-permute-start.4 = (f32[128,512]{1,0:T(8,128)S(1)}, f32[128,512]{1,0:T(8,128)S(1)}, u32[]{:S(2)}, u32[]{:S(2)}) collective-permute-start(f32[128,512]{1,0:T(8,128)S(1)} %both_bands.1.after), channel_id=1, source_target_pairs={{56,48},{57,49},{58,50},{59,51},{60,52},{61,53},{62,54},{63,55}} | collective-permute-start | bytes 786440 | tf_op jit(solution)/shard_map/ppermute | solution.py:732
  17.7 10.8 %collective-permute-start.3 = (f32[128,512]{1,0:T(8,128)S(1)}, f32[128,512]{1,0:T(8,128)S(1)}, u32[]{:S(2)}, u32[]{:S(2)}) collective-permute-start(f32[128,512]{1,0:T(8,128)S(1)} %both_bands.1.after), channel_id=1, source_target_pairs={{56,120},{57,121},{58,122},{59,123},{60,124},{61,125},{62,126},{63... | collective-permute-start | bytes 786440 | tf_op jit(solution)/shard_map/ppermute | solution.py:732
  18.6 10.0 %collective-permute-start.2 = (f32[128,512]{1,0:T(8,128)S(1)}, f32[128,512]{1,0:T(8,128)S(1)}, u32[]{:S(2)}, u32[]{:S(2)}) collective-permute-start(f32[128,512]{1,0:T(8,128)S(1)} %both_bands.1.after), channel_id=1, source_target_pairs={{56,88},{57,89},{58,90},{59,91},{60,92},{61,93},{62,94},{63,95}} | collective-permute-start | bytes 786440 | tf_op jit(solution)/shard_map/ppermute | solution.py:732
  28.6 7.3 %collective-permute-start.7 = (f32[128,512]{1,0:T(8,128)S(1)}, f32[128,512]{1,0:T(8,128)S(1)}, u32[]{:S(2)}, u32[]{:S(2)}) collective-permute-start(f32[128,512]{1,0:T(8,128)S(1)} %add_add_fusion.1), channel_id=1, source_target_pairs={{32,96},{48,112},{33,97},{49,113},{34,98},{50,114},{35,99},{51,115... | collective-permute-start | bytes 786440 | tf_op jit(solution)/shard_map/ppermute | solution.py:741
  29.3 10.8 %collective-permute-start.6 = (f32[128,512]{1,0:T(8,128)S(1)}, f32[128,512]{1,0:T(8,128)S(1)}, u32[]{:S(2)}, u32[]{:S(2)}) collective-permute-start(f32[128,512]{1,0:T(8,128)S(1)} %add_add_fusion.1), channel_id=1, source_target_pairs={{32,64},{48,80},{88,72},{120,104},{33,65},{49,81},{89,73},{121,105... | collective-permute-start | bytes 786440 | tf_op jit(solution)/shard_map/ppermute | solution.py:741
  30.6 18.5 %collective-permute-start.10 = (f32[160,512]{1,0:T(8,128)S(1)}, f32[160,512]{1,0:T(8,128)S(1)}, u32[]{:S(2)}, u32[]{:S(2)}) collective-permute-start(f32[160,512]{1,0:T(8,128)S(1)} %get-tuple-element.87.bottom), channel_id=1, source_target_pairs={{0,8},{8,16},{16,24},{24,32},{32,40},{40,48},{48,56},{1,9},{9,17},... | collective-permute-start | bytes 983048 | tf_op jit(solution)/shard_map/ppermute | solution.py:697
  33.8 15.3 %collective-permute-start.11 = (f32[160,512]{1,0:T(8,128)S(1)}, f32[160,512]{1,0:T(8,128)S(1)}, u32[]{:S(2)}, u32[]{:S(2)}) collective-permute-start(f32[160,512]{1,0:T(8,128)S(1)} %get-tuple-element.88.top), channel_id=1, source_target_pairs={{8,0},{16,8},{24,16},{32,24},{40,32},{48,40},{56,48},{9,1},{17,9},... | collective-permute-start | bytes 983048 | tf_op jit(solution)/shard_map/ppermute | solution.py:698
  40.2 10.2 %collective-permute-start.9 = (f32[128,512]{1,0:T(8,128)S(1)}, f32[128,512]{1,0:T(8,128)S(1)}, u32[]{:S(2)}, u32[]{:S(2)}) collective-permute-start(f32[128,512]{1,0:T(8,128)S(1)} %add_add_fusion.after), channel_id=1, source_target_pairs={{64,70},{65,71},{66,64},{67,65},{68,66},{69,67},{70,68},{71,69},{7... | collective-permute-start | bytes 786440 | tf_op jit(solution)/shard_map/ppermute | solution.py:755
  42.1 15.2 %collective-permute-start.12 = (f32[128,512]{1,0:T(8,128)S(1)}, f32[128,512]{1,0:T(8,128)S(1)}, u32[]{:S(2)}, u32[]{:S(2)}) collective-permute-start(f32[128,512]{1,0:T(8,128)S(1)} %add_add_fusion.after), channel_id=1, source_target_pairs={{64,68},{65,69},{66,70},{67,71},{68,64},{69,65},{70,66},{71,67},{7... | collective-permute-start | bytes 786440 | tf_op jit(solution)/shard_map/ppermute | solution.py:755
  47.2 12.3 %collective-permute-start.8 = (f32[128,512]{1,0:T(8,128)S(1)}, f32[128,512]{1,0:T(8,128)S(1)}, u32[]{:S(2)}, u32[]{:S(2)}) collective-permute-start(f32[128,512]{1,0:T(8,128)S(1)} %add_add_fusion.after), channel_id=1, source_target_pairs={{64,66},{65,67},{66,68},{67,69},{68,70},{69,71},{70,64},{71,65},{7... | collective-permute-start | bytes 786440 | tf_op jit(solution)/shard_map/ppermute | solution.py:755
  50.4 11.6 %collective-permute-start.13 = (f32[128,512]{1,0:T(8,128)S(1)}, f32[128,512]{1,0:T(8,128)S(1)}, u32[]{:S(2)}, u32[]{:S(2)}) collective-permute-start(f32[128,512]{1,0:T(8,128)S(1)} %get-tuple-element.96), channel_id=1, source_target_pairs={{0,1},{1,2},{2,3},{3,4},{4,5},{5,6},{6,7},{8,9},{9,10},{10,11},{11... | collective-permute-start | bytes 786440 | tf_op jit(solution)/shard_map/ppermute | solution.py:697
  55.4 7.7 %collective-permute-start.14 = (f32[128,512]{1,0:T(8,128)S(1)}, f32[128,512]{1,0:T(8,128)S(1)}, u32[]{:S(2)}, u32[]{:S(2)}) collective-permute-start(f32[128,512]{1,0:T(8,128)S(1)} %get-tuple-element.97), channel_id=1, source_target_pairs={{1,0},{2,1},{3,2},{4,3},{5,4},{6,5},{7,6},{9,8},{10,9},{11,10},{12... | collective-permute-start | bytes 786440 | tf_op jit(solution)/shard_map/ppermute | solution.py:698
  63.2 6.9 %collective-permute-start.15 = (f32[4,128,512]{2,1,0:T(8,128)S(1)}, f32[4,128,512]{2,1,0:T(8,128)S(1)}, u32[]{:S(2)}, u32[]{:S(2)}) collective-permute-start(f32[4,128,512]{2,1,0:T(8,128)S(1)} %pad_maximum_fusion.own), channel_id=1, source_target_pairs={{64,65},{65,64},{66,67},{67,66},{68,69},{69,68},{70,71},{71,70},{7... | collective-permute-start | bytes 3145736 | tf_op jit(solution)/shard_map/ppermute | solution.py:766
  65.5 4.6 %copy-start.1 = (f32[1,64,32,512]{3,2,1,0:T(8,128)S(1)}, f32[1,64,32,512]{3,2,1,0:T(8,128)}, u32[]{:S(2)}) copy-start(f32[1,64,32,512]{3,2,1,0:T(8,128)} %param.9) | copy-start | bytes 12582916

commit v11 on v10

--- a/solution.py
+++ b/solution.py
@@ -523,17 +523,16 @@
     )(*halos, tables, *edges, after)
 
 
-def split_table(pieces, table):
+def split_table(pieces, band, table, at):
     half = pieces.shape[1] // 2
     for k in range(pieces.shape[0]):
-        for band in range(2):
-            upper, lower = halves(pieces[k, band * half : (band + 1) * half])
-            table[2 * band, k * half : (k + 1) * half] = upper
-            table[2 * band + 1, k * half : (k + 1) * half] = lower
+        upper, lower = halves(pieces[k, band * half : (band + 1) * half])
+        table[at, k * half : (k + 1) * half] = upper
+        table[at + 1, k * half : (k + 1) * half] = lower
 
 
 def own_source_kernel(
-    one, added, stencil_high, stencil_low, edge_high, edge_low, own, sum_one, source, edge_source, table
+    one, added, stencil_high, stencil_low, edge_high, edge_low, own, sum_one, edge_source, table
 ):
     count_r, rows, width = one.shape
     columns = table.shape[1]
@@ -541,14 +540,13 @@
 
     @pl.when(in_product())
     def _():
-        split_table(own, table)
+        split_table(own, 0, table, 0)
 
         def body(n, carry):
             cut = pl.ds(pl.multiple_of(n * size, size), size)
             part = pl.ds(n * LAST, LAST)
             weights = (stencil_high[cut], stencil_low[cut])
             sum_one[part] = one[part] + product(weights, table[0], table[1]).reshape(LAST, rows, width)
-            source[cut] = product(weights, table[2], table[3])
             return carry
 
         lax.fori_loop(0, count_r // LAST, body, 0)
@@ -564,27 +562,25 @@
 
 
 def own_source(one, added, matrices, own):
-    count_r, rows, width = one.shape
-    points = count_r * rows
+    width = one.shape[2]
     return pl.pallas_call(
         own_source_kernel,
         in_specs=[VMEM] * 7,
-        out_specs=[VMEM] * 3,
+        out_specs=[VMEM] * 2,
         out_shape=[
             jax.ShapeDtypeStruct(one.shape, F32),
-            jax.ShapeDtypeStruct((points, width), F32),
             jax.ShapeDtypeStruct((matrices[2].shape[0], width), F32),
         ],
-        scratch_shapes=[pltpu.VMEM((4, own.shape[0] * own.shape[1] // 2, width), BF16)],
+        scratch_shapes=[pltpu.VMEM((2, own.shape[0] * own.shape[1] // 2, width), BF16)],
         compiler_params=pltpu.CompilerParams(vmem_limit_bytes=16 * MIB),
-        cost_estimate=pl.CostEstimate(flops=7_000_000_000, bytes_accessed=20 * MIB, transcendentals=0),
+        cost_estimate=pl.CostEstimate(flops=100_000_000_000, bytes_accessed=200 * MIB, transcendentals=0),
         name="own_source",
     )(one, added, *matrices, own)
 
 
 def last_kernel(
-    one, source, edge_source, packet, potential, tables, up, down, left, right, high, low,
-    stencil_high, stencil_low, edge_high, edge_low, other,
+    one, edge_source, packet, potential, tables, up, down, left, right, high, low,
+    own_high, own_low, stencil_high, stencil_low, edge_high, edge_low, own, other,
     earlier, latest, field, done, sides, table, ends, sems,
 ):
     count_r, rows, width = packet.shape
@@ -615,7 +611,9 @@
 
     @pl.when(is_product)
     def _():
-        split_table(other, table)
+        split_table(other, 0, table, 0)
+        split_table(own, 1, table, 2)
+        split_table(other, 1, table, 4)
         ends[...] = edge_source[...] + product(
             (edge_high[:, columns : 2 * columns], edge_low[:, columns : 2 * columns]), table[0], table[1]
         )
@@ -638,10 +636,12 @@
         lax.fori_loop(0, steps, add, 0)
 
         def body(n, carry):
-            matrix = weights(n)
+            mine, theirs = (own_high[cut(n)], own_low[cut(n)]), weights(n)
 
             def more(lanes):
-                return source[cut(n), lanes] + product(matrix, table[2, :, lanes], table[3, :, lanes])
+                return product(mine, table[2, :, lanes], table[3, :, lanes]) + product(
+                    theirs, table[4, :, lanes], table[5, :, lanes]
+                )
 
             advance(n, LAST, field, sides, packet, potential, tables, high, low, put, more)
             latests(n).start()
@@ -669,26 +669,26 @@
         latests(n).wait()
 
 
-def last_iteration(own_sums, packet, potential, tables, halos, high, low, matrices, other):
+def last_iteration(own_sums, packet, potential, tables, halos, high, low, matrices, pieces):
     count_r, rows, width = packet.shape
     steps = count_r // LAST
     return pl.pallas_call(
         last_kernel,
-        in_specs=[VMEM] * 17,
+        in_specs=[VMEM] * 19,
         out_specs=[HBM, HBM],
         out_shape=[jax.ShapeDtypeStruct(packet.shape, F32)] * 2,
         scratch_shapes=[
             pltpu.VMEM((count_r + 2 * HALO, rows, width), F32),
             pltpu.VMEM(packet.shape, F32),
             pltpu.VMEM((count_r, 8, width), F32),
-            pltpu.VMEM((4, other.shape[0] * other.shape[1] // 2, width), BF16),
+            pltpu.VMEM((6, pieces[0].shape[0] * pieces[0].shape[1] // 2, width), BF16),
             pltpu.VMEM((2 * HALO * (rows + count_r), width), F32),
             pltpu.SemaphoreType.DMA((2, steps)),
         ],
         compiler_params=pltpu.CompilerParams(vmem_limit_bytes=20 * MIB),
         cost_estimate=pl.CostEstimate(flops=14_000_000_000, bytes_accessed=36 * MIB, transcendentals=0),
         name="last_iteration",
-    )(*own_sums, packet, potential, tables, *halos, high, low, *matrices, other)
+    )(*own_sums, packet, potential, tables, *halos, high, low, *matrices, *pieces)
 
 
 def neighbours(axis, upward, downward):
@@ -761,15 +761,15 @@
     *edge_matrix, up, down, first, last, added = edge_matrix_and_ends
     rest[1], edge_matrix, first, last = lax.optimization_barrier((rest[1], edge_matrix, first, last))
     left, right = neighbours("row", last, first)
-    *rest, left, right = lax.optimization_barrier((*rest, left, right))
     own = jnp.stack([spread, rest[0], rest[2], rest[1]], axis=0)
     other = lax.ppermute(
         own, line, [(count_row + i, count_row + i + 1 - 2 * (i % CORES)) for i in range(count_row)]
     )
+    left, right, added = lax.optimization_barrier((left, right, added))
     own_sums = own_source(one, added, (*matrix[:2], *edge_matrix), own)
     other, own_sums = lax.optimization_barrier((other, own_sums))
     earlier, latest = last_iteration(
-        own_sums, near_packet, near_potential, tables, (up, down, left, right), high, low, (*matrix[2:], *edge_matrix), other
+        own_sums, near_packet, near_potential, tables, (up, down, left, right), high, low, (*matrix, *edge_matrix), (own, other)
     )
     return latest[None], earlier[None]
 

time: 82.9 us -> 80.8 us (0.975)
  the two profiles are of different devices: /device:TPU:43 before, /device:TPU:7 now
where the time goes in v11:
time: 80.8 us; the launch traced here: 79.3 us
  starting transfers between devices  38.2 us (47%)
  Pallas kernels  33.2 us (41%)
  waiting for transfers between devices  6.39 us (8%)
  between operations  0.96 us (1%)
    pallas_call x1, Pallas kernels, last_iteration(): pl.pallas_call(last_kernel, in_specs=[VMEM] * 19, out_specs=[HBM, HBM], o...  13.8 us
    ppermute x3, starting transfers between devices, neighbours(): lax.ppermute(upward, axis, [(i, i + 1) for i in range(count - 1)])  10.8 us
    ppermute x3, starting transfers between devices, around(): return lax.ppermute(spread, line, pairs)  10.2 us
    ppermute x3, starting transfers between devices, neighbours(): lax.ppermute(downward, axis, [(i + 1, i) for i in range(count - 1)])  9.63 us
    pallas_call x1, Pallas kernels, first_iteration(): pl.pallas_call(first_kernel, in_specs=[HBM, *[VMEM] * 9, ANY], out_specs=...  8.96 us
    pallas_call x1, Pallas kernels, stencil_matrix(): pl.pallas_call(stencil_kernel, in_specs=[VMEM, ANY], out_specs=[VMEM] * 4...  4.04 us
    ppermute x3, waiting for transfers between devices, around(): return lax.ppermute(spread, line, pairs)  3.6 us
    ppermute x4, starting transfers between devices, local(): crossed = [lax.ppermute(table, plane, [(start, relay)]) for relay in relays]  3.1 us
  transfers between devices with their start and end apart: 16, of which 2 were waited for; matrix products, arithmetic and copies ran while one was open for 0% of the time, Pallas kernels for 21%

profile of v11, /device:TPU:7, one launch (start us, length us, event | category | flops | bytes accessed | tf_op | source)
XLA Modules:
  0.0 79.3 jit_solution(6159358576621980884)
XLA Ops:
  0.6 2.6 %prepare.1 = (f32[32,128]{1,0:T(8,128)S(1)}, f32[32,128]{1,0:T(8,128)S(1)}, f32[176,512]{1,0:T(8,128)S(1)}, f32[176,512]{1,0:T(8,128)S(1)}, f32[10,32,128]{2,1,0...) custom-call(f32[64,32,512]{2,1,0:T(8,128)} %bitcast.24, f32[64,32,512]{2,1,0:T(8,128)} %bitcast.21, ...), custom_call_target="tpu_custom_call" | custom-call | flops 1000000 | bytes 6291456 | tf_op jit(solution)/shard_map/prepare/pallas_call | solution.py:236
  3.2 4.1 %collective-permute-start = (f32[176,512]{1,0:T(8,128)S(1)}, f32[176,512]{1,0:T(8,128)S(1)}, u32[]{:S(2)}, u32[]{:S(2)}) collective-permute-start(f32[176,512]{1,0:T(8,128)S(1)} %get-tuple-element.59), channel_id=1, source_target_pairs={{0,1},{1,2},{2,3},{3,4},{4,5},{5,6},{6,7},{8,9},{9,10},{10,11},{11... | collective-permute-start | bytes 1081352 | tf_op jit(solution)/shard_map/ppermute | solution.py:697
  7.3 1.9 %collective-permute-start.1 = (f32[176,512]{1,0:T(8,128)S(1)}, f32[176,512]{1,0:T(8,128)S(1)}, u32[]{:S(2)}, u32[]{:S(2)}) collective-permute-start(f32[176,512]{1,0:T(8,128)S(1)} %get-tuple-element.60.after), channel_id=1, source_target_pairs={{1,0},{2,1},{3,2},{4,3},{5,4},{6,5},{7,6},{9,8},{10,9},{11,10},{12... | collective-permute-start | bytes 1081352 | tf_op jit(solution)/shard_map/ppermute | solution.py:698
  9.3 4.0 %stencil_matrix.1 = (bf16[2048,256]{1,0:T(8,128)(2,1)S(1)}, bf16[2048,256]{1,0:T(8,128)(2,1)S(1)}, bf16[2048,256]{1,0:T(8,128)(2,1)S(1)}, bf16[2048,256]{1,0:T(8,128)(2,1)S(1)}) custom-call(f32[10,32,128]{2,1,0:T(8,128)S(1)} %get-tuple-element.58.tables, f32[176,512]{1,0:T(8,128)S(1)} %get-tuple-element.60.after), custom_call_target="tpu_custom_call" | custom-call | flops 15000000 | bytes 6291456 | tf_op jit(solution)/shard_map/stencil_matrix/pallas_call | solution.py:431
  13.3 0.0 collective-permute-done.left
  13.3 2.8 %collective-permute-done.1.right = f32[176,512]{1,0:T(8,128)S(1)} collective-permute-done((f32[176,512]{1,0:T(8,128)S(1)}, f32[176,512]{1,0:T(8,128)S(1)}, u32[]{:S(2)}, u32[]{:S(2)}) %collective-permute-start.1) | collective-permute-done | bytes 360480 | tf_op jit(solution)/shard_map/ppermute | solution.py:698
  16.1 0.0 copy-start
  16.1 0.0 copy-start.2
  16.1 0.8 %collective-permute-start.5 = (f32[128,512]{1,0:T(8,128)S(1)}, f32[128,512]{1,0:T(8,128)S(1)}, u32[]{:S(2)}, u32[]{:S(2)}) collective-permute-start(f32[128,512]{1,0:T(8,128)S(1)} %both_bands.1.after), channel_id=1, source_target_pairs={{56,32},{57,33},{58,34},{59,35},{60,36},{61,37},{62,38},{63,39}} | collective-permute-start | bytes 786440 | tf_op jit(solution)/shard_map/ppermute | solution.py:732
  16.9 0.8 %collective-permute-start.4 = (f32[128,512]{1,0:T(8,128)S(1)}, f32[128,512]{1,0:T(8,128)S(1)}, u32[]{:S(2)}, u32[]{:S(2)}) collective-permute-start(f32[128,512]{1,0:T(8,128)S(1)} %both_bands.1.after), channel_id=1, source_target_pairs={{56,48},{57,49},{58,50},{59,51},{60,52},{61,53},{62,54},{63,55}} | collective-permute-start | bytes 786440 | tf_op jit(solution)/shard_map/ppermute | solution.py:732
  17.7 0.8 %collective-permute-start.3 = (f32[128,512]{1,0:T(8,128)S(1)}, f32[128,512]{1,0:T(8,128)S(1)}, u32[]{:S(2)}, u32[]{:S(2)}) collective-permute-start(f32[128,512]{1,0:T(8,128)S(1)} %both_bands.1.after), channel_id=1, source_target_pairs={{56,120},{57,121},{58,122},{59,123},{60,124},{61,125},{62,126},{63... | collective-permute-start | bytes 786440 | tf_op jit(solution)/shard_map/ppermute | solution.py:732
  18.6 0.7 collective-permute-start.2
  19.2 0.0 copy-done
  19.3 0.3 copy-done.2
  19.5 9.0 %first_iteration.1 = (f32[64,32,512]{2,1,0:T(8,128)S(1)}, f32[160,512]{1,0:T(8,128)S(1)}, f32[160,512]{1,0:T(8,128)S(1)}, f32[128,512]{1,0:T(8,128)S(1)}, f32[128,512]{1,0:T(8,128)S(1)}) custom-call(f32[64,32,512]{2,1,0:T(8,128)} %bitcast.26, f32[64,32,512]{2,1,0:T(8,128)S(1)} %bitcast.23, f32[64,32,512]{2,1,0:T(8,128)S(1)} %bitcast.30, ...), custom_call_target="tpu_custom_call" | custom-call | flops 7000000000 | bytes 20971520 | tf_op jit(solution)/shard_map/first_iteration/pallas_call | solution.py:361
  28.5 0.0 collective-permute-done.5
  28.5 0.0 collective-permute-done.4
  28.5 0.0 collective-permute-done.3
  28.5 0.0 collective-permute-done.2
  28.5 0.1 add_add_fusion.1
  28.6 1.3 %collective-permute-start.7 = (f32[128,512]{1,0:T(8,128)S(1)}, f32[128,512]{1,0:T(8,128)S(1)}, u32[]{:S(2)}, u32[]{:S(2)}) collective-permute-start(f32[128,512]{1,0:T(8,128)S(1)} %add_add_fusion.1), channel_id=1, source_target_pairs={{32,96},{48,112},{33,97},{49,113},{34,98},{50,114},{35,99},{51,115... | collective-permute-start | bytes 786440 | tf_op jit(solution)/shard_map/ppermute | solution.py:741
  29.9 0.7 collective-permute-start.6
  30.6 3.2 %collective-permute-start.11 = (f32[160,512]{1,0:T(8,128)S(1)}, f32[160,512]{1,0:T(8,128)S(1)}, u32[]{:S(2)}, u32[]{:S(2)}) collective-permute-start(f32[160,512]{1,0:T(8,128)S(1)} %get-tuple-element.83.bottom), channel_id=1, source_target_pairs={{0,8},{8,16},{16,24},{24,32},{32,40},{40,48},{48,56},{1,9},{9,17},... | collective-permute-start | bytes 983048 | tf_op jit(solution)/shard_map/ppermute | solution.py:697
  33.8 5.8 %collective-permute-start.12 = (f32[160,512]{1,0:T(8,128)S(1)}, f32[160,512]{1,0:T(8,128)S(1)}, u32[]{:S(2)}, u32[]{:S(2)}) collective-permute-start(f32[160,512]{1,0:T(8,128)S(1)} %get-tuple-element.84.top), channel_id=1, source_target_pairs={{8,0},{16,8},{24,16},{32,24},{40,32},{48,40},{56,48},{9,1},{17,9},... | collective-permute-start | bytes 983048 | tf_op jit(solution)/shard_map/ppermute | solution.py:698
  39.6 0.0 collective-permute-done.7
  39.6 0.0 collective-permute-done.6
  39.7 0.1 add_add_fusion.after
  39.7 1.9 %collective-permute-start.10 = (f32[128,512]{1,0:T(8,128)S(1)}, f32[128,512]{1,0:T(8,128)S(1)}, u32[]{:S(2)}, u32[]{:S(2)}) collective-permute-start(f32[128,512]{1,0:T(8,128)S(1)} %add_add_fusion.after), channel_id=1, source_target_pairs={{64,70},{65,71},{66,64},{67,65},{68,66},{69,67},{70,68},{71,69},{7... | collective-permute-start | bytes 786440 | tf_op jit(solution)/shard_map/ppermute | solution.py:755
  41.6 5.5 %collective-permute-start.9 = (f32[128,512]{1,0:T(8,128)S(1)}, f32[128,512]{1,0:T(8,128)S(1)}, u32[]{:S(2)}, u32[]{:S(2)}) collective-permute-start(f32[128,512]{1,0:T(8,128)S(1)} %add_add_fusion.after), channel_id=1, source_target_pairs={{64,68},{65,69},{66,70},{67,71},{68,64},{69,65},{70,66},{71,67},{7... | collective-permute-start | bytes 786440 | tf_op jit(solution)/shard_map/ppermute | solution.py:755
  47.1 2.8 %collective-permute-start.8 = (f32[128,512]{1,0:T(8,128)S(1)}, f32[128,512]{1,0:T(8,128)S(1)}, u32[]{:S(2)}, u32[]{:S(2)}) collective-permute-start(f32[128,512]{1,0:T(8,128)S(1)} %add_add_fusion.after), channel_id=1, source_target_pairs={{64,66},{65,67},{66,68},{67,69},{68,70},{69,71},{70,64},{71,65},{7... | collective-permute-start | bytes 786440 | tf_op jit(solution)/shard_map/ppermute | solution.py:755
  49.9 0.0 collective-permute-done.11.up
  49.9 0.0 collective-permute-done.12.down
  49.9 0.9 %finish_edges.1 = (bf16[384,512]{1,0:T(8,128)(2,1)S(1)}, bf16[384,512]{1,0:T(8,128)(2,1)S(1)}, f32[64,512]{1,0:T(8,128)S(1)}, f32[64,512]{1,0:T(8,128)S(1)}, f32...) custom-call(f32[160,512]{1,0:T(8,128)S(1)} %collective-permute-done.11.up, ...), custom_call_target="tpu_custom_call" | custom-call | flops 2000000 | bytes 3145728 | tf_op jit(solution)/shard_map/finish_edges/pallas_call | solution.py:510
  50.9 0.0 collective-permute-done.10
  50.9 3.5 %collective-permute-start.14 = (f32[128,512]{1,0:T(8,128)S(1)}, f32[128,512]{1,0:T(8,128)S(1)}, u32[]{:S(2)}, u32[]{:S(2)}) collective-permute-start(f32[128,512]{1,0:T(8,128)S(1)} %get-tuple-element.93), channel_id=1, source_target_pairs={{0,1},{1,2},{2,3},{3,4},{4,5},{5,6},{6,7},{8,9},{9,10},{10,11},{11... | collective-permute-start | bytes 786440 | tf_op jit(solution)/shard_map/ppermute | solution.py:697
  54.4 1.9 %collective-permute-start.15 = (f32[128,512]{1,0:T(8,128)S(1)}, f32[128,512]{1,0:T(8,128)S(1)}, u32[]{:S(2)}, u32[]{:S(2)}) collective-permute-start(f32[128,512]{1,0:T(8,128)S(1)} %get-tuple-element.94), channel_id=1, source_target_pairs={{1,0},{2,1},{3,2},{4,3},{5,4},{6,5},{7,6},{9,8},{10,9},{11,10},{12... | collective-permute-start | bytes 786440 | tf_op jit(solution)/shard_map/ppermute | solution.py:698
  56.3 0.0 collective-permute-done.9
  56.3 3.6 %collective-permute-done.8 = f32[128,512]{1,0:T(8,128)S(1)} collective-permute-done((f32[128,512]{1,0:T(8,128)S(1)}, f32[128,512]{1,0:T(8,128)S(1)}, u32[]{:S(2)}, u32[]{:S(2)}) %collective-permute-start.8) | collective-permute-done | bytes 262176 | tf_op jit(solution)/shard_map/ppermute | solution.py:755
  59.9 0.1 pad_maximum_fusion.own
  60.0 2.5 %collective-permute-start.13 = (f32[4,128,512]{2,1,0:T(8,128)S(1)}, f32[4,128,512]{2,1,0:T(8,128)S(1)}, u32[]{:S(2)}, u32[]{:S(2)}) collective-permute-start(f32[4,128,512]{2,1,0:T(8,128)S(1)} %pad_maximum_fusion.own), channel_id=1, source_target_pairs={{64,65},{65,64},{66,67},{67,66},{68,69},{69,68},{70,71},{71,70},{7... | collective-permute-start | bytes 3145736 | tf_op jit(solution)/shard_map/ppermute | solution.py:765
  62.5 0.0 collective-permute-done.14.left
  62.5 0.0 collective-permute-done.15.right
  62.6 0.0 copy-start.1
  62.6 2.9 %own_source.1 = (f32[64,32,512]{2,1,0:T(8,128)S(1)}, f32[384,512]{1,0:T(8,128)S(1)}) custom-call(f32[64,32,512]{2,1,0:T(8,128)S(1)} %get-tuple-element.92.one, f32[4,32,512]{2,1,0:T(8,128)S(1)} %get-tuple-element.96.added, bf16[2048,256]{1,0:T(8,128)(2,1)S(1)} %get-tuple-element.97.stencil_high.own_high, ...), custom_call_target="tpu_custom_call" | custom-call | flops 99999997952 | bytes 209715200 | tf_op jit(solution)/shard_map/own_source/pallas_call | solution.py:566
  65.4 0.0 collective-permute-done.13.other
  65.4 0.0 copy-done.1
  65.4 13.8 %last_iteration.1 = (f32[64,32,512]{2,1,0:T(8,128)}, f32[64,32,512]{2,1,0:T(8,128)}) custom-call(f32[64,32,512]{2,1,0:T(8,128)S(1)} %get-tuple-element.103.one, f32[384,512]{1,0:T(8,128)S(1)} %get-tuple-element.104.edge_source, f32[64,32,512]{2,1,0:T(8,128)S(1)} %bitcast.27, f32[64,32,512]{2,1,0:T(8,128)S(1)} %bitcast.31, ...), custom_call_target="tpu_custom_call" | custom-call | flops 14000000000 | bytes 37748736 | tf_op jit(solution)/shard_map/last_iteration/pallas_call | solution.py:675
  (1 shorter events, 0.0 us)
Async XLA Ops:
  3.2 10.1 %collective-permute-start = (f32[176,512]{1,0:T(8,128)S(1)}, f32[176,512]{1,0:T(8,128)S(1)}, u32[]{:S(2)}, u32[]{:S(2)}) collective-permute-start(f32[176,512]{1,0:T(8,128)S(1)} %get-tuple-element.59), channel_id=1, source_target_pairs={{0,1},{1,2},{2,3},{3,4},{4,5},{5,6},{6,7},{8,9},{9,10},{10,11},{11... | collective-permute-start | bytes 1081352 | tf_op jit(solution)/shard_map/ppermute | solution.py:697
  7.3 8.7 %collective-permute-start.1 = (f32[176,512]{1,0:T(8,128)S(1)}, f32[176,512]{1,0:T(8,128)S(1)}, u32[]{:S(2)}, u32[]{:S(2)}) collective-permute-start(f32[176,512]{1,0:T(8,128)S(1)} %get-tuple-element.60.after), channel_id=1, source_target_pairs={{1,0},{2,1},{3,2},{4,3},{5,4},{6,5},{7,6},{9,8},{10,9},{11,10},{12... | collective-permute-start | bytes 1081352 | tf_op jit(solution)/shard_map/ppermute | solution.py:698
  16.1 3.2 %copy-start = (f32[1,64,32,512]{3,2,1,0:T(8,128)S(1)}, f32[1,64,32,512]{3,2,1,0:T(8,128)}, u32[]{:S(2)}) copy-start(f32[1,64,32,512]{3,2,1,0:T(8,128)} %param.10) | copy-start | bytes 12582916
  16.1 3.5 %copy-start.2 = (f32[1,64,32,512]{3,2,1,0:T(8,128)S(1)}, f32[1,64,32,512]{3,2,1,0:T(8,128)}, u32[]{:S(2)}) copy-start(f32[1,64,32,512]{3,2,1,0:T(8,128)} %param.11) | copy-start | bytes 12582916
  16.1 12.4 %collective-permute-start.5 = (f32[128,512]{1,0:T(8,128)S(1)}, f32[128,512]{1,0:T(8,128)S(1)}, u32[]{:S(2)}, u32[]{:S(2)}) collective-permute-start(f32[128,512]{1,0:T(8,128)S(1)} %both_bands.1.after), channel_id=1, source_target_pairs={{56,32},{57,33},{58,34},{59,35},{60,36},{61,37},{62,38},{63,39}} | collective-permute-start | bytes 786440 | tf_op jit(solution)/shard_map/ppermute | solution.py:732
  16.9 11.6 %collective-permute-start.4 = (f32[128,512]{1,0:T(8,128)S(1)}, f32[128,512]{1,0:T(8,128)S(1)}, u32[]{:S(2)}, u32[]{:S(2)}) collective-permute-start(f32[128,512]{1,0:T(8,128)S(1)} %both_bands.1.after), channel_id=1, source_target_pairs={{56,48},{57,49},{58,50},{59,51},{60,52},{61,53},{62,54},{63,55}} | collective-permute-start | bytes 786440 | tf_op jit(solution)/shard_map/ppermute | solution.py:732
  17.7 10.8 %collective-permute-start.3 = (f32[128,512]{1,0:T(8,128)S(1)}, f32[128,512]{1,0:T(8,128)S(1)}, u32[]{:S(2)}, u32[]{:S(2)}) collective-permute-start(f32[128,512]{1,0:T(8,128)S(1)} %both_bands.1.after), channel_id=1, source_target_pairs={{56,120},{57,121},{58,122},{59,123},{60,124},{61,125},{62,126},{63... | collective-permute-start | bytes 786440 | tf_op jit(solution)/shard_map/ppermute | solution.py:732
  18.6 10.0 %collective-permute-start.2 = (f32[128,512]{1,0:T(8,128)S(1)}, f32[128,512]{1,0:T(8,128)S(1)}, u32[]{:S(2)}, u32[]{:S(2)}) collective-permute-start(f32[128,512]{1,0:T(8,128)S(1)} %both_bands.1.after), channel_id=1, source_target_pairs={{56,88},{57,89},{58,90},{59,91},{60,92},{61,93},{62,94},{63,95}} | collective-permute-start | bytes 786440 | tf_op jit(solution)/shard_map/ppermute | solution.py:732
  28.6 11.0 %collective-permute-start.7 = (f32[128,512]{1,0:T(8,128)S(1)}, f32[128,512]{1,0:T(8,128)S(1)}, u32[]{:S(2)}, u32[]{:S(2)}) collective-permute-start(f32[128,512]{1,0:T(8,128)S(1)} %add_add_fusion.1), channel_id=1, source_target_pairs={{32,96},{48,112},{33,97},{49,113},{34,98},{50,114},{35,99},{51,115... | collective-permute-start | bytes 786440 | tf_op jit(solution)/shard_map/ppermute | solution.py:741
  29.9 9.7 %collective-permute-start.6 = (f32[128,512]{1,0:T(8,128)S(1)}, f32[128,512]{1,0:T(8,128)S(1)}, u32[]{:S(2)}, u32[]{:S(2)}) collective-permute-start(f32[128,512]{1,0:T(8,128)S(1)} %add_add_fusion.1), channel_id=1, source_target_pairs={{32,64},{48,80},{88,72},{120,104},{33,65},{49,81},{89,73},{121,105... | collective-permute-start | bytes 786440 | tf_op jit(solution)/shard_map/ppermute | solution.py:741
  30.6 19.3 %collective-permute-start.11 = (f32[160,512]{1,0:T(8,128)S(1)}, f32[160,512]{1,0:T(8,128)S(1)}, u32[]{:S(2)}, u32[]{:S(2)}) collective-permute-start(f32[160,512]{1,0:T(8,128)S(1)} %get-tuple-element.83.bottom), channel_id=1, source_target_pairs={{0,8},{8,16},{16,24},{24,32},{32,40},{40,48},{48,56},{1,9},{9,17},... | collective-permute-start | bytes 983048 | tf_op jit(solution)/shard_map/ppermute | solution.py:697
  33.8 16.1 %collective-permute-start.12 = (f32[160,512]{1,0:T(8,128)S(1)}, f32[160,512]{1,0:T(8,128)S(1)}, u32[]{:S(2)}, u32[]{:S(2)}) collective-permute-start(f32[160,512]{1,0:T(8,128)S(1)} %get-tuple-element.84.top), channel_id=1, source_target_pairs={{8,0},{16,8},{24,16},{32,24},{40,32},{48,40},{56,48},{9,1},{17,9},... | collective-permute-start | bytes 983048 | tf_op jit(solution)/shard_map/ppermute | solution.py:698
  39.7 11.2 %collective-permute-start.10 = (f32[128,512]{1,0:T(8,128)S(1)}, f32[128,512]{1,0:T(8,128)S(1)}, u32[]{:S(2)}, u32[]{:S(2)}) collective-permute-start(f32[128,512]{1,0:T(8,128)S(1)} %add_add_fusion.after), channel_id=1, source_target_pairs={{64,70},{65,71},{66,64},{67,65},{68,66},{69,67},{70,68},{71,69},{7... | collective-permute-start | bytes 786440 | tf_op jit(solution)/shard_map/ppermute | solution.py:755
  41.6 14.7 %collective-permute-start.9 = (f32[128,512]{1,0:T(8,128)S(1)}, f32[128,512]{1,0:T(8,128)S(1)}, u32[]{:S(2)}, u32[]{:S(2)}) collective-permute-start(f32[128,512]{1,0:T(8,128)S(1)} %add_add_fusion.after), channel_id=1, source_target_pairs={{64,68},{65,69},{66,70},{67,71},{68,64},{69,65},{70,66},{71,67},{7... | collective-permute-start | bytes 786440 | tf_op jit(solution)/shard_map/ppermute | solution.py:755
  47.1 12.8 %collective-permute-start.8 = (f32[128,512]{1,0:T(8,128)S(1)}, f32[128,512]{1,0:T(8,128)S(1)}, u32[]{:S(2)}, u32[]{:S(2)}) collective-permute-start(f32[128,512]{1,0:T(8,128)S(1)} %add_add_fusion.after), channel_id=1, source_target_pairs={{64,66},{65,67},{66,68},{67,69},{68,70},{69,71},{70,64},{71,65},{7... | collective-permute-start | bytes 786440 | tf_op jit(solution)/shard_map/ppermute | solution.py:755
  50.9 11.7 %collective-permute-start.14 = (f32[128,512]{1,0:T(8,128)S(1)}, f32[128,512]{1,0:T(8,128)S(1)}, u32[]{:S(2)}, u32[]{:S(2)}) collective-permute-start(f32[128,512]{1,0:T(8,128)S(1)} %get-tuple-element.93), channel_id=1, source_target_pairs={{0,1},{1,2},{2,3},{3,4},{4,5},{5,6},{6,7},{8,9},{9,10},{10,11},{11... | collective-permute-start | bytes 786440 | tf_op jit(solution)/shard_map/ppermute | solution.py:697
  54.4 8.2 %collective-permute-start.15 = (f32[128,512]{1,0:T(8,128)S(1)}, f32[128,512]{1,0:T(8,128)S(1)}, u32[]{:S(2)}, u32[]{:S(2)}) collective-permute-start(f32[128,512]{1,0:T(8,128)S(1)} %get-tuple-element.94), channel_id=1, source_target_pairs={{1,0},{2,1},{3,2},{4,3},{5,4},{6,5},{7,6},{9,8},{10,9},{11,10},{12... | collective-permute-start | bytes 786440 | tf_op jit(solution)/shard_map/ppermute | solution.py:698
  60.0 5.4 %collective-permute-start.13 = (f32[4,128,512]{2,1,0:T(8,128)S(1)}, f32[4,128,512]{2,1,0:T(8,128)S(1)}, u32[]{:S(2)}, u32[]{:S(2)}) collective-permute-start(f32[4,128,512]{2,1,0:T(8,128)S(1)} %pad_maximum_fusion.own), channel_id=1, source_target_pairs={{64,65},{65,64},{66,67},{67,66},{68,69},{69,68},{70,71},{71,70},{7... | collective-permute-start | bytes 3145736 | tf_op jit(solution)/shard_map/ppermute | solution.py:765
  62.6 2.9 %copy-start.1 = (f32[1,64,32,512]{3,2,1,0:T(8,128)S(1)}, f32[1,64,32,512]{3,2,1,0:T(8,128)}, u32[]{:S(2)}) copy-start(f32[1,64,32,512]{3,2,1,0:T(8,128)} %param.9) | copy-start | bytes 12582916

commit v12 on v11

--- a/solution.py
+++ b/solution.py
@@ -164,9 +164,9 @@
 
 
 def prepare_kernel(
-    packet, previous, potential, rotation, damping, absorber, index, weight, angular,
-    upper, lower, first, last, tables, high, low,
-    sides, others, factors, masks, indices, weights, matrix, sems,
+    packet, previous, potential, rotation, damping, absorber, index, weight,
+    upper, lower, first, last, tables,
+    sides, others, factors, masks, indices, weights, sems,
 ):
     count_r, rows, width = packet.shape
     small = [
@@ -181,7 +181,6 @@
         pltpu.make_async_copy(packet.at[:, pl.ds(rows - 8, 8)], sides.at[1], sems.at[6]),
         pltpu.make_async_copy(previous.at[pl.ds(count_r - BAND, BAND)], others.at[0], sems.at[7]),
         pltpu.make_async_copy(potential.at[pl.ds(count_r - BAND, BAND)], others.at[1], sems.at[8]),
-        pltpu.make_async_copy(angular, matrix, sems.at[9]),
     ]
     for copy in small + copies:
         copy.start()
@@ -225,19 +224,17 @@
         for k in range(count_r):
             for r in range(HALO):
                 out[r * count_r + k : r * count_r + k + 1] = sides[n, k, near + r : near + r + 1]
-    high[...], low[...] = halves(matrix[...])
-
-
-def prepare(packet, previous, potential, rotation, damping, absorber, index, weight, angular):
+
+
+def prepare(packet, previous, potential, rotation, damping, absorber, index, weight):
     count_r, rows, width = packet.shape
     ends = jax.ShapeDtypeStruct((rows, LANES), F32)
     sides = jax.ShapeDtypeStruct((HALO * count_r + EXTRA + OFBAND, width), F32)
-    part = jax.ShapeDtypeStruct(angular.shape, BF16)
     return pl.pallas_call(
         prepare_kernel,
-        in_specs=[HBM] * 9,
-        out_specs=[VMEM] * 7,
-        out_shape=[ends, ends, sides, sides, jax.ShapeDtypeStruct((TABLES, rows, LANES), F32), part, part],
+        in_specs=[HBM] * 8,
+        out_specs=[VMEM] * 5,
+        out_shape=[ends, ends, sides, sides, jax.ShapeDtypeStruct((TABLES, rows, LANES), F32)],
         scratch_shapes=[
             pltpu.VMEM((2, count_r, 8, width), F32),
             pltpu.VMEM((2, BAND, rows, width), F32),
@@ -245,13 +242,12 @@
             pltpu.VMEM((rows, count_r), jnp.int32),
             pltpu.VMEM((STENCILS, rows, count_r), jnp.int32),
             pltpu.VMEM((STENCILS, rows, count_r), F32),
-            pltpu.VMEM(angular.shape, F32),
-            pltpu.SemaphoreType.DMA((10,)),
+            pltpu.SemaphoreType.DMA((9,)),
         ],
         compiler_params=pltpu.CompilerParams(vmem_limit_bytes=16 * MIB),
         cost_estimate=pl.CostEstimate(flops=1_000_000, bytes_accessed=6 * MIB, transcendentals=0),
         name="prepare",
-    )(packet, previous, potential, rotation, damping, absorber, index, weight, angular)
+    )(packet, previous, potential, rotation, damping, absorber, index, weight)
 
 
 def put_sides(sides, left, right, count_r, left_more=None, right_more=None):
@@ -401,11 +397,12 @@
         low[pl.ds(at, rows), tile : tile + LANES] = lower
 
 
-def stencil_kernel(tables, after, high, low, other_high, other_low):
+def stencil_kernel(tables, angular, after, high, low, other_high, other_low, angular_high, angular_low):
     _, rows, _ = tables.shape
     count_r = high.shape[0] // rows
     group = 8
     half = high.shape[1]
+    angular_high[...], angular_low[...] = halves(angular[...])
 
     @pl.when(in_product())
     def _():
@@ -425,18 +422,18 @@
         lax.fori_loop(0, count_r // group, body, 0)
 
 
-def stencil_matrix(tables, count_r, columns, after):
+def matrices_of(tables, angular, count_r, columns, after):
     rows = tables.shape[1]
     points = jax.ShapeDtypeStruct((count_r * rows, columns // CORES), BF16)
     return pl.pallas_call(
         stencil_kernel,
-        in_specs=[VMEM, ANY],
-        out_specs=[VMEM] * 4,
-        out_shape=[points] * 4,
+        in_specs=[VMEM, VMEM, ANY],
+        out_specs=[VMEM] * 6,
+        out_shape=[points] * 4 + [jax.ShapeDtypeStruct(angular.shape, BF16)] * 2,
         compiler_params=pltpu.CompilerParams(vmem_limit_bytes=16 * MIB),
         cost_estimate=pl.CostEstimate(flops=15_000_000, bytes_accessed=6 * MIB, transcendentals=0),
         name="stencil_matrix",
-    )(tables, after)
+    )(tables, angular, after)
 
 
 def edge_kernel(
@@ -708,19 +705,19 @@
     rotation, damping, absorber = (jnp.swapaxes(value, 0, 1) for value in (rotation, damping, absorber))
     stencil_index, stencil_weight = (jnp.swapaxes(value, 1, 2) for value in (stencil_index, stencil_weight))
     near_packet, near_previous, near_potential = packet, previous, potential
-    packet, previous, potential, rotation, damping, absorber, stencil_index, stencil_weight, angular = (
+    packet, previous, potential, rotation, damping, absorber, stencil_index, stencil_weight = (
         in_hbm(value)
         for value in (
-            packet, previous, potential, rotation, damping, absorber, stencil_index, stencil_weight, angular
+            packet, previous, potential, rotation, damping, absorber, stencil_index, stencil_weight
         )
     )
 
-    upper, lower, first, last, tables, high, low = prepare(
-        packet, previous, potential, rotation, damping, absorber, stencil_index, stencil_weight, angular
+    upper, lower, first, last, tables = prepare(
+        packet, previous, potential, rotation, damping, absorber, stencil_index, stencil_weight
     )
     columns = count_row * rows * BAND
     left, right = neighbours("row", last, first)
-    matrix = stencil_matrix(tables, count_r, columns, first)
+    *matrix, high, low = matrices_of(tables, angular, count_r, columns, first)
     left, right, matrix = lax.optimization_barrier((left, right, matrix))
     table = bands(packet, previous, potential, tables, left, right, high, low)
 
@@ -738,7 +735,7 @@
     near = [(low_side, count_rr), (high_side, count_rr + half - 2)]
     near += [(count_rr + half - 1, count_rr + half - 3), (count_rr + start, count_rr + start - 2)]
     opposite = [(low_side, count_rr + low_side), (high_side, count_rr + high_side)]
-    arrived = [lax.ppermute(piece, plane, near), lax.ppermute(piece, plane, opposite)]
+    arrived = [lax.ppermute(piece, plane, opposite), lax.ppermute(piece, plane, near)]
     top, bottom, first, last = edges
     top, bottom, piece = lax.optimization_barrier((top, bottom, piece))
     up, down = neighbours("rr", bottom, top)
@@ -759,7 +756,7 @@
         (up, down, left, right), tables, (top, bottom, first, last), rows, count_r, columns, spread
     )
     *edge_matrix, up, down, first, last, added = edge_matrix_and_ends
-    rest[1], edge_matrix, first, last = lax.optimization_barrier((rest[1], edge_matrix, first, last))
+    rest[2], edge_matrix, first, last = lax.optimization_barrier((rest[2], edge_matrix, first, last))
     left, right = neighbours("row", last, first)
     own = jnp.stack([spread, rest[0], rest[2], rest[1]], axis=0)
     other = lax.ppermute(

time: 80.8 us -> 79.9 us (0.989)
    ppermute x3, waiting for transfers between devices: 3.6 us -> 2.15 us  [around(): return lax.ppermute(spread, line, pairs)]
    ppermute x3, waiting for transfers between devices: 2.77 us -> 3.93 us  [neighbours(): lax.ppermute(downward, axis, [(i + 1, i) for i in range(count - 1)])]
  transfers between devices with their start and end apart: 16 -> 16, of which waited for: 2 -> 4; matrix products, arithmetic and copies ran while one was open for 0% -> 0% of each run, Pallas kernels for 21% -> 21%
where the time goes in v12:
time: 79.9 us; the launch traced here: 78.9 us
  starting transfers between devices  38.5 us (48%)
  Pallas kernels  32.9 us (41%)
  waiting for transfers between devices  6.11 us (8%)
  between operations  0.95 us (1%)
    pallas_call x1, Pallas kernels, last_iteration(): pl.pallas_call(last_kernel, in_specs=[VMEM] * 19, out_specs=[HBM, HBM], o...  13.8 us
    ppermute x3, starting transfers between devices, around(): return lax.ppermute(spread, line, pairs)  10.8 us
    ppermute x3, starting transfers between devices, neighbours(): lax.ppermute(upward, axis, [(i, i + 1) for i in range(count - 1)])  10.4 us
    ppermute x3, starting transfers between devices, neighbours(): lax.ppermute(downward, axis, [(i + 1, i) for i in range(count - 1)])  9.61 us
    pallas_call x1, Pallas kernels, first_iteration(): pl.pallas_call(first_kernel, in_specs=[HBM, *[VMEM] * 9, ANY], out_specs=...  8.97 us
    pallas_call x1, Pallas kernels, matrices_of(): pl.pallas_call(stencil_kernel, in_specs=[VMEM, VMEM, ANY], out_specs=[VME...  4.17 us
    ppermute x3, waiting for transfers between devices, neighbours(): lax.ppermute(downward, axis, [(i + 1, i) for i in range(count - 1)])  3.93 us
    ppermute x4, starting transfers between devices, local(): crossed = [lax.ppermute(table, plane, [(start, relay)]) for relay in relays]  3.1 us
  transfers between devices with their start and end apart: 16, of which 4 were waited for; matrix products, arithmetic and copies ran while one was open for 0% of the time, Pallas kernels for 21%

profile of v12, /device:TPU:7, one launch (start us, length us, event | category | flops | bytes accessed | tf_op | source)
XLA Modules:
  0.0 78.9 jit_solution(12849944345639829880)
XLA Ops:
  0.6 0.0 copy-start.3
  0.6 2.1 %prepare.1 = (f32[32,128]{1,0:T(8,128)S(1)}, f32[32,128]{1,0:T(8,128)S(1)}, f32[176,512]{1,0:T(8,128)S(1)}, f32[176,512]{1,0:T(8,128)S(1)}, f32[10,32,128]{2,1,0:T(8,128)S(1)}) custom-call(f32[64,32,512]{2,1,0:T(8,128)} %bitcast.24, f32[64,32,512]{2,1,0:T(8,128)} %bitcast.21, f32[64,32,512]{2,1,0:T(8,128)} %bitcast.28, f32[32,64]{1,0:T(8,128)} %bitcast.39, ...), custom_call_target="tpu_custom_call" | custom-call | flops 1000000 | bytes 6291456 | tf_op jit(solution)/shard_map/prepare/pallas_call | solution.py:233
  2.8 4.1 %collective-permute-start = (f32[176,512]{1,0:T(8,128)S(1)}, f32[176,512]{1,0:T(8,128)S(1)}, u32[]{:S(2)}, u32[]{:S(2)}) collective-permute-start(f32[176,512]{1,0:T(8,128)S(1)} %get-tuple-element.59), channel_id=1, source_target_pairs={{0,1},{1,2},{2,3},{3,4},{4,5},{5,6},{6,7},{8,9},{9,10},{10,11},{11... | collective-permute-start | bytes 1081352 | tf_op jit(solution)/shard_map/ppermute | solution.py:694
  6.9 1.9 %collective-permute-start.1 = (f32[176,512]{1,0:T(8,128)S(1)}, f32[176,512]{1,0:T(8,128)S(1)}, u32[]{:S(2)}, u32[]{:S(2)}) collective-permute-start(f32[176,512]{1,0:T(8,128)S(1)} %get-tuple-element.60.after), channel_id=1, source_target_pairs={{1,0},{2,1},{3,2},{4,3},{5,4},{6,5},{7,6},{9,8},{10,9},{11,10},{12... | collective-permute-start | bytes 1081352 | tf_op jit(solution)/shard_map/ppermute | solution.py:695
  8.8 0.0 copy-done.3
  8.8 4.2 %stencil_matrix.1 = (bf16[2048,256]{1,0:T(8,128)(2,1)S(1)}, bf16[2048,256]{1,0:T(8,128)(2,1)S(1)}, bf16[2048,256]{1,0:T(8,128)(2,1)S(1)}, bf16[2048,256]{1,0:T(8...) custom-call(f32[10,32,128]{2,1,0:T(8,128)S(1)} %get-tuple-element.58.tables, ...), custom_call_target="tpu_custom_call" | custom-call | flops 15000000 | bytes 6291456 | tf_op jit(solution)/shard_map/stencil_matrix/pallas_call | solution.py:428
  13.0 0.0 collective-permute-done.left
  13.0 2.6 %collective-permute-done.1.right = f32[176,512]{1,0:T(8,128)S(1)} collective-permute-done((f32[176,512]{1,0:T(8,128)S(1)}, f32[176,512]{1,0:T(8,128)S(1)}, u32[]{:S(2)}, u32[]{:S(2)}) %collective-permute-start.1) | collective-permute-done | bytes 360480 | tf_op jit(solution)/shard_map/ppermute | solution.py:695
  15.6 0.0 copy-start
  15.6 0.0 copy-start.2
  15.7 0.8 %collective-permute-start.5 = (f32[128,512]{1,0:T(8,128)S(1)}, f32[128,512]{1,0:T(8,128)S(1)}, u32[]{:S(2)}, u32[]{:S(2)}) collective-permute-start(f32[128,512]{1,0:T(8,128)S(1)} %both_bands.1.after), channel_id=1, source_target_pairs={{56,32},{57,33},{58,34},{59,35},{60,36},{61,37},{62,38},{63,39}} | collective-permute-start | bytes 786440 | tf_op jit(solution)/shard_map/ppermute | solution.py:729
  16.5 0.8 %collective-permute-start.4 = (f32[128,512]{1,0:T(8,128)S(1)}, f32[128,512]{1,0:T(8,128)S(1)}, u32[]{:S(2)}, u32[]{:S(2)}) collective-permute-start(f32[128,512]{1,0:T(8,128)S(1)} %both_bands.1.after), channel_id=1, source_target_pairs={{56,48},{57,49},{58,50},{59,51},{60,52},{61,53},{62,54},{63,55}} | collective-permute-start | bytes 786440 | tf_op jit(solution)/shard_map/ppermute | solution.py:729
  17.3 0.8 %collective-permute-start.3 = (f32[128,512]{1,0:T(8,128)S(1)}, f32[128,512]{1,0:T(8,128)S(1)}, u32[]{:S(2)}, u32[]{:S(2)}) collective-permute-start(f32[128,512]{1,0:T(8,128)S(1)} %both_bands.1.after), channel_id=1, source_target_pairs={{56,120},{57,121},{58,122},{59,123},{60,124},{61,125},{62,126},{63... | collective-permute-start | bytes 786440 | tf_op jit(solution)/shard_map/ppermute | solution.py:729
  18.1 0.7 collective-permute-start.2
  18.8 0.0 copy-done
  18.8 0.3 copy-done.2
  19.1 9.0 %first_iteration.1 = (f32[64,32,512]{2,1,0:T(8,128)S(1)}, f32[160,512]{1,0:T(8,128)S(1)}, f32[160,512]{1,0:T(8,128)S(1)}, f32[128,512]{1,0:T(8,128)S(1)}, f32[128,512]{1,0:T(8,128)S(1)}) custom-call(f32[64,32,512]{2,1,0:T(8,128)} %bitcast.26, f32[64,32,512]{2,1,0:T(8,128)S(1)} %bitcast.23, f32[64,32,512]{2,1,0:T(8,128)S(1)} %bitcast.30, ...), custom_call_target="tpu_custom_call" | custom-call | flops 7000000000 | bytes 20971520 | tf_op jit(solution)/shard_map/first_iteration/pallas_call | solution.py:357
  28.1 0.0 collective-permute-done.5
  28.1 0.0 collective-permute-done.4
  28.1 0.0 collective-permute-done.3
  28.1 0.0 collective-permute-done.2
  28.1 0.1 add_add_fusion.1
  28.2 0.7 collective-permute-start.7
  28.9 1.3 %collective-permute-start.6 = (f32[128,512]{1,0:T(8,128)S(1)}, f32[128,512]{1,0:T(8,128)S(1)}, u32[]{:S(2)}, u32[]{:S(2)}) collective-permute-start(f32[128,512]{1,0:T(8,128)S(1)} %add_add_fusion.1), channel_id=1, source_target_pairs={{32,96},{48,112},{33,97},{49,113},{34,98},{50,114},{35,99},{51,115... | collective-permute-start | bytes 786440 | tf_op jit(solution)/shard_map/ppermute | solution.py:738
  30.2 3.2 %collective-permute-start.10 = (f32[160,512]{1,0:T(8,128)S(1)}, f32[160,512]{1,0:T(8,128)S(1)}, u32[]{:S(2)}, u32[]{:S(2)}) collective-permute-start(f32[160,512]{1,0:T(8,128)S(1)} %get-tuple-element.83.bottom), channel_id=1, source_target_pairs={{0,8},{8,16},{16,24},{24,32},{32,40},{40,48},{48,56},{1,9},{9,17},... | collective-permute-start | bytes 983048 | tf_op jit(solution)/shard_map/ppermute | solution.py:694
  33.4 5.8 %collective-permute-start.11 = (f32[160,512]{1,0:T(8,128)S(1)}, f32[160,512]{1,0:T(8,128)S(1)}, u32[]{:S(2)}, u32[]{:S(2)}) collective-permute-start(f32[160,512]{1,0:T(8,128)S(1)} %get-tuple-element.84.top), channel_id=1, source_target_pairs={{8,0},{16,8},{24,16},{32,24},{40,32},{48,40},{56,48},{9,1},{17,9},... | collective-permute-start | bytes 983048 | tf_op jit(solution)/shard_map/ppermute | solution.py:695
  39.2 0.0 collective-permute-done.7
  39.2 0.0 collective-permute-done.6
  39.2 0.1 add_add_fusion.after
  39.2 5.5 %collective-permute-start.9 = (f32[128,512]{1,0:T(8,128)S(1)}, f32[128,512]{1,0:T(8,128)S(1)}, u32[]{:S(2)}, u32[]{:S(2)}) collective-permute-start(f32[128,512]{1,0:T(8,128)S(1)} %add_add_fusion.after), channel_id=1, source_target_pairs={{64,68},{65,69},{66,70},{67,71},{68,64},{69,65},{70,66},{71,67},{7... | collective-permute-start | bytes 786440 | tf_op jit(solution)/shard_map/ppermute | solution.py:752
  44.7 2.4 %collective-permute-start.12 = (f32[128,512]{1,0:T(8,128)S(1)}, f32[128,512]{1,0:T(8,128)S(1)}, u32[]{:S(2)}, u32[]{:S(2)}) collective-permute-start(f32[128,512]{1,0:T(8,128)S(1)} %add_add_fusion.after), channel_id=1, source_target_pairs={{64,70},{65,71},{66,64},{67,65},{68,66},{69,67},{70,68},{71,69},{7... | collective-permute-start | bytes 786440 | tf_op jit(solution)/shard_map/ppermute | solution.py:752
  47.1 2.9 %collective-permute-start.8 = (f32[128,512]{1,0:T(8,128)S(1)}, f32[128,512]{1,0:T(8,128)S(1)}, u32[]{:S(2)}, u32[]{:S(2)}) collective-permute-start(f32[128,512]{1,0:T(8,128)S(1)} %add_add_fusion.after), channel_id=1, source_target_pairs={{64,66},{65,67},{66,68},{67,69},{68,70},{69,71},{70,64},{71,65},{7... | collective-permute-start | bytes 786440 | tf_op jit(solution)/shard_map/ppermute | solution.py:752
  50.0 0.0 collective-permute-done.10.up
  50.1 0.0 collective-permute-done.11.down
  50.1 0.9 %finish_edges.1 = (bf16[384,512]{1,0:T(8,128)(2,1)S(1)}, bf16[384,512]{1,0:T(8,128)(2,1)S(1)}, f32[64,512]{1,0:T(8,128)S(1)}, f32[64,512]{1,0:T(8,128)S(1)}, f32...) custom-call(f32[160,512]{1,0:T(8,128)S(1)} %collective-permute-done.10.up, ...), custom_call_target="tpu_custom_call" | custom-call | flops 2000000 | bytes 3145728 | tf_op jit(solution)/shard_map/finish_edges/pallas_call | solution.py:507
  51.0 0.4 collective-permute-done.9
  51.4 3.1 %collective-permute-start.14 = (f32[128,512]{1,0:T(8,128)S(1)}, f32[128,512]{1,0:T(8,128)S(1)}, u32[]{:S(2)}, u32[]{:S(2)}) collective-permute-start(f32[128,512]{1,0:T(8,128)S(1)} %get-tuple-element.93), channel_id=1, source_target_pairs={{0,1},{1,2},{2,3},{3,4},{4,5},{5,6},{6,7},{8,9},{9,10},{10,11},{11... | collective-permute-start | bytes 786440 | tf_op jit(solution)/shard_map/ppermute | solution.py:694
  54.6 1.9 %collective-permute-start.15 = (f32[128,512]{1,0:T(8,128)S(1)}, f32[128,512]{1,0:T(8,128)S(1)}, u32[]{:S(2)}, u32[]{:S(2)}) collective-permute-start(f32[128,512]{1,0:T(8,128)S(1)} %get-tuple-element.94), channel_id=1, source_target_pairs={{1,0},{2,1},{3,2},{4,3},{5,4},{6,5},{7,6},{9,8},{10,9},{11,10},{12... | collective-permute-start | bytes 786440 | tf_op jit(solution)/shard_map/ppermute | solution.py:695
  56.5 0.0 collective-permute-done.12
  56.5 1.8 %collective-permute-done.8 = f32[128,512]{1,0:T(8,128)S(1)} collective-permute-done((f32[128,512]{1,0:T(8,128)S(1)}, f32[128,512]{1,0:T(8,128)S(1)}, u32[]{:S(2)}, u32[]{:S(2)}) %collective-permute-start.8) | collective-permute-done | bytes 262176 | tf_op jit(solution)/shard_map/ppermute | solution.py:752
  58.3 0.1 pad_maximum_fusion.own
  58.3 2.6 %collective-permute-start.13 = (f32[4,128,512]{2,1,0:T(8,128)S(1)}, f32[4,128,512]{2,1,0:T(8,128)S(1)}, u32[]{:S(2)}, u32[]{:S(2)}) collective-permute-start(f32[4,128,512]{2,1,0:T(8,128)S(1)} %pad_maximum_fusion.own), channel_id=1, source_target_pairs={{64,65},{65,64},{66,67},{67,66},{68,69},{69,68},{70,71},{71,70},{7... | collective-permute-start | bytes 3145736 | tf_op jit(solution)/shard_map/ppermute | solution.py:762
  60.9 0.0 collective-permute-done.14.left
  60.9 1.3 %collective-permute-done.15.right = f32[128,512]{1,0:T(8,128)S(1)} collective-permute-done((f32[128,512]{1,0:T(8,128)S(1)}, f32[128,512]{1,0:T(8,128)S(1)}, u32[]{:S(2)}, u32[]{:S(2)}) %collective-permute-start.15) | collective-permute-done | bytes 262176 | tf_op jit(solution)/shard_map/ppermute | solution.py:695
  62.3 0.0 copy-start.1
  62.3 2.8 %own_source.1 = (f32[64,32,512]{2,1,0:T(8,128)S(1)}, f32[384,512]{1,0:T(8,128)S(1)}) custom-call(f32[64,32,512]{2,1,0:T(8,128)S(1)} %get-tuple-element.92.one, f32[4,32,512]{2,1,0:T(8,128)S(1)} %get-tuple-element.96.added, bf16[2048,256]{1,0:T(8,128)(2,1)S(1)} %get-tuple-element.97.stencil_high.own_high, ...), custom_call_target="tpu_custom_call" | custom-call | flops 99999997952 | bytes 209715200 | tf_op jit(solution)/shard_map/own_source/pallas_call | solution.py:563
  65.1 0.0 collective-permute-done.13.other
  65.1 0.0 copy-done.1
  65.1 13.8 %last_iteration.1 = (f32[64,32,512]{2,1,0:T(8,128)}, f32[64,32,512]{2,1,0:T(8,128)}) custom-call(f32[64,32,512]{2,1,0:T(8,128)S(1)} %get-tuple-element.103.one, f32[384,512]{1,0:T(8,128)S(1)} %get-tuple-element.104.edge_source, f32[64,32,512]{2,1,0:T(8,128)S(1)} %bitcast.27, f32[64,32,512]{2,1,0:T(8,128)S(1)} %bitcast.31, ...), custom_call_target="tpu_custom_call" | custom-call | flops 14000000000 | bytes 37748736 | tf_op jit(solution)/shard_map/last_iteration/pallas_call | solution.py:672
  (1 shorter events, 0.0 us)
Async XLA Ops:
  0.6 8.2 %copy-start.3 = (f32[1,512,512]{2,1,0:T(8,128)S(1)}, f32[1,512,512]{2,1,0:T(8,128)}, u32[]{:S(2)}) copy-start(f32[1,512,512]{2,1,0:T(8,128)} %param.13) | copy-start | bytes 3145732
  2.8 10.2 %collective-permute-start = (f32[176,512]{1,0:T(8,128)S(1)}, f32[176,512]{1,0:T(8,128)S(1)}, u32[]{:S(2)}, u32[]{:S(2)}) collective-permute-start(f32[176,512]{1,0:T(8,128)S(1)} %get-tuple-element.59), channel_id=1, source_target_pairs={{0,1},{1,2},{2,3},{3,4},{4,5},{5,6},{6,7},{8,9},{9,10},{10,11},{11... | collective-permute-start | bytes 1081352 | tf_op jit(solution)/shard_map/ppermute | solution.py:694
  6.9 8.7 %collective-permute-start.1 = (f32[176,512]{1,0:T(8,128)S(1)}, f32[176,512]{1,0:T(8,128)S(1)}, u32[]{:S(2)}, u32[]{:S(2)}) collective-permute-start(f32[176,512]{1,0:T(8,128)S(1)} %get-tuple-element.60.after), channel_id=1, source_target_pairs={{1,0},{2,1},{3,2},{4,3},{5,4},{6,5},{7,6},{9,8},{10,9},{11,10},{12... | collective-permute-start | bytes 1081352 | tf_op jit(solution)/shard_map/ppermute | solution.py:695
  15.6 3.2 %copy-start = (f32[1,64,32,512]{3,2,1,0:T(8,128)S(1)}, f32[1,64,32,512]{3,2,1,0:T(8,128)}, u32[]{:S(2)}) copy-start(f32[1,64,32,512]{3,2,1,0:T(8,128)} %param.10) | copy-start | bytes 12582916
  15.6 3.5 %copy-start.2 = (f32[1,64,32,512]{3,2,1,0:T(8,128)S(1)}, f32[1,64,32,512]{3,2,1,0:T(8,128)}, u32[]{:S(2)}) copy-start(f32[1,64,32,512]{3,2,1,0:T(8,128)} %param.11) | copy-start | bytes 12582916
  15.7 12.4 %collective-permute-start.5 = (f32[128,512]{1,0:T(8,128)S(1)}, f32[128,512]{1,0:T(8,128)S(1)}, u32[]{:S(2)}, u32[]{:S(2)}) collective-permute-start(f32[128,512]{1,0:T(8,128)S(1)} %both_bands.1.after), channel_id=1, source_target_pairs={{56,32},{57,33},{58,34},{59,35},{60,36},{61,37},{62,38},{63,39}} | collective-permute-start | bytes 786440 | tf_op jit(solution)/shard_map/ppermute | solution.py:729
  16.5 11.6 %collective-permute-start.4 = (f32[128,512]{1,0:T(8,128)S(1)}, f32[128,512]{1,0:T(8,128)S(1)}, u32[]{:S(2)}, u32[]{:S(2)}) collective-permute-start(f32[128,512]{1,0:T(8,128)S(1)} %both_bands.1.after), channel_id=1, source_target_pairs={{56,48},{57,49},{58,50},{59,51},{60,52},{61,53},{62,54},{63,55}} | collective-permute-start | bytes 786440 | tf_op jit(solution)/shard_map/ppermute | solution.py:729
  17.3 10.8 %collective-permute-start.3 = (f32[128,512]{1,0:T(8,128)S(1)}, f32[128,512]{1,0:T(8,128)S(1)}, u32[]{:S(2)}, u32[]{:S(2)}) collective-permute-start(f32[128,512]{1,0:T(8,128)S(1)} %both_bands.1.after), channel_id=1, source_target_pairs={{56,120},{57,121},{58,122},{59,123},{60,124},{61,125},{62,126},{63... | collective-permute-start | bytes 786440 | tf_op jit(solution)/shard_map/ppermute | solution.py:729
  18.1 10.0 %collective-permute-start.2 = (f32[128,512]{1,0:T(8,128)S(1)}, f32[128,512]{1,0:T(8,128)S(1)}, u32[]{:S(2)}, u32[]{:S(2)}) collective-permute-start(f32[128,512]{1,0:T(8,128)S(1)} %both_bands.1.after), channel_id=1, source_target_pairs={{56,88},{57,89},{58,90},{59,91},{60,92},{61,93},{62,94},{63,95}} | collective-permute-start | bytes 786440 | tf_op jit(solution)/shard_map/ppermute | solution.py:729
  28.2 11.0 %collective-permute-start.7 = (f32[128,512]{1,0:T(8,128)S(1)}, f32[128,512]{1,0:T(8,128)S(1)}, u32[]{:S(2)}, u32[]{:S(2)}) collective-permute-start(f32[128,512]{1,0:T(8,128)S(1)} %add_add_fusion.1), channel_id=1, source_target_pairs={{32,64},{48,80},{88,72},{120,104},{33,65},{49,81},{89,73},{121,105... | collective-permute-start | bytes 786440 | tf_op jit(solution)/shard_map/ppermute | solution.py:738
  28.9 10.3 %collective-permute-start.6 = (f32[128,512]{1,0:T(8,128)S(1)}, f32[128,512]{1,0:T(8,128)S(1)}, u32[]{:S(2)}, u32[]{:S(2)}) collective-permute-start(f32[128,512]{1,0:T(8,128)S(1)} %add_add_fusion.1), channel_id=1, source_target_pairs={{32,96},{48,112},{33,97},{49,113},{34,98},{50,114},{35,99},{51,115... | collective-permute-start | bytes 786440 | tf_op jit(solution)/shard_map/ppermute | solution.py:738
  30.2 19.9 %collective-permute-start.10 = (f32[160,512]{1,0:T(8,128)S(1)}, f32[160,512]{1,0:T(8,128)S(1)}, u32[]{:S(2)}, u32[]{:S(2)}) collective-permute-start(f32[160,512]{1,0:T(8,128)S(1)} %get-tuple-element.83.bottom), channel_id=1, source_target_pairs={{0,8},{8,16},{16,24},{24,32},{32,40},{40,48},{48,56},{1,9},{9,17},... | collective-permute-start | bytes 983048 | tf_op jit(solution)/shard_map/ppermute | solution.py:694
  33.4 16.7 %collective-permute-start.11 = (f32[160,512]{1,0:T(8,128)S(1)}, f32[160,512]{1,0:T(8,128)S(1)}, u32[]{:S(2)}, u32[]{:S(2)}) collective-permute-start(f32[160,512]{1,0:T(8,128)S(1)} %get-tuple-element.84.top), channel_id=1, source_target_pairs={{8,0},{16,8},{24,16},{32,24},{40,32},{48,40},{56,48},{9,1},{17,9},... | collective-permute-start | bytes 983048 | tf_op jit(solution)/shard_map/ppermute | solution.py:695
  39.2 12.2 %collective-permute-start.9 = (f32[128,512]{1,0:T(8,128)S(1)}, f32[128,512]{1,0:T(8,128)S(1)}, u32[]{:S(2)}, u32[]{:S(2)}) collective-permute-start(f32[128,512]{1,0:T(8,128)S(1)} %add_add_fusion.after), channel_id=1, source_target_pairs={{64,68},{65,69},{66,70},{67,71},{68,64},{69,65},{70,66},{71,67},{7... | collective-permute-start | bytes 786440 | tf_op jit(solution)/shard_map/ppermute | solution.py:752
  44.7 11.7 %collective-permute-start.12 = (f32[128,512]{1,0:T(8,128)S(1)}, f32[128,512]{1,0:T(8,128)S(1)}, u32[]{:S(2)}, u32[]{:S(2)}) collective-permute-start(f32[128,512]{1,0:T(8,128)S(1)} %add_add_fusion.after), channel_id=1, source_target_pairs={{64,70},{65,71},{66,64},{67,65},{68,66},{69,67},{70,68},{71,69},{7... | collective-permute-start | bytes 786440 | tf_op jit(solution)/shard_map/ppermute | solution.py:752
  47.1 11.1 %collective-permute-start.8 = (f32[128,512]{1,0:T(8,128)S(1)}, f32[128,512]{1,0:T(8,128)S(1)}, u32[]{:S(2)}, u32[]{:S(2)}) collective-permute-start(f32[128,512]{1,0:T(8,128)S(1)} %add_add_fusion.after), channel_id=1, source_target_pairs={{64,66},{65,67},{66,68},{67,69},{68,70},{69,71},{70,64},{71,65},{7... | collective-permute-start | bytes 786440 | tf_op jit(solution)/shard_map/ppermute | solution.py:752
  51.4 9.5 %collective-permute-start.14 = (f32[128,512]{1,0:T(8,128)S(1)}, f32[128,512]{1,0:T(8,128)S(1)}, u32[]{:S(2)}, u32[]{:S(2)}) collective-permute-start(f32[128,512]{1,0:T(8,128)S(1)} %get-tuple-element.93), channel_id=1, source_target_pairs={{0,1},{1,2},{2,3},{3,4},{4,5},{5,6},{6,7},{8,9},{9,10},{10,11},{11... | collective-permute-start | bytes 786440 | tf_op jit(solution)/shard_map/ppermute | solution.py:694
  54.6 7.7 %collective-permute-start.15 = (f32[128,512]{1,0:T(8,128)S(1)}, f32[128,512]{1,0:T(8,128)S(1)}, u32[]{:S(2)}, u32[]{:S(2)}) collective-permute-start(f32[128,512]{1,0:T(8,128)S(1)} %get-tuple-element.94), channel_id=1, source_target_pairs={{1,0},{2,1},{3,2},{4,3},{5,4},{6,5},{7,6},{9,8},{10,9},{11,10},{12... | collective-permute-start | bytes 786440 | tf_op jit(solution)/shard_map/ppermute | solution.py:695
  58.3 6.8 %collective-permute-start.13 = (f32[4,128,512]{2,1,0:T(8,128)S(1)}, f32[4,128,512]{2,1,0:T(8,128)S(1)}, u32[]{:S(2)}, u32[]{:S(2)}) collective-permute-start(f32[4,128,512]{2,1,0:T(8,128)S(1)} %pad_maximum_fusion.own), channel_id=1, source_target_pairs={{64,65},{65,64},{66,67},{67,66},{68,69},{69,68},{70,71},{71,70},{7... | collective-permute-start | bytes 3145736 | tf_op jit(solution)/shard_map/ppermute | solution.py:762
  62.3 2.9 %copy-start.1 = (f32[1,64,32,512]{3,2,1,0:T(8,128)S(1)}, f32[1,64,32,512]{3,2,1,0:T(8,128)}, u32[]{:S(2)}) copy-start(f32[1,64,32,512]{3,2,1,0:T(8,128)} %param.9) | copy-start | bytes 12582916

commit v13 on v12

--- a/solution.py
+++ b/solution.py
@@ -529,9 +529,10 @@
 
 
 def own_source_kernel(
-    one, added, stencil_high, stencil_low, edge_high, edge_low, own, sum_one, edge_source, table
+    one, added, stencil_high, stencil_low, edge_high, edge_low, own, after, sum_one, edge_source, table, *, begin
 ):
     count_r, rows, width = one.shape
+    count = sum_one.shape[0]
     columns = table.shape[1]
     size = LAST * rows
 
@@ -540,43 +541,47 @@
         split_table(own, 0, table, 0)
 
         def body(n, carry):
-            cut = pl.ds(pl.multiple_of(n * size, size), size)
-            part = pl.ds(n * LAST, LAST)
+            cut = pl.ds(pl.multiple_of(begin * rows + n * size, size), size)
             weights = (stencil_high[cut], stencil_low[cut])
-            sum_one[part] = one[part] + product(weights, table[0], table[1]).reshape(LAST, rows, width)
+            more = product(weights, table[0], table[1]).reshape(LAST, rows, width)
+            sum_one[pl.ds(n * LAST, LAST)] = one[pl.ds(begin + n * LAST, LAST)] + more
             return carry
 
-        lax.fori_loop(0, count_r // LAST, body, 0)
-        edge_source[...] = product((edge_high[:, 0:columns], edge_low[:, 0:columns]), table[0], table[1])
+        lax.fori_loop(0, count // LAST, body, 0)
+        if begin == 0:
+            edge_source[...] = product((edge_high[:, 0:columns], edge_low[:, 0:columns]), table[0], table[1])
 
     @pl.when(jnp.logical_not(in_product()))
     def _():
-        sum_one[...] = one[...]
+        sum_one[...] = one[begin : begin + count]
 
     for k in range(HALO):
-        sum_one[k] += added[k]
-        sum_one[count_r - HALO + k] += added[HALO + k]
-
-
-def own_source(one, added, matrices, own):
-    width = one.shape[2]
+        if begin == 0:
+            sum_one[k] += added[k]
+        if begin + count == count_r:
+            sum_one[count - HALO + k] += added[HALO + k]
+
+
+def own_source(one, added, matrices, own, after, begin, count, flops):
+    _, rows, width = one.shape
+    edge_rows = matrices[2].shape[0] if begin == 0 else 8
     return pl.pallas_call(
-        own_source_kernel,
-        in_specs=[VMEM] * 7,
+        functools.partial(own_source_kernel, begin=begin),
+        in_specs=[*[VMEM] * 7, ANY],
         out_specs=[VMEM] * 2,
         out_shape=[
-            jax.ShapeDtypeStruct(one.shape, F32),
-            jax.ShapeDtypeStruct((matrices[2].shape[0], width), F32),
+            jax.ShapeDtypeStruct((count, rows, width), F32),
+            jax.ShapeDtypeStruct((edge_rows, width), F32),
         ],
         scratch_shapes=[pltpu.VMEM((2, own.shape[0] * own.shape[1] // 2, width), BF16)],
         compiler_params=pltpu.CompilerParams(vmem_limit_bytes=16 * MIB),
-        cost_estimate=pl.CostEstimate(flops=100_000_000_000, bytes_accessed=200 * MIB, transcendentals=0),
+        cost_estimate=pl.CostEstimate(flops=flops, bytes_accessed=flops // 500, transcendentals=0),
         name="own_source",
-    )(one, added, *matrices, own)
+    )(one, added, *matrices, own, after)
 
 
 def last_kernel(
-    one, edge_source, packet, potential, tables, up, down, left, right, high, low,
+    one, one_end, edge_source, packet, potential, tables, up, down, left, right, high, low,
     own_high, own_low, stencil_high, stencil_low, edge_high, edge_low, own, other,
     earlier, latest, field, done, sides, table, ends, sems,
 ):
@@ -630,7 +635,10 @@
             earliers(n).start()
             return carry
 
-        lax.fori_loop(0, steps, add, 0)
+        lax.fori_loop(0, steps - 1, add, 0)
+        more = product(weights(steps - 1), table[0], table[1]).reshape(LAST, rows, width)
+        field[HALO + count_r - LAST : HALO + count_r] = one_end[...] + more
+        earliers(steps - 1).start()
 
         def body(n, carry):
             mine, theirs = (own_high[cut(n)], own_low[cut(n)]), weights(n)
@@ -651,7 +659,7 @@
         put_ends(up, down)
         put_sides(sides, left, right, count_r)
         for n in range(steps):
-            field[pl.ds(HALO + n * LAST, LAST)] = one[part(n)]
+            field[pl.ds(HALO + n * LAST, LAST)] = one[part(n)] if n + 1 < steps else one_end[...]
             earliers(n).start()
 
         def body(n, carry):
@@ -671,7 +679,7 @@
     steps = count_r // LAST
     return pl.pallas_call(
         last_kernel,
-        in_specs=[VMEM] * 19,
+        in_specs=[VMEM] * 20,
         out_specs=[HBM, HBM],
         out_shape=[jax.ShapeDtypeStruct(packet.shape, F32)] * 2,
         scratch_shapes=[
@@ -762,8 +770,11 @@
     other = lax.ppermute(
         own, line, [(count_row + i, count_row + i + 1 - 2 * (i % CORES)) for i in range(count_row)]
     )
-    left, right, added = lax.optimization_barrier((left, right, added))
-    own_sums = own_source(one, added, (*matrix[:2], *edge_matrix), own)
+    own_matrices = (*matrix[:2], *edge_matrix)
+    one_begin, edge_source = own_source(one, added, own_matrices, own, own, 0, count_r - LAST, 1_000_000)
+    left, right, added, one_begin = lax.optimization_barrier((left, right, added, one_begin))
+    one_end, _ = own_source(one, added, own_matrices, own, one_begin, count_r - LAST, LAST, 100_000_000_000)
+    own_sums = (one_begin, one_end, edge_source)
     other, own_sums = lax.optimization_barrier((other, own_sums))
     earlier, latest = last_iteration(
         own_sums, near_packet, near_potential, tables, (up, down, left, right), high, low, (*matrix, *edge_matrix), (own, other)

time: 79.9 us -> 79.6 us (level)
  waiting for transfers between devices: 6.11 us -> 4.79 us
  local copies, waits for them, and re-layouts: 0.29 us -> 1.28 us
    ppermute x3, waiting for transfers between devices: 3.93 us -> 2.63 us  [neighbours(): lax.ppermute(downward, axis, [(i + 1, i) for i in range(count - 1)])]
    unnamed x8, local copies, waits for them, and re-layouts: 0.29 us -> 1.28 us
    pallas_call x2 -> x3, Pallas kernels: 16.7 us -> 17.3 us  [the longest x1 13.8 us: last_iteration(): pl.pallas_call(last_kernel, in_specs=[VMEM] * 20, out_specs=[HBM, HBM], o...]
  transfers between devices with their start and end apart: 16 -> 16, of which waited for: 4 -> 3; matrix products, arithmetic and copies ran while one was open for 0% -> 0% of each run, Pallas kernels for 21% -> 22%
where the time goes in v13:
time: 79.6 us; the launch traced here: 79.2 us
  starting transfers between devices  38.5 us (48%)
  Pallas kernels  33.5 us (42%)
  waiting for transfers between devices  4.79 us (6%)
  local copies, waits for them, and re-layouts  1.28 us (2%)
  between operations  0.95 us (1%)
    pallas_call x1, Pallas kernels, last_iteration(): pl.pallas_call(last_kernel, in_specs=[VMEM] * 20, out_specs=[HBM, HBM], o...  13.8 us
    ppermute x3, starting transfers between devices, around(): return lax.ppermute(spread, line, pairs)  10.8 us
    ppermute x3, starting transfers between devices, neighbours(): lax.ppermute(upward, axis, [(i, i + 1) for i in range(count - 1)])  10.5 us
    ppermute x3, starting transfers between devices, neighbours(): lax.ppermute(downward, axis, [(i + 1, i) for i in range(count - 1)])  9.61 us
    pallas_call x1, Pallas kernels, first_iteration(): pl.pallas_call(first_kernel, in_specs=[HBM, *[VMEM] * 9, ANY], out_specs=...  8.97 us
    pallas_call x1, Pallas kernels, matrices_of(): pl.pallas_call(stencil_kernel, in_specs=[VMEM, VMEM, ANY], out_specs=[VME...  4.17 us
    pallas_call x2, Pallas kernels, own_source(): pl.pallas_call(functools.partial(own_source_kernel, begin=begin), in_spec...  3.47 us
    ppermute x4, starting transfers between devices, local(): crossed = [lax.ppermute(table, plane, [(start, relay)]) for relay in relays]  3.1 us
  transfers between devices with their start and end apart: 16, of which 3 were waited for; matrix products, arithmetic and copies ran while one was open for 0% of the time, Pallas kernels for 22%

profile of v13, /device:TPU:7, one launch (start us, length us, event | category | flops | bytes accessed | tf_op | source)
XLA Modules:
  0.0 79.2 jit_solution(2085531182711820696)
XLA Ops:
  0.6 0.0 copy-start.3
  0.6 2.1 %prepare.1 = (f32[32,128]{1,0:T(8,128)S(1)}, f32[32,128]{1,0:T(8,128)S(1)}, f32[176,512]{1,0:T(8,128)S(1)}, f32[176,512]{1,0:T(8,128)S(1)}, f32[10,32,128]{2,1,0:T(8,128)S(1)}) custom-call(f32[64,32,512]{2,1,0:T(8,128)} %bitcast.24, f32[64,32,512]{2,1,0:T(8,128)} %bitcast.21, f32[64,32,512]{2,1,0:T(8,128)} %bitcast.28, f32[32,64]{1,0:T(8,128)} %bitcast.39, ...), custom_call_target="tpu_custom_call" | custom-call | flops 1000000 | bytes 6291456 | tf_op jit(solution)/shard_map/prepare/pallas_call | solution.py:233
  2.8 4.1 %collective-permute-start = (f32[176,512]{1,0:T(8,128)S(1)}, f32[176,512]{1,0:T(8,128)S(1)}, u32[]{:S(2)}, u32[]{:S(2)}) collective-permute-start(f32[176,512]{1,0:T(8,128)S(1)} %get-tuple-element.62), channel_id=1, source_target_pairs={{0,1},{1,2},{2,3},{3,4},{4,5},{5,6},{6,7},{8,9},{9,10},{10,11},{11... | collective-permute-start | bytes 1081352 | tf_op jit(solution)/shard_map/ppermute | solution.py:702
  6.9 1.9 %collective-permute-start.1 = (f32[176,512]{1,0:T(8,128)S(1)}, f32[176,512]{1,0:T(8,128)S(1)}, u32[]{:S(2)}, u32[]{:S(2)}) collective-permute-start(f32[176,512]{1,0:T(8,128)S(1)} %get-tuple-element.63.after), channel_id=1, source_target_pairs={{1,0},{2,1},{3,2},{4,3},{5,4},{6,5},{7,6},{9,8},{10,9},{11,10},{12... | collective-permute-start | bytes 1081352 | tf_op jit(solution)/shard_map/ppermute | solution.py:703
  8.8 0.0 copy-done.3
  8.8 4.2 %stencil_matrix.1 = (bf16[2048,256]{1,0:T(8,128)(2,1)S(1)}, bf16[2048,256]{1,0:T(8,128)(2,1)S(1)}, bf16[2048,256]{1,0:T(8,128)(2,1)S(1)}, bf16[2048,256]{1,0:T(8...) custom-call(f32[10,32,128]{2,1,0:T(8,128)S(1)} %get-tuple-element.61.tables, ...), custom_call_target="tpu_custom_call" | custom-call | flops 15000000 | bytes 6291456 | tf_op jit(solution)/shard_map/stencil_matrix/pallas_call | solution.py:428
  13.0 0.0 collective-permute-done.left
  13.0 2.6 %collective-permute-done.1.right = f32[176,512]{1,0:T(8,128)S(1)} collective-permute-done((f32[176,512]{1,0:T(8,128)S(1)}, f32[176,512]{1,0:T(8,128)S(1)}, u32[]{:S(2)}, u32[]{:S(2)}) %collective-permute-start.1) | collective-permute-done | bytes 360480 | tf_op jit(solution)/shard_map/ppermute | solution.py:703
  15.6 0.0 copy-start
  15.6 0.0 copy-start.2
  15.7 0.8 %collective-permute-start.5 = (f32[128,512]{1,0:T(8,128)S(1)}, f32[128,512]{1,0:T(8,128)S(1)}, u32[]{:S(2)}, u32[]{:S(2)}) collective-permute-start(f32[128,512]{1,0:T(8,128)S(1)} %both_bands.1.after), channel_id=1, source_target_pairs={{56,32},{57,33},{58,34},{59,35},{60,36},{61,37},{62,38},{63,39}} | collective-permute-start | bytes 786440 | tf_op jit(solution)/shard_map/ppermute | solution.py:737
  16.5 0.8 %collective-permute-start.4 = (f32[128,512]{1,0:T(8,128)S(1)}, f32[128,512]{1,0:T(8,128)S(1)}, u32[]{:S(2)}, u32[]{:S(2)}) collective-permute-start(f32[128,512]{1,0:T(8,128)S(1)} %both_bands.1.after), channel_id=1, source_target_pairs={{56,48},{57,49},{58,50},{59,51},{60,52},{61,53},{62,54},{63,55}} | collective-permute-start | bytes 786440 | tf_op jit(solution)/shard_map/ppermute | solution.py:737
  17.3 0.8 %collective-permute-start.3 = (f32[128,512]{1,0:T(8,128)S(1)}, f32[128,512]{1,0:T(8,128)S(1)}, u32[]{:S(2)}, u32[]{:S(2)}) collective-permute-start(f32[128,512]{1,0:T(8,128)S(1)} %both_bands.1.after), channel_id=1, source_target_pairs={{56,120},{57,121},{58,122},{59,123},{60,124},{61,125},{62,126},{63... | collective-permute-start | bytes 786440 | tf_op jit(solution)/shard_map/ppermute | solution.py:737
  18.1 0.7 collective-permute-start.2
  18.8 0.0 copy-done
  18.8 0.3 copy-done.2
  19.1 9.0 %first_iteration.1 = (f32[64,32,512]{2,1,0:T(8,128)S(1)}, f32[160,512]{1,0:T(8,128)S(1)}, f32[160,512]{1,0:T(8,128)S(1)}, f32[128,512]{1,0:T(8,128)S(1)}, f32[128,512]{1,0:T(8,128)S(1)}) custom-call(f32[64,32,512]{2,1,0:T(8,128)} %bitcast.26, f32[64,32,512]{2,1,0:T(8,128)S(1)} %bitcast.23, f32[64,32,512]{2,1,0:T(8,128)S(1)} %bitcast.30, ...), custom_call_target="tpu_custom_call" | custom-call | flops 7000000000 | bytes 20971520 | tf_op jit(solution)/shard_map/first_iteration/pallas_call | solution.py:357
  28.1 0.0 collective-permute-done.5
  28.1 0.0 collective-permute-done.4
  28.1 0.0 collective-permute-done.3
  28.1 0.0 collective-permute-done.2
  28.1 0.1 add_add_fusion.1
  28.2 0.7 collective-permute-start.7
  28.9 1.3 %collective-permute-start.6 = (f32[128,512]{1,0:T(8,128)S(1)}, f32[128,512]{1,0:T(8,128)S(1)}, u32[]{:S(2)}, u32[]{:S(2)}) collective-permute-start(f32[128,512]{1,0:T(8,128)S(1)} %add_add_fusion.1), channel_id=1, source_target_pairs={{32,96},{48,112},{33,97},{49,113},{34,98},{50,114},{35,99},{51,115... | collective-permute-start | bytes 786440 | tf_op jit(solution)/shard_map/ppermute | solution.py:746
  30.2 3.2 %collective-permute-start.10 = (f32[160,512]{1,0:T(8,128)S(1)}, f32[160,512]{1,0:T(8,128)S(1)}, u32[]{:S(2)}, u32[]{:S(2)}) collective-permute-start(f32[160,512]{1,0:T(8,128)S(1)} %get-tuple-element.86.bottom), channel_id=1, source_target_pairs={{0,8},{8,16},{16,24},{24,32},{32,40},{40,48},{48,56},{1,9},{9,17},... | collective-permute-start | bytes 983048 | tf_op jit(solution)/shard_map/ppermute | solution.py:702
  33.4 5.8 %collective-permute-start.11 = (f32[160,512]{1,0:T(8,128)S(1)}, f32[160,512]{1,0:T(8,128)S(1)}, u32[]{:S(2)}, u32[]{:S(2)}) collective-permute-start(f32[160,512]{1,0:T(8,128)S(1)} %get-tuple-element.87.top), channel_id=1, source_target_pairs={{8,0},{16,8},{24,16},{32,24},{40,32},{48,40},{56,48},{9,1},{17,9},... | collective-permute-start | bytes 983048 | tf_op jit(solution)/shard_map/ppermute | solution.py:703
  39.2 0.0 collective-permute-done.7
  39.2 0.0 collective-permute-done.6
  39.2 0.1 add_add_fusion.after
  39.2 5.5 %collective-permute-start.9 = (f32[128,512]{1,0:T(8,128)S(1)}, f32[128,512]{1,0:T(8,128)S(1)}, u32[]{:S(2)}, u32[]{:S(2)}) collective-permute-start(f32[128,512]{1,0:T(8,128)S(1)} %add_add_fusion.after), channel_id=1, source_target_pairs={{64,68},{65,69},{66,70},{67,71},{68,64},{69,65},{70,66},{71,67},{7... | collective-permute-start | bytes 786440 | tf_op jit(solution)/shard_map/ppermute | solution.py:760
  44.7 2.4 %collective-permute-start.12 = (f32[128,512]{1,0:T(8,128)S(1)}, f32[128,512]{1,0:T(8,128)S(1)}, u32[]{:S(2)}, u32[]{:S(2)}) collective-permute-start(f32[128,512]{1,0:T(8,128)S(1)} %add_add_fusion.after), channel_id=1, source_target_pairs={{64,70},{65,71},{66,64},{67,65},{68,66},{69,67},{70,68},{71,69},{7... | collective-permute-start | bytes 786440 | tf_op jit(solution)/shard_map/ppermute | solution.py:760
  47.1 2.9 %collective-permute-start.8 = (f32[128,512]{1,0:T(8,128)S(1)}, f32[128,512]{1,0:T(8,128)S(1)}, u32[]{:S(2)}, u32[]{:S(2)}) collective-permute-start(f32[128,512]{1,0:T(8,128)S(1)} %add_add_fusion.after), channel_id=1, source_target_pairs={{64,66},{65,67},{66,68},{67,69},{68,70},{69,71},{70,64},{71,65},{7... | collective-permute-start | bytes 786440 | tf_op jit(solution)/shard_map/ppermute | solution.py:760
  50.0 0.0 collective-permute-done.10.up
  50.1 0.0 collective-permute-done.11.down
  50.1 0.9 %finish_edges.1 = (bf16[384,512]{1,0:T(8,128)(2,1)S(1)}, bf16[384,512]{1,0:T(8,128)(2,1)S(1)}, f32[64,512]{1,0:T(8,128)S(1)}, f32[64,512]{1,0:T(8,128)S(1)}, f32...) custom-call(f32[160,512]{1,0:T(8,128)S(1)} %collective-permute-done.10.up, ...), custom_call_target="tpu_custom_call" | custom-call | flops 2000000 | bytes 3145728 | tf_op jit(solution)/shard_map/finish_edges/pallas_call | solution.py:507
  51.0 0.4 collective-permute-done.9
  51.4 3.1 %collective-permute-start.14 = (f32[128,512]{1,0:T(8,128)S(1)}, f32[128,512]{1,0:T(8,128)S(1)}, u32[]{:S(2)}, u32[]{:S(2)}) collective-permute-start(f32[128,512]{1,0:T(8,128)S(1)} %get-tuple-element.95), channel_id=1, source_target_pairs={{0,1},{1,2},{2,3},{3,4},{4,5},{5,6},{6,7},{8,9},{9,10},{10,11},{11... | collective-permute-start | bytes 786440 | tf_op jit(solution)/shard_map/ppermute | solution.py:702
  54.6 1.9 %collective-permute-start.15 = (f32[128,512]{1,0:T(8,128)S(1)}, f32[128,512]{1,0:T(8,128)S(1)}, u32[]{:S(2)}, u32[]{:S(2)}) collective-permute-start(f32[128,512]{1,0:T(8,128)S(1)} %get-tuple-element.96), channel_id=1, source_target_pairs={{1,0},{2,1},{3,2},{4,3},{5,4},{6,5},{7,6},{9,8},{10,9},{11,10},{12... | collective-permute-start | bytes 786440 | tf_op jit(solution)/shard_map/ppermute | solution.py:703
  56.5 0.0 collective-permute-done.12
  56.5 1.7 %collective-permute-done.8 = f32[128,512]{1,0:T(8,128)S(1)} collective-permute-done((f32[128,512]{1,0:T(8,128)S(1)}, f32[128,512]{1,0:T(8,128)S(1)}, u32[]{:S(2)}, u32[]{:S(2)}) %collective-permute-start.8) | collective-permute-done | bytes 262176 | tf_op jit(solution)/shard_map/ppermute | solution.py:760
  58.2 0.1 pad_maximum_fusion.own.after
  58.3 2.6 %collective-permute-start.13 = (f32[4,128,512]{2,1,0:T(8,128)S(1)}, f32[4,128,512]{2,1,0:T(8,128)S(1)}, u32[]{:S(2)}, u32[]{:S(2)}) collective-permute-start(f32[4,128,512]{2,1,0:T(8,128)S(1)} %pad_maximum_fusion.own.after), channel_id=1, source_target_pairs={{64,65},{65,64},{66,67},{67,66},{68,69},{69,68},{70,71},{71,70},{7... | collective-permute-start | bytes 3145736 | tf_op jit(solution)/shard_map/ppermute | solution.py:770
  60.9 2.3 %own_source.2 = (f32[48,32,512]{2,1,0:T(8,128)S(1)}, f32[384,512]{1,0:T(8,128)S(1)}) custom-call(f32[64,32,512]{2,1,0:T(8,128)S(1)} %get-tuple-element.98.one, f32[4,32,512]{2,1,0:T(8,128)S(1)} %get-tuple-element.105.added, bf16[2048,256]{1,0:T(8,128)(2,1)S(1)} %get-tuple-element.99.stencil_high.own_high, ...), custom_call_target="tpu_custom_call" | custom-call | flops 1000000 | bytes 2000 | tf_op jit(solution)/shard_map/own_source/pallas_call | solution.py:568
  63.2 0.0 collective-permute-done.14.left
  63.2 0.0 collective-permute-done.15.right
  63.2 0.0 copy-start.1
  63.2 1.2 %own_source.3 = (f32[16,32,512]{2,1,0:T(8,128)S(1)}, f32[8,512]{1,0:T(8,128)}) custom-call(f32[64,32,512]{2,1,0:T(8,128)S(1)} %get-tuple-element.98.one, f32[4,32,512]{2,1,0:T(8,128)S(1)} %get-tuple-element.105.added, bf16[2048,256]{1,0:T(8,128)(2,1)S(1)} %get-tuple-element.99.stencil_high.own_high, ...), custom_call_target="tpu_custom_call" | custom-call | flops 99999997952 | bytes 200000000 | tf_op jit(solution)/shard_map/own_source/pallas_call | solution.py:568
  64.4 0.0 collective-permute-done.13.other
  64.4 1.0 %copy-done.1 = f32[1,64,32,512]{3,2,1,0:T(8,128)S(1)} copy-done((f32[1,64,32,512]{3,2,1,0:T(8,128)S(1)}, f32[1,64,32,512]{3,2,1,0:T(8,128)}, u32[]{:S(2)}) %copy-start.1) | copy-done | bytes 4194328
  65.4 13.8 %last_iteration.1 = (f32[64,32,512]{2,1,0:T(8,128)}, f32[64,32,512]{2,1,0:T(8,128)}) custom-call(f32[48,32,512]{2,1,0:T(8,128)S(1)} %get-tuple-element.108.after.one, f32[16,32,512]{2,1,0:T(8,128)S(1)} %get-tuple-element.109.one_end, f32[384,512]{1,0:T(8,128)S(1)} %get-tuple-element.110.edge_source, f32[64,32,512]{2,1,0:T(8,128)S(1)} %bitcast.27, ...), custom_call_target="tpu_custom_call" | custom-call | flops 14000000000 | bytes 37748736 | tf_op jit(solution)/shard_map/last_iteration/pallas_call | solution.py:680
  (1 shorter events, 0.0 us)
Async XLA Ops:
  0.6 8.2 %copy-start.3 = (f32[1,512,512]{2,1,0:T(8,128)S(1)}, f32[1,512,512]{2,1,0:T(8,128)}, u32[]{:S(2)}) copy-start(f32[1,512,512]{2,1,0:T(8,128)} %param.13) | copy-start | bytes 3145732
  2.8 10.2 %collective-permute-start = (f32[176,512]{1,0:T(8,128)S(1)}, f32[176,512]{1,0:T(8,128)S(1)}, u32[]{:S(2)}, u32[]{:S(2)}) collective-permute-start(f32[176,512]{1,0:T(8,128)S(1)} %get-tuple-element.62), channel_id=1, source_target_pairs={{0,1},{1,2},{2,3},{3,4},{4,5},{5,6},{6,7},{8,9},{9,10},{10,11},{11... | collective-permute-start | bytes 1081352 | tf_op jit(solution)/shard_map/ppermute | solution.py:702
  6.9 8.7 %collective-permute-start.1 = (f32[176,512]{1,0:T(8,128)S(1)}, f32[176,512]{1,0:T(8,128)S(1)}, u32[]{:S(2)}, u32[]{:S(2)}) collective-permute-start(f32[176,512]{1,0:T(8,128)S(1)} %get-tuple-element.63.after), channel_id=1, source_target_pairs={{1,0},{2,1},{3,2},{4,3},{5,4},{6,5},{7,6},{9,8},{10,9},{11,10},{12... | collective-permute-start | bytes 1081352 | tf_op jit(solution)/shard_map/ppermute | solution.py:703
  15.6 3.2 %copy-start = (f32[1,64,32,512]{3,2,1,0:T(8,128)S(1)}, f32[1,64,32,512]{3,2,1,0:T(8,128)}, u32[]{:S(2)}) copy-start(f32[1,64,32,512]{3,2,1,0:T(8,128)} %param.10) | copy-start | bytes 12582916
  15.6 3.5 %copy-start.2 = (f32[1,64,32,512]{3,2,1,0:T(8,128)S(1)}, f32[1,64,32,512]{3,2,1,0:T(8,128)}, u32[]{:S(2)}) copy-start(f32[1,64,32,512]{3,2,1,0:T(8,128)} %param.11) | copy-start | bytes 12582916
  15.7 12.4 %collective-permute-start.5 = (f32[128,512]{1,0:T(8,128)S(1)}, f32[128,512]{1,0:T(8,128)S(1)}, u32[]{:S(2)}, u32[]{:S(2)}) collective-permute-start(f32[128,512]{1,0:T(8,128)S(1)} %both_bands.1.after), channel_id=1, source_target_pairs={{56,32},{57,33},{58,34},{59,35},{60,36},{61,37},{62,38},{63,39}} | collective-permute-start | bytes 786440 | tf_op jit(solution)/shard_map/ppermute | solution.py:737
  16.5 11.6 %collective-permute-start.4 = (f32[128,512]{1,0:T(8,128)S(1)}, f32[128,512]{1,0:T(8,128)S(1)}, u32[]{:S(2)}, u32[]{:S(2)}) collective-permute-start(f32[128,512]{1,0:T(8,128)S(1)} %both_bands.1.after), channel_id=1, source_target_pairs={{56,48},{57,49},{58,50},{59,51},{60,52},{61,53},{62,54},{63,55}} | collective-permute-start | bytes 786440 | tf_op jit(solution)/shard_map/ppermute | solution.py:737
  17.3 10.8 %collective-permute-start.3 = (f32[128,512]{1,0:T(8,128)S(1)}, f32[128,512]{1,0:T(8,128)S(1)}, u32[]{:S(2)}, u32[]{:S(2)}) collective-permute-start(f32[128,512]{1,0:T(8,128)S(1)} %both_bands.1.after), channel_id=1, source_target_pairs={{56,120},{57,121},{58,122},{59,123},{60,124},{61,125},{62,126},{63... | collective-permute-start | bytes 786440 | tf_op jit(solution)/shard_map/ppermute | solution.py:737
  18.1 10.0 %collective-permute-start.2 = (f32[128,512]{1,0:T(8,128)S(1)}, f32[128,512]{1,0:T(8,128)S(1)}, u32[]{:S(2)}, u32[]{:S(2)}) collective-permute-start(f32[128,512]{1,0:T(8,128)S(1)} %both_bands.1.after), channel_id=1, source_target_pairs={{56,88},{57,89},{58,90},{59,91},{60,92},{61,93},{62,94},{63,95}} | collective-permute-start | bytes 786440 | tf_op jit(solution)/shard_map/ppermute | solution.py:737
  28.2 11.0 %collective-permute-start.7 = (f32[128,512]{1,0:T(8,128)S(1)}, f32[128,512]{1,0:T(8,128)S(1)}, u32[]{:S(2)}, u32[]{:S(2)}) collective-permute-start(f32[128,512]{1,0:T(8,128)S(1)} %add_add_fusion.1), channel_id=1, source_target_pairs={{32,64},{48,80},{88,72},{120,104},{33,65},{49,81},{89,73},{121,105... | collective-permute-start | bytes 786440 | tf_op jit(solution)/shard_map/ppermute | solution.py:746
  28.9 10.3 %collective-permute-start.6 = (f32[128,512]{1,0:T(8,128)S(1)}, f32[128,512]{1,0:T(8,128)S(1)}, u32[]{:S(2)}, u32[]{:S(2)}) collective-permute-start(f32[128,512]{1,0:T(8,128)S(1)} %add_add_fusion.1), channel_id=1, source_target_pairs={{32,96},{48,112},{33,97},{49,113},{34,98},{50,114},{35,99},{51,115... | collective-permute-start | bytes 786440 | tf_op jit(solution)/shard_map/ppermute | solution.py:746
  30.2 19.9 %collective-permute-start.10 = (f32[160,512]{1,0:T(8,128)S(1)}, f32[160,512]{1,0:T(8,128)S(1)}, u32[]{:S(2)}, u32[]{:S(2)}) collective-permute-start(f32[160,512]{1,0:T(8,128)S(1)} %get-tuple-element.86.bottom), channel_id=1, source_target_pairs={{0,8},{8,16},{16,24},{24,32},{32,40},{40,48},{48,56},{1,9},{9,17},... | collective-permute-start | bytes 983048 | tf_op jit(solution)/shard_map/ppermute | solution.py:702
  33.4 16.7 %collective-permute-start.11 = (f32[160,512]{1,0:T(8,128)S(1)}, f32[160,512]{1,0:T(8,128)S(1)}, u32[]{:S(2)}, u32[]{:S(2)}) collective-permute-start(f32[160,512]{1,0:T(8,128)S(1)} %get-tuple-element.87.top), channel_id=1, source_target_pairs={{8,0},{16,8},{24,16},{32,24},{40,32},{48,40},{56,48},{9,1},{17,9},... | collective-permute-start | bytes 983048 | tf_op jit(solution)/shard_map/ppermute | solution.py:703
  39.2 12.2 %collective-permute-start.9 = (f32[128,512]{1,0:T(8,128)S(1)}, f32[128,512]{1,0:T(8,128)S(1)}, u32[]{:S(2)}, u32[]{:S(2)}) collective-permute-start(f32[128,512]{1,0:T(8,128)S(1)} %add_add_fusion.after), channel_id=1, source_target_pairs={{64,68},{65,69},{66,70},{67,71},{68,64},{69,65},{70,66},{71,67},{7... | collective-permute-start | bytes 786440 | tf_op jit(solution)/shard_map/ppermute | solution.py:760
  44.7 11.8 %collective-permute-start.12 = (f32[128,512]{1,0:T(8,128)S(1)}, f32[128,512]{1,0:T(8,128)S(1)}, u32[]{:S(2)}, u32[]{:S(2)}) collective-permute-start(f32[128,512]{1,0:T(8,128)S(1)} %add_add_fusion.after), channel_id=1, source_target_pairs={{64,70},{65,71},{66,64},{67,65},{68,66},{69,67},{70,68},{71,69},{7... | collective-permute-start | bytes 786440 | tf_op jit(solution)/shard_map/ppermute | solution.py:760
  47.1 11.1 %collective-permute-start.8 = (f32[128,512]{1,0:T(8,128)S(1)}, f32[128,512]{1,0:T(8,128)S(1)}, u32[]{:S(2)}, u32[]{:S(2)}) collective-permute-start(f32[128,512]{1,0:T(8,128)S(1)} %add_add_fusion.after), channel_id=1, source_target_pairs={{64,66},{65,67},{66,68},{67,69},{68,70},{69,71},{70,64},{71,65},{7... | collective-permute-start | bytes 786440 | tf_op jit(solution)/shard_map/ppermute | solution.py:760
  51.4 11.8 %collective-permute-start.14 = (f32[128,512]{1,0:T(8,128)S(1)}, f32[128,512]{1,0:T(8,128)S(1)}, u32[]{:S(2)}, u32[]{:S(2)}) collective-permute-start(f32[128,512]{1,0:T(8,128)S(1)} %get-tuple-element.95), channel_id=1, source_target_pairs={{0,1},{1,2},{2,3},{3,4},{4,5},{5,6},{6,7},{8,9},{9,10},{10,11},{11... | collective-permute-start | bytes 786440 | tf_op jit(solution)/shard_map/ppermute | solution.py:702
  54.6 8.7 %collective-permute-start.15 = (f32[128,512]{1,0:T(8,128)S(1)}, f32[128,512]{1,0:T(8,128)S(1)}, u32[]{:S(2)}, u32[]{:S(2)}) collective-permute-start(f32[128,512]{1,0:T(8,128)S(1)} %get-tuple-element.96), channel_id=1, source_target_pairs={{1,0},{2,1},{3,2},{4,3},{5,4},{6,5},{7,6},{9,8},{10,9},{11,10},{12... | collective-permute-start | bytes 786440 | tf_op jit(solution)/shard_map/ppermute | solution.py:703
  58.3 6.1 %collective-permute-start.13 = (f32[4,128,512]{2,1,0:T(8,128)S(1)}, f32[4,128,512]{2,1,0:T(8,128)S(1)}, u32[]{:S(2)}, u32[]{:S(2)}) collective-permute-start(f32[4,128,512]{2,1,0:T(8,128)S(1)} %pad_maximum_fusion.own.after), channel_id=1, source_target_pairs={{64,65},{65,64},{66,67},{67,66},{68,69},{69,68},{70,71},{71,70},{7... | collective-permute-start | bytes 3145736 | tf_op jit(solution)/shard_map/ppermute | solution.py:770
  63.2 2.2 %copy-start.1 = (f32[1,64,32,512]{3,2,1,0:T(8,128)S(1)}, f32[1,64,32,512]{3,2,1,0:T(8,128)}, u32[]{:S(2)}) copy-start(f32[1,64,32,512]{3,2,1,0:T(8,128)} %param.9) | copy-start | bytes 12582916

commit v14 on v13

--- a/solution.py
+++ b/solution.py
@@ -305,30 +305,20 @@
 
 def first_kernel(
     packet, previous, potential, tables, upper, lower, left, right, high, low, after,
-    done, top, bottom, first, last, field, sides, sems,
+    done, top, bottom, first, last, field, sides,
 ):
     count_r, rows, width = packet.shape
     steps = count_r // CHUNK
 
-    def copies(n):
-        part = pl.ds(n * CHUNK, CHUNK)
-        return pltpu.make_async_copy(packet.at[part], field.at[pl.ds(HALO + n * CHUNK, CHUNK)], sems.at[n])
-
-    for n in range(steps):
-        copies(n).start()
+    field[HALO : HALO + count_r] = packet[...]
     field[0:HALO] = jnp.zeros((HALO, rows, width), F32)
     field[HALO + count_r :] = jnp.zeros((HALO, rows, width), F32)
     put_sides(sides, left, right, count_r)
-    copies(0).wait()
 
     def put(k, lanes, value):
         done[k, :, lanes] = value
 
     def body(n, carry):
-        @pl.when(n + 1 < steps)
-        def _():
-            copies(n + 1).wait()
-
         advance(n, CHUNK, field, sides, previous, potential, tables, high, low, put)
         for k in range(CHUNK):
             for r in range(HALO):
@@ -356,13 +346,12 @@
     sides = jax.ShapeDtypeStruct((HALO * count_r, width), F32)
     return pl.pallas_call(
         first_kernel,
-        in_specs=[HBM, *[VMEM] * 9, ANY],
+        in_specs=[*[VMEM] * 10, ANY],
         out_specs=[VMEM] * 5,
         out_shape=[jax.ShapeDtypeStruct(packet.shape, F32), ends, ends, sides, sides],
         scratch_shapes=[
             pltpu.VMEM((count_r + 2 * HALO, rows, width), F32),
             pltpu.VMEM((count_r, 8, width), F32),
-            pltpu.SemaphoreType.DMA((count_r // CHUNK,)),
         ],
         compiler_params=pltpu.CompilerParams(vmem_limit_bytes=14 * MIB),
         cost_estimate=pl.CostEstimate(flops=7_000_000_000, bytes_accessed=20 * MIB, transcendentals=0),
@@ -736,7 +725,7 @@
     relays = [count_rr + half - 1, count_rr + start, high_side, low_side]
     crossed = [lax.ppermute(table, plane, [(start, relay)]) for relay in relays]
     one, *edges = first_iteration(
-        packet, near_previous, near_potential, tables, upper, lower, left, right, high, low, table
+        near_packet, near_previous, near_potential, tables, upper, lower, left, right, high, low, table
     )
     *crossed, one, edges = lax.optimization_barrier((*crossed, one, edges))
     piece = sum(crossed)

time: 79.6 us -> 78.9 us (level)
  Pallas kernels: 33.5 us -> 32.5 us
    pallas_call x1, Pallas kernels: 8.97 us -> 8 us  [first_iteration(): pl.pallas_call(first_kernel, in_specs=[*[VMEM] * 10, ANY], out_specs=[VME...]
  transfers between devices with their start and end apart: 16 -> 16, of which waited for: 3 -> 3; matrix products, arithmetic and copies ran while one was open for 0% -> 0% of each run, Pallas kernels for 22% -> 21%
where the time goes in v14:
time: 78.9 us; the launch traced here: 78.4 us
  starting transfers between devices  38.5 us (49%)
  Pallas kernels  32.5 us (41%)
  waiting for transfers between devices  4.97 us (6%)
  local copies, waits for them, and re-layouts  1.35 us (2%)
  between operations  0.95 us (1%)
    pallas_call x1, Pallas kernels, last_iteration(): pl.pallas_call(last_kernel, in_specs=[VMEM] * 20, out_specs=[HBM, HBM], o...  13.8 us
    ppermute x3, starting transfers between devices, around(): return lax.ppermute(spread, line, pairs)  10.7 us
    ppermute x3, starting transfers between devices, neighbours(): lax.ppermute(upward, axis, [(i, i + 1) for i in range(count - 1)])  10.4 us
    ppermute x3, starting transfers between devices, neighbours(): lax.ppermute(downward, axis, [(i + 1, i) for i in range(count - 1)])  9.61 us
    pallas_call x1, Pallas kernels, first_iteration(): pl.pallas_call(first_kernel, in_specs=[*[VMEM] * 10, ANY], out_specs=[VME...  8 us
    pallas_call x1, Pallas kernels, matrices_of(): pl.pallas_call(stencil_kernel, in_specs=[VMEM, VMEM, ANY], out_specs=[VME...  4.17 us
    pallas_call x2, Pallas kernels, own_source(): pl.pallas_call(functools.partial(own_source_kernel, begin=begin), in_spec...  3.47 us
    ppermute x4, starting transfers between devices, local(): crossed = [lax.ppermute(table, plane, [(start, relay)]) for relay in relays]  3.24 us
  transfers between devices with their start and end apart: 16, of which 3 were waited for; matrix products, arithmetic and copies ran while one was open for 0% of the time, Pallas kernels for 21%

profile of v14, /device:TPU:7, one launch (start us, length us, event | category | flops | bytes accessed | tf_op | source)
XLA Modules:
  0.0 78.4 jit_solution(15488093942600501346)
XLA Ops:
  0.6 0.0 copy-start.3
  0.6 2.1 %prepare.1 = (f32[32,128]{1,0:T(8,128)S(1)}, f32[32,128]{1,0:T(8,128)S(1)}, f32[176,512]{1,0:T(8,128)S(1)}, f32[176,512]{1,0:T(8,128)S(1)}, f32[10,32,128]{2,1,0:T(8,128)S(1)}) custom-call(f32[64,32,512]{2,1,0:T(8,128)} %bitcast.24, f32[64,32,512]{2,1,0:T(8,128)} %bitcast.21, f32[64,32,512]{2,1,0:T(8,128)} %bitcast.28, f32[32,64]{1,0:T(8,128)} %bitcast.39, ...), custom_call_target="tpu_custom_call" | custom-call | flops 1000000 | bytes 6291456 | tf_op jit(solution)/shard_map/prepare/pallas_call | solution.py:233
  2.8 4.1 %collective-permute-start = (f32[176,512]{1,0:T(8,128)S(1)}, f32[176,512]{1,0:T(8,128)S(1)}, u32[]{:S(2)}, u32[]{:S(2)}) collective-permute-start(f32[176,512]{1,0:T(8,128)S(1)} %get-tuple-element.62), channel_id=1, source_target_pairs={{0,1},{1,2},{2,3},{3,4},{4,5},{5,6},{6,7},{8,9},{9,10},{10,11},{11... | collective-permute-start | bytes 1081352 | tf_op jit(solution)/shard_map/ppermute | solution.py:691
  6.9 1.9 %collective-permute-start.1 = (f32[176,512]{1,0:T(8,128)S(1)}, f32[176,512]{1,0:T(8,128)S(1)}, u32[]{:S(2)}, u32[]{:S(2)}) collective-permute-start(f32[176,512]{1,0:T(8,128)S(1)} %get-tuple-element.63.after), channel_id=1, source_target_pairs={{1,0},{2,1},{3,2},{4,3},{5,4},{6,5},{7,6},{9,8},{10,9},{11,10},{12... | collective-permute-start | bytes 1081352 | tf_op jit(solution)/shard_map/ppermute | solution.py:692
  8.8 0.0 copy-done.3
  8.8 4.2 %stencil_matrix.1 = (bf16[2048,256]{1,0:T(8,128)(2,1)S(1)}, bf16[2048,256]{1,0:T(8,128)(2,1)S(1)}, bf16[2048,256]{1,0:T(8,128)(2,1)S(1)}, bf16[2048,256]{1,0:T(8...) custom-call(f32[10,32,128]{2,1,0:T(8,128)S(1)} %get-tuple-element.61.tables, ...), custom_call_target="tpu_custom_call" | custom-call | flops 15000000 | bytes 6291456 | tf_op jit(solution)/shard_map/stencil_matrix/pallas_call | solution.py:417
  13.0 0.0 collective-permute-done.left
  13.0 2.6 %collective-permute-done.1.right = f32[176,512]{1,0:T(8,128)S(1)} collective-permute-done((f32[176,512]{1,0:T(8,128)S(1)}, f32[176,512]{1,0:T(8,128)S(1)}, u32[]{:S(2)}, u32[]{:S(2)}) %collective-permute-start.1) | collective-permute-done | bytes 360480 | tf_op jit(solution)/shard_map/ppermute | solution.py:692
  15.6 0.0 copy-start
  15.6 0.0 copy-start.1
  15.6 0.0 copy-start.2
  15.7 0.8 %collective-permute-start.5 = (f32[128,512]{1,0:T(8,128)S(1)}, f32[128,512]{1,0:T(8,128)S(1)}, u32[]{:S(2)}, u32[]{:S(2)}) collective-permute-start(f32[128,512]{1,0:T(8,128)S(1)} %both_bands.1.after), channel_id=1, source_target_pairs={{56,32},{57,33},{58,34},{59,35},{60,36},{61,37},{62,38},{63,39}} | collective-permute-start | bytes 786440 | tf_op jit(solution)/shard_map/ppermute | solution.py:726
  16.5 0.8 %collective-permute-start.4 = (f32[128,512]{1,0:T(8,128)S(1)}, f32[128,512]{1,0:T(8,128)S(1)}, u32[]{:S(2)}, u32[]{:S(2)}) collective-permute-start(f32[128,512]{1,0:T(8,128)S(1)} %both_bands.1.after), channel_id=1, source_target_pairs={{56,48},{57,49},{58,50},{59,51},{60,52},{61,53},{62,54},{63,55}} | collective-permute-start | bytes 786440 | tf_op jit(solution)/shard_map/ppermute | solution.py:726
  17.3 0.8 %collective-permute-start.3 = (f32[128,512]{1,0:T(8,128)S(1)}, f32[128,512]{1,0:T(8,128)S(1)}, u32[]{:S(2)}, u32[]{:S(2)}) collective-permute-start(f32[128,512]{1,0:T(8,128)S(1)} %both_bands.1.after), channel_id=1, source_target_pairs={{56,120},{57,121},{58,122},{59,123},{60,124},{61,125},{62,126},{63... | collective-permute-start | bytes 786440 | tf_op jit(solution)/shard_map/ppermute | solution.py:726
  18.1 0.8 %collective-permute-start.2 = (f32[128,512]{1,0:T(8,128)S(1)}, f32[128,512]{1,0:T(8,128)S(1)}, u32[]{:S(2)}, u32[]{:S(2)}) collective-permute-start(f32[128,512]{1,0:T(8,128)S(1)} %both_bands.1.after), channel_id=1, source_target_pairs={{56,88},{57,89},{58,90},{59,91},{60,92},{61,93},{62,94},{63,95}} | collective-permute-start | bytes 786440 | tf_op jit(solution)/shard_map/ppermute | solution.py:726
  18.9 0.0 copy-done
  18.9 0.1 copy-done.1
  19.1 1.2 %copy-done.2 = f32[1,64,32,512]{3,2,1,0:T(8,128)S(1)} copy-done((f32[1,64,32,512]{3,2,1,0:T(8,128)S(1)}, f32[1,64,32,512]{3,2,1,0:T(8,128)}, u32[]{:S(2)}) %copy-start.2) | copy-done | bytes 4194328
  20.3 8.0 %first_iteration.1 = (f32[64,32,512]{2,1,0:T(8,128)S(1)}, f32[160,512]{1,0:T(8,128)S(1)}, f32[160,512]{1,0:T(8,128)S(1)}, f32[128,512]{1,0:T(8,128)S(1)}, f32[128,512]{1,0:T(8,128)S(1)}) custom-call(f32[64,32,512]{2,1,0:T(8,128)S(1)} %bitcast.26, f32[64,32,512]{2,1,0:T(8,128)S(1)} %bitcast.23, f32[64,32,512]{2,1,0:T(8,128)S(1)} %bitcast.30, ...), custom_call_target="tpu_custom_call" | custom-call | flops 7000000000 | bytes 20971520 | tf_op jit(solution)/shard_map/first_iteration/pallas_call | solution.py:347
  28.3 0.0 collective-permute-done.5
  28.3 0.0 collective-permute-done.4
  28.3 0.0 collective-permute-done.3
  28.3 0.0 collective-permute-done.2
  28.3 0.1 add_add_fusion.1
  28.4 0.7 collective-permute-start.7
  29.1 1.3 %collective-permute-start.6 = (f32[128,512]{1,0:T(8,128)S(1)}, f32[128,512]{1,0:T(8,128)S(1)}, u32[]{:S(2)}, u32[]{:S(2)}) collective-permute-start(f32[128,512]{1,0:T(8,128)S(1)} %add_add_fusion.1), channel_id=1, source_target_pairs={{32,96},{48,112},{33,97},{49,113},{34,98},{50,114},{35,99},{51,115... | collective-permute-start | bytes 786440 | tf_op jit(solution)/shard_map/ppermute | solution.py:735
  30.4 3.2 %collective-permute-start.10 = (f32[160,512]{1,0:T(8,128)S(1)}, f32[160,512]{1,0:T(8,128)S(1)}, u32[]{:S(2)}, u32[]{:S(2)}) collective-permute-start(f32[160,512]{1,0:T(8,128)S(1)} %get-tuple-element.86.bottom), channel_id=1, source_target_pairs={{0,8},{8,16},{16,24},{24,32},{32,40},{40,48},{48,56},{1,9},{9,17},... | collective-permute-start | bytes 983048 | tf_op jit(solution)/shard_map/ppermute | solution.py:691
  33.6 5.8 %collective-permute-start.11 = (f32[160,512]{1,0:T(8,128)S(1)}, f32[160,512]{1,0:T(8,128)S(1)}, u32[]{:S(2)}, u32[]{:S(2)}) collective-permute-start(f32[160,512]{1,0:T(8,128)S(1)} %get-tuple-element.87.top), channel_id=1, source_target_pairs={{8,0},{16,8},{24,16},{32,24},{40,32},{48,40},{56,48},{9,1},{17,9},... | collective-permute-start | bytes 983048 | tf_op jit(solution)/shard_map/ppermute | solution.py:692
  39.4 0.0 collective-permute-done.7
  39.4 0.0 collective-permute-done.6
  39.4 0.1 add_add_fusion.after
  39.5 5.4 %collective-permute-start.9 = (f32[128,512]{1,0:T(8,128)S(1)}, f32[128,512]{1,0:T(8,128)S(1)}, u32[]{:S(2)}, u32[]{:S(2)}) collective-permute-start(f32[128,512]{1,0:T(8,128)S(1)} %add_add_fusion.after), channel_id=1, source_target_pairs={{64,68},{65,69},{66,70},{67,71},{68,64},{69,65},{70,66},{71,67},{7... | collective-permute-start | bytes 786440 | tf_op jit(solution)/shard_map/ppermute | solution.py:749
  44.9 2.5 %collective-permute-start.12 = (f32[128,512]{1,0:T(8,128)S(1)}, f32[128,512]{1,0:T(8,128)S(1)}, u32[]{:S(2)}, u32[]{:S(2)}) collective-permute-start(f32[128,512]{1,0:T(8,128)S(1)} %add_add_fusion.after), channel_id=1, source_target_pairs={{64,70},{65,71},{66,64},{67,65},{68,66},{69,67},{70,68},{71,69},{7... | collective-permute-start | bytes 786440 | tf_op jit(solution)/shard_map/ppermute | solution.py:749
  47.3 2.8 %collective-permute-start.8 = (f32[128,512]{1,0:T(8,128)S(1)}, f32[128,512]{1,0:T(8,128)S(1)}, u32[]{:S(2)}, u32[]{:S(2)}) collective-permute-start(f32[128,512]{1,0:T(8,128)S(1)} %add_add_fusion.after), channel_id=1, source_target_pairs={{64,66},{65,67},{66,68},{67,69},{68,70},{69,71},{70,64},{71,65},{7... | collective-permute-start | bytes 786440 | tf_op jit(solution)/shard_map/ppermute | solution.py:749
  50.2 0.0 collective-permute-done.10.up
  50.2 0.0 collective-permute-done.11.down
  50.2 0.9 %finish_edges.1 = (bf16[384,512]{1,0:T(8,128)(2,1)S(1)}, bf16[384,512]{1,0:T(8,128)(2,1)S(1)}, f32[64,512]{1,0:T(8,128)S(1)}, f32[64,512]{1,0:T(8,128)S(1)}, f32...) custom-call(f32[160,512]{1,0:T(8,128)S(1)} %collective-permute-done.10.up, ...), custom_call_target="tpu_custom_call" | custom-call | flops 2000000 | bytes 3145728 | tf_op jit(solution)/shard_map/finish_edges/pallas_call | solution.py:496
  51.1 0.4 collective-permute-done.9
  51.5 3.1 %collective-permute-start.14 = (f32[128,512]{1,0:T(8,128)S(1)}, f32[128,512]{1,0:T(8,128)S(1)}, u32[]{:S(2)}, u32[]{:S(2)}) collective-permute-start(f32[128,512]{1,0:T(8,128)S(1)} %get-tuple-element.95), channel_id=1, source_target_pairs={{0,1},{1,2},{2,3},{3,4},{4,5},{5,6},{6,7},{8,9},{9,10},{10,11},{11... | collective-permute-start | bytes 786440 | tf_op jit(solution)/shard_map/ppermute | solution.py:691
  54.6 1.9 %collective-permute-start.15 = (f32[128,512]{1,0:T(8,128)S(1)}, f32[128,512]{1,0:T(8,128)S(1)}, u32[]{:S(2)}, u32[]{:S(2)}) collective-permute-start(f32[128,512]{1,0:T(8,128)S(1)} %get-tuple-element.96), channel_id=1, source_target_pairs={{1,0},{2,1},{3,2},{4,3},{5,4},{6,5},{7,6},{9,8},{10,9},{11,10},{12... | collective-permute-start | bytes 786440 | tf_op jit(solution)/shard_map/ppermute | solution.py:692
  56.5 0.0 collective-permute-done.12
  56.5 1.9 %collective-permute-done.8 = f32[128,512]{1,0:T(8,128)S(1)} collective-permute-done((f32[128,512]{1,0:T(8,128)S(1)}, f32[128,512]{1,0:T(8,128)S(1)}, u32[]{:S(2)}, u32[]{:S(2)}) %collective-permute-start.8) | collective-permute-done | bytes 262176 | tf_op jit(solution)/shard_map/ppermute | solution.py:749
  58.5 0.1 pad_maximum_fusion.own.after
  58.6 2.6 %collective-permute-start.13 = (f32[4,128,512]{2,1,0:T(8,128)S(1)}, f32[4,128,512]{2,1,0:T(8,128)S(1)}, u32[]{:S(2)}, u32[]{:S(2)}) collective-permute-start(f32[4,128,512]{2,1,0:T(8,128)S(1)} %pad_maximum_fusion.own.after), channel_id=1, source_target_pairs={{64,65},{65,64},{66,67},{67,66},{68,69},{69,68},{70,71},{71,70},{7... | collective-permute-start | bytes 3145736 | tf_op jit(solution)/shard_map/ppermute | solution.py:759
  61.2 2.3 %own_source.2 = (f32[48,32,512]{2,1,0:T(8,128)S(1)}, f32[384,512]{1,0:T(8,128)S(1)}) custom-call(f32[64,32,512]{2,1,0:T(8,128)S(1)} %get-tuple-element.98.one, f32[4,32,512]{2,1,0:T(8,128)S(1)} %get-tuple-element.105.added, bf16[2048,256]{1,0:T(8,128)(2,1)S(1)} %get-tuple-element.99.stencil_high.own_high, ...), custom_call_target="tpu_custom_call" | custom-call | flops 1000000 | bytes 2000 | tf_op jit(solution)/shard_map/own_source/pallas_call | solution.py:557
  63.4 0.0 collective-permute-done.14.left
  63.5 0.0 collective-permute-done.15.right
  63.5 1.2 %own_source.3 = (f32[16,32,512]{2,1,0:T(8,128)S(1)}, f32[8,512]{1,0:T(8,128)}) custom-call(f32[64,32,512]{2,1,0:T(8,128)S(1)} %get-tuple-element.98.one, f32[4,32,512]{2,1,0:T(8,128)S(1)} %get-tuple-element.105.added, bf16[2048,256]{1,0:T(8,128)(2,1)S(1)} %get-tuple-element.99.stencil_high.own_high, ...), custom_call_target="tpu_custom_call" | custom-call | flops 99999997952 | bytes 200000000 | tf_op jit(solution)/shard_map/own_source/pallas_call | solution.py:557
  64.7 0.0 collective-permute-done.13.other
  64.7 13.8 %last_iteration.1 = (f32[64,32,512]{2,1,0:T(8,128)}, f32[64,32,512]{2,1,0:T(8,128)}) custom-call(f32[48,32,512]{2,1,0:T(8,128)S(1)} %get-tuple-element.108.after.one, f32[16,32,512]{2,1,0:T(8,128)S(1)} %get-tuple-element.109.one_end, f32[384,512]{1,0:T(8,128)S(1)} %get-tuple-element.110.edge_source, f32[64,32,512]{2,1,0:T(8,128)S(1)} %bitcast.27, ...), custom_call_target="tpu_custom_call" | custom-call | flops 14000000000 | bytes 37748736 | tf_op jit(solution)/shard_map/last_iteration/pallas_call | solution.py:669
  (1 shorter events, 0.0 us)
Async XLA Ops:
  0.6 8.2 %copy-start.3 = (f32[1,512,512]{2,1,0:T(8,128)S(1)}, f32[1,512,512]{2,1,0:T(8,128)}, u32[]{:S(2)}) copy-start(f32[1,512,512]{2,1,0:T(8,128)} %param.13) | copy-start | bytes 3145732
  2.8 10.2 %collective-permute-start = (f32[176,512]{1,0:T(8,128)S(1)}, f32[176,512]{1,0:T(8,128)S(1)}, u32[]{:S(2)}, u32[]{:S(2)}) collective-permute-start(f32[176,512]{1,0:T(8,128)S(1)} %get-tuple-element.62), channel_id=1, source_target_pairs={{0,1},{1,2},{2,3},{3,4},{4,5},{5,6},{6,7},{8,9},{9,10},{10,11},{11... | collective-permute-start | bytes 1081352 | tf_op jit(solution)/shard_map/ppermute | solution.py:691
  6.9 8.7 %collective-permute-start.1 = (f32[176,512]{1,0:T(8,128)S(1)}, f32[176,512]{1,0:T(8,128)S(1)}, u32[]{:S(2)}, u32[]{:S(2)}) collective-permute-start(f32[176,512]{1,0:T(8,128)S(1)} %get-tuple-element.63.after), channel_id=1, source_target_pairs={{1,0},{2,1},{3,2},{4,3},{5,4},{6,5},{7,6},{9,8},{10,9},{11,10},{12... | collective-permute-start | bytes 1081352 | tf_op jit(solution)/shard_map/ppermute | solution.py:692
  15.6 3.3 %copy-start = (f32[1,64,32,512]{3,2,1,0:T(8,128)S(1)}, f32[1,64,32,512]{3,2,1,0:T(8,128)}, u32[]{:S(2)}) copy-start(f32[1,64,32,512]{3,2,1,0:T(8,128)} %param.10) | copy-start | bytes 12582916
  15.6 3.5 %copy-start.1 = (f32[1,64,32,512]{3,2,1,0:T(8,128)S(1)}, f32[1,64,32,512]{3,2,1,0:T(8,128)}, u32[]{:S(2)}) copy-start(f32[1,64,32,512]{3,2,1,0:T(8,128)} %param.9) | copy-start | bytes 12582916
  15.6 4.7 %copy-start.2 = (f32[1,64,32,512]{3,2,1,0:T(8,128)S(1)}, f32[1,64,32,512]{3,2,1,0:T(8,128)}, u32[]{:S(2)}) copy-start(f32[1,64,32,512]{3,2,1,0:T(8,128)} %param.11) | copy-start | bytes 12582916
  15.7 12.6 %collective-permute-start.5 = (f32[128,512]{1,0:T(8,128)S(1)}, f32[128,512]{1,0:T(8,128)S(1)}, u32[]{:S(2)}, u32[]{:S(2)}) collective-permute-start(f32[128,512]{1,0:T(8,128)S(1)} %both_bands.1.after), channel_id=1, source_target_pairs={{56,32},{57,33},{58,34},{59,35},{60,36},{61,37},{62,38},{63,39}} | collective-permute-start | bytes 786440 | tf_op jit(solution)/shard_map/ppermute | solution.py:726
  16.5 11.8 %collective-permute-start.4 = (f32[128,512]{1,0:T(8,128)S(1)}, f32[128,512]{1,0:T(8,128)S(1)}, u32[]{:S(2)}, u32[]{:S(2)}) collective-permute-start(f32[128,512]{1,0:T(8,128)S(1)} %both_bands.1.after), channel_id=1, source_target_pairs={{56,48},{57,49},{58,50},{59,51},{60,52},{61,53},{62,54},{63,55}} | collective-permute-start | bytes 786440 | tf_op jit(solution)/shard_map/ppermute | solution.py:726
  17.3 11.0 %collective-permute-start.3 = (f32[128,512]{1,0:T(8,128)S(1)}, f32[128,512]{1,0:T(8,128)S(1)}, u32[]{:S(2)}, u32[]{:S(2)}) collective-permute-start(f32[128,512]{1,0:T(8,128)S(1)} %both_bands.1.after), channel_id=1, source_target_pairs={{56,120},{57,121},{58,122},{59,123},{60,124},{61,125},{62,126},{63... | collective-permute-start | bytes 786440 | tf_op jit(solution)/shard_map/ppermute | solution.py:726
  18.1 10.2 %collective-permute-start.2 = (f32[128,512]{1,0:T(8,128)S(1)}, f32[128,512]{1,0:T(8,128)S(1)}, u32[]{:S(2)}, u32[]{:S(2)}) collective-permute-start(f32[128,512]{1,0:T(8,128)S(1)} %both_bands.1.after), channel_id=1, source_target_pairs={{56,88},{57,89},{58,90},{59,91},{60,92},{61,93},{62,94},{63,95}} | collective-permute-start | bytes 786440 | tf_op jit(solution)/shard_map/ppermute | solution.py:726
  28.4 11.0 %collective-permute-start.7 = (f32[128,512]{1,0:T(8,128)S(1)}, f32[128,512]{1,0:T(8,128)S(1)}, u32[]{:S(2)}, u32[]{:S(2)}) collective-permute-start(f32[128,512]{1,0:T(8,128)S(1)} %add_add_fusion.1), channel_id=1, source_target_pairs={{32,64},{48,80},{88,72},{120,104},{33,65},{49,81},{89,73},{121,105... | collective-permute-start | bytes 786440 | tf_op jit(solution)/shard_map/ppermute | solution.py:735
  29.1 10.3 %collective-permute-start.6 = (f32[128,512]{1,0:T(8,128)S(1)}, f32[128,512]{1,0:T(8,128)S(1)}, u32[]{:S(2)}, u32[]{:S(2)}) collective-permute-start(f32[128,512]{1,0:T(8,128)S(1)} %add_add_fusion.1), channel_id=1, source_target_pairs={{32,96},{48,112},{33,97},{49,113},{34,98},{50,114},{35,99},{51,115... | collective-permute-start | bytes 786440 | tf_op jit(solution)/shard_map/ppermute | solution.py:735
  30.4 19.8 %collective-permute-start.10 = (f32[160,512]{1,0:T(8,128)S(1)}, f32[160,512]{1,0:T(8,128)S(1)}, u32[]{:S(2)}, u32[]{:S(2)}) collective-permute-start(f32[160,512]{1,0:T(8,128)S(1)} %get-tuple-element.86.bottom), channel_id=1, source_target_pairs={{0,8},{8,16},{16,24},{24,32},{32,40},{40,48},{48,56},{1,9},{9,17},... | collective-permute-start | bytes 983048 | tf_op jit(solution)/shard_map/ppermute | solution.py:691
  33.6 16.6 %collective-permute-start.11 = (f32[160,512]{1,0:T(8,128)S(1)}, f32[160,512]{1,0:T(8,128)S(1)}, u32[]{:S(2)}, u32[]{:S(2)}) collective-permute-start(f32[160,512]{1,0:T(8,128)S(1)} %get-tuple-element.87.top), channel_id=1, source_target_pairs={{8,0},{16,8},{24,16},{32,24},{40,32},{48,40},{56,48},{9,1},{17,9},... | collective-permute-start | bytes 983048 | tf_op jit(solution)/shard_map/ppermute | solution.py:692
  39.5 12.1 %collective-permute-start.9 = (f32[128,512]{1,0:T(8,128)S(1)}, f32[128,512]{1,0:T(8,128)S(1)}, u32[]{:S(2)}, u32[]{:S(2)}) collective-permute-start(f32[128,512]{1,0:T(8,128)S(1)} %add_add_fusion.after), channel_id=1, source_target_pairs={{64,68},{65,69},{66,70},{67,71},{68,64},{69,65},{70,66},{71,67},{7... | collective-permute-start | bytes 786440 | tf_op jit(solution)/shard_map/ppermute | solution.py:749
  44.9 11.7 %collective-permute-start.12 = (f32[128,512]{1,0:T(8,128)S(1)}, f32[128,512]{1,0:T(8,128)S(1)}, u32[]{:S(2)}, u32[]{:S(2)}) collective-permute-start(f32[128,512]{1,0:T(8,128)S(1)} %add_add_fusion.after), channel_id=1, source_target_pairs={{64,70},{65,71},{66,64},{67,65},{68,66},{69,67},{70,68},{71,69},{7... | collective-permute-start | bytes 786440 | tf_op jit(solution)/shard_map/ppermute | solution.py:749
  47.3 11.1 %collective-permute-start.8 = (f32[128,512]{1,0:T(8,128)S(1)}, f32[128,512]{1,0:T(8,128)S(1)}, u32[]{:S(2)}, u32[]{:S(2)}) collective-permute-start(f32[128,512]{1,0:T(8,128)S(1)} %add_add_fusion.after), channel_id=1, source_target_pairs={{64,66},{65,67},{66,68},{67,69},{68,70},{69,71},{70,64},{71,65},{7... | collective-permute-start | bytes 786440 | tf_op jit(solution)/shard_map/ppermute | solution.py:749
  51.5 11.9 %collective-permute-start.14 = (f32[128,512]{1,0:T(8,128)S(1)}, f32[128,512]{1,0:T(8,128)S(1)}, u32[]{:S(2)}, u32[]{:S(2)}) collective-permute-start(f32[128,512]{1,0:T(8,128)S(1)} %get-tuple-element.95), channel_id=1, source_target_pairs={{0,1},{1,2},{2,3},{3,4},{4,5},{5,6},{6,7},{8,9},{9,10},{10,11},{11... | collective-permute-start | bytes 786440 | tf_op jit(solution)/shard_map/ppermute | solution.py:691
  54.6 8.8 %collective-permute-start.15 = (f32[128,512]{1,0:T(8,128)S(1)}, f32[128,512]{1,0:T(8,128)S(1)}, u32[]{:S(2)}, u32[]{:S(2)}) collective-permute-start(f32[128,512]{1,0:T(8,128)S(1)} %get-tuple-element.96), channel_id=1, source_target_pairs={{1,0},{2,1},{3,2},{4,3},{5,4},{6,5},{7,6},{9,8},{10,9},{11,10},{12... | collective-permute-start | bytes 786440 | tf_op jit(solution)/shard_map/ppermute | solution.py:692
  58.6 6.1 %collective-permute-start.13 = (f32[4,128,512]{2,1,0:T(8,128)S(1)}, f32[4,128,512]{2,1,0:T(8,128)S(1)}, u32[]{:S(2)}, u32[]{:S(2)}) collective-permute-start(f32[4,128,512]{2,1,0:T(8,128)S(1)} %pad_maximum_fusion.own.after), channel_id=1, source_target_pairs={{64,65},{65,64},{66,67},{67,66},{68,69},{69,68},{70,71},{71,70},{7... | collective-permute-start | bytes 3145736 | tf_op jit(solution)/shard_map/ppermute | solution.py:759
